TPU v7x, 32 devices: a whole 2x2x4 slice. The times are simulated.
32 devices in a mesh: groups: 2 (over x), replica: 8 (over z, y), tensor: 2 (over core).
Axes of the slice: x: 2, y: 2, z: 4, core: 2. Of those that a mesh axis runs over, the one named last changes fastest.
Arguments:
- hidden_in: bfloat16 [64, 8192], P(('groups', 'replica'), 'tensor'), parts along dimension 0, may hold values from -0.0625 to 0.0625
- queries: bfloat16 [64, 4096], P(('groups', 'replica'), 'tensor'), parts along dimension 0, may hold values from -5.5 to 5.5
- stored_keys: bfloat16 [64, 1024, 512], P(('groups', 'replica'), None, 'tensor'), parts along dimension 0, may hold values from -5.5 to 5.5
- stored_values: bfloat16 [64, 1024, 512], P(('groups', 'replica'), None, 'tensor'), parts along dimension 0, may hold values from -6 to 6
- fresh_token_key: bfloat16 [64, 512], P(('groups', 'replica'), 'tensor'), parts along dimension 0, may hold values from -5.5 to 5.5
- lengths: int32 [64], P(('groups', 'replica')), parts along dimension 0, may hold values from 1 to 1024, as said below
- served_value_weight: bfloat16 [8192, 512], P(None, 'tensor'), may hold values from -6 to 6
- adapter_in: bfloat16 [128, 8192], P('groups', 'replica'), parts along dimension 0, may hold values from -6 to 6
- adapter_out: bfloat16 [128, 512], P(('groups', 'replica'), 'tensor'), parts along dimension 0, may hold values from -0.75 to 0.75
- owner_rank: int32 [16], P('groups'), parts along dimension 0, may hold values from 0 to 7, each once
Outputs:
- merged: bfloat16 [16384, 512], P('groups', 'tensor'), parts along dimension 0
- fresh_token_value: bfloat16 [64, 512], P(('groups', 'replica'), 'tensor'), parts along dimension 0
- attended: bfloat16 [64, 4096], P(('groups', 'replica'), 'tensor'), parts along dimension 0
There are 2 independent parts, one for each index of `groups`. A program takes and returns all parts, laid end to end along the dimension named above; an argument that names none is the same for every part. Nothing has to cross between parts.
Inputs may be any that keep to these rules, and one draw needn't show every extreme that they name: Row lengths; some row has exactly 1024. `owner_rank`: each slot named once.
All inputs are finite; a program needn't handle non-finite values.
Results may differ from a plain program's by a relative error of at most 0.0054.
Values may be sent and summed in bfloat16 or wider, within the bound.
No kernel may reach another device: no remote copies, remote signals or barrier semaphores. Data moves between devices by JAX's collectives and lax.ppermute only.
A program may use at most 64 MiB of HBM per device.

v0:
```python
import jax
import jax.numpy as jnp
from jax import lax
from jax.sharding import PartitionSpec as P

HEAD_SIZE = 128


adapter_scale = 2.0


def fold_rows(factor_rows, up_factor, rows_served):
    weight_update = lax.dot_general(
        factor_rows, up_factor, (((0,), (0,)), ((), ())), preferred_element_type=jnp.float32
    )
    return (rows_served.astype(jnp.float32) + adapter_scale * weight_update).astype(jnp.bfloat16)


def body(
    hidden_in,
    queries,
    stored_keys,
    stored_values,
    fresh_token_key,
    lengths,
    served_value_weight,
    adapter_in,
    adapter_out,
    owner_rank,
):
    features = lax.all_gather(hidden_in, "tensor", axis=1, tiled=True)
    up_factor = lax.all_gather(adapter_out, "replica", axis=0, tiled=True)
    row_count = queries.shape[0]
    local_heads = stored_keys.shape[2] // HEAD_SIZE
    query_group_size = queries.shape[1] // (local_heads * HEAD_SIZE)
    cache_len = stored_keys.shape[1]
    scaling = 1.0 / HEAD_SIZE**0.5
    head_queries = queries.reshape(row_count, local_heads, query_group_size, HEAD_SIZE)
    head_keys = stored_keys.reshape(row_count, cache_len, local_heads, HEAD_SIZE)
    head_values = stored_values.reshape(row_count, cache_len, local_heads, HEAD_SIZE)
    self_key = fresh_token_key.reshape(row_count, local_heads, HEAD_SIZE)
    scores = (
        jnp.einsum("rhgd,rlhd->rhgl", head_queries, head_keys, preferred_element_type=jnp.float32)
        * scaling
    )
    own_score = (
        jnp.einsum("rhgd,rhd->rhg", head_queries, self_key, preferred_element_type=jnp.float32)
        * scaling
    )
    valid = jnp.arange(cache_len, dtype=jnp.int32)[None, :] < lengths[:, None]
    valid = valid[:, None, None, :]
    masked = jnp.where(valid, scores, -1e30)
    largest = jnp.maximum(jnp.max(masked, axis=-1), own_score)
    cached_exp = jnp.where(valid, jnp.exp(masked - largest[..., None]), 0.0)
    own_exp = jnp.exp(own_score - largest)
    normaliser = jnp.sum(cached_exp, axis=-1) + own_exp
    weights_cached = (cached_exp / normaliser[..., None]).astype(jnp.bfloat16)
    weight_own = (own_exp / normaliser).astype(jnp.bfloat16)
    context = jnp.einsum(
        "rhgl,rlhd->rhgd", weights_cached, head_values, preferred_element_type=jnp.float32
    )
    shard_width = adapter_in.shape[1]
    replicas = lax.axis_size("replica")
    model_width = served_value_weight.shape[0]
    gathered = lax.all_gather(adapter_in, "replica", axis=1, tiled=True)
    ordered = jnp.take(
        gathered.reshape(gathered.shape[0], replicas, shard_width), owner_rank, axis=1
    )
    merged = fold_rows(
        ordered.reshape(gathered.shape[0], model_width), up_factor, served_value_weight
    )
    fresh_token_value = jnp.dot(features, merged, preferred_element_type=jnp.float32).astype(
        jnp.bfloat16
    )
    self_value = fresh_token_value.reshape(row_count, local_heads, HEAD_SIZE).astype(jnp.float32)
    context = context + weight_own.astype(jnp.float32)[..., None] * self_value[:, :, None, :]
    attended = context.reshape(row_count, queries.shape[1]).astype(jnp.bfloat16)
    return (merged, fresh_token_value, attended)


def solution(mesh):
    in_specs = (
        P(("groups", "replica"), "tensor"),
        P(("groups", "replica"), "tensor"),
        P(("groups", "replica"), None, "tensor"),
        P(("groups", "replica"), None, "tensor"),
        P(("groups", "replica"), "tensor"),
        P(("groups", "replica")),
        P(None, "tensor"),
        P("groups", "replica"),
        P(("groups", "replica"), "tensor"),
        P("groups"),
    )
    out_specs = (
        P("groups", "tensor"),
        P(("groups", "replica"), "tensor"),
        P(("groups", "replica"), "tensor"),
    )
    return jax.shard_map(body, mesh=mesh, in_specs=in_specs, out_specs=out_specs, check_vma=False)
```

profile of v0, /device:TPU:0, one launch (start us, length us, event | category | flops | bytes accessed | tf_op | source)
XLA Modules:
  0.0 73.0 jit_solution(14333040067863797198)
XLA Ops:
  7.2 0.0 copy-start
  7.2 0.0 all-gather.2.cloned.1.call-start
  7.2 0.7 all-gather.2.cloned.1.call-update
  7.9 0.7 compare_and_fusion
  8.6 0.1 broadcast_bitcast_fusion
  8.7 0.7 reshape.77
  9.4 32.5 %all_gather.10 = bf16[64,256]{1,0:T(8,128)(2,1)S(1)} all-gather(bf16[8,256]{1,0:T(8,128)(2,1)} %param.18), channel_id=1, replica_groups=mesh['groups'=2,'replica'=8,'tensor'=2] {'replica'}, dimensions={0}, use_global_device_ids=true | all-gather | bytes 36864 | tf_op jit(solution)/shard_map/all_gather | solution.py:32
  41.9 2.1 %all_gather.11 = bf16[4,8192]{1,0:T(4,128)(2,1)S(1)} all-gather(bf16[4,4096]{1,0:T(4,128)(2,1)} %param.10), channel_id=1, replica_groups=mesh['groups'=2,'replica'=8,'tensor'=2] {'tensor'}, dimensions={1}, use_global_device_ids=true | all-gather | bytes 98304 | tf_op jit(solution)/shard_map/all_gather | solution.py:31
  43.9 0.7 compare_select_fusion
  44.6 0.7 iota_compare_fusion
  45.3 0.8 %fusion.32 = f32[4,2,1,8]{3,2,1,0:T(1,128)S(1)} fusion(bf16[4,2,128,1]{2,3,1,0:T(2,128)(2,1)S(1)} %reshape.77, bf16[1,4,16,128]{3,1,2,0:T(4,128)(2,1)} %bitcast.65), kind=kOutput, calls=%fused_computation.30 | convolution fusion | flops 16384 | bytes 18688 | tf_op jit(solution)/shard_map/rhgd,rhd->rhg/dot_general | solution.py:47
  46.2 0.0 copy-done
  46.2 1.4 %fusion.41 = (f32[4,2,8]{2,1,0:T(2,128)S(1)}, f32[4,2,8,1024]{3,2,1,0:T(8,128)S(1)}) fusion(bf16[1,4,16,128]{3,1,2,0:T(4,128)(2,1)} %bitcast.66, pred[4,1024]{1,0:T(4,128)(4,1)S(1)} %iota_compare_fusion, bf16[4,1024,256]{2,1,0:T(8,128)(2,1)S(1)} %copy-done), kind=kOutput, calls=%fused_computation.47 | convolution fusion | flops 16973760 | bytes 2380032 | tf_op jit(solution)/shard_map/rhgd,rlhd->rhgl/dot_general | solution.py:43
  47.6 0.2 fusion.27
  47.9 5.2 %all-gather.2.cloned.1.call-done = bf16[64,8192]{1,0:T(8,128)(2,1)} async-done(((bf16[64,1024]{1,0:T(8,128)(2,1)}), bf16[64,8192]{1,0:T(8,128)(2,1)}) %all-gather.2.cloned.1.call-update) | async-done | bytes 1048592 | tf_op jit(solution)/shard_map/all_gather | solution.py:65
  53.1 1.3 %copy.63 = bf16[8,8,8,1024]{3,2,0,1:T(8,128)(2,1)S(1)} copy(bf16[8,8,8,1024]{3,2,1,0:T(8,128)(2,1)} %bitcast.63) | data formatting | bytes 2097152 | tf_op jit(solution)/shard_map/reshape | solution.py:67
  54.4 1.6 %gather_fusion = bf16[8,64,1024]{2,1,0:T(8,128)(2,1)} fusion(bf16[64,8,1024]{2,0,1:T(8,128)(2,1)S(1)} %bitcast.61, s32[1024]{0:T(1024)S(1)} %pad_clamp_fusion), kind=kCustom, calls=%fused_computation | custom fusion | bytes 2097184 | tf_op jit(solution)/shard_map/jit(_take)/gather | solution.py:66
  56.0 1.3 %copy.26 = bf16[8,8,8,1024]{3,2,0,1:T(8,128)(2,1)S(1)} copy(bf16[8,8,8,1024]{3,2,1,0:T(8,128)(2,1)} %bitcast.62) | data formatting | bytes 2097152 | tf_op jit(solution)/shard_map/jit(_take)/gather | solution.py:66
  57.3 3.5 %fusion.1 = bf16[8192,256]{1,0:T(8,128)(2,1)S(1)} fusion(bf16[64,256]{1,0:T(8,128)(2,1)S(1)} %all_gather.10, bf16[8192,256]{1,0:T(8,128)(2,1)} %param.16, bf16[64,8192]{1,0:T(8,128)(2,1)S(1)} %bitcast.64, pred[8192]{0:T(1024)(128)(4,1)S(1)} %bitcast.70), kind=kOutput, calls=%fused_computation.3 | convolution fusion | flops 277348352 | bytes 9478144 | tf_op jit(solution)/shard_map/dot_general | solution.py:13
  60.8 0.0 copy-start.1
  60.8 2.0 %copy-done.1 = bf16[8192,256]{1,0:T(8,128)(2,1)} copy-done((bf16[8192,256]{1,0:T(8,128)(2,1)}, bf16[8192,256]{1,0:T(8,128)(2,1)S(1)}, u32[]{:S(2)}) %copy-start.1) | copy-done | bytes 4194328
  62.8 0.6 fusion.23
  63.4 2.0 %fusion.20 = bf16[1,4,16,128]{3,2,1,0:T(8,128)(2,1)S(1)} fusion(f32[4,2,8,1024]{3,2,1,0:T(8,128)S(1)} %get-tuple-element.6, f32[4,2,8]{2,1,0:T(2,128)S(1)} %get-tuple-element.4, f32[4,2,8]{2,1,0:T(2,128)S(1)} %multiply_maximum_fusion, pred[4,1024]{1,0:T(4,128)(4,1)S(1)} %iota_compare_fusion, f32[4,2,128]{2,1,0:T(2,128)S(1)} %reshape.64, ...), kind=kOutput, calls=%fused_computation.14 | convolution fusion | flops 17063936 | bytes 2384640 | tf_op jit(solution)/shard_map/rhgl,rlhd->rhgd/dot_general | solution.py:59
  65.5 0.6 copy.65
  (7 shorter events, 0.1 us)
Async XLA Ops:
  7.2 39.0 %copy-start = (bf16[4,1024,256]{2,1,0:T(8,128)(2,1)S(1)}, bf16[4,1024,256]{2,1,0:T(8,128)(2,1)}, u32[]{:S(2)}) copy-start(bf16[4,1024,256]{2,1,0:T(8,128)(2,1)} %param.12) | copy-start | bytes 6291460
  7.2 45.9 %all-gather.2.cloned.1.call-start = ((), (), s32[]{:S(2)}) async-start(), calls=%async_computation | async-start | bytes 1179648 | tf_op jit(solution)/shard_map/all_gather | solution.py:65
  60.8 2.0 %copy-start.1 = (bf16[8192,256]{1,0:T(8,128)(2,1)}, bf16[8192,256]{1,0:T(8,128)(2,1)S(1)}, u32[]{:S(2)}) copy-start(bf16[8192,256]{1,0:T(8,128)(2,1)S(1)} %fusion.1) | copy-start | bytes 12582916
  63.4 2.7 %copy-start.2 = (bf16[4,256]{1,0:T(4,128)(2,1)}, bf16[4,256]{1,0:T(4,128)(2,1)S(1)}, u32[]{:S(2)}) copy-start(bf16[4,256]{1,0:T(4,128)(2,1)S(1)} %fusion.23) | copy-start | bytes 6148
Sparse Core Ops, SparseCore 0:
  10.2 42.8 all-gather.1
where the time goes:
time: 73.4 us; the launch traced here: 73 us
  blocking collectives  34.6 us (47%)
  between operations  14.1 us (19%)
  matrix products  8.45 us (12%)
  local copies, waits for them, and re-layouts  7.63 us (10%)
  waiting for transfers between devices  5.87 us (8%)
  other arithmetic  2.29 us (3%)
    all_gather x1, blocking collectives, body(): up_factor = lax.all_gather(adapter_out, 'replica', axis=0, tiled=True)  32.5 us
    all_gather x1, waiting for transfers between devices, body(): gathered = lax.all_gather(adapter_in, 'replica', axis=1, tiled=True)  5.19 us
    dot_general x1, matrix products, fold_rows(): lax.dot_general(factor_rows, up_factor, (((0,), (0,)), ((), ())), preferr...  3.48 us
    gather x2, local copies, waits for them, and re-layouts, body(): jnp.take(gathered.reshape(gathered.shape[0], replicas, shard_width), owne...  2.89 us
    unnamed x9, local copies, waits for them, and re-layouts  2.73 us
    all_gather x1, blocking collectives, body(): features = lax.all_gather(hidden_in, 'tensor', axis=1, tiled=True)  2.05 us
    dot_general x1, matrix products, body(): jnp.einsum('rhgl,rlhd->rhgd', weights_cached, head_values, preferred_elem...  2.04 us
  transfers between devices with their start and end apart: 1, of which 1 were waited for; matrix products, arithmetic and copies ran while one was open for 7% of the time, Pallas kernels for 0%

commit v1 on v0

v1 whole, which is shorter than its diff:
```python
import functools

import jax
import jax.numpy as jnp
from jax import lax
from jax.experimental import pallas as pl
from jax.experimental.pallas import tpu as pltpu
from jax.sharding import PartitionSpec as P

HEAD_SIZE = 128
ADAPTER_SCALE = 2.0


def attend_kernel(lengths_ref, q_ref, k_ref, v_ref, own_k_ref, context_ref, own_weight_ref):
    row = pl.program_id(0)
    length = lengths_ref[row]
    q = q_ref[0]
    heads = q.shape[0]
    local_heads = k_ref.shape[2] // HEAD_SIZE
    group = heads // local_heads
    cache_len = k_ref.shape[1]
    scaling = 1.0 / HEAD_SIZE**0.5
    head_of = lax.broadcasted_iota(jnp.int32, (heads, HEAD_SIZE), 0) // group
    q32 = q.astype(jnp.float32)
    spread = jnp.concatenate(
        [jnp.where(head_of == h, q32, 0.0) for h in range(local_heads)], axis=1
    )
    scores = (
        lax.dot_general(
            spread.astype(jnp.bfloat16), k_ref[0], (((1,), (1,)), ((), ())),
            preferred_element_type=jnp.float32,
        )
        * scaling
    )
    own_key = own_k_ref[pl.ds(row, 1), :]
    own = jnp.sum(spread * own_key, axis=1, keepdims=True) * scaling
    valid = lax.broadcasted_iota(jnp.int32, (heads, cache_len), 1) < length
    masked = jnp.where(valid, scores, -1e30)
    largest = jnp.maximum(jnp.max(masked, axis=1, keepdims=True), own)
    cached_exp = jnp.where(valid, jnp.exp(masked - largest), 0.0)
    own_exp = jnp.exp(own - largest)
    normaliser = jnp.sum(cached_exp, axis=1, keepdims=True) + own_exp
    weights = (cached_exp / normaliser).astype(jnp.bfloat16)
    weight_own = (own_exp / normaliser).astype(jnp.bfloat16).astype(jnp.float32)
    wide = jnp.dot(weights, v_ref[0], preferred_element_type=jnp.float32)
    context = wide[:, :HEAD_SIZE]
    for h in range(1, local_heads):
        context = jnp.where(
            head_of == h, wide[:, h * HEAD_SIZE : (h + 1) * HEAD_SIZE], context
        )
    context_ref[0] = context
    own_weight_ref[0] = jnp.broadcast_to(weight_own, (heads, HEAD_SIZE))


def attend(queries, stored_keys, stored_values, fresh_token_key, lengths):
    rows, cache_len, width = stored_keys.shape
    heads = queries.shape[1] // HEAD_SIZE
    out = jax.ShapeDtypeStruct((rows, heads, HEAD_SIZE), jnp.float32)
    spec = pl.BlockSpec((1, heads, HEAD_SIZE), lambda i: (i, 0, 0))
    cache_spec = pl.BlockSpec((1, cache_len, width), lambda i: (i, 0, 0))
    return pl.pallas_call(
        attend_kernel,
        grid=(rows,),
        out_shape=(out, out),
        in_specs=[
            pl.BlockSpec(memory_space=pltpu.SMEM),
            spec,
            cache_spec,
            cache_spec,
            pl.BlockSpec((rows, width), lambda i: (0, 0)),
        ],
        out_specs=(spec, spec),
        compiler_params=pltpu.CompilerParams(vmem_limit_bytes=16 * 2**20),
        cost_estimate=pl.CostEstimate(
            flops=4 * rows * heads * cache_len * width,
            bytes_accessed=4 * rows * cache_len * width,
            transcendentals=rows * heads * cache_len,
        ),
        name="attend_cache",
    )(
        lengths,
        queries.reshape(rows, heads, HEAD_SIZE),
        stored_keys,
        stored_values,
        fresh_token_key.astype(jnp.float32),
    )


def fold_kernel(slots, place_ref, own_first_ref, up_ref, hid_own_ref, hid_other_ref, context_ref,
                own_weight_ref, *rest):
    blocks = rest[:slots]
    served, merged, fresh_ref, attended_ref, w_buf, m_buf, feat, in_sem, out_sem = rest[slots:]
    width = blocks[0].shape[1]
    half = hid_own_ref.shape[1]

    def place(slot):
        return pl.ds(pl.multiple_of(place_ref[slot] * width, width), width)

    def fetch(slot):
        return pltpu.make_async_copy(served.at[place(slot)], w_buf.at[slot], in_sem.at[slot])

    def store(slot):
        return pltpu.make_async_copy(m_buf.at[slot], merged.at[place(slot)], out_sem.at[slot])

    for slot in range(slots):
        fetch(slot).start()
    mine = own_first_ref[0]
    feat[mine] = hid_own_ref[...]
    feat[1 - mine] = hid_other_ref[...]
    up = up_ref[...]
    total = jnp.zeros(fresh_ref.shape, jnp.float32)
    for slot in range(slots):
        update = lax.dot_general(
            blocks[slot][...], up, (((0,), (0,)), ((), ())), preferred_element_type=jnp.float32
        )
        fetch(slot).wait()
        rows = (w_buf[slot].astype(jnp.float32) + ADAPTER_SCALE * update).astype(jnp.bfloat16)
        m_buf[slot] = rows
        store(slot).start()
        first = place_ref[slot] * width
        in_half = first // half
        features = feat[in_half, :, pl.ds(pl.multiple_of(first - in_half * half, width), width)]
        total = total + jnp.dot(features, rows, preferred_element_type=jnp.float32)
    fresh = total.astype(jnp.bfloat16)
    fresh_ref[...] = fresh
    value = fresh.astype(jnp.float32)
    heads = attended_ref.shape[1] // HEAD_SIZE
    group = heads // (fresh_ref.shape[1] // HEAD_SIZE)
    for h in range(heads):
        cols = slice(h * HEAD_SIZE, (h + 1) * HEAD_SIZE)
        at = (h // group) * HEAD_SIZE
        attended_ref[:, cols] = (
            context_ref[:, cols] + own_weight_ref[:, cols] * value[:, at : at + HEAD_SIZE]
        ).astype(jnp.bfloat16)
    for slot in range(slots):
        store(slot).wait()


def fold(place, own_first, up, hid_own, hid_other, context, own_weight, blocks, served):
    slots = len(blocks)
    rank, width = blocks[0].shape
    rows = hid_own.shape[0]
    depth, cols = served.shape
    vmem = pl.BlockSpec(memory_space=pltpu.VMEM)
    smem = pl.BlockSpec(memory_space=pltpu.SMEM)
    hbm = pl.BlockSpec(memory_space=pl.ANY)
    return pl.pallas_call(
        functools.partial(fold_kernel, slots),
        out_shape=(
            jax.ShapeDtypeStruct((depth, cols), jnp.bfloat16),
            jax.ShapeDtypeStruct((rows, cols), jnp.bfloat16),
            jax.ShapeDtypeStruct(context.shape, jnp.bfloat16),
        ),
        in_specs=[smem, smem] + [vmem] * (5 + slots) + [hbm],
        out_specs=(hbm, vmem, vmem),
        scratch_shapes=[
            pltpu.VMEM((slots, width, cols), jnp.bfloat16),
            pltpu.VMEM((slots, width, cols), jnp.bfloat16),
            pltpu.VMEM((2,) + hid_own.shape, jnp.bfloat16),
            pltpu.SemaphoreType.DMA((slots,)),
            pltpu.SemaphoreType.DMA((slots,)),
        ],
        compiler_params=pltpu.CompilerParams(vmem_limit_bytes=24 * 2**20),
        cost_estimate=pl.CostEstimate(
            flops=2 * depth * cols * (rank + rows),
            bytes_accessed=4 * depth * cols + 2 * rank * depth,
            transcendentals=0,
        ),
        name="fold_blocks",
    )(place, own_first, up, hid_own, hid_other, context, own_weight, *blocks, served)


def ring_member(spot, n):
    return jnp.where(spot < (n + 1) // 2, 2 * spot, 2 * (n - 1 - spot) + 1)


def body(
    hidden_in,
    queries,
    stored_keys,
    stored_values,
    fresh_token_key,
    lengths,
    served_value_weight,
    adapter_in,
    adapter_out,
    owner_rank,
):
    n = lax.axis_size("replica")
    replica = lax.axis_index("replica")
    core = lax.axis_index("tensor")
    swap = [(0, 1), (1, 0)]
    order = list(range(0, n, 2)) + list(range(n - 1 - n % 2, 0, -2))
    around = []
    for spot in range(n):
        here, there = order[spot], order[(spot + 1) % n]
        around.append((here * 2, there * 2))
        around.append((there * 2 + 1, here * 2 + 1))

    ring = [adapter_in]
    crossed = []
    for step in range(1, n // 2 + 1):
        ring.append(lax.ppermute(ring[-1], ("replica", "tensor"), around))
        if 2 * step < n:
            crossed.append(lax.ppermute(ring[-1], "tensor", swap))
    hid_other = lax.ppermute(hidden_in, "tensor", swap)
    ups = [adapter_out]
    for step in range(1, n):
        ups.append(lax.ppermute(adapter_out, "replica", [(i, (i + step) % n) for i in range(n)]))

    context, own_weight = attend(queries, stored_keys, stored_values, fresh_token_key, lengths)
    context = context.reshape(queries.shape)
    own_weight = own_weight.reshape(queries.shape)

    up = jnp.concatenate(ups[::-1] + ups[::-1], axis=0)
    per = adapter_out.shape[0]
    up = lax.dynamic_slice_in_dim(up, (n - 1 - replica) * per, n * per, axis=0)

    spot = jnp.where(replica % 2 == 0, replica // 2, n - 1 - replica // 2)
    way = jnp.where(core == 0, -1, 1)
    shifts = list(range(n // 2 + 1)) + [-k for k in range(1, len(crossed) + 1)]
    source = ring_member((spot + way * jnp.array(shifts, jnp.int32) + n) % n, n)
    spots = jnp.arange(n, dtype=jnp.int32)[None, :]
    place = jnp.sum(jnp.where(owner_rank[None, :] == source[:, None], spots, 0), axis=1)

    merged, fresh_token_value, attended = fold(
        place.astype(jnp.int32), core.astype(jnp.int32).reshape(1), up, hidden_in, hid_other,
        context, own_weight, ring + crossed, served_value_weight,
    )
    return (merged, fresh_token_value, attended)


def solution(mesh):
    in_specs = (
        P(("groups", "replica"), "tensor"),
        P(("groups", "replica"), "tensor"),
        P(("groups", "replica"), None, "tensor"),
        P(("groups", "replica"), None, "tensor"),
        P(("groups", "replica"), "tensor"),
        P(("groups", "replica")),
        P(None, "tensor"),
        P("groups", "replica"),
        P(("groups", "replica"), "tensor"),
        P("groups"),
    )
    out_specs = (
        P("groups", "tensor"),
        P(("groups", "replica"), "tensor"),
        P(("groups", "replica"), "tensor"),
    )
    return jax.shard_map(body, mesh=mesh, in_specs=in_specs, out_specs=out_specs, check_vma=False)
```

time: 73.4 us -> 54.5 us (0.74)
  blocking collectives: 34.6 us -> 0 us
  starting transfers between devices: 0.04 us -> 15.3 us
  waiting for transfers between devices: 5.87 us -> 20.5 us
  between operations: 14.1 us -> 0.81 us
  Pallas kernels: 0 us -> 9.83 us
  matrix products: 8.45 us -> 0 us
  other arithmetic: 2.29 us -> 0.89 us
  local copies, waits for them, and re-layouts: 7.63 us -> 6.84 us
    all_gather x2 -> x0, blocking collectives: 34.6 us -> none  [the longest x1 32.5 us: body(): up_factor = lax.all_gather(adapter_out, 'replica', axis=0, tiled=True)]
    ppermute x0 -> x15, waiting for transfers between devices: none -> 20.5 us  [the longest x4 12.6 us: body(): ring.append(lax.ppermute(ring[-1], ('replica', 'tensor'), around))]
    ppermute x0 -> x15, starting transfers between devices: none -> 15.3 us  [the longest x7 12.9 us: body(): lax.ppermute(adapter_out, 'replica', [(i, (i + step) % n) for i in range(...]
    pallas_call x0 -> x2, Pallas kernels: none -> 9.83 us  [the longest x1 6.4 us: fold(): pl.pallas_call(functools.partial(fold_kernel, slots), out_shape=(jax.Shap...]
    dot_general x5 -> x0, matrix products: 8.45 us -> none  [the longest x1 3.48 us: fold_rows(): lax.dot_general(factor_rows, up_factor, (((0,), (0,)), ((), ())), preferr...]
    all_gather x1 -> x0, waiting for transfers between devices: 5.19 us -> none  [body(): gathered = lax.all_gather(adapter_in, 'replica', axis=1, tiled=True)]
    unnamed x9 -> x34, local copies, waits for them, and re-layouts: 2.73 us -> 6.8 us
    gather x2 -> x0, local copies, waits for them, and re-layouts: 2.89 us -> none  [body(): jnp.take(gathered.reshape(gathered.shape[0], replicas, shard_width), owne...]
  transfers between devices with their start and end apart: 1 -> 15, of which waited for: 1 -> 6; matrix products, arithmetic and copies ran while one was open for 7% -> 3% of each run, Pallas kernels for 0% -> 6%
where the time goes in v1:
time: 54.5 us; the launch traced here: 54.2 us
  waiting for transfers between devices  20.5 us (38%)
  starting transfers between devices  15.3 us (28%)
  Pallas kernels  9.83 us (18%)
  local copies, waits for them, and re-layouts  6.84 us (13%)
  other arithmetic  0.89 us (2%)
  between operations  0.81 us (1%)
    ppermute x7, starting transfers between devices, body(): lax.ppermute(adapter_out, 'replica', [(i, (i + step) % n) for i in range(...  12.9 us
    ppermute x4, waiting for transfers between devices, body(): ring.append(lax.ppermute(ring[-1], ('replica', 'tensor'), around))  12.6 us
    ppermute x7, waiting for transfers between devices, body(): lax.ppermute(adapter_out, 'replica', [(i, (i + step) % n) for i in range(...  6.89 us
    unnamed x34, local copies, waits for them, and re-layouts  6.8 us
    pallas_call x1, Pallas kernels, fold(): pl.pallas_call(functools.partial(fold_kernel, slots), out_shape=(jax.Shap...  6.4 us
    pallas_call x1, Pallas kernels, attend(): pl.pallas_call(attend_kernel, grid=(rows,), out_shape=(out, out), in_spec...  3.44 us
    ppermute x4, starting transfers between devices, body(): ring.append(lax.ppermute(ring[-1], ('replica', 'tensor'), around))  1.78 us
  transfers between devices with their start and end apart: 15, of which 6 were waited for; matrix products, arithmetic and copies ran while one was open for 3% of the time, Pallas kernels for 6%

profile of v1, /device:TPU:0, one launch (start us, length us, event | category | flops | bytes accessed | tf_op | source)
XLA Modules:
  0.0 54.2 jit_solution(40490742858006158)
XLA Ops:
  0.7 3.1 %collective-permute-start.5 = (bf16[8,256]{1,0:T(8,128)(2,1)}, bf16[8,256]{1,0:T(8,128)(2,1)S(1)}, u32[]{:S(2)}, u32[]{:S(2)}) collective-permute-start(bf16[8,256]{1,0:T(8,128)(2,1)} %param.19), channel_id=1, source_target_pairs={{0,4},{2,6},{4,8},{6,10},{8,12},{10,14},{12,0},{14,2},{1,5},{3,7},... | collective-permute-start | bytes 12296 | tf_op jit(solution)/shard_map/ppermute | solution.py:209
  3.8 2.5 %collective-permute-start.4 = (bf16[8,256]{1,0:T(8,128)(2,1)}, bf16[8,256]{1,0:T(8,128)(2,1)S(1)}, u32[]{:S(2)}, u32[]{:S(2)}) collective-permute-start(bf16[8,256]{1,0:T(8,128)(2,1)} %param.19), channel_id=1, source_target_pairs={{0,6},{2,8},{4,10},{6,12},{8,14},{10,0},{12,2},{14,4},{1,7},{3,9},... | collective-permute-start | bytes 12296 | tf_op jit(solution)/shard_map/ppermute | solution.py:209
  6.3 1.2 %collective-permute-start.3 = (bf16[8,256]{1,0:T(8,128)(2,1)}, bf16[8,256]{1,0:T(8,128)(2,1)S(1)}, u32[]{:S(2)}, u32[]{:S(2)}) collective-permute-start(bf16[8,256]{1,0:T(8,128)(2,1)} %param.19), channel_id=1, source_target_pairs={{0,8},{2,10},{4,12},{6,14},{8,0},{10,2},{12,4},{14,6},{1,9},{3,11}... | collective-permute-start | bytes 12296 | tf_op jit(solution)/shard_map/ppermute | solution.py:209
  7.5 2.6 %collective-permute-start.2 = (bf16[8,256]{1,0:T(8,128)(2,1)}, bf16[8,256]{1,0:T(8,128)(2,1)S(1)}, u32[]{:S(2)}, u32[]{:S(2)}) collective-permute-start(bf16[8,256]{1,0:T(8,128)(2,1)} %param.19), channel_id=1, source_target_pairs={{0,10},{2,12},{4,14},{6,0},{8,2},{10,4},{12,6},{14,8},{1,11},{3,13... | collective-permute-start | bytes 12296 | tf_op jit(solution)/shard_map/ppermute | solution.py:209
  10.2 1.4 %collective-permute-start = (bf16[8,256]{1,0:T(8,128)(2,1)}, bf16[8,256]{1,0:T(8,128)(2,1)S(1)}, u32[]{:S(2)}, u32[]{:S(2)}) collective-permute-start(bf16[8,256]{1,0:T(8,128)(2,1)} %param.19), channel_id=1, source_target_pairs={{0,14},{2,0},{4,2},{6,4},{8,6},{10,8},{12,10},{14,12},{1,15},{3,1}... | collective-permute-start | bytes 12296 | tf_op jit(solution)/shard_map/ppermute | solution.py:209
  11.6 0.7 %convert_element_type.3.own_k_ref = f32[4,256]{1,0:T(4,128)S(1)} convert(bf16[4,256]{1,0:T(4,128)(2,1)} %param.15) | non-fusion elementwise | flops 1024 | bytes 6144 | tf_op jit(solution)/shard_map/convert_element_type | solution.py:85
  12.3 0.7 %copy.20 = bf16[1,4,16,128]{3,2,1,0:T(8,128)(2,1)S(1)} copy(bf16[1,4,16,128]{3,1,2,0:T(4,128)(2,1)} %bitcast.14) | data formatting | bytes 32768
  13.0 1.6 %copy-done.1 = bf16[4,1024,256]{2,1,0:T(8,128)(2,1)S(1)} copy-done((bf16[4,1024,256]{2,1,0:T(8,128)(2,1)S(1)}, bf16[4,1024,256]{2,1,0:T(8,128)(2,1)}, u32[]{:S(2)}) %copy-start.1) | copy-done | bytes 2097176
  14.6 1.6 %copy-done.2 = bf16[4,1024,256]{2,1,0:T(8,128)(2,1)S(1)} copy-done((bf16[4,1024,256]{2,1,0:T(8,128)(2,1)S(1)}, bf16[4,1024,256]{2,1,0:T(8,128)(2,1)}, u32[]{:S(2)}) %copy-start.2) | copy-done | bytes 2097176
  16.2 0.7 %copy-done.5 = s32[4]{0:T(128)S(1)} copy-done((s32[4]{0:T(128)S(1)}, s32[4]{0:T(128)}, u32[]{:S(2)}) %copy-start.5) | copy-done | bytes 40
  16.8 3.4 %attend_cache.1 = (f32[4,16,128]{2,1,0:T(8,128)S(1)}, f32[4,16,128]{2,1,0:T(8,128)S(1)}) custom-call(s32[4]{0:T(128)S(1)} %copy-done.5, bf16[4,16,128]{2,1,0:T(8,128)(2,1)S(1)} %bitcast.11, bf16[4,1024,256]{2,1,0:T(8,128)(2,1)S(1)} %copy-done.1, bf16[4,1024,256]{2,1,0:T(8,128)(2,1)S(1)} %copy-done.2, f32[4,256]{1,0:T(4,128)S(1)} %convert_element_type.3.own_k_ref), custom_call_target="tpu_custom_call" | custom-call | flops 67108864 | bytes 4194304 | tf_op jit(solution)/shard_map/attend_cache/pallas_call | solution.py:61
  20.5 1.4 %collective-permute-start.1 = (bf16[8,256]{1,0:T(8,128)(2,1)S(1)}, bf16[8,256]{1,0:T(8,128)(2,1)S(1)}, u32[]{:S(2)}, u32[]{:S(2)}) collective-permute-start(bf16[8,256]{1,0:T(8,128)(2,1)S(1)} %copy-done.6), channel_id=1, source_target_pairs={{0,12},{2,14},{4,0},{6,2},{8,4},{10,6},{12,8},{14,10},{1,13},{3,15... | collective-permute-start | bytes 12296 | tf_op jit(solution)/shard_map/ppermute | solution.py:209
  21.9 2.3 %collective-permute-done.1 = bf16[8,256]{1,0:T(8,128)(2,1)S(1)} collective-permute-done((bf16[8,256]{1,0:T(8,128)(2,1)S(1)}, bf16[8,256]{1,0:T(8,128)(2,1)S(1)}, u32[]{:S(2)}, u32[]{:S(2)}) %collective-permute-start.1) | collective-permute-done | bytes 4128 | tf_op jit(solution)/shard_map/ppermute | solution.py:209
  24.2 0.6 %collective-permute-start.6 = (bf16[8,256]{1,0:T(8,128)(2,1)S(1)}, bf16[8,256]{1,0:T(8,128)(2,1)S(1)}, u32[]{:S(2)}, u32[]{:S(2)}) collective-permute-start(bf16[8,256]{1,0:T(8,128)(2,1)S(1)} %copy-done.6), channel_id=1, source_target_pairs={{0,2},{2,4},{4,6},{6,8},{8,10},{10,12},{12,14},{14,0},{1,3},{3,5},... | collective-permute-start | bytes 12296 | tf_op jit(solution)/shard_map/ppermute | solution.py:209
  24.9 1.0 %collective-permute-start.8 = (bf16[64,1024]{1,0:T(8,128)(2,1)S(1)}, bf16[64,1024]{1,0:T(8,128)(2,1)S(1)}, u32[]{:S(2)}, u32[]{:S(2)}) collective-permute-start(bf16[64,1024]{1,0:T(8,128)(2,1)S(1)} %copy-done.3), channel_id=1, source_target_pairs={{0,4},{5,1},{4,8},{9,5},{8,12},{13,9},{12,14},{15,13},{14,10},{11,... | collective-permute-start | bytes 393224 | tf_op jit(solution)/shard_map/ppermute | solution.py:203
  26.0 4.6 %collective-permute-done.6 = bf16[8,256]{1,0:T(8,128)(2,1)S(1)} collective-permute-done((bf16[8,256]{1,0:T(8,128)(2,1)S(1)}, bf16[8,256]{1,0:T(8,128)(2,1)S(1)}, u32[]{:S(2)}, u32[]{:S(2)}) %collective-permute-start.6) | collective-permute-done | bytes 4128 | tf_op jit(solution)/shard_map/ppermute | solution.py:209
  30.6 0.3 collective-permute-start.9
  30.9 4.7 %collective-permute-done.9.rest_2_ = bf16[64,1024]{1,0:T(8,128)(2,1)S(1)} collective-permute-done((bf16[64,1024]{1,0:T(8,128)(2,1)S(1)}, bf16[64,1024]{1,0:T(8,128)(2,1)S(1)}, u32[]{:S(2)}, u32[]{:S(2)}) %collective-permute-start.9) | collective-permute-done | bytes 131104 | tf_op jit(solution)/shard_map/ppermute | solution.py:203
  35.9 0.5 collective-permute-start.13
  36.4 4.2 %collective-permute-done.10.rest_3_ = bf16[64,1024]{1,0:T(8,128)(2,1)S(1)} collective-permute-done((bf16[64,1024]{1,0:T(8,128)(2,1)S(1)}, bf16[64,1024]{1,0:T(8,128)(2,1)S(1)}, u32[]{:S(2)}, u32[]{:S(2)}) %collective-permute-start.10) | collective-permute-done | bytes 131104 | tf_op jit(solution)/shard_map/ppermute | solution.py:203
  40.9 1.1 %collective-permute-done.14.rest_7_ = bf16[64,1024]{1,0:T(8,128)(2,1)S(1)} collective-permute-done((bf16[64,1024]{1,0:T(8,128)(2,1)S(1)}, bf16[64,1024]{1,0:T(8,128)(2,1)S(1)}, u32[]{:S(2)}, u32[]{:S(2)}) %collective-permute-start.14) | collective-permute-done | bytes 131104 | tf_op jit(solution)/shard_map/ppermute | solution.py:205
  42.0 3.6 %collective-permute-done.11.rest_4_ = bf16[64,1024]{1,0:T(8,128)(2,1)S(1)} collective-permute-done((bf16[64,1024]{1,0:T(8,128)(2,1)S(1)}, bf16[64,1024]{1,0:T(8,128)(2,1)S(1)}, u32[]{:S(2)}, u32[]{:S(2)}) %collective-permute-start.11) | collective-permute-done | bytes 131104 | tf_op jit(solution)/shard_map/ppermute | solution.py:203
  45.6 2.2 %copy-done = bf16[8192,256]{1,0:T(8,128)(2,1)S(1)} copy-done((bf16[8192,256]{1,0:T(8,128)(2,1)S(1)}, bf16[8192,256]{1,0:T(8,128)(2,1)}, u32[]{:S(2)}) %copy-start) | copy-done | bytes 4194328
  47.8 6.4 %fold_blocks.1 = (bf16[8192,256]{1,0:T(8,128)(2,1)}, bf16[4,256]{1,0:T(4,128)(2,1)}, bf16[4,2048]{1,0:T(4,128)(2,1)}) custom-call(s32[8]{0:T(128)S(1)} %select_reduce_fusion.place_ref, s32[1]{0:T(128)} %bitcast.own_first_ref, bf16[64,256]{1,0:T(8,128)(2,1)S(1)} %constant_dynamic-slice_fusion.up_ref, bf16[4,4096]{1,0:T(4,128)(2,1)S(1)} %copy-done.4, ...), custom_call_target="tpu_custom_call" | custom-call | flops 285212672 | bytes 9437184 | tf_op jit(solution)/shard_map/fold_blocks/pallas_call | solution.py:147
  (48 shorter events, 0.9 us)
Async XLA Ops:
  0.6 19.7 %copy-start.7 = (s32[8]{0:T(128)S(1)}, s32[8]{0:T(128)}, u32[]{:S(2)}) copy-start(s32[8]{0:T(128)} %constant.62.clone) | copy-start | bytes 100
  0.6 19.9 %copy-start.6 = (bf16[8,256]{1,0:T(8,128)(2,1)S(1)}, bf16[8,256]{1,0:T(8,128)(2,1)}, u32[]{:S(2)}) copy-start(bf16[8,256]{1,0:T(8,128)(2,1)} %param.19) | copy-start | bytes 12292
  0.7 19.7 %copy-start.8 = (s32[8]{0:T(128)S(1)}, s32[8]{0:T(128)}, u32[]{:S(2)}) copy-start(s32[8]{0:T(128)} %param.20) | copy-start | bytes 100
  0.7 24.2 %copy-start.4 = (bf16[4,4096]{1,0:T(4,128)(2,1)S(1)}, bf16[4,4096]{1,0:T(4,128)(2,1)}, u32[]{:S(2)}) copy-start(bf16[4,4096]{1,0:T(4,128)(2,1)} %hid_own_ref.1) | copy-start | bytes 98308
  0.7 25.3 %collective-permute-start.5 = (bf16[8,256]{1,0:T(8,128)(2,1)}, bf16[8,256]{1,0:T(8,128)(2,1)S(1)}, u32[]{:S(2)}, u32[]{:S(2)}) collective-permute-start(bf16[8,256]{1,0:T(8,128)(2,1)} %param.19), channel_id=1, source_target_pairs={{0,4},{2,6},{4,8},{6,10},{8,12},{10,14},{12,0},{14,2},{1,5},{3,7},... | collective-permute-start | bytes 12296 | tf_op jit(solution)/shard_map/ppermute | solution.py:209
  3.8 22.2 %collective-permute-start.4 = (bf16[8,256]{1,0:T(8,128)(2,1)}, bf16[8,256]{1,0:T(8,128)(2,1)S(1)}, u32[]{:S(2)}, u32[]{:S(2)}) collective-permute-start(bf16[8,256]{1,0:T(8,128)(2,1)} %param.19), channel_id=1, source_target_pairs={{0,6},{2,8},{4,10},{6,12},{8,14},{10,0},{12,2},{14,4},{1,7},{3,9},... | collective-permute-start | bytes 12296 | tf_op jit(solution)/shard_map/ppermute | solution.py:209
  6.3 18.6 %collective-permute-start.3 = (bf16[8,256]{1,0:T(8,128)(2,1)}, bf16[8,256]{1,0:T(8,128)(2,1)S(1)}, u32[]{:S(2)}, u32[]{:S(2)}) collective-permute-start(bf16[8,256]{1,0:T(8,128)(2,1)} %param.19), channel_id=1, source_target_pairs={{0,8},{2,10},{4,12},{6,14},{8,0},{10,2},{12,4},{14,6},{1,9},{3,11}... | collective-permute-start | bytes 12296 | tf_op jit(solution)/shard_map/ppermute | solution.py:209
  7.5 17.3 %collective-permute-start.2 = (bf16[8,256]{1,0:T(8,128)(2,1)}, bf16[8,256]{1,0:T(8,128)(2,1)S(1)}, u32[]{:S(2)}, u32[]{:S(2)}) collective-permute-start(bf16[8,256]{1,0:T(8,128)(2,1)} %param.19), channel_id=1, source_target_pairs={{0,10},{2,12},{4,14},{6,0},{8,2},{10,4},{12,6},{14,8},{1,11},{3,13... | collective-permute-start | bytes 12296 | tf_op jit(solution)/shard_map/ppermute | solution.py:209
  10.2 10.4 %collective-permute-start = (bf16[8,256]{1,0:T(8,128)(2,1)}, bf16[8,256]{1,0:T(8,128)(2,1)S(1)}, u32[]{:S(2)}, u32[]{:S(2)}) collective-permute-start(bf16[8,256]{1,0:T(8,128)(2,1)} %param.19), channel_id=1, source_target_pairs={{0,14},{2,0},{4,2},{6,4},{8,6},{10,8},{12,10},{14,12},{1,15},{3,1}... | collective-permute-start | bytes 12296 | tf_op jit(solution)/shard_map/ppermute | solution.py:209
  13.0 1.6 %copy-start.1 = (bf16[4,1024,256]{2,1,0:T(8,128)(2,1)S(1)}, bf16[4,1024,256]{2,1,0:T(8,128)(2,1)}, u32[]{:S(2)}) copy-start(bf16[4,1024,256]{2,1,0:T(8,128)(2,1)} %k_ref.1) | copy-start | bytes 6291460
  14.6 1.6 %copy-start.2 = (bf16[4,1024,256]{2,1,0:T(8,128)(2,1)S(1)}, bf16[4,1024,256]{2,1,0:T(8,128)(2,1)}, u32[]{:S(2)}) copy-start(bf16[4,1024,256]{2,1,0:T(8,128)(2,1)} %v_ref.1) | copy-start | bytes 6291460
  16.2 0.7 %copy-start.5 = (s32[4]{0:T(128)S(1)}, s32[4]{0:T(128)}, u32[]{:S(2)}) copy-start(s32[4]{0:T(128)} %lengths_ref.1) | copy-start | bytes 52
  16.8 8.1 %copy-start.3 = (bf16[64,1024]{1,0:T(8,128)(2,1)S(1)}, bf16[64,1024]{1,0:T(8,128)(2,1)}, u32[]{:S(2)}) copy-start(bf16[64,1024]{1,0:T(8,128)(2,1)} %rest_0_.1) | copy-start | bytes 393220
  20.5 3.7 %collective-permute-start.1 = (bf16[8,256]{1,0:T(8,128)(2,1)S(1)}, bf16[8,256]{1,0:T(8,128)(2,1)S(1)}, u32[]{:S(2)}, u32[]{:S(2)}) collective-permute-start(bf16[8,256]{1,0:T(8,128)(2,1)S(1)} %copy-done.6), channel_id=1, source_target_pairs={{0,12},{2,14},{4,0},{6,2},{8,4},{10,6},{12,8},{14,10},{1,13},{3,15... | collective-permute-start | bytes 12296 | tf_op jit(solution)/shard_map/ppermute | solution.py:209
  24.2 6.4 %collective-permute-start.6 = (bf16[8,256]{1,0:T(8,128)(2,1)S(1)}, bf16[8,256]{1,0:T(8,128)(2,1)S(1)}, u32[]{:S(2)}, u32[]{:S(2)}) collective-permute-start(bf16[8,256]{1,0:T(8,128)(2,1)S(1)} %copy-done.6), channel_id=1, source_target_pairs={{0,2},{2,4},{4,6},{6,8},{8,10},{10,12},{12,14},{14,0},{1,3},{3,5},... | collective-permute-start | bytes 12296 | tf_op jit(solution)/shard_map/ppermute | solution.py:209
  24.8 16.0 %collective-permute-start.7 = (bf16[4,4096]{1,0:T(4,128)(2,1)S(1)}, bf16[4,4096]{1,0:T(4,128)(2,1)S(1)}, u32[]{:S(2)}, u32[]{:S(2)}) collective-permute-start(bf16[4,4096]{1,0:T(4,128)(2,1)S(1)} %copy-done.4), channel_id=1, source_target_pairs={{0,1},{1,0},{2,3},{3,2},{4,5},{5,4},{6,7},{7,6},{8,9},{9,8},{10,11... | collective-permute-start | bytes 98312 | tf_op jit(solution)/shard_map/ppermute | solution.py:206
  24.9 5.7 %collective-permute-start.8 = (bf16[64,1024]{1,0:T(8,128)(2,1)S(1)}, bf16[64,1024]{1,0:T(8,128)(2,1)S(1)}, u32[]{:S(2)}, u32[]{:S(2)}) collective-permute-start(bf16[64,1024]{1,0:T(8,128)(2,1)S(1)} %copy-done.3), channel_id=1, source_target_pairs={{0,4},{5,1},{4,8},{9,5},{8,12},{13,9},{12,14},{15,13},{14,10},{11,... | collective-permute-start | bytes 393224 | tf_op jit(solution)/shard_map/ppermute | solution.py:203
  30.6 5.0 %collective-permute-start.9 = (bf16[64,1024]{1,0:T(8,128)(2,1)S(1)}, bf16[64,1024]{1,0:T(8,128)(2,1)S(1)}, u32[]{:S(2)}, u32[]{:S(2)}) collective-permute-start(bf16[64,1024]{1,0:T(8,128)(2,1)S(1)} %collective-permute-done.8.rest_1_), channel_id=1, source_target_pairs={{0,4},{5,1},{4,8},{9,5},{8,12},{13,9},{12,14},{15,13},{14,10},{11,... | collective-permute-start | bytes 393224 | tf_op jit(solution)/shard_map/ppermute | solution.py:203
  35.7 5.0 %collective-permute-start.10 = (bf16[64,1024]{1,0:T(8,128)(2,1)S(1)}, bf16[64,1024]{1,0:T(8,128)(2,1)S(1)}, u32[]{:S(2)}, u32[]{:S(2)}) collective-permute-start(bf16[64,1024]{1,0:T(8,128)(2,1)S(1)} %collective-permute-done.9.rest_2_), channel_id=1, source_target_pairs={{0,4},{5,1},{4,8},{9,5},{8,12},{13,9},{12,14},{15,13},{14,10},{11,... | collective-permute-start | bytes 393224 | tf_op jit(solution)/shard_map/ppermute | solution.py:203
  35.9 5.0 %collective-permute-start.12 = (bf16[64,1024]{1,0:T(8,128)(2,1)S(1)}, bf16[64,1024]{1,0:T(8,128)(2,1)S(1)}, u32[]{:S(2)}, u32[]{:S(2)}) collective-permute-start(bf16[64,1024]{1,0:T(8,128)(2,1)S(1)} %collective-permute-done.8.rest_1_), channel_id=1, source_target_pairs={{0,1},{1,0},{2,3},{3,2},{4,5},{5,4},{6,7},{7,6},{8,9},{9,8},{10,11... | collective-permute-start | bytes 393224 | tf_op jit(solution)/shard_map/ppermute | solution.py:205
  35.9 5.0 %collective-permute-start.13 = (bf16[64,1024]{1,0:T(8,128)(2,1)S(1)}, bf16[64,1024]{1,0:T(8,128)(2,1)S(1)}, u32[]{:S(2)}, u32[]{:S(2)}) collective-permute-start(bf16[64,1024]{1,0:T(8,128)(2,1)S(1)} %collective-permute-done.9.rest_2_), channel_id=1, source_target_pairs={{0,1},{1,0},{2,3},{3,2},{4,5},{5,4},{6,7},{7,6},{8,9},{9,8},{10,11... | collective-permute-start | bytes 393224 | tf_op jit(solution)/shard_map/ppermute | solution.py:205
  40.6 1.3 %collective-permute-start.14 = (bf16[64,1024]{1,0:T(8,128)(2,1)S(1)}, bf16[64,1024]{1,0:T(8,128)(2,1)S(1)}, u32[]{:S(2)}, u32[]{:S(2)}) collective-permute-start(bf16[64,1024]{1,0:T(8,128)(2,1)S(1)} %collective-permute-done.10.rest_3_), channel_id=1, source_target_pairs={{0,1},{1,0},{2,3},{3,2},{4,5},{5,4},{6,7},{7,6},{8,9},{9,8},{10,11... | collective-permute-start | bytes 393224 | tf_op jit(solution)/shard_map/ppermute | solution.py:205
  40.6 5.0 %collective-permute-start.11 = (bf16[64,1024]{1,0:T(8,128)(2,1)S(1)}, bf16[64,1024]{1,0:T(8,128)(2,1)S(1)}, u32[]{:S(2)}, u32[]{:S(2)}) collective-permute-start(bf16[64,1024]{1,0:T(8,128)(2,1)S(1)} %collective-permute-done.10.rest_3_), channel_id=1, source_target_pairs={{0,4},{5,1},{4,8},{9,5},{8,12},{13,9},{12,14},{15,13},{14,10},{11,... | collective-permute-start | bytes 393224 | tf_op jit(solution)/shard_map/ppermute | solution.py:203
  45.6 2.2 %copy-start = (bf16[8192,256]{1,0:T(8,128)(2,1)S(1)}, bf16[8192,256]{1,0:T(8,128)(2,1)}, u32[]{:S(2)}) copy-start(bf16[8192,256]{1,0:T(8,128)(2,1)} %rest_8_.1) | copy-start | bytes 12582916

commit v2 on v1

--- a/solution.py
+++ b/solution.py
@@ -1,5 +1,3 @@
-import functools
-
 import jax
 import jax.numpy as jnp
 from jax import lax
@@ -58,6 +56,9 @@
     out = jax.ShapeDtypeStruct((rows, heads, HEAD_SIZE), jnp.float32)
     spec = pl.BlockSpec((1, heads, HEAD_SIZE), lambda i: (i, 0, 0))
     cache_spec = pl.BlockSpec((1, cache_len, width), lambda i: (i, 0, 0))
+    stored_keys, stored_values = (
+        pltpu.with_memory_space_constraint(x, pltpu.HBM) for x in (stored_keys, stored_values)
+    )
     return pl.pallas_call(
         attend_kernel,
         grid=(rows,),
@@ -86,35 +87,33 @@
     )
 
 
-def fold_kernel(slots, place_ref, own_first_ref, up_ref, hid_own_ref, hid_other_ref, context_ref,
-                own_weight_ref, *rest):
-    blocks = rest[:slots]
-    served, merged, fresh_ref, attended_ref, w_buf, m_buf, feat, in_sem, out_sem = rest[slots:]
-    width = blocks[0].shape[1]
+def fold_kernel(place_ref, core_ref, up_ref, hid_own_ref, hid_other_ref, context_ref,
+                own_weight_ref, mine_ref, theirs_ref, served, merged, fresh_ref, attended_ref,
+                m_buf, feat, out_sem):
+    slots, _, width = mine_ref.shape
+    rank = up_ref.shape[0]
+    part = rank // 2
     half = hid_own_ref.shape[1]
 
     def place(slot):
         return pl.ds(pl.multiple_of(place_ref[slot] * width, width), width)
 
-    def fetch(slot):
-        return pltpu.make_async_copy(served.at[place(slot)], w_buf.at[slot], in_sem.at[slot])
-
     def store(slot):
         return pltpu.make_async_copy(m_buf.at[slot], merged.at[place(slot)], out_sem.at[slot])
 
-    for slot in range(slots):
-        fetch(slot).start()
-    mine = own_first_ref[0]
-    feat[mine] = hid_own_ref[...]
-    feat[1 - mine] = hid_other_ref[...]
-    up = up_ref[...]
+    core = core_ref[0]
+    feat[core] = hid_own_ref[...]
+    feat[1 - core] = hid_other_ref[...]
+    up = up_ref[...].astype(jnp.float32) * ADAPTER_SCALE
+    low, high = up[:part], up[part:]
+    up = jnp.where(core == 0, up, jnp.concatenate([high, low], axis=0)).astype(jnp.bfloat16)
     total = jnp.zeros(fresh_ref.shape, jnp.float32)
     for slot in range(slots):
+        block = jnp.concatenate([mine_ref[slot, :part], theirs_ref[slot, :part]], axis=0)
         update = lax.dot_general(
-            blocks[slot][...], up, (((0,), (0,)), ((), ())), preferred_element_type=jnp.float32
+            block, up, (((0,), (0,)), ((), ())), preferred_element_type=jnp.float32
         )
-        fetch(slot).wait()
-        rows = (w_buf[slot].astype(jnp.float32) + ADAPTER_SCALE * update).astype(jnp.bfloat16)
+        rows = (served[place(slot), :].astype(jnp.float32) + update).astype(jnp.bfloat16)
         m_buf[slot] = rows
         store(slot).start()
         first = place_ref[slot] * width
@@ -136,28 +135,26 @@
         store(slot).wait()
 
 
-def fold(place, own_first, up, hid_own, hid_other, context, own_weight, blocks, served):
-    slots = len(blocks)
-    rank, width = blocks[0].shape
+def fold(place, core, up, hid_own, hid_other, context, own_weight, mine, theirs, served):
+    slots, _, width = mine.shape
+    rank = up.shape[0]
     rows = hid_own.shape[0]
     depth, cols = served.shape
     vmem = pl.BlockSpec(memory_space=pltpu.VMEM)
     smem = pl.BlockSpec(memory_space=pltpu.SMEM)
-    hbm = pl.BlockSpec(memory_space=pl.ANY)
+    hbm = pl.BlockSpec(memory_space=pltpu.HBM)
     return pl.pallas_call(
-        functools.partial(fold_kernel, slots),
+        fold_kernel,
         out_shape=(
             jax.ShapeDtypeStruct((depth, cols), jnp.bfloat16),
             jax.ShapeDtypeStruct((rows, cols), jnp.bfloat16),
             jax.ShapeDtypeStruct(context.shape, jnp.bfloat16),
         ),
-        in_specs=[smem, smem] + [vmem] * (5 + slots) + [hbm],
+        in_specs=[smem, smem] + [vmem] * 8,
         out_specs=(hbm, vmem, vmem),
         scratch_shapes=[
             pltpu.VMEM((slots, width, cols), jnp.bfloat16),
-            pltpu.VMEM((slots, width, cols), jnp.bfloat16),
             pltpu.VMEM((2,) + hid_own.shape, jnp.bfloat16),
-            pltpu.SemaphoreType.DMA((slots,)),
             pltpu.SemaphoreType.DMA((slots,)),
         ],
         compiler_params=pltpu.CompilerParams(vmem_limit_bytes=24 * 2**20),
@@ -167,11 +164,7 @@
             transcendentals=0,
         ),
         name="fold_blocks",
-    )(place, own_first, up, hid_own, hid_other, context, own_weight, *blocks, served)
-
-
-def ring_member(spot, n):
-    return jnp.where(spot < (n + 1) // 2, 2 * spot, 2 * (n - 1 - spot) + 1)
+    )(place, core, up, hid_own, hid_other, context, own_weight, mine, theirs, served)
 
 
 def body(
@@ -187,45 +180,39 @@
     owner_rank,
 ):
     n = lax.axis_size("replica")
-    replica = lax.axis_index("replica")
     core = lax.axis_index("tensor")
     swap = [(0, 1), (1, 0)]
-    order = list(range(0, n, 2)) + list(range(n - 1 - n % 2, 0, -2))
-    around = []
-    for spot in range(n):
-        here, there = order[spot], order[(spot + 1) % n]
-        around.append((here * 2, there * 2))
-        around.append((there * 2 + 1, here * 2 + 1))
-
-    ring = [adapter_in]
-    crossed = []
-    for step in range(1, n // 2 + 1):
-        ring.append(lax.ppermute(ring[-1], ("replica", "tensor"), around))
-        if 2 * step < n:
-            crossed.append(lax.ppermute(ring[-1], "tensor", swap))
+    rank, width = adapter_in.shape
+    part = rank // 2
+    up_rows = adapter_out.size // width
+    spare = -(part + up_rows) % 8
+
+    load = jnp.concatenate(
+        [
+            lax.dynamic_slice_in_dim(adapter_in, core * part, part, axis=0),
+            adapter_out.reshape(up_rows, width),
+            jnp.zeros((spare, width), adapter_in.dtype),
+        ],
+        axis=0,
+    )
+    load = jnp.broadcast_to(load[None], (n,) + load.shape)
+    mine = lax.all_to_all(load, "replica", split_axis=0, concat_axis=0)
     hid_other = lax.ppermute(hidden_in, "tensor", swap)
-    ups = [adapter_out]
-    for step in range(1, n):
-        ups.append(lax.ppermute(adapter_out, "replica", [(i, (i + step) % n) for i in range(n)]))
+    theirs = lax.ppermute(mine, "tensor", swap)
 
     context, own_weight = attend(queries, stored_keys, stored_values, fresh_token_key, lengths)
     context = context.reshape(queries.shape)
     own_weight = own_weight.reshape(queries.shape)
 
-    up = jnp.concatenate(ups[::-1] + ups[::-1], axis=0)
-    per = adapter_out.shape[0]
-    up = lax.dynamic_slice_in_dim(up, (n - 1 - replica) * per, n * per, axis=0)
-
-    spot = jnp.where(replica % 2 == 0, replica // 2, n - 1 - replica // 2)
-    way = jnp.where(core == 0, -1, 1)
-    shifts = list(range(n // 2 + 1)) + [-k for k in range(1, len(crossed) + 1)]
-    source = ring_member((spot + way * jnp.array(shifts, jnp.int32) + n) % n, n)
-    spots = jnp.arange(n, dtype=jnp.int32)[None, :]
-    place = jnp.sum(jnp.where(owner_rank[None, :] == source[:, None], spots, 0), axis=1)
+    up = mine[:, part : part + up_rows].reshape(rank, adapter_out.shape[1])
+    spots = jnp.arange(n, dtype=jnp.int32)
+    place = jnp.sum(
+        jnp.where(owner_rank[None, :] == spots[:, None], spots[None, :], 0), axis=1
+    ).astype(jnp.int32)
 
     merged, fresh_token_value, attended = fold(
-        place.astype(jnp.int32), core.astype(jnp.int32).reshape(1), up, hidden_in, hid_other,
-        context, own_weight, ring + crossed, served_value_weight,
+        place, core.astype(jnp.int32).reshape(1), up, hidden_in, hid_other,
+        context, own_weight, mine, theirs, served_value_weight,
     )
     return (merged, fresh_token_value, attended)
 

time: 54.5 us -> 40.6 us (0.74)
  blocking collectives: 0 us -> 24.8 us
  waiting for transfers between devices: 20.5 us -> 0.01 us
  starting transfers between devices: 15.3 us -> 0.51 us
  local copies, waits for them, and re-layouts: 6.84 us -> 4.61 us
  Pallas kernels: 9.83 us -> 8.71 us
    all_to_all x0 -> x1, blocking collectives: none -> 24.8 us  [body(): mine = lax.all_to_all(load, 'replica', split_axis=0, concat_axis=0)]
    ppermute x14 -> x1, waiting for transfers between devices: 20.5 us -> 0.01 us  [body(): theirs = lax.ppermute(mine, 'tensor', swap)]
    ppermute x14 -> x1, starting transfers between devices: 15.2 us -> 0.01 us  [body(): theirs = lax.ppermute(mine, 'tensor', swap)]
    unnamed x34 -> x11, local copies, waits for them, and re-layouts: 6.8 us -> 3.62 us
    pallas_call x1, Pallas kernels: 6.4 us -> 4.06 us  [fold(): pl.pallas_call(fold_kernel, out_shape=(jax.ShapeDtypeStruct((depth, cols)...]
    pallas_call x1, Pallas kernels: 3.44 us -> 4.65 us  [attend(): pl.pallas_call(attend_kernel, grid=(rows,), out_shape=(out, out), in_spec...]
    reshape x0 -> x2, local copies, waits for them, and re-layouts: none -> 0.77 us  [the longest x1 0.75 us: body(): adapter_out.reshape(up_rows, width)]
  transfers between devices with their start and end apart: 15 -> 2, of which waited for: 6 -> 0; matrix products, arithmetic and copies ran while one was open for 3% -> 4% of each run, Pallas kernels for 6% -> 12%
where the time goes in v2:
time: 40.6 us; the launch traced here: 40.2 us
  blocking collectives  24.8 us (61%)
  Pallas kernels  8.71 us (21%)
  local copies, waits for them, and re-layouts  4.61 us (11%)
  other arithmetic  0.88 us (2%)
  between operations  0.74 us (2%)
  starting transfers between devices  0.51 us (1%)
    all_to_all x1, blocking collectives, body(): mine = lax.all_to_all(load, 'replica', split_axis=0, concat_axis=0)  24.8 us
    pallas_call x1, Pallas kernels, attend(): pl.pallas_call(attend_kernel, grid=(rows,), out_shape=(out, out), in_spec...  4.65 us
    pallas_call x1, Pallas kernels, fold(): pl.pallas_call(fold_kernel, out_shape=(jax.ShapeDtypeStruct((depth, cols)...  4.06 us
    unnamed x11, local copies, waits for them, and re-layouts  3.62 us
  transfers between devices with their start and end apart: 2, of which 0 were waited for; matrix products, arithmetic and copies ran while one was open for 4% of the time, Pallas kernels for 12%

profile of v2, /device:TPU:0, one launch (start us, length us, event | category | flops | bytes accessed | tf_op | source)
XLA Modules:
  0.0 40.2 jit_solution(5990968230641313784)
XLA Ops:
  0.6 0.0 copy-start
  0.6 0.0 copy-start.2
  0.7 0.0 copy-start.4
  0.7 0.8 %reshape.27 = bf16[2,1024]{1,0:T(2,128)(2,1)S(1)} reshape(bf16[8,256]{1,0:T(8,128)(2,1)} %param.18) | data formatting | bytes 8192 | tf_op jit(solution)/shard_map/reshape | solution.py:193
  1.4 0.1 pad.2.clone
  1.5 0.0 copy-done
  1.6 0.1 maximum_maximum_fusion
  1.6 0.1 broadcast_in_dim.27
  1.7 24.8 %all_to_all.5.mine_ref = bf16[8,40,1024]{2,1,0:T(8,128)(2,1)S(1)} all-to-all(bf16[8,40,1024]{2,1,0:T(8,128)(2,1)S(1)} %broadcast_in_dim.27), channel_id=1, replica_groups=mesh['groups'=2,'replica'=8,'tensor'=2] {'replica'}, dimensions={0} | all-to-all | bytes 1310720 | tf_op jit(solution)/shard_map/all_to_all | solution.py:199
  26.5 0.0 collective-permute-start.1
  26.5 0.5 %collective-permute-start = (bf16[4,4096]{1,0:T(4,128)(2,1)}, bf16[4,4096]{1,0:T(4,128)(2,1)S(1)}, u32[]{:S(2)}, u32[]{:S(2)}) collective-permute-start(bf16[4,4096]{1,0:T(4,128)(2,1)} %hid_own_ref.1), channel_id=1, source_target_pairs={{0,1},{1,0},{2,3},{3,2},{4,5},{5,4},{6,7},{7,6},{8,9},{9,8},{10,11... | collective-permute-start | bytes 98312 | tf_op jit(solution)/shard_map/ppermute | solution.py:200
  27.0 0.7 %convert_element_type.3.own_k_ref = f32[4,256]{1,0:T(4,128)S(1)} convert(bf16[4,256]{1,0:T(4,128)(2,1)} %param.14) | non-fusion elementwise | flops 1024 | bytes 6144 | tf_op jit(solution)/shard_map/convert_element_type | solution.py:86
  27.7 0.7 %copy.19 = bf16[1,4,16,128]{3,2,1,0:T(8,128)(2,1)S(1)} copy(bf16[1,4,16,128]{3,1,2,0:T(4,128)(2,1)} %bitcast.14) | data formatting | bytes 32768
  28.4 0.0 copy-start.3
  28.4 0.7 %copy-done.3 = s32[4]{0:T(128)S(1)} copy-done((s32[4]{0:T(128)S(1)}, s32[4]{0:T(128)}, u32[]{:S(2)}) %copy-start.3) | copy-done | bytes 40
  29.1 4.6 %attend_cache.1 = (f32[4,16,128]{2,1,0:T(8,128)S(1)}, f32[4,16,128]{2,1,0:T(8,128)S(1)}) custom-call(s32[4]{0:T(128)S(1)} %copy-done.3, bf16[4,16,128]{2,1,0:T(8,128)(2,1)S(1)} %bitcast.11, bf16[4,1024,256]{2,1,0:T(8,128)(2,1)} %k_ref.1, bf16[4,1024,256]{2,1,0:T(8,128)(2,1)} %v_ref.1, f32[4,256]{1,0:T(4,128)S(1)} %convert_element_type.3.own_k_ref), custom_call_target="tpu_custom_call" | custom-call | flops 67108864 | bytes 4194304 | tf_op jit(solution)/shard_map/attend_cache/pallas_call | solution.py:62
  33.8 0.0 copy-done.4
  33.8 0.1 select_reduce_fusion.place_ref
  34.0 0.0 collective-permute-done.hid_other_ref
  34.0 0.0 collective-permute-done.1.theirs_ref
  34.0 0.0 copy-done.2
  34.0 0.0 copy-start.1
  34.0 2.2 %copy-done.1 = bf16[8192,256]{1,0:T(8,128)(2,1)S(1)} copy-done((bf16[8192,256]{1,0:T(8,128)(2,1)S(1)}, bf16[8192,256]{1,0:T(8,128)(2,1)}, u32[]{:S(2)}) %copy-start.1) | copy-done | bytes 4194328
  36.2 4.1 %fold_blocks.1 = (bf16[8192,256]{1,0:T(8,128)(2,1)}, bf16[4,256]{1,0:T(4,128)(2,1)}, bf16[4,2048]{1,0:T(4,128)(2,1)}) custom-call(s32[8]{0:T(128)S(1)} %select_reduce_fusion.place_ref, s32[1]{0:T(128)} %bitcast.core_ref, bf16[64,256]{1,0:T(8,128)(2,1)S(1)} %reshape.28.up_ref, bf16[4,4096]{1,0:T(4,128)(2,1)S(1)} %copy-done.2, ...), custom_call_target="tpu_custom_call" | custom-call | flops 285212672 | bytes 9437184 | tf_op jit(solution)/shard_map/fold_blocks/pallas_call | solution.py:146
  (5 shorter events, 0.1 us)
Async XLA Ops:
  0.6 0.9 %copy-start = (bf16[64,1024]{1,0:T(8,128)(2,1)S(1)}, bf16[64,1024]{1,0:T(8,128)(2,1)}, u32[]{:S(2)}) copy-start(bf16[64,1024]{1,0:T(8,128)(2,1)} %param.17) | copy-start | bytes 393220
  0.6 33.3 %copy-start.2 = (bf16[4,4096]{1,0:T(4,128)(2,1)S(1)}, bf16[4,4096]{1,0:T(4,128)(2,1)}, u32[]{:S(2)}) copy-start(bf16[4,4096]{1,0:T(4,128)(2,1)} %hid_own_ref.1) | copy-start | bytes 98308
  0.7 33.1 %copy-start.4 = (s32[8]{0:T(128)S(1)}, s32[8]{0:T(128)}, u32[]{:S(2)}) copy-start(s32[8]{0:T(128)} %param.19) | copy-start | bytes 100
  26.5 7.5 %collective-permute-start.1 = (bf16[8,40,1024]{2,1,0:T(8,128)(2,1)S(1)}, bf16[8,40,1024]{2,1,0:T(8,128)(2,1)S(1)}, u32[]{:S(2)}, u32[]{:S(2)}) collective-permute-start(bf16[8,40,1024]{2,1,0:T(8,128)(2,1)S(1)} %all_to_all.5.mine_ref), channel_id=1, source_target_pairs={{0,1},{1,0},{2,3},{3,2},{4,5},{5,4},{6,7},{7,6},{8,9},{9,8},{10,11... | collective-permute-start | bytes 1966088 | tf_op jit(solution)/shard_map/ppermute | solution.py:201
  26.5 7.4 %collective-permute-start = (bf16[4,4096]{1,0:T(4,128)(2,1)}, bf16[4,4096]{1,0:T(4,128)(2,1)S(1)}, u32[]{:S(2)}, u32[]{:S(2)}) collective-permute-start(bf16[4,4096]{1,0:T(4,128)(2,1)} %hid_own_ref.1), channel_id=1, source_target_pairs={{0,1},{1,0},{2,3},{3,2},{4,5},{5,4},{6,7},{7,6},{8,9},{9,8},{10,11... | collective-permute-start | bytes 98312 | tf_op jit(solution)/shard_map/ppermute | solution.py:200
  28.4 0.7 %copy-start.3 = (s32[4]{0:T(128)S(1)}, s32[4]{0:T(128)}, u32[]{:S(2)}) copy-start(s32[4]{0:T(128)} %lengths_ref.1) | copy-start | bytes 52
  34.0 2.2 %copy-start.1 = (bf16[8192,256]{1,0:T(8,128)(2,1)S(1)}, bf16[8192,256]{1,0:T(8,128)(2,1)}, u32[]{:S(2)}) copy-start(bf16[8192,256]{1,0:T(8,128)(2,1)} %served.1) | copy-start | bytes 12582916

commit v3 on v1

v3 whole, which is shorter than its diff:
```python
import functools

import jax
import jax.numpy as jnp
from jax import lax
from jax.experimental import pallas as pl
from jax.experimental.pallas import tpu as pltpu
from jax.sharding import PartitionSpec as P

HEAD_SIZE = 128
ADAPTER_SCALE = 2.0


def attend_kernel(start, lengths_ref, q_ref, k_ref, v_ref, own_k_ref, after_ref, context_ref,
                  own_weight_ref):
    row = start + pl.program_id(0)
    length = lengths_ref[row]
    q = q_ref[0]
    heads = q.shape[0]
    local_heads = k_ref.shape[2] // HEAD_SIZE
    group = heads // local_heads
    cache_len = k_ref.shape[1]
    scaling = 1.0 / HEAD_SIZE**0.5
    head_of = lax.broadcasted_iota(jnp.int32, (heads, HEAD_SIZE), 0) // group
    q32 = q.astype(jnp.float32)
    spread = jnp.concatenate(
        [jnp.where(head_of == h, q32, 0.0) for h in range(local_heads)], axis=1
    )
    scores = (
        lax.dot_general(
            spread.astype(jnp.bfloat16), k_ref[0], (((1,), (1,)), ((), ())),
            preferred_element_type=jnp.float32,
        )
        * scaling
    )
    own_key = own_k_ref[pl.ds(row, 1), :]
    own = jnp.sum(spread * own_key, axis=1, keepdims=True) * scaling
    valid = lax.broadcasted_iota(jnp.int32, (heads, cache_len), 1) < length
    masked = jnp.where(valid, scores, -1e30)
    largest = jnp.maximum(jnp.max(masked, axis=1, keepdims=True), own)
    cached_exp = jnp.where(valid, jnp.exp(masked - largest), 0.0)
    own_exp = jnp.exp(own - largest)
    normaliser = jnp.sum(cached_exp, axis=1, keepdims=True) + own_exp
    weights = (cached_exp / normaliser).astype(jnp.bfloat16)
    weight_own = (own_exp / normaliser).astype(jnp.bfloat16).astype(jnp.float32)
    wide = jnp.dot(weights, v_ref[0], preferred_element_type=jnp.float32)
    context = wide[:, :HEAD_SIZE]
    for h in range(1, local_heads):
        context = jnp.where(
            head_of == h, wide[:, h * HEAD_SIZE : (h + 1) * HEAD_SIZE], context
        )
    context_ref[0] = context
    own_weight_ref[0] = jnp.broadcast_to(weight_own, (heads, HEAD_SIZE))


def attend(start, count, queries, stored_keys, stored_values, own_key, lengths, after):
    rows, cache_len, width = stored_keys.shape
    heads = queries.shape[1]
    out = jax.ShapeDtypeStruct((count, heads, HEAD_SIZE), jnp.float32)
    spec = pl.BlockSpec((1, heads, HEAD_SIZE), lambda i: (i, 0, 0))
    cache_spec = pl.BlockSpec((1, cache_len, width), lambda i: (start + i, 0, 0))
    return pl.pallas_call(
        functools.partial(attend_kernel, start),
        grid=(count,),
        out_shape=(out, out),
        in_specs=[
            pl.BlockSpec(memory_space=pltpu.SMEM),
            pl.BlockSpec((1, heads, HEAD_SIZE), lambda i: (start + i, 0, 0)),
            cache_spec,
            cache_spec,
            pl.BlockSpec((rows, width), lambda i: (0, 0)),
            pl.BlockSpec(memory_space=pl.ANY),
        ],
        out_specs=(spec, spec),
        compiler_params=pltpu.CompilerParams(vmem_limit_bytes=16 * 2**20),
        cost_estimate=pl.CostEstimate(
            flops=4 * count * heads * cache_len * width,
            bytes_accessed=4 * count * cache_len * width,
            transcendentals=count * heads * cache_len,
        ),
        name="attend_cache",
    )(lengths, queries, stored_keys, stored_values, own_key, after)


def fold_kernel(slots, first, prefetch, last, place_ref, core_ref, up_ref, hid_own_ref, hid_other_ref, *rest):
    rest = list(rest)
    served = rest.pop(0)
    blocks = [rest.pop(0) for _ in slots]
    if not first:
        rest.pop(0)
        total = rest.pop(0)[...]
    if last:
        ahead, context_ref, own_weight_ref = rest[:3]
        merged, fresh_ref, attended_ref = rest[3:6]
        rest = rest[6:]
    else:
        merged, total_ref = rest[:2]
        rest = rest[2:]
        if prefetch:
            ahead = rest.pop(0)
    w_buf, m_buf, feat, in_sem, out_sem = rest
    width = blocks[0].shape[1]
    half = hid_own_ref.shape[1]
    final = place_ref.shape[0] - 1

    def rows_of(slot):
        return pl.ds(pl.multiple_of(place_ref[slot] * width, width), width)

    def fetch(i, slot, into):
        return pltpu.make_async_copy(served.at[rows_of(slot)], into, in_sem.at[i])

    def store(i):
        return pltpu.make_async_copy(m_buf.at[i], merged.at[rows_of(slots[i])], out_sem.at[i])

    if not last:
        for i, slot in enumerate(slots):
            fetch(i, slot, w_buf.at[i]).start()
        if prefetch:
            fetch(len(slots), final, ahead).start()
    core = core_ref[0]
    feat[core] = hid_own_ref[...]
    feat[1 - core] = hid_other_ref[...]
    up = (up_ref[...].astype(jnp.float32) * ADAPTER_SCALE).astype(jnp.bfloat16)
    if first:
        total = jnp.zeros(total_ref.shape, jnp.float32)
    for i, slot in enumerate(slots):
        update = lax.dot_general(
            blocks[i][...], up, (((0,), (0,)), ((), ())), preferred_element_type=jnp.float32
        )
        if last:
            rows = ahead[...]
        else:
            fetch(i, slot, w_buf.at[i]).wait()
            rows = w_buf[i]
        rows = (rows.astype(jnp.float32) + update).astype(jnp.bfloat16)
        m_buf[i] = rows
        store(i).start()
        top = place_ref[slot] * width
        in_half = top // half
        features = feat[in_half, :, pl.ds(pl.multiple_of(top - in_half * half, width), width)]
        total = total + jnp.dot(features, rows, preferred_element_type=jnp.float32)
    if last:
        fresh = total.astype(jnp.bfloat16)
        fresh_ref[...] = fresh
        value = fresh.astype(jnp.float32)
        heads = attended_ref.shape[1] // HEAD_SIZE
        group = heads // (fresh_ref.shape[1] // HEAD_SIZE)
        for h in range(heads):
            cols = slice(h * HEAD_SIZE, (h + 1) * HEAD_SIZE)
            at = (h // group) * HEAD_SIZE
            attended_ref[:, cols] = (
                context_ref[:, cols] + own_weight_ref[:, cols] * value[:, at : at + HEAD_SIZE]
            ).astype(jnp.bfloat16)
    else:
        total_ref[...] = total
        if prefetch:
            fetch(len(slots), final, ahead).wait()
    for i in range(len(slots)):
        store(i).wait()


def fold(slots, place, core, up, hid_own, hid_other, served, blocks, prefetch=False, state=(),
         finish=()):
    first, last = not state, bool(finish)
    count = len(slots)
    rank, width = blocks[0].shape
    rows = hid_own.shape[0]
    depth, cols = served.shape
    vmem = pl.BlockSpec(memory_space=pltpu.VMEM)
    smem = pl.BlockSpec(memory_space=pltpu.SMEM)
    hbm = pl.BlockSpec(memory_space=pltpu.HBM)
    in_specs = [smem, smem, vmem, vmem, vmem, hbm] + [vmem] * count
    operands = [place, core, up, hid_own, hid_other, served, *blocks]
    aliases = {}
    if not first:
        aliases = {len(operands): 0}
        in_specs += [hbm, vmem]
        operands += state
    in_specs += [vmem] * len(finish)
    operands += finish
    out_shape = [jax.ShapeDtypeStruct((depth, cols), jnp.bfloat16)]
    if last:
        out_shape += [
            jax.ShapeDtypeStruct((rows, cols), jnp.bfloat16),
            jax.ShapeDtypeStruct(finish[1].shape, jnp.bfloat16),
        ]
    else:
        out_shape += [jax.ShapeDtypeStruct((rows, cols), jnp.float32)]
        if prefetch:
            out_shape += [jax.ShapeDtypeStruct((width, cols), jnp.bfloat16)]
    return pl.pallas_call(
        functools.partial(fold_kernel, slots, first, prefetch, last),
        out_shape=out_shape,
        in_specs=in_specs,
        out_specs=[hbm] + [vmem] * (len(out_shape) - 1),
        input_output_aliases=aliases,
        scratch_shapes=[
            pltpu.VMEM((1 if last else count, width, cols), jnp.bfloat16),
            pltpu.VMEM((count, width, cols), jnp.bfloat16),
            pltpu.VMEM((2,) + hid_own.shape, jnp.bfloat16),
            pltpu.SemaphoreType.DMA((count + 1,)),
            pltpu.SemaphoreType.DMA((count,)),
        ],
        compiler_params=pltpu.CompilerParams(vmem_limit_bytes=24 * 2**20),
        cost_estimate=pl.CostEstimate(
            flops=2 * count * width * cols * (rank + rows),
            bytes_accessed=4 * count * width * cols,
            transcendentals=0,
        ),
        name="fold_blocks",
    )(*operands)


def ring_member(spot, n):
    return jnp.where(spot < (n + 1) // 2, 2 * spot, 2 * (n - 1 - spot) + 1)


def body(
    hidden_in,
    queries,
    stored_keys,
    stored_values,
    fresh_token_key,
    lengths,
    served_value_weight,
    adapter_in,
    adapter_out,
    owner_rank,
):
    n = lax.axis_size("replica")
    replica = lax.axis_index("replica")
    core = lax.axis_index("tensor")
    swap = [(0, 1), (1, 0)]
    order = list(range(0, n, 2)) + list(range(n - 1 - n % 2, 0, -2))
    around = []
    for spot in range(n):
        here, there = order[spot], order[(spot + 1) % n]
        around.append((here * 2, there * 2))
        around.append((there * 2 + 1, here * 2 + 1))

    rows = queries.shape[0]
    split = rows // 2
    cache = [
        pltpu.with_memory_space_constraint(x, pltpu.HBM) for x in (stored_keys, stored_values)
    ]
    given = (queries.reshape(rows, -1, HEAD_SIZE), *cache, fresh_token_key.astype(jnp.float32), lengths)
    parts = []

    steps = n // 2
    shifts, cuts = [0], []
    for step in range(1, steps + 1):
        shifts += [step, -step] if 2 * step < n else [step]
        cuts.append(len(shifts))
    spot = jnp.where(replica % 2 == 0, replica // 2, n - 1 - replica // 2)
    way = jnp.where(core == 0, -1, 1)
    source = ring_member((spot + way * jnp.array(shifts, jnp.int32) + n) % n, n)
    spots = jnp.arange(n, dtype=jnp.int32)[None, :]
    place = jnp.sum(jnp.where(owner_rank[None, :] == source[:, None], spots, 0), axis=1)

    served = pltpu.with_memory_space_constraint(served_value_weight, pltpu.HBM)
    blocks, state, done = [adapter_in], [], 0
    passed = adapter_in
    for step in range(1, steps + 1):
        passed = lax.ppermute(passed, ("replica", "tensor"), around)
        if step == 1:
            hid_other = lax.ppermute(hidden_in, "tensor", swap)
            up = lax.all_to_all(
                jnp.broadcast_to(adapter_out[None], (n,) + adapter_out.shape),
                "replica", split_axis=0, concat_axis=0,
            ).reshape(n * adapter_out.shape[0], adapter_out.shape[1])
            common = (
                place.astype(jnp.int32), core.astype(jnp.int32).reshape(1), up, hidden_in,
                hid_other, served,
            )
            parts.append(attend(0, split, *given, up))
            beside = parts[0]
        elif step == 2:
            parts.append(attend(split, rows - split, *given, blocks[1]))
            beside = parts[1]
        else:
            upto = n - 1 if step == steps else cuts[step - 3]
            state = fold(
                range(done, upto), *common, blocks[done:upto], prefetch=step == steps, state=state
            )
            beside, done = state, upto
        if step < steps:
            passed, beside = lax.optimization_barrier((passed, beside))
            if step <= 2:
                parts[-1] = beside
            else:
                state = beside
        blocks.append(passed)
        if 2 * step < n:
            blocks.append(lax.ppermute(passed, "tensor", swap))
    context, own_weight = (
        jnp.concatenate(pair, axis=0).reshape(queries.shape) for pair in zip(*parts)
    )
    merged, total, ahead = state
    merged, fresh_token_value, attended = fold(
        range(done, n), *common, blocks[done:], state=[merged, total],
        finish=[ahead, context, own_weight],
    )
    return (merged, fresh_token_value, attended)


def solution(mesh):
    in_specs = (
        P(("groups", "replica"), "tensor"),
        P(("groups", "replica"), "tensor"),
        P(("groups", "replica"), None, "tensor"),
        P(("groups", "replica"), None, "tensor"),
        P(("groups", "replica"), "tensor"),
        P(("groups", "replica")),
        P(None, "tensor"),
        P("groups", "replica"),
        P(("groups", "replica"), "tensor"),
        P("groups"),
    )
    out_specs = (
        P("groups", "tensor"),
        P(("groups", "replica"), "tensor"),
        P(("groups", "replica"), "tensor"),
    )
    return jax.shard_map(body, mesh=mesh, in_specs=in_specs, out_specs=out_specs, check_vma=False)
```

time: 54.5 us -> 38.2 us (0.70)
  waiting for transfers between devices: 20.5 us -> 8.09 us
  Pallas kernels: 9.83 us -> 15.5 us
  starting transfers between devices: 15.3 us -> 9.85 us
  local copies, waits for them, and re-layouts: 6.84 us -> 2.73 us
    ppermute x14 -> x7, waiting for transfers between devices: 20.5 us -> 2.81 us  [the longest x4 2.09 us: body(): passed = lax.ppermute(passed, ('replica', 'tensor'), around)]
    ppermute x14 -> x7, starting transfers between devices: 15.2 us -> 5.02 us  [the longest x4 4.45 us: body(): passed = lax.ppermute(passed, ('replica', 'tensor'), around)]
    pallas_call x2 -> x5, Pallas kernels: 9.83 us -> 15.5 us  [the longest x3 10.1 us: fold(): pl.pallas_call(functools.partial(fold_kernel, slots, first, prefetch, las...]
    unnamed x34 -> x15, local copies, waits for them, and re-layouts: 6.8 us -> 1.43 us
    all_to_all x0 -> x1, waiting for transfers between devices: none -> 5.28 us  [body(): lax.all_to_all(jnp.broadcast_to(adapter_out[None], (n,) + adapter_out.sha...]
    all_to_all x0 -> x1, starting transfers between devices: none -> 4.82 us  [body(): lax.all_to_all(jnp.broadcast_to(adapter_out[None], (n,) + adapter_out.sha...]
    broadcast_in_dim x0 -> x1, local copies, waits for them, and re-layouts: none -> 1.3 us  [body(): jnp.broadcast_to(adapter_out[None], (n,) + adapter_out.shape)]
  transfers between devices with their start and end apart: 15 -> 9, of which waited for: 6 -> 4; matrix products, arithmetic and copies ran while one was open for 3% -> 8% of each run, Pallas kernels for 6% -> 35%
where the time goes in v3:
time: 38.2 us; the launch traced here: 37.8 us
  Pallas kernels  15.5 us (41%)
  starting transfers between devices  9.85 us (26%)
  waiting for transfers between devices  8.09 us (21%)
  local copies, waits for them, and re-layouts  2.73 us (7%)
  other arithmetic  0.89 us (2%)
  between operations  0.74 us (2%)
    pallas_call x3, Pallas kernels, fold(): pl.pallas_call(functools.partial(fold_kernel, slots, first, prefetch, las...  10.1 us
    pallas_call x2, Pallas kernels, attend(): pl.pallas_call(functools.partial(attend_kernel, start), grid=(count,), ou...  5.37 us
    all_to_all x1, waiting for transfers between devices, body(): lax.all_to_all(jnp.broadcast_to(adapter_out[None], (n,) + adapter_out.sha...  5.28 us
    all_to_all x1, starting transfers between devices, body(): lax.all_to_all(jnp.broadcast_to(adapter_out[None], (n,) + adapter_out.sha...  4.82 us
    ppermute x4, starting transfers between devices, body(): passed = lax.ppermute(passed, ('replica', 'tensor'), around)  4.45 us
    ppermute x4, waiting for transfers between devices, body(): passed = lax.ppermute(passed, ('replica', 'tensor'), around)  2.09 us
    unnamed x15, local copies, waits for them, and re-layouts  1.43 us
    broadcast_in_dim x1, local copies, waits for them, and re-layouts, body(): jnp.broadcast_to(adapter_out[None], (n,) + adapter_out.shape)  1.3 us
  transfers between devices with their start and end apart: 9, of which 4 were waited for; matrix products, arithmetic and copies ran while one was open for 8% of the time, Pallas kernels for 35%

profile of v3, /device:TPU:0, one launch (start us, length us, event | category | flops | bytes accessed | tf_op | source)
XLA Modules:
  0.0 37.8 jit_solution(15747300443236246866)
XLA Ops:
  0.6 0.0 copy-start.3
  0.7 3.1 %collective-permute-start.1 = (bf16[64,1024]{1,0:T(8,128)(2,1)}, bf16[64,1024]{1,0:T(8,128)(2,1)S(1)}, u32[]{:S(2)}, u32[]{:S(2)}) collective-permute-start(bf16[64,1024]{1,0:T(8,128)(2,1)} %rest_1_.1), channel_id=1, source_target_pairs={{0,4},{5,1},{4,8},{9,5},{8,12},{13,9},{12,14},{15,13},{14,10},{11,... | collective-permute-start | bytes 393224 | tf_op jit(solution)/shard_map/ppermute | solution.py:264
  3.7 1.3 %broadcast_in_dim.23 = bf16[8,8,256]{2,1,0:T(8,128)(2,1)} broadcast(bf16[8,256]{1,0:T(8,128)(2,1)} %param.19), dimensions={1,2} | broadcast | bytes 36864 | tf_op jit(solution)/shard_map/broadcast_in_dim | solution.py:268
  5.0 4.8 %all-to-all-start = ((bf16[8,8,256]{2,1,0:T(8,128)(2,1)}), bf16[8,8,256]{2,1,0:T(8,128)(2,1)S(1)}, u32[]{:S(2)}, u32[]{:S(2)}) async-start(bf16[8,8,256]{2,1,0:T(8,128)(2,1)} %broadcast_in_dim.23), calls=%async_computation | async-start | bytes 65536 | tf_op jit(solution)/shard_map/all_to_all | solution.py:267
  9.9 0.7 %convert_element_type.3.own_k_ref = f32[4,256]{1,0:T(4,128)S(1)} convert(bf16[4,256]{1,0:T(4,128)(2,1)} %param.15) | non-fusion elementwise | flops 1024 | bytes 6144 | tf_op jit(solution)/shard_map/convert_element_type | solution.py:246
  10.5 0.7 %copy.24 = bf16[1,4,16,128]{3,2,1,0:T(8,128)(2,1)S(1)} copy(bf16[1,4,16,128]{3,1,2,0:T(4,128)(2,1)} %bitcast.24) | data formatting | bytes 32768
  11.3 5.3 %all-to-all-done = bf16[8,8,256]{2,1,0:T(8,128)(2,1)S(1)} async-done(((bf16[8,8,256]{2,1,0:T(8,128)(2,1)}), bf16[8,8,256]{2,1,0:T(8,128)(2,1)S(1)}, u32[]{:S(2)}, u32[]{:S(2)}) %all-to-all-start) | async-done | bytes 32800 | tf_op jit(solution)/shard_map/all_to_all | solution.py:267
  16.5 0.7 %copy-done.2 = s32[4]{0:T(128)S(1)} copy-done((s32[4]{0:T(128)S(1)}, s32[4]{0:T(128)}, u32[]{:S(2)}) %copy-start.2) | copy-done | bytes 40
  17.2 2.7 %attend_cache.2 = (f32[2,16,128]{2,1,0:T(8,128)S(1)}, f32[2,16,128]{2,1,0:T(8,128)S(1)}) custom-call(s32[4]{0:T(128)S(1)} %copy-done.2, bf16[4,16,128]{2,1,0:T(8,128)(2,1)S(1)} %bitcast.20, bf16[4,1024,256]{2,1,0:T(8,128)(2,1)} %k_ref.3, bf16[4,1024,256]{2,1,0:T(8,128)(2,1)} %v_ref.3, f32[4,256]{1,0:T(4,128)S(1)} %convert_element_type.3.own_k_ref, ...), custom_call_target="tpu_custom_call" | custom-call | flops 33554432 | bytes 2097152 | tf_op jit(solution)/shard_map/attend_cache/pallas_call | solution.py:62
  19.9 0.0 collective-permute-done.1.after_ref.rest_2_
  19.9 0.4 %collective-permute-start.2 = (bf16[64,1024]{1,0:T(8,128)(2,1)S(1)}, bf16[64,1024]{1,0:T(8,128)(2,1)S(1)}, u32[]{:S(2)}, u32[]{:S(2)}) collective-permute-start(bf16[64,1024]{1,0:T(8,128)(2,1)S(1)} %collective-permute-done.1.after_ref.rest_2_), channel_id=1, source_target_pairs={{0,4},{5,1},{4,8},{9,5},{8,12},{13,9},{12,14},{15,13},{14,10},{11,... | collective-permute-start | bytes 393224 | tf_op jit(solution)/shard_map/ppermute | solution.py:264
  20.3 0.5 %collective-permute-start.4 = (bf16[64,1024]{1,0:T(8,128)(2,1)S(1)}, bf16[64,1024]{1,0:T(8,128)(2,1)S(1)}, u32[]{:S(2)}, u32[]{:S(2)}) collective-permute-start(bf16[64,1024]{1,0:T(8,128)(2,1)S(1)} %collective-permute-done.1.after_ref.rest_2_), channel_id=1, source_target_pairs={{0,1},{1,0},{2,3},{3,2},{4,5},{5,4},{6,7},{7,6},{8,9},{9,8},{10,11... | collective-permute-start | bytes 393224 | tf_op jit(solution)/shard_map/ppermute | solution.py:294
  20.9 2.6 %attend_cache.3 = (f32[2,16,128]{2,1,0:T(8,128)S(1)}, f32[2,16,128]{2,1,0:T(8,128)S(1)}) custom-call(s32[4]{0:T(128)S(1)} %copy-done.3, bf16[4,16,128]{2,1,0:T(8,128)(2,1)S(1)} %bitcast.21, bf16[4,1024,256]{2,1,0:T(8,128)(2,1)} %k_ref.3, bf16[4,1024,256]{2,1,0:T(8,128)(2,1)} %v_ref.3, f32[4,256]{1,0:T(4,128)S(1)} %convert_element_type.3.own_k_ref, ...), custom_call_target="tpu_custom_call" | custom-call | flops 33554432 | bytes 2097152 | tf_op jit(solution)/shard_map/attend_cache/pallas_call | solution.py:62
  23.5 1.4 %collective-permute-done.2.rest_1_ = bf16[64,1024]{1,0:T(8,128)(2,1)S(1)} collective-permute-done((bf16[64,1024]{1,0:T(8,128)(2,1)S(1)}, bf16[64,1024]{1,0:T(8,128)(2,1)S(1)}, u32[]{:S(2)}, u32[]{:S(2)}) %collective-permute-start.2) | collective-permute-done | bytes 131104 | tf_op jit(solution)/shard_map/ppermute | solution.py:264
  24.9 0.4 %collective-permute-start.3 = (bf16[64,1024]{1,0:T(8,128)(2,1)S(1)}, bf16[64,1024]{1,0:T(8,128)(2,1)S(1)}, u32[]{:S(2)}, u32[]{:S(2)}) collective-permute-start(bf16[64,1024]{1,0:T(8,128)(2,1)S(1)} %collective-permute-done.2.rest_1_), channel_id=1, source_target_pairs={{0,4},{5,1},{4,8},{9,5},{8,12},{13,9},{12,14},{15,13},{14,10},{11,... | collective-permute-start | bytes 393224 | tf_op jit(solution)/shard_map/ppermute | solution.py:264
  25.3 0.2 select_reduce_fusion.place_ref
  25.5 0.1 collective-permute-start.6
  25.6 0.0 collective-permute-done.hid_other_ref
  25.6 3.6 %fold_blocks.3 = (bf16[8192,256]{1,0:T(8,128)(2,1)}, f32[4,256]{1,0:T(4,128)S(1)}) custom-call(s32[8]{0:T(128)S(1)} %select_reduce_fusion.place_ref, s32[1]{0:T(128)} %bitcast.core_ref, bf16[64,256]{1,0:T(8,128)(2,1)S(1)} %bitcast.17, bf16[4,4096]{1,0:T(4,128)(2,1)S(1)} %copy-done, bf16[4,4096]{1,0:T(4,128)(2,1)S(1)} %collective-permute-done.hid_other_ref, ...), custom_call_target="tpu_custom_call" | custom-call | flops 106954752 | bytes 3145728 | tf_op jit(solution)/shard_map/fold_blocks/pallas_call | solution.py:191
  29.2 0.7 %collective-permute-done.3.rest_3_ = bf16[64,1024]{1,0:T(8,128)(2,1)S(1)} collective-permute-done((bf16[64,1024]{1,0:T(8,128)(2,1)S(1)}, bf16[64,1024]{1,0:T(8,128)(2,1)S(1)}, u32[]{:S(2)}, u32[]{:S(2)}) %collective-permute-start.3) | collective-permute-done | bytes 131104 | tf_op jit(solution)/shard_map/ppermute | solution.py:264
  29.9 0.6 %collective-permute-start.5 = (bf16[64,1024]{1,0:T(8,128)(2,1)S(1)}, bf16[64,1024]{1,0:T(8,128)(2,1)S(1)}, u32[]{:S(2)}, u32[]{:S(2)}) collective-permute-start(bf16[64,1024]{1,0:T(8,128)(2,1)S(1)} %collective-permute-done.3.rest_3_), channel_id=1, source_target_pairs={{0,4},{5,1},{4,8},{9,5},{8,12},{13,9},{12,14},{15,13},{14,10},{11,... | collective-permute-start | bytes 393224 | tf_op jit(solution)/shard_map/ppermute | solution.py:264
  30.5 0.7 %collective-permute-done.7.rest_4_ = bf16[64,1024]{1,0:T(8,128)(2,1)S(1)} collective-permute-done((bf16[64,1024]{1,0:T(8,128)(2,1)S(1)}, bf16[64,1024]{1,0:T(8,128)(2,1)S(1)}, u32[]{:S(2)}, u32[]{:S(2)}) %collective-permute-start.7) | collective-permute-done | bytes 131104 | tf_op jit(solution)/shard_map/ppermute | solution.py:294
  31.2 4.2 %fold_blocks.4 = (bf16[8192,256]{1,0:T(8,128)(2,1)}, f32[4,256]{1,0:T(4,128)S(1)}, bf16[1024,256]{1,0:T(8,128)(2,1)S(1)}) custom-call(s32[8]{0:T(128)S(1)} %select_reduce_fusion.place_ref, s32[1]{0:T(128)} %bitcast.core_ref, bf16[64,256]{1,0:T(8,128)(2,1)S(1)} %bitcast.18, bf16[4,4096]{1,0:T(4,128)(2,1)S(1)} %copy-done, ...), custom_call_target="tpu_custom_call", output_to_operand_aliasing={{0}: (10, {})} | custom-call | flops 142606336 | bytes 4194304 | tf_op jit(solution)/shard_map/fold_blocks/pallas_call | solution.py:191
  35.5 2.3 %fold_blocks.5 = (bf16[8192,256]{1,0:T(8,128)(2,1)}, bf16[4,256]{1,0:T(4,128)(2,1)}, bf16[4,2048]{1,0:T(4,128)(2,1)}) custom-call(s32[8]{0:T(128)S(1)} %select_reduce_fusion.place_ref, s32[1]{0:T(128)} %bitcast.core_ref, bf16[64,256]{1,0:T(8,128)(2,1)S(1)} %bitcast.19, bf16[4,4096]{1,0:T(4,128)(2,1)S(1)} %copy-done, ...), custom_call_target="tpu_custom_call", output_to_operand_aliasing={{0}: (7, {})} | custom-call | flops 35651584 | bytes 1048576 | tf_op jit(solution)/shard_map/fold_blocks/pallas_call | solution.py:191
  (19 shorter events, 0.1 us)
Async XLA Ops:
  0.6 20.2 %copy-start.3 = (s32[4]{0:T(128)S(1)}, s32[4]{0:T(128)}, u32[]{:S(2)}) copy-start(s32[4]{0:T(128)} %lengths_ref.3) | copy-start | bytes 52
  0.6 19.7 %copy-start = (bf16[4,4096]{1,0:T(4,128)(2,1)S(1)}, bf16[4,4096]{1,0:T(4,128)(2,1)}, u32[]{:S(2)}) copy-start(bf16[4,4096]{1,0:T(4,128)(2,1)} %hid_own_ref.5) | copy-start | bytes 98308
  0.7 19.3 %collective-permute-start.1 = (bf16[64,1024]{1,0:T(8,128)(2,1)}, bf16[64,1024]{1,0:T(8,128)(2,1)S(1)}, u32[]{:S(2)}, u32[]{:S(2)}) collective-permute-start(bf16[64,1024]{1,0:T(8,128)(2,1)} %rest_1_.1), channel_id=1, source_target_pairs={{0,4},{5,1},{4,8},{9,5},{8,12},{13,9},{12,14},{15,13},{14,10},{11,... | collective-permute-start | bytes 393224 | tf_op jit(solution)/shard_map/ppermute | solution.py:264
  5.0 11.5 %all-to-all-start = ((bf16[8,8,256]{2,1,0:T(8,128)(2,1)}), bf16[8,8,256]{2,1,0:T(8,128)(2,1)S(1)}, u32[]{:S(2)}, u32[]{:S(2)}) async-start(bf16[8,8,256]{2,1,0:T(8,128)(2,1)} %broadcast_in_dim.23), calls=%async_computation | async-start | bytes 65536 | tf_op jit(solution)/shard_map/all_to_all | solution.py:267
  16.5 0.7 %copy-start.2 = (s32[4]{0:T(128)S(1)}, s32[4]{0:T(128)}, u32[]{:S(2)}) copy-start(s32[4]{0:T(128)} %lengths_ref.3) | copy-start | bytes 52
  17.2 8.1 %copy-start.4 = (s32[8]{0:T(128)S(1)}, s32[8]{0:T(128)}, u32[]{:S(2)}) copy-start(s32[8]{0:T(128)} %constant.60.clone) | copy-start | bytes 100
  17.2 8.1 %copy-start.5 = (s32[8]{0:T(128)S(1)}, s32[8]{0:T(128)}, u32[]{:S(2)}) copy-start(s32[8]{0:T(128)} %param.20) | copy-start | bytes 100
  17.2 8.4 %copy-start.1 = (bf16[64,1024]{1,0:T(8,128)(2,1)S(1)}, bf16[64,1024]{1,0:T(8,128)(2,1)}, u32[]{:S(2)}) copy-start(bf16[64,1024]{1,0:T(8,128)(2,1)} %rest_1_.1) | copy-start | bytes 393220
  19.9 5.0 %collective-permute-start.2 = (bf16[64,1024]{1,0:T(8,128)(2,1)S(1)}, bf16[64,1024]{1,0:T(8,128)(2,1)S(1)}, u32[]{:S(2)}, u32[]{:S(2)}) collective-permute-start(bf16[64,1024]{1,0:T(8,128)(2,1)S(1)} %collective-permute-done.1.after_ref.rest_2_), channel_id=1, source_target_pairs={{0,4},{5,1},{4,8},{9,5},{8,12},{13,9},{12,14},{15,13},{14,10},{11,... | collective-permute-start | bytes 393224 | tf_op jit(solution)/shard_map/ppermute | solution.py:264
  20.3 5.2 %collective-permute-start = (bf16[4,4096]{1,0:T(4,128)(2,1)S(1)}, bf16[4,4096]{1,0:T(4,128)(2,1)S(1)}, u32[]{:S(2)}, u32[]{:S(2)}) collective-permute-start(bf16[4,4096]{1,0:T(4,128)(2,1)S(1)} %copy-done), channel_id=1, source_target_pairs={{0,1},{1,0},{2,3},{3,2},{4,5},{5,4},{6,7},{7,6},{8,9},{9,8},{10,11... | collective-permute-start | bytes 98312 | tf_op jit(solution)/shard_map/ppermute | solution.py:266
  20.3 5.3 %collective-permute-start.4 = (bf16[64,1024]{1,0:T(8,128)(2,1)S(1)}, bf16[64,1024]{1,0:T(8,128)(2,1)S(1)}, u32[]{:S(2)}, u32[]{:S(2)}) collective-permute-start(bf16[64,1024]{1,0:T(8,128)(2,1)S(1)} %collective-permute-done.1.after_ref.rest_2_), channel_id=1, source_target_pairs={{0,1},{1,0},{2,3},{3,2},{4,5},{5,4},{6,7},{7,6},{8,9},{9,8},{10,11... | collective-permute-start | bytes 393224 | tf_op jit(solution)/shard_map/ppermute | solution.py:294
  24.9 5.0 %collective-permute-start.3 = (bf16[64,1024]{1,0:T(8,128)(2,1)S(1)}, bf16[64,1024]{1,0:T(8,128)(2,1)S(1)}, u32[]{:S(2)}, u32[]{:S(2)}) collective-permute-start(bf16[64,1024]{1,0:T(8,128)(2,1)S(1)} %collective-permute-done.2.rest_1_), channel_id=1, source_target_pairs={{0,4},{5,1},{4,8},{9,5},{8,12},{13,9},{12,14},{15,13},{14,10},{11,... | collective-permute-start | bytes 393224 | tf_op jit(solution)/shard_map/ppermute | solution.py:264
  25.5 5.0 %collective-permute-start.6 = (bf16[64,1024]{1,0:T(8,128)(2,1)S(1)}, bf16[64,1024]{1,0:T(8,128)(2,1)S(1)}, u32[]{:S(2)}, u32[]{:S(2)}) collective-permute-start(bf16[64,1024]{1,0:T(8,128)(2,1)S(1)} %collective-permute-done.2.rest_1_), channel_id=1, source_target_pairs={{0,1},{1,0},{2,3},{3,2},{4,5},{5,4},{6,7},{7,6},{8,9},{9,8},{10,11... | collective-permute-start | bytes 393224 | tf_op jit(solution)/shard_map/ppermute | solution.py:294
  29.9 1.3 %collective-permute-start.7 = (bf16[64,1024]{1,0:T(8,128)(2,1)S(1)}, bf16[64,1024]{1,0:T(8,128)(2,1)S(1)}, u32[]{:S(2)}, u32[]{:S(2)}) collective-permute-start(bf16[64,1024]{1,0:T(8,128)(2,1)S(1)} %collective-permute-done.3.rest_3_), channel_id=1, source_target_pairs={{0,1},{1,0},{2,3},{3,2},{4,5},{5,4},{6,7},{7,6},{8,9},{9,8},{10,11... | collective-permute-start | bytes 393224 | tf_op jit(solution)/shard_map/ppermute | solution.py:294
  29.9 5.6 %collective-permute-start.5 = (bf16[64,1024]{1,0:T(8,128)(2,1)S(1)}, bf16[64,1024]{1,0:T(8,128)(2,1)S(1)}, u32[]{:S(2)}, u32[]{:S(2)}) collective-permute-start(bf16[64,1024]{1,0:T(8,128)(2,1)S(1)} %collective-permute-done.3.rest_3_), channel_id=1, source_target_pairs={{0,4},{5,1},{4,8},{9,5},{8,12},{13,9},{12,14},{15,13},{14,10},{11,... | collective-permute-start | bytes 393224 | tf_op jit(solution)/shard_map/ppermute | solution.py:264

commit v4 on v3

v4 whole, which is shorter than its diff:
```python
import functools

import jax
import jax.numpy as jnp
from jax import lax
from jax.experimental import pallas as pl
from jax.experimental.pallas import tpu as pltpu
from jax.sharding import PartitionSpec as P

HEAD_SIZE = 128
ADAPTER_SCALE = 2.0

SMEM = pl.BlockSpec(memory_space=pltpu.SMEM)
VMEM = pl.BlockSpec(memory_space=pltpu.VMEM)
HBM = pl.BlockSpec(memory_space=pltpu.HBM)


def in_hbm(*arrays):
    return [pltpu.with_memory_space_constraint(x, pltpu.HBM) for x in arrays]


def attend_kernel(rows, lengths_hbm, q_ref, own_k_ref, k_hbm, v_hbm, *rest):
    context_ref, own_weight_ref, lengths, k_buf, v_buf, length_sem, k_sem, v_sem = rest[-8:]

    def copies(i, row):
        return (
            pltpu.make_async_copy(k_hbm.at[row], k_buf.at[i], k_sem.at[i]),
            pltpu.make_async_copy(v_hbm.at[row], v_buf.at[i], v_sem.at[i]),
        )

    get_lengths = pltpu.make_async_copy(lengths_hbm, lengths, length_sem)
    get_lengths.start()
    for i, row in enumerate(rows):
        for copy in copies(i, row):
            copy.start()
    queries = q_ref[...].astype(jnp.float32)
    own_keys = own_k_ref[...].astype(jnp.float32)
    heads = queries.shape[1] // HEAD_SIZE
    cache_len, width = k_buf.shape[1:]
    local_heads = width // HEAD_SIZE
    group = heads // local_heads
    scaling = 1.0 / HEAD_SIZE**0.5
    head_of = lax.broadcasted_iota(jnp.int32, (heads, HEAD_SIZE), 0) // group
    position = lax.broadcasted_iota(jnp.int32, (heads, cache_len), 1)
    get_lengths.wait()
    for i, row in enumerate(rows):
        q = jnp.concatenate(
            [
                queries[row : row + 1, h * HEAD_SIZE : (h + 1) * HEAD_SIZE]
                for h in range(heads)
            ],
            axis=0,
        )
        spread = jnp.concatenate(
            [jnp.where(head_of == h, q, 0.0) for h in range(local_heads)], axis=1
        )
        own = jnp.sum(spread * own_keys[row : row + 1], axis=1, keepdims=True) * scaling
        get_keys, get_values = copies(i, row)
        get_keys.wait()
        scores = (
            lax.dot_general(
                spread.astype(jnp.bfloat16), k_buf[i], (((1,), (1,)), ((), ())),
                preferred_element_type=jnp.float32,
            )
            * scaling
        )
        valid = position < lengths[row]
        masked = jnp.where(valid, scores, -1e30)
        largest = jnp.maximum(jnp.max(masked, axis=1, keepdims=True), own)
        cached_exp = jnp.where(valid, jnp.exp(masked - largest), 0.0)
        own_exp = jnp.exp(own - largest)
        normaliser = jnp.sum(cached_exp, axis=1, keepdims=True) + own_exp
        weights = (cached_exp / normaliser).astype(jnp.bfloat16)
        weight_own = (own_exp / normaliser).astype(jnp.bfloat16).astype(jnp.float32)
        get_values.wait()
        wide = jnp.dot(weights, v_buf[i], preferred_element_type=jnp.float32)
        context = wide[:, :HEAD_SIZE]
        for h in range(1, local_heads):
            context = jnp.where(
                head_of == h, wide[:, h * HEAD_SIZE : (h + 1) * HEAD_SIZE], context
            )
        context_ref[i] = context
        own_weight_ref[i] = jnp.broadcast_to(weight_own, (heads, HEAD_SIZE))


def attend(rows, lengths, queries, own_key, stored_keys, stored_values, after):
    cache_len, width = stored_keys.shape[1:]
    heads = queries.shape[1] // HEAD_SIZE
    count = len(rows)
    out = jax.ShapeDtypeStruct((count, heads, HEAD_SIZE), jnp.float32)
    return pl.pallas_call(
        functools.partial(attend_kernel, rows),
        out_shape=(out, out),
        in_specs=[HBM, VMEM, VMEM, HBM, HBM] + [pl.BlockSpec(memory_space=pl.ANY)] * len(after),
        out_specs=(VMEM, VMEM),
        scratch_shapes=[
            pltpu.SMEM(lengths.shape, jnp.int32),
            pltpu.VMEM((count, cache_len, width), jnp.bfloat16),
            pltpu.VMEM((count, cache_len, width), jnp.bfloat16),
            pltpu.SemaphoreType.DMA,
            pltpu.SemaphoreType.DMA((count,)),
            pltpu.SemaphoreType.DMA((count,)),
        ],
        compiler_params=pltpu.CompilerParams(vmem_limit_bytes=16 * 2**20),
        cost_estimate=pl.CostEstimate(
            flops=4 * count * heads * cache_len * width,
            bytes_accessed=4 * count * cache_len * width,
            transcendentals=count * heads * cache_len,
        ),
        name="attend_cache",
    )(lengths, queries, own_key, stored_keys, stored_values, *after)


def fold_kernel(slots, first, prefetch, last, place_hbm, up_ref, features_ref, served, *rest):
    rest = list(rest)
    count, ahead_count = len(slots), len(prefetch)
    blocks = [rest.pop(0) for _ in slots]
    if not first:
        rest.pop(0)
        total = rest.pop(0)[...]
    if last:
        ahead, context_ref, own_weight_ref = rest[:3]
        merged, fresh_hbm, attended_hbm = rest[3:6]
        place, place_sem, m_buf, out_sem, fresh_ref, attended_ref, small_sem = rest[6:]
    else:
        merged, total_ref = rest[:2]
        rest = rest[2:]
        if prefetch:
            ahead = rest.pop(0)
        place, place_sem, m_buf, out_sem, w_buf, in_sem = rest
    width = blocks[0].shape[1]

    def rows_of(slot):
        return pl.ds(pl.multiple_of(place[slot] * width, width), width)

    def fetch(i, slot, into):
        return pltpu.make_async_copy(served.at[rows_of(slot)], into, in_sem.at[i])

    def store(i):
        return pltpu.make_async_copy(m_buf.at[i], merged.at[rows_of(slots[i])], out_sem.at[i])

    get_place = pltpu.make_async_copy(place_hbm, place, place_sem)
    get_place.start()
    up = (up_ref[...].astype(jnp.float32) * ADAPTER_SCALE).astype(jnp.bfloat16)
    if not last:
        get_place.wait()
        for i, slot in enumerate(slots):
            fetch(i, slot, w_buf.at[i]).start()
        for i, slot in enumerate(prefetch):
            fetch(count + i, slot, ahead.at[i]).start()
    if first:
        total = jnp.zeros(total_ref.shape, jnp.float32)
    for i, slot in enumerate(slots):
        update = lax.dot_general(
            blocks[i][...], up, (((0,), (0,)), ((), ())), preferred_element_type=jnp.float32
        )
        if last:
            rows = ahead[i]
        else:
            fetch(i, slot, w_buf.at[i]).wait()
            rows = w_buf[i]
        rows = (rows.astype(jnp.float32) + update).astype(jnp.bfloat16)
        m_buf[i] = rows
        if last and i == 0:
            get_place.wait()
        store(i).start()
        total = total + jnp.dot(
            features_ref[:, rows_of(slot)], rows, preferred_element_type=jnp.float32
        )
    if last:
        fresh = total.astype(jnp.bfloat16)
        fresh_ref[...] = fresh
        put_fresh = pltpu.make_async_copy(fresh_ref, fresh_hbm, small_sem.at[0])
        put_fresh.start()
        value = fresh.astype(jnp.float32)
        heads = attended_ref.shape[1] // HEAD_SIZE
        group = heads // (fresh_ref.shape[1] // HEAD_SIZE)
        for h in range(heads):
            cols = slice(h * HEAD_SIZE, (h + 1) * HEAD_SIZE)
            at = (h // group) * HEAD_SIZE
            attended_ref[:, cols] = (
                context_ref[:, cols] + own_weight_ref[:, cols] * value[:, at : at + HEAD_SIZE]
            ).astype(jnp.bfloat16)
        put_attended = pltpu.make_async_copy(attended_ref, attended_hbm, small_sem.at[1])
        put_attended.start()
        put_fresh.wait()
        put_attended.wait()
    else:
        total_ref[...] = total
        for i, slot in enumerate(prefetch):
            fetch(count + i, slot, ahead.at[i]).wait()
    for i in range(count):
        store(i).wait()


def fold(slots, place, up, features, served, blocks, prefetch=(), state=(), finish=()):
    first, last = not state, bool(finish)
    count = len(slots)
    rank, width = blocks[0].shape
    rows = features.shape[0]
    depth, cols = served.shape
    in_specs = [HBM, VMEM, VMEM, HBM] + [VMEM] * count
    operands = [place, up, features, served, *blocks]
    aliases = {}
    if not first:
        aliases = {len(operands): 0}
        in_specs += [HBM, VMEM]
        operands += state
    in_specs += [VMEM] * len(finish)
    operands += finish
    out_shape = [jax.ShapeDtypeStruct((depth, cols), jnp.bfloat16)]
    out_specs = [HBM]
    scratch = [
        pltpu.SMEM(place.shape, jnp.int32),
        pltpu.SemaphoreType.DMA,
        pltpu.VMEM((count, width, cols), jnp.bfloat16),
        pltpu.SemaphoreType.DMA((count,)),
    ]
    if last:
        smalls = [(rows, cols), finish[1].shape]
        out_shape += [jax.ShapeDtypeStruct(shape, jnp.bfloat16) for shape in smalls]
        out_specs += [HBM, HBM]
        scratch += [pltpu.VMEM(shape, jnp.bfloat16) for shape in smalls]
        scratch += [pltpu.SemaphoreType.DMA((2,))]
    else:
        out_shape += [jax.ShapeDtypeStruct((rows, cols), jnp.float32)]
        out_specs += [VMEM]
        if prefetch:
            out_shape += [jax.ShapeDtypeStruct((len(prefetch), width, cols), jnp.bfloat16)]
            out_specs += [VMEM]
        scratch += [
            pltpu.VMEM((count, width, cols), jnp.bfloat16),
            pltpu.SemaphoreType.DMA((count + len(prefetch),)),
        ]
    return pl.pallas_call(
        functools.partial(fold_kernel, slots, first, prefetch, last),
        out_shape=out_shape,
        in_specs=in_specs,
        out_specs=out_specs,
        input_output_aliases=aliases,
        scratch_shapes=scratch,
        compiler_params=pltpu.CompilerParams(vmem_limit_bytes=24 * 2**20),
        cost_estimate=pl.CostEstimate(
            flops=2 * count * width * cols * (rank + rows),
            bytes_accessed=4 * count * width * cols,
            transcendentals=0,
        ),
        name="fold_blocks",
    )(*operands)


def ring_member(spot, n):
    return jnp.where(spot < (n + 1) // 2, 2 * spot, 2 * (n - 1 - spot) + 1)


def body(
    hidden_in,
    queries,
    stored_keys,
    stored_values,
    fresh_token_key,
    lengths,
    served_value_weight,
    adapter_in,
    adapter_out,
    owner_rank,
):
    n = lax.axis_size("replica")
    replica = lax.axis_index("replica")
    core = lax.axis_index("tensor")
    swap = [(0, 1), (1, 0)]
    order = list(range(0, n, 2)) + list(range(n - 1 - n % 2, 0, -2))
    around = []
    for spot in range(n):
        here, there = order[spot], order[(spot + 1) % n]
        around.append((here * 2, there * 2))
        around.append((there * 2 + 1, here * 2 + 1))
    steps = n // 2
    rows = queries.shape[0]
    split = rows // 2
    given = (*in_hbm(lengths), queries, fresh_token_key, *in_hbm(stored_keys, stored_values))

    shifts, cuts = [0], []
    for step in range(1, steps + 1):
        shifts += [step, -step] if 2 * step < n else [step]
        cuts.append(len(shifts))
    spot = jnp.where(replica % 2 == 0, replica // 2, n - 1 - replica // 2)
    way = jnp.where(core == 0, -1, 1)
    source = ring_member((spot + way * jnp.array(shifts, jnp.int32) + n) % n, n)
    spots = jnp.arange(n, dtype=jnp.int32)[None, :]
    place = jnp.sum(jnp.where(owner_rank[None, :] == source[:, None], spots, 0), axis=1)
    place = place.astype(jnp.int32)

    def doubled(have):
        size = have.shape[0] // adapter_out.shape[0]
        more = have[: min(size, n - size) * adapter_out.shape[0]]
        back = [(i, (i - size) % n) for i in range(n)]
        return lax.ppermute(more, "replica", back)

    (served,) = in_hbm(served_value_weight)
    blocks, state, done = [adapter_in], [], 0
    parts = []
    passed = adapter_in
    up = adapter_out
    for step in range(1, steps + 1):
        passed = lax.ppermute(passed, ("replica", "tensor"), around)
        if step == 1:
            more = doubled(up)
        if step <= 2:
            part = range(split) if step == 1 else range(split, rows)
            beside = attend(part, *given, blocks[1:2])
            passed, beside, more = lax.optimization_barrier((passed, beside, more))
            parts.append(beside)
            up = jnp.concatenate([up, more], axis=0)
            more = doubled(up)
        if step == 1:
            hid_other, parts[0] = lax.optimization_barrier((hidden_in, parts[0]))
            hid_other = lax.ppermute(hid_other, "tensor", swap)
        if step == 2:
            up = jnp.concatenate([up, more], axis=0)
            while up.shape[0] < n * adapter_out.shape[0]:
                up = jnp.concatenate([up, doubled(up)], axis=0)
            up = jnp.roll(up, replica * adapter_out.shape[0], axis=0)
            features = jnp.concatenate([hidden_in, hid_other], axis=1)
            features = jnp.where(
                core == 0, features, jnp.concatenate([hid_other, hidden_in], axis=1)
            )
            common = (place, up, features, served)
        if step > 2:
            upto = n - 1 if step == steps else cuts[step - 3]
            prefetch = range(upto, n) if step == steps else ()
            state = fold(range(done, upto), *common, blocks[done:upto], prefetch, state)
            done = upto
            if step < steps:
                passed, state = lax.optimization_barrier((passed, state))
        blocks.append(passed)
        if 2 * step < n:
            blocks.append(lax.ppermute(passed, "tensor", swap))
    context, own_weight = (
        jnp.concatenate(pair, axis=0).reshape(queries.shape) for pair in zip(*parts)
    )
    merged, total, ahead = state
    merged, fresh_token_value, attended = fold(
        range(done, n), *common, blocks[done:], state=[merged, total],
        finish=[ahead, context, own_weight],
    )
    return (merged, fresh_token_value, attended)


def solution(mesh):
    in_specs = (
        P(("groups", "replica"), "tensor"),
        P(("groups", "replica"), "tensor"),
        P(("groups", "replica"), None, "tensor"),
        P(("groups", "replica"), None, "tensor"),
        P(("groups", "replica"), "tensor"),
        P(("groups", "replica")),
        P(None, "tensor"),
        P("groups", "replica"),
        P(("groups", "replica"), "tensor"),
        P("groups"),
    )
    out_specs = (
        P("groups", "tensor"),
        P(("groups", "replica"), "tensor"),
        P(("groups", "replica"), "tensor"),
    )
    return jax.shard_map(body, mesh=mesh, in_specs=in_specs, out_specs=out_specs, check_vma=False)
```

time: 38.2 us -> 36 us (0.942)
  waiting for transfers between devices: 8.09 us -> 4.46 us
  starting transfers between devices: 9.85 us -> 12.2 us
  Pallas kernels: 15.5 us -> 14.5 us
  other arithmetic: 0.89 us -> 1.56 us
  local copies, waits for them, and re-layouts: 2.73 us -> 2.15 us
    ppermute x1 -> x4, starting transfers between devices: 0.01 us -> 9.16 us  [the longest x3 8.15 us: doubled(): return lax.ppermute(more, 'replica', back)]
    all_to_all x1 -> x0, waiting for transfers between devices: 5.28 us -> none  [body(): lax.all_to_all(jnp.broadcast_to(adapter_out[None], (n,) + adapter_out.sha...]
    all_to_all x1 -> x0, starting transfers between devices: 4.82 us -> none  [body(): lax.all_to_all(jnp.broadcast_to(adapter_out[None], (n,) + adapter_out.sha...]
    ppermute x1 -> x4, waiting for transfers between devices: 0.01 us -> 3.53 us  [the longest x3 3.53 us: doubled(): return lax.ppermute(more, 'replica', back)]
    ppermute x4, waiting for transfers between devices: 2.09 us -> 0.01 us  [body(): passed = lax.ppermute(passed, ('replica', 'tensor'), around)]
    ppermute x4, starting transfers between devices: 4.45 us -> 2.84 us  [body(): passed = lax.ppermute(passed, ('replica', 'tensor'), around)]
    broadcast_in_dim x1 -> x0, local copies, waits for them, and re-layouts: 1.3 us -> none  [body(): jnp.broadcast_to(adapter_out[None], (n,) + adapter_out.shape)]
    pallas_call x3, Pallas kernels: 10.1 us -> 9.25 us  [fold(): pl.pallas_call(functools.partial(fold_kernel, slots, first, prefetch, las...]
  transfers between devices with their start and end apart: 9 -> 11, of which waited for: 4 -> 3; matrix products, arithmetic and copies ran while one was open for 8% -> 6% of each run, Pallas kernels for 35% -> 37%
where the time goes in v4:
time: 36 us; the launch traced here: 35.6 us
  Pallas kernels  14.5 us (40%)
  starting transfers between devices  12.2 us (34%)
  waiting for transfers between devices  4.46 us (12%)
  local copies, waits for them, and re-layouts  2.15 us (6%)
  other arithmetic  1.56 us (4%)
  between operations  0.82 us (2%)
    pallas_call x3, Pallas kernels, fold(): pl.pallas_call(functools.partial(fold_kernel, slots, first, prefetch, las...  9.25 us
    ppermute x3, starting transfers between devices, doubled(): return lax.ppermute(more, 'replica', back)  8.15 us
    pallas_call x2, Pallas kernels, attend(): pl.pallas_call(functools.partial(attend_kernel, rows), out_shape=(out, ou...  5.24 us
    ppermute x3, waiting for transfers between devices, doubled(): return lax.ppermute(more, 'replica', back)  3.53 us
    ppermute x4, starting transfers between devices, body(): passed = lax.ppermute(passed, ('replica', 'tensor'), around)  2.84 us
    unnamed x19, local copies, waits for them, and re-layouts  2.14 us
    ppermute x1, starting transfers between devices, body(): hid_other = lax.ppermute(hid_other, 'tensor', swap)  1.02 us
    ppermute x3, waiting for transfers between devices, body(): blocks.append(lax.ppermute(passed, 'tensor', swap))  0.91 us
  transfers between devices with their start and end apart: 11, of which 3 were waited for; matrix products, arithmetic and copies ran while one was open for 6% of the time, Pallas kernels for 37%

profile of v4, /device:TPU:0, one launch (start us, length us, event | category | flops | bytes accessed | tf_op | source)
XLA Modules:
  0.0 35.6 jit_solution(15388983414258488934)
XLA Ops:
  0.6 0.0 copy-start.3
  0.7 6.1 %collective-permute-start.1 = (bf16[8,256]{1,0:T(8,128)(2,1)}, bf16[8,256]{1,0:T(8,128)(2,1)S(1)}, u32[]{:S(2)}, u32[]{:S(2)}) collective-permute-start(bf16[8,256]{1,0:T(8,128)(2,1)} %param.19), channel_id=1, source_target_pairs={{0,14},{2,0},{4,2},{6,4},{8,6},{10,8},{12,10},{14,12},{1,15},{3,1}... | collective-permute-start | bytes 12296 | tf_op jit(solution)/shard_map/ppermute | solution.py:298
  6.7 0.7 %compare_select_fusion.2 = s32[8]{0:T(128)S(1)} fusion(s32[8]{0:T(128)} %constant.81.clone, s32[]{:T(128)S(6)} %select_n.56, s32[]{:T(128)S(6)} %select_n.55), kind=kLoop, calls=%fused_computation.18 | loop fusion | flops 160 | bytes 72 | tf_op jit(solution)/shard_map/jit(_where)/select_n | solution.py:253
  7.4 0.7 %constant_dynamic-update-slice_fusion.7 = bf16[128,256]{1,0:T(8,128)(2,1)S(1)} fusion(bf16[8,256]{1,0:T(8,128)(2,1)} %param.19), kind=kLoop, calls=%fused_computation.12 | loop fusion | bytes 8192
  8.1 0.8 %select_reduce_fusion.place_hbm = s32[8]{0:T(128)S(1)} fusion(s32[8]{0:T(128)} %param.20, s32[8]{0:T(128)S(1)} %compare_select_fusion.2), kind=kLoop, calls=%fused_computation.15 | loop fusion | flops 184 | bytes 96 | tf_op jit(solution)/shard_map/reduce_sum | solution.py:291
  8.9 0.0 copy-start.1
  8.9 0.7 %copy-done.1 = bf16[4,2048]{1,0:T(4,128)(2,1)S(1)} copy-done((bf16[4,2048]{1,0:T(4,128)(2,1)S(1)}, bf16[4,2048]{1,0:T(4,128)(2,1)}, u32[]{:S(2)}) %copy-start.1) | copy-done | bytes 16408
  9.6 0.7 %copy-done.2 = bf16[4,256]{1,0:T(4,128)(2,1)S(1)} copy-done((bf16[4,256]{1,0:T(4,128)(2,1)S(1)}, bf16[4,256]{1,0:T(4,128)(2,1)}, u32[]{:S(2)}) %copy-start.2) | copy-done | bytes 2072
  10.3 2.6 %attend_cache.2 = (f32[2,16,128]{2,1,0:T(8,128)S(1)}, f32[2,16,128]{2,1,0:T(8,128)S(1)}) custom-call(s32[4]{0:T(128)} %lengths_hbm.3, bf16[4,2048]{1,0:T(4,128)(2,1)S(1)} %copy-done.1, bf16[4,256]{1,0:T(4,128)(2,1)S(1)} %copy-done.2, bf16[4,1024,256]{2,1,0:T(8,128)(2,1)} %k_hbm.3, bf16[4,1024,256]{2,1,0:T(8,128)(2,1)} %v_hbm.3), custom_call_target="tpu_custom_call" | custom-call | flops 33554432 | bytes 2097152 | tf_op jit(solution)/shard_map/attend_cache/pallas_call | solution.py:91
  13.0 0.1 collective-permute-start.7
  13.1 1.3 %collective-permute-start.2 = (bf16[64,1024]{1,0:T(8,128)(2,1)S(1)}, bf16[64,1024]{1,0:T(8,128)(2,1)S(1)}, u32[]{:S(2)}, u32[]{:S(2)}) collective-permute-start(bf16[64,1024]{1,0:T(8,128)(2,1)S(1)} %collective-permute-done.rest_0_.rest_1_), channel_id=1, source_target_pairs={{0,4},{5,1},{4,8},{9,5},{8,12},{13,9},{12,14},{15,13},{14,10},{11,... | collective-permute-start | bytes 393224 | tf_op jit(solution)/shard_map/ppermute | solution.py:306
  14.4 1.0 %collective-permute-start.5 = (bf16[4,4096]{1,0:T(4,128)(2,1)S(1)}, bf16[4,4096]{1,0:T(4,128)(2,1)S(1)}, u32[]{:S(2)}, u32[]{:S(2)}) collective-permute-start(bf16[4,4096]{1,0:T(4,128)(2,1)S(1)} %copy-done.4), channel_id=1, source_target_pairs={{0,1},{1,0},{2,3},{3,2},{4,5},{5,4},{6,7},{7,6},{8,9},{9,8},{10,11... | collective-permute-start | bytes 98312 | tf_op jit(solution)/shard_map/ppermute | solution.py:318
  15.4 0.4 %collective-permute-start.3 = (bf16[16,256]{1,0:T(8,128)(2,1)S(1)}, bf16[16,256]{1,0:T(8,128)(2,1)S(1)}, u32[]{:S(2)}, u32[]{:S(2)}) collective-permute-start(bf16[16,256]{1,0:T(8,128)(2,1)S(1)} %pad_maximum_fusion.1), channel_id=1, source_target_pairs={{0,12},{2,14},{4,0},{6,2},{8,4},{10,6},{12,8},{14,10},{1,13},{3,15... | collective-permute-start | bytes 24584 | tf_op jit(solution)/shard_map/ppermute | solution.py:298
  15.8 2.6 %attend_cache.3 = (f32[2,16,128]{2,1,0:T(8,128)S(1)}, f32[2,16,128]{2,1,0:T(8,128)S(1)}) custom-call(s32[4]{0:T(128)} %lengths_hbm.3, bf16[4,2048]{1,0:T(4,128)(2,1)S(1)} %copy-done.1, bf16[4,256]{1,0:T(4,128)(2,1)S(1)} %copy-done.2, bf16[4,1024,256]{2,1,0:T(8,128)(2,1)} %k_hbm.3, bf16[4,1024,256]{2,1,0:T(8,128)(2,1)} %v_hbm.3, ...), custom_call_target="tpu_custom_call" | custom-call | flops 33554432 | bytes 2097152 | tf_op jit(solution)/shard_map/attend_cache/pallas_call | solution.py:91
  18.5 0.5 %collective-permute-done.3 = bf16[16,256]{1,0:T(8,128)(2,1)S(1)} collective-permute-done((bf16[16,256]{1,0:T(8,128)(2,1)S(1)}, bf16[16,256]{1,0:T(8,128)(2,1)S(1)}, u32[]{:S(2)}, u32[]{:S(2)}) %collective-permute-start.3) | collective-permute-done | bytes 8224 | tf_op jit(solution)/shard_map/ppermute | solution.py:298
  19.0 1.2 %collective-permute-start.6 = (bf16[64,1024]{1,0:T(8,128)(2,1)S(1)}, bf16[64,1024]{1,0:T(8,128)(2,1)S(1)}, u32[]{:S(2)}, u32[]{:S(2)}) collective-permute-start(bf16[64,1024]{1,0:T(8,128)(2,1)S(1)} %collective-permute-done.2.rest_0_), channel_id=1, source_target_pairs={{0,4},{5,1},{4,8},{9,5},{8,12},{13,9},{12,14},{15,13},{14,10},{11,... | collective-permute-start | bytes 393224 | tf_op jit(solution)/shard_map/ppermute | solution.py:306
  20.2 1.6 %collective-permute-start.4 = (bf16[32,256]{1,0:T(8,128)(2,1)S(1)}, bf16[32,256]{1,0:T(8,128)(2,1)S(1)}, u32[]{:S(2)}, u32[]{:S(2)}) collective-permute-start(bf16[32,256]{1,0:T(8,128)(2,1)S(1)} %pad_maximum_fusion), channel_id=1, source_target_pairs={{0,8},{2,10},{4,12},{6,14},{8,0},{10,2},{12,4},{14,6},{1,9},{3,11}... | collective-permute-start | bytes 49160 | tf_op jit(solution)/shard_map/ppermute | solution.py:298
  21.9 3.0 %collective-permute-done.4 = bf16[32,256]{1,0:T(8,128)(2,1)S(1)} collective-permute-done((bf16[32,256]{1,0:T(8,128)(2,1)S(1)}, bf16[32,256]{1,0:T(8,128)(2,1)S(1)}, u32[]{:S(2)}, u32[]{:S(2)}) %collective-permute-start.4) | collective-permute-done | bytes 16416 | tf_op jit(solution)/shard_map/ppermute | solution.py:298
  24.9 3.6 %fold_blocks.3 = (bf16[8192,256]{1,0:T(8,128)(2,1)}, f32[4,256]{1,0:T(4,128)S(1)}) custom-call(s32[8]{0:T(128)S(1)} %select_reduce_fusion.place_hbm, bf16[64,256]{1,0:T(8,128)(2,1)S(1)} %constant_dynamic-slice_fusion.up_ref, bf16[4,8192]{1,0:T(4,128)(2,1)S(1)} %maximum_select_fusion.features_ref, bf16[8192,256]{1,0:T(8,128)(2,1)} %served.5, ...), custom_call_target="tpu_custom_call" | custom-call | flops 106954752 | bytes 3145728 | tf_op jit(solution)/shard_map/fold_blocks/pallas_call | solution.py:235
  28.5 0.1 collective-permute-start.10
  28.6 0.4 %collective-permute-start.8 = (bf16[64,1024]{1,0:T(8,128)(2,1)S(1)}, bf16[64,1024]{1,0:T(8,128)(2,1)S(1)}, u32[]{:S(2)}, u32[]{:S(2)}) collective-permute-start(bf16[64,1024]{1,0:T(8,128)(2,1)S(1)} %collective-permute-done.6.rest_2_), channel_id=1, source_target_pairs={{0,4},{5,1},{4,8},{9,5},{8,12},{13,9},{12,14},{15,13},{14,10},{11,... | collective-permute-start | bytes 393224 | tf_op jit(solution)/shard_map/ppermute | solution.py:306
  29.0 0.9 %collective-permute-done.10.rest_3_ = bf16[64,1024]{1,0:T(8,128)(2,1)S(1)} collective-permute-done((bf16[64,1024]{1,0:T(8,128)(2,1)S(1)}, bf16[64,1024]{1,0:T(8,128)(2,1)S(1)}, u32[]{:S(2)}, u32[]{:S(2)}) %collective-permute-start.10) | collective-permute-done | bytes 131104 | tf_op jit(solution)/shard_map/ppermute | solution.py:338
  29.9 4.2 %fold_blocks.4 = (bf16[8192,256]{1,0:T(8,128)(2,1)}, f32[4,256]{1,0:T(4,128)S(1)}, bf16[1,1024,256]{2,1,0:T(8,128)(2,1)S(1)}) custom-call(s32[8]{0:T(128)S(1)} %select_reduce_fusion.place_hbm, bf16[64,256]{1,0:T(8,128)(2,1)S(1)} %constant_dynamic-slice_fusion.up_ref, ...), custom_call_target="tpu_custom_call", output_to_operand_aliasing={{0}: (8, {})} | custom-call | flops 142606336 | bytes 4194304 | tf_op jit(solution)/shard_map/fold_blocks/pallas_call | solution.py:235
  34.2 1.5 %fold_blocks.5 = (bf16[8192,256]{1,0:T(8,128)(2,1)}, bf16[4,256]{1,0:T(4,128)(2,1)}, bf16[4,2048]{1,0:T(4,128)(2,1)}) custom-call(s32[8]{0:T(128)S(1)} %select_reduce_fusion.place_hbm, bf16[64,256]{1,0:T(8,128)(2,1)S(1)} %constant_dynamic-slice_fusion.up_ref, bf16[4,8192]{1,0:T(4,128)(2,1)S(1)} %maximum_select_fusion.features_ref, ...), custom_call_target="tpu_custom_call", output_to_operand_aliasing={{0}: (5, {})} | custom-call | flops 35651584 | bytes 1048576 | tf_op jit(solution)/shard_map/fold_blocks/pallas_call | solution.py:235
  (30 shorter events, 0.1 us)
Async XLA Ops:
  0.6 13.7 %copy-start.3 = (bf16[8,256]{1,0:T(8,128)(2,1)S(1)}, bf16[8,256]{1,0:T(8,128)(2,1)}, u32[]{:S(2)}) copy-start(bf16[8,256]{1,0:T(8,128)(2,1)} %param.19) | copy-start | bytes 12292
  0.6 13.7 %copy-start.4 = (bf16[4,4096]{1,0:T(4,128)(2,1)S(1)}, bf16[4,4096]{1,0:T(4,128)(2,1)}, u32[]{:S(2)}) copy-start(bf16[4,4096]{1,0:T(4,128)(2,1)} %param.11) | copy-start | bytes 98308
  0.7 12.3 %collective-permute-start.1 = (bf16[8,256]{1,0:T(8,128)(2,1)}, bf16[8,256]{1,0:T(8,128)(2,1)S(1)}, u32[]{:S(2)}, u32[]{:S(2)}) collective-permute-start(bf16[8,256]{1,0:T(8,128)(2,1)} %param.19), channel_id=1, source_target_pairs={{0,14},{2,0},{4,2},{6,4},{8,6},{10,8},{12,10},{14,12},{1,15},{3,1}... | collective-permute-start | bytes 12296 | tf_op jit(solution)/shard_map/ppermute | solution.py:298
  6.7 6.3 %collective-permute-start = (bf16[64,1024]{1,0:T(8,128)(2,1)}, bf16[64,1024]{1,0:T(8,128)(2,1)S(1)}, u32[]{:S(2)}, u32[]{:S(2)}) collective-permute-start(bf16[64,1024]{1,0:T(8,128)(2,1)} %rest_0_.1), channel_id=1, source_target_pairs={{0,4},{5,1},{4,8},{9,5},{8,12},{13,9},{12,14},{15,13},{14,10},{11,... | collective-permute-start | bytes 393224 | tf_op jit(solution)/shard_map/ppermute | solution.py:306
  8.9 0.7 %copy-start.1 = (bf16[4,2048]{1,0:T(4,128)(2,1)S(1)}, bf16[4,2048]{1,0:T(4,128)(2,1)}, u32[]{:S(2)}) copy-start(bf16[4,2048]{1,0:T(4,128)(2,1)} %q_ref.3) | copy-start | bytes 49156
  9.6 0.7 %copy-start.2 = (bf16[4,256]{1,0:T(4,128)(2,1)S(1)}, bf16[4,256]{1,0:T(4,128)(2,1)}, u32[]{:S(2)}) copy-start(bf16[4,256]{1,0:T(4,128)(2,1)} %own_k_ref.3) | copy-start | bytes 6148
  10.3 14.6 %copy-start = (bf16[64,1024]{1,0:T(8,128)(2,1)S(1)}, bf16[64,1024]{1,0:T(8,128)(2,1)}, u32[]{:S(2)}) copy-start(bf16[64,1024]{1,0:T(8,128)(2,1)} %rest_0_.1) | copy-start | bytes 393220
  13.0 11.9 %collective-permute-start.7 = (bf16[64,1024]{1,0:T(8,128)(2,1)S(1)}, bf16[64,1024]{1,0:T(8,128)(2,1)S(1)}, u32[]{:S(2)}, u32[]{:S(2)}) collective-permute-start(bf16[64,1024]{1,0:T(8,128)(2,1)S(1)} %collective-permute-done.rest_0_.rest_1_), channel_id=1, source_target_pairs={{0,1},{1,0},{2,3},{3,2},{4,5},{5,4},{6,7},{7,6},{8,9},{9,8},{10,11... | collective-permute-start | bytes 393224 | tf_op jit(solution)/shard_map/ppermute | solution.py:338
  13.1 6.0 %collective-permute-start.2 = (bf16[64,1024]{1,0:T(8,128)(2,1)S(1)}, bf16[64,1024]{1,0:T(8,128)(2,1)S(1)}, u32[]{:S(2)}, u32[]{:S(2)}) collective-permute-start(bf16[64,1024]{1,0:T(8,128)(2,1)S(1)} %collective-permute-done.rest_0_.rest_1_), channel_id=1, source_target_pairs={{0,4},{5,1},{4,8},{9,5},{8,12},{13,9},{12,14},{15,13},{14,10},{11,... | collective-permute-start | bytes 393224 | tf_op jit(solution)/shard_map/ppermute | solution.py:306
  14.4 4.1 %collective-permute-start.5 = (bf16[4,4096]{1,0:T(4,128)(2,1)S(1)}, bf16[4,4096]{1,0:T(4,128)(2,1)S(1)}, u32[]{:S(2)}, u32[]{:S(2)}) collective-permute-start(bf16[4,4096]{1,0:T(4,128)(2,1)S(1)} %copy-done.4), channel_id=1, source_target_pairs={{0,1},{1,0},{2,3},{3,2},{4,5},{5,4},{6,7},{7,6},{8,9},{9,8},{10,11... | collective-permute-start | bytes 98312 | tf_op jit(solution)/shard_map/ppermute | solution.py:318
  15.4 3.7 %collective-permute-start.3 = (bf16[16,256]{1,0:T(8,128)(2,1)S(1)}, bf16[16,256]{1,0:T(8,128)(2,1)S(1)}, u32[]{:S(2)}, u32[]{:S(2)}) collective-permute-start(bf16[16,256]{1,0:T(8,128)(2,1)S(1)} %pad_maximum_fusion.1), channel_id=1, source_target_pairs={{0,12},{2,14},{4,0},{6,2},{8,4},{10,6},{12,8},{14,10},{1,13},{3,15... | collective-permute-start | bytes 24584 | tf_op jit(solution)/shard_map/ppermute | solution.py:298
  19.0 10.0 %collective-permute-start.9 = (bf16[64,1024]{1,0:T(8,128)(2,1)S(1)}, bf16[64,1024]{1,0:T(8,128)(2,1)S(1)}, u32[]{:S(2)}, u32[]{:S(2)}) collective-permute-start(bf16[64,1024]{1,0:T(8,128)(2,1)S(1)} %collective-permute-done.2.rest_0_), channel_id=1, source_target_pairs={{0,1},{1,0},{2,3},{3,2},{4,5},{5,4},{6,7},{7,6},{8,9},{9,8},{10,11... | collective-permute-start | bytes 393224 | tf_op jit(solution)/shard_map/ppermute | solution.py:338
  19.0 9.5 %collective-permute-start.6 = (bf16[64,1024]{1,0:T(8,128)(2,1)S(1)}, bf16[64,1024]{1,0:T(8,128)(2,1)S(1)}, u32[]{:S(2)}, u32[]{:S(2)}) collective-permute-start(bf16[64,1024]{1,0:T(8,128)(2,1)S(1)} %collective-permute-done.2.rest_0_), channel_id=1, source_target_pairs={{0,4},{5,1},{4,8},{9,5},{8,12},{13,9},{12,14},{15,13},{14,10},{11,... | collective-permute-start | bytes 393224 | tf_op jit(solution)/shard_map/ppermute | solution.py:306
  20.2 4.6 %collective-permute-start.4 = (bf16[32,256]{1,0:T(8,128)(2,1)S(1)}, bf16[32,256]{1,0:T(8,128)(2,1)S(1)}, u32[]{:S(2)}, u32[]{:S(2)}) collective-permute-start(bf16[32,256]{1,0:T(8,128)(2,1)S(1)} %pad_maximum_fusion), channel_id=1, source_target_pairs={{0,8},{2,10},{4,12},{6,14},{8,0},{10,2},{12,4},{14,6},{1,9},{3,11}... | collective-permute-start | bytes 49160 | tf_op jit(solution)/shard_map/ppermute | solution.py:298
  28.5 1.4 %collective-permute-start.10 = (bf16[64,1024]{1,0:T(8,128)(2,1)S(1)}, bf16[64,1024]{1,0:T(8,128)(2,1)S(1)}, u32[]{:S(2)}, u32[]{:S(2)}) collective-permute-start(bf16[64,1024]{1,0:T(8,128)(2,1)S(1)} %collective-permute-done.6.rest_2_), channel_id=1, source_target_pairs={{0,1},{1,0},{2,3},{3,2},{4,5},{5,4},{6,7},{7,6},{8,9},{9,8},{10,11... | collective-permute-start | bytes 393224 | tf_op jit(solution)/shard_map/ppermute | solution.py:338
  28.6 5.6 %collective-permute-start.8 = (bf16[64,1024]{1,0:T(8,128)(2,1)S(1)}, bf16[64,1024]{1,0:T(8,128)(2,1)S(1)}, u32[]{:S(2)}, u32[]{:S(2)}) collective-permute-start(bf16[64,1024]{1,0:T(8,128)(2,1)S(1)} %collective-permute-done.6.rest_2_), channel_id=1, source_target_pairs={{0,4},{5,1},{4,8},{9,5},{8,12},{13,9},{12,14},{15,13},{14,10},{11,... | collective-permute-start | bytes 393224 | tf_op jit(solution)/shard_map/ppermute | solution.py:306

commit v5 on v4

v5 whole, which is shorter than its diff:
```python
import functools

import jax
import jax.numpy as jnp
from jax import lax
from jax.experimental import pallas as pl
from jax.experimental.pallas import tpu as pltpu
from jax.sharding import PartitionSpec as P

HEAD_SIZE = 128
ADAPTER_SCALE = 2.0

SMEM = pl.BlockSpec(memory_space=pltpu.SMEM)
VMEM = pl.BlockSpec(memory_space=pltpu.VMEM)
HBM = pl.BlockSpec(memory_space=pltpu.HBM)


def in_hbm(*arrays):
    return [pltpu.with_memory_space_constraint(x, pltpu.HBM) for x in arrays]


def attend_kernel(rows, lengths_hbm, q_ref, own_k_ref, k_hbm, v_hbm, served_hbm, context_ref,
                  own_weight_ref, served_ref, lengths, k_buf, v_buf, length_sem, k_sem, v_sem,
                  served_sem):
    def copies(i, row):
        return (
            pltpu.make_async_copy(k_hbm.at[row], k_buf.at[i], k_sem.at[i]),
            pltpu.make_async_copy(v_hbm.at[row], v_buf.at[i], v_sem.at[i]),
        )

    get_lengths = pltpu.make_async_copy(lengths_hbm, lengths, length_sem)
    get_lengths.start()
    for i, row in enumerate(rows):
        for copy in copies(i, row):
            copy.start()
    get_served = pltpu.make_async_copy(served_hbm, served_ref, served_sem)
    get_served.start()
    queries = q_ref[...].astype(jnp.float32)
    own_keys = own_k_ref[...].astype(jnp.float32)
    heads = queries.shape[1] // HEAD_SIZE
    cache_len, width = k_buf.shape[1:]
    local_heads = width // HEAD_SIZE
    group = heads // local_heads
    scaling = 1.0 / HEAD_SIZE**0.5
    head_of = lax.broadcasted_iota(jnp.int32, (heads, HEAD_SIZE), 0) // group
    position = lax.broadcasted_iota(jnp.int32, (heads, cache_len), 1)
    get_lengths.wait()
    for i, row in enumerate(rows):
        q = jnp.concatenate(
            [
                queries[row : row + 1, h * HEAD_SIZE : (h + 1) * HEAD_SIZE]
                for h in range(heads)
            ],
            axis=0,
        )
        spread = jnp.concatenate(
            [jnp.where(head_of == h, q, 0.0) for h in range(local_heads)], axis=1
        )
        own = jnp.sum(spread * own_keys[row : row + 1], axis=1, keepdims=True) * scaling
        get_keys, get_values = copies(i, row)
        get_keys.wait()
        scores = (
            lax.dot_general(
                spread.astype(jnp.bfloat16), k_buf[i], (((1,), (1,)), ((), ())),
                preferred_element_type=jnp.float32,
            )
            * scaling
        )
        valid = position < lengths[row]
        masked = jnp.where(valid, scores, -1e30)
        largest = jnp.maximum(jnp.max(masked, axis=1, keepdims=True), own)
        cached_exp = jnp.where(valid, jnp.exp(masked - largest), 0.0)
        own_exp = jnp.exp(own - largest)
        normaliser = jnp.sum(cached_exp, axis=1, keepdims=True) + own_exp
        weights = (cached_exp / normaliser).astype(jnp.bfloat16)
        weight_own = (own_exp / normaliser).astype(jnp.bfloat16).astype(jnp.float32)
        get_values.wait()
        wide = jnp.dot(weights, v_buf[i], preferred_element_type=jnp.float32)
        context = wide[:, :HEAD_SIZE]
        for h in range(1, local_heads):
            context = jnp.where(
                head_of == h, wide[:, h * HEAD_SIZE : (h + 1) * HEAD_SIZE], context
            )
        context_ref[i] = context
        own_weight_ref[i] = jnp.broadcast_to(weight_own, (heads, HEAD_SIZE))
    get_served.wait()


def attend(lengths, queries, own_key, stored_keys, stored_values, served):
    count, cache_len, width = stored_keys.shape
    heads = queries.shape[1] // HEAD_SIZE
    out = jax.ShapeDtypeStruct((count, heads, HEAD_SIZE), jnp.float32)
    return pl.pallas_call(
        functools.partial(attend_kernel, range(count)),
        out_shape=(out, out, jax.ShapeDtypeStruct(served.shape, served.dtype)),
        in_specs=[HBM, VMEM, VMEM, HBM, HBM, HBM],
        out_specs=(VMEM, VMEM, VMEM),
        scratch_shapes=[
            pltpu.SMEM(lengths.shape, jnp.int32),
            pltpu.VMEM((count, cache_len, width), jnp.bfloat16),
            pltpu.VMEM((count, cache_len, width), jnp.bfloat16),
            pltpu.SemaphoreType.DMA,
            pltpu.SemaphoreType.DMA((count,)),
            pltpu.SemaphoreType.DMA((count,)),
            pltpu.SemaphoreType.DMA,
        ],
        compiler_params=pltpu.CompilerParams(vmem_limit_bytes=16 * 2**20),
        cost_estimate=pl.CostEstimate(
            flops=4 * count * heads * cache_len * width,
            bytes_accessed=4 * count * cache_len * width + 4 * served.size,
            transcendentals=count * heads * cache_len,
        ),
        name="attend_cache",
    )(lengths, queries, own_key, stored_keys, stored_values, served)


def fold_kernel(groups, count, last, start_hbm, up_ref, features_ref, served_ref, *rest):
    rest = list(rest)
    arrays = [rest.pop(0) for _ in groups]
    if last:
        rest.pop(0)
        total_ref, context_ref, own_weight_ref = rest[:3]
        merged, fresh_hbm, attended_hbm = rest[3:6]
        start, start_sem, m_buf, out_sem, fresh_ref, attended_ref, small_sem = rest[6:]
        total = total_ref[...]
    else:
        merged, total_ref, start, start_sem, m_buf, out_sem = rest
        total = jnp.zeros(total_ref.shape, jnp.float32)
    rank = up_ref.shape[0]
    width = arrays[0].shape[2]

    get_start = pltpu.make_async_copy(start_hbm, start, start_sem)
    get_start.start()
    up = (up_ref[...].astype(jnp.float32) * ADAPTER_SCALE).astype(jnp.bfloat16)
    stores = []
    for array, (entry, slab, size) in zip(arrays, groups):
        for i in range(size):
            update = lax.dot_general(
                array[slab + i, :rank], up, (((0,), (0,)), ((), ())),
                preferred_element_type=jnp.float32,
            )
            if not stores:
                get_start.wait()
            rows = pl.ds(pl.multiple_of(start[entry + i], width), width)
            fold = (served_ref[rows, :].astype(jnp.float32) + update).astype(jnp.bfloat16)
            at = len(stores)
            m_buf[at] = fold
            stores.append(pltpu.make_async_copy(m_buf.at[at], merged.at[rows], out_sem.at[at]))
            stores[-1].start()
            total = total + jnp.dot(
                features_ref[:, rows], fold, preferred_element_type=jnp.float32
            )
    if last:
        fresh = total.astype(jnp.bfloat16)
        fresh_ref[...] = fresh
        put_fresh = pltpu.make_async_copy(fresh_ref, fresh_hbm, small_sem.at[0])
        put_fresh.start()
        value = fresh.astype(jnp.float32)
        heads = attended_ref.shape[1] // HEAD_SIZE
        group = heads // (fresh_ref.shape[1] // HEAD_SIZE)
        for h in range(heads):
            cols = slice(h * HEAD_SIZE, (h + 1) * HEAD_SIZE)
            at = (h // group) * HEAD_SIZE
            attended_ref[:, cols] = (
                context_ref[:, cols] + own_weight_ref[:, cols] * value[:, at : at + HEAD_SIZE]
            ).astype(jnp.bfloat16)
        put_attended = pltpu.make_async_copy(attended_ref, attended_hbm, small_sem.at[1])
        put_attended.start()
        put_fresh.wait()
        put_attended.wait()
    else:
        total_ref[...] = total
    for store in stores:
        store.wait()


def fold(groups, start, up, features, served, arrays, state=(), finish=()):
    count = sum(size for _, _, size in groups)
    last = bool(finish)
    rank, cols = up.shape
    width = arrays[0].shape[2]
    rows, depth = features.shape
    in_specs = [HBM, VMEM, VMEM, VMEM] + [VMEM] * len(arrays)
    operands = [start, up, features, served, *arrays]
    aliases = {}
    out_shape = [jax.ShapeDtypeStruct((depth, cols), jnp.bfloat16)]
    out_specs = [HBM]
    scratch = [
        pltpu.SMEM(start.shape, jnp.int32),
        pltpu.SemaphoreType.DMA,
        pltpu.VMEM((count, width, cols), jnp.bfloat16),
        pltpu.SemaphoreType.DMA((count,)),
    ]
    if last:
        aliases = {len(operands): 0}
        in_specs += [HBM, VMEM] + [VMEM] * len(finish)
        operands += [*state, *finish]
        smalls = [(rows, cols), finish[0].shape]
        out_shape += [jax.ShapeDtypeStruct(shape, jnp.bfloat16) for shape in smalls]
        out_specs += [HBM, HBM]
        scratch += [pltpu.VMEM(shape, jnp.bfloat16) for shape in smalls]
        scratch += [pltpu.SemaphoreType.DMA((2,))]
    else:
        out_shape += [jax.ShapeDtypeStruct((rows, cols), jnp.float32)]
        out_specs += [VMEM]
    return pl.pallas_call(
        functools.partial(fold_kernel, groups, count, last),
        out_shape=out_shape,
        in_specs=in_specs,
        out_specs=out_specs,
        input_output_aliases=aliases,
        scratch_shapes=scratch,
        compiler_params=pltpu.CompilerParams(vmem_limit_bytes=24 * 2**20),
        cost_estimate=pl.CostEstimate(
            flops=2 * count * width * cols * (rank + rows),
            bytes_accessed=4 * count * width * cols,
            transcendentals=0,
        ),
        name="fold_blocks",
    )(*operands)


def body(
    hidden_in,
    queries,
    stored_keys,
    stored_values,
    fresh_token_key,
    lengths,
    served_value_weight,
    adapter_in,
    adapter_out,
    owner_rank,
):
    n = lax.axis_size("replica")
    replica = lax.axis_index("replica")
    core = lax.axis_index("tensor")
    swap = [(0, 1), (1, 0)]
    rank, full = adapter_in.shape
    width = full // 2
    per, cols = adapter_out.shape

    bits = [n >> i for i in range(1, n.bit_length())]
    ways = [bits, bits[:-2] + bits[:-3:-1]]

    def exchange(x, step):
        pairs = [(2 * i + c, 2 * (i ^ ways[c][step]) + c) for i in range(n) for c in range(2)]
        return lax.ppermute(x, ("replica", "tensor"), pairs)

    slab = jnp.arange(n, dtype=jnp.int32)
    sources = []
    for way in ways:
        source = replica
        for step, bit in enumerate(way):
            source = source ^ (((slab >> step) & 1) * bit)
        sources.append(source)
    mine = jnp.where(core == 0, sources[0], sources[1])
    theirs = jnp.where(core == 0, sources[1], sources[0])

    source = jnp.concatenate([mine, theirs])
    place = jnp.sum(jnp.where(owner_rank[None, :] == source[:, None], slab[None, :], 0), axis=1)
    half = jnp.concatenate([jnp.full((n,), core), jnp.full((n,), 1 - core)])
    start = (place * full + half * width).astype(jnp.int32)

    up_rows = -(-per * cols // width)
    spare = -up_rows % 8
    slabs = jnp.concatenate(
        [
            lax.dynamic_slice_in_dim(adapter_in, core * width, width, axis=1),
            adapter_out.reshape(up_rows, width),
            jnp.zeros((spare, width), adapter_in.dtype),
        ],
        axis=0,
    )[None]
    *early, final = range(len(bits))
    for step in early:
        came = exchange(slabs, step)
        if step == early[0]:
            context, own_weight, served = attend(
                *in_hbm(lengths), queries, fresh_token_key,
                *in_hbm(stored_keys, stored_values, served_value_weight),
            )
            came, hidden, context, own_weight, served = lax.optimization_barrier(
                (came, hidden_in, context, own_weight, served)
            )
            hid_other = lax.ppermute(hidden, "tensor", swap)
        slabs = jnp.concatenate([slabs, came], axis=0)
    last = exchange(slabs, final)
    crossed = lax.ppermute(slabs, "tensor", swap)
    last_crossed = lax.ppermute(last, "tensor", swap)

    features = jnp.concatenate([hidden_in, hid_other], axis=1)
    features = jnp.where(core == 0, features, jnp.concatenate([hid_other, hidden_in], axis=1))

    ups = jnp.concatenate([slabs[:, rank : rank + up_rows], last[:, rank : rank + up_rows]], axis=0)
    ups = ups.reshape(n, per, cols)
    pick = (slab[:, None] == mine[None, :]).astype(jnp.bfloat16)
    up = jnp.einsum("ij,jkc->ikc", pick, ups, preferred_element_type=jnp.float32)
    up = up.astype(jnp.bfloat16).reshape(rank, cols)

    early_count = slabs.shape[0]
    late_count = n - early_count
    state = fold(
        [(0, 0, early_count), (n, 0, early_count), (early_count, 0, late_count)],
        start, up, features, served, [slabs, crossed, last],
    )
    context, own_weight = (x.reshape(queries.shape) for x in (context, own_weight))
    merged, fresh_token_value, attended = fold(
        [(n + early_count, 0, late_count)], start, up, features, served, [last_crossed],
        state=state, finish=[context, own_weight],
    )
    return (merged, fresh_token_value, attended)


def solution(mesh):
    in_specs = (
        P(("groups", "replica"), "tensor"),
        P(("groups", "replica"), "tensor"),
        P(("groups", "replica"), None, "tensor"),
        P(("groups", "replica"), None, "tensor"),
        P(("groups", "replica"), "tensor"),
        P(("groups", "replica")),
        P(None, "tensor"),
        P("groups", "replica"),
        P(("groups", "replica"), "tensor"),
        P("groups"),
    )
    out_specs = (
        P("groups", "tensor"),
        P(("groups", "replica"), "tensor"),
        P(("groups", "replica"), "tensor"),
    )
    return jax.shard_map(body, mesh=mesh, in_specs=in_specs, out_specs=out_specs, check_vma=False)
```

time: 36 us -> 34.5 us (0.958)
  Pallas kernels: 14.5 us -> 9.54 us
  starting transfers between devices: 12.2 us -> 7.47 us
  local copies, waits for them, and re-layouts: 2.15 us -> 6.58 us
  waiting for transfers between devices: 4.46 us -> 8.61 us
  other arithmetic: 1.56 us -> 1.03 us
    pallas_call x5 -> x3, Pallas kernels: 14.5 us -> 9.54 us  [the longest x2 5.37 us: fold(): pl.pallas_call(functools.partial(fold_kernel, groups, count, last), out_s...]
    ppermute x11 -> x6, starting transfers between devices: 12.2 us -> 7.47 us  [the longest x3 7.33 us: exchange(): return lax.ppermute(x, ('replica', 'tensor'), pairs)]
    ppermute x11 -> x6, waiting for transfers between devices: 4.46 us -> 8.61 us  [the longest x3 8.6 us: exchange(): return lax.ppermute(x, ('replica', 'tensor'), pairs)]
    unnamed x19 -> x12, local copies, waits for them, and re-layouts: 2.14 us -> 5.69 us
    reshape x0 -> x3, local copies, waits for them, and re-layouts: none -> 0.77 us  [the longest x1 0.73 us: body(): adapter_out.reshape(up_rows, width)]
    select_n x1, other arithmetic: 0.67 us -> 0.01 us  [body(): theirs = jnp.where(core == 0, sources[1], sources[0])]
  transfers between devices with their start and end apart: 11 -> 6, of which waited for: 3 -> 2; matrix products, arithmetic and copies ran while one was open for 6% -> 3% of each run, Pallas kernels for 37% -> 22%
where the time goes in v5:
time: 34.5 us; the launch traced here: 34.1 us
  Pallas kernels  9.54 us (28%)
  waiting for transfers between devices  8.61 us (25%)
  starting transfers between devices  7.47 us (22%)
  local copies, waits for them, and re-layouts  6.58 us (19%)
  other arithmetic  1.03 us (3%)
  between operations  0.78 us (2%)
    ppermute x3, waiting for transfers between devices, exchange(): return lax.ppermute(x, ('replica', 'tensor'), pairs)  8.6 us
    ppermute x3, starting transfers between devices, exchange(): return lax.ppermute(x, ('replica', 'tensor'), pairs)  7.33 us
    unnamed x12, local copies, waits for them, and re-layouts  5.69 us
    pallas_call x2, Pallas kernels, fold(): pl.pallas_call(functools.partial(fold_kernel, groups, count, last), out_s...  5.37 us
    pallas_call x1, Pallas kernels, attend(): pl.pallas_call(functools.partial(attend_kernel, range(count)), out_shape=...  4.17 us
    reduce_sum x1, other arithmetic, body(): jnp.sum(jnp.where(owner_rank[None, :] == source[:, None], slab[None, :],...  0.74 us
    reshape x1, local copies, waits for them, and re-layouts, body(): adapter_out.reshape(up_rows, width)  0.73 us
  transfers between devices with their start and end apart: 6, of which 2 were waited for; matrix products, arithmetic and copies ran while one was open for 3% of the time, Pallas kernels for 22%

profile of v5, /device:TPU:0, one launch (start us, length us, event | category | flops | bytes accessed | tf_op | source)
XLA Modules:
  0.0 34.1 jit_solution(13849053746119678055)
XLA Ops:
  0.6 0.0 copy-start
  0.7 0.7 %reshape.43 = bf16[4,512]{1,0:T(4,128)(2,1)S(1)} reshape(bf16[8,256]{1,0:T(8,128)(2,1)} %param.18) | data formatting | bytes 8192 | tf_op jit(solution)/shard_map/reshape | solution.py:270
  1.4 0.1 pad.14.clone
  1.5 0.1 copy-done
  1.6 0.1 maximum_bitcast_fusion
  1.6 4.1 %collective-permute-start = (bf16[1,72,512]{2,1,0:T(8,128)(2,1)S(1)}, bf16[1,72,512]{2,1,0:T(8,128)(2,1)S(1)}, u32[]{:S(2)}, u32[]{:S(2)}) collective-permute-start(bf16[1,72,512]{2,1,0:T(8,128)(2,1)S(1)} %maximum_bitcast_fusion), channel_id=1, source_target_pairs={{0,8},{1,9},{2,10},{3,11},{4,12},{5,13},{6,14},{7,15},{8,0},{9,1},... | collective-permute-start | bytes 221192 | tf_op jit(solution)/shard_map/ppermute | solution.py:248
  5.8 0.1 pad_add_fusion
  5.8 0.7 %select_reduce_fusion = s32[16]{0:T(128)S(1)} fusion(s32[16]{0:T(128)S(1)} %pad_add_fusion, s32[8]{0:T(128)} %param.19), kind=kLoop, calls=%fused_computation.11 | loop fusion | flops 368 | bytes 160 | tf_op jit(solution)/shard_map/reduce_sum | solution.py:261
  6.6 0.0 copy-start.3
  6.6 0.7 %copy-done.3 = bf16[4,2048]{1,0:T(4,128)(2,1)S(1)} copy-done((bf16[4,2048]{1,0:T(4,128)(2,1)S(1)}, bf16[4,2048]{1,0:T(4,128)(2,1)}, u32[]{:S(2)}) %copy-start.3) | copy-done | bytes 16408
  7.3 0.7 %copy-done.4 = bf16[4,256]{1,0:T(4,128)(2,1)S(1)} copy-done((bf16[4,256]{1,0:T(4,128)(2,1)S(1)}, bf16[4,256]{1,0:T(4,128)(2,1)}, u32[]{:S(2)}) %copy-start.4) | copy-done | bytes 2072
  8.0 4.2 %attend_cache.1 = (f32[4,16,128]{2,1,0:T(8,128)S(1)}, f32[4,16,128]{2,1,0:T(8,128)S(1)}, bf16[8192,256]{1,0:T(8,128)(2,1)S(1)}) custom-call(s32[4]{0:T(128)} %lengths_hbm.1, bf16[4,2048]{1,0:T(4,128)(2,1)S(1)} %copy-done.3, bf16[4,256]{1,0:T(4,128)(2,1)S(1)} %copy-done.4, bf16[4,1024,256]{2,1,0:T(8,128)(2,1)} %k_hbm.1, bf16[4,1024,256]{2,1,0:T(8,128)(2,1)} %v_hbm.1, ...), custom_call_target="tpu_custom_call" | custom-call | flops 67108864 | bytes 12582912 | tf_op jit(solution)/shard_map/attend_cache/pallas_call | solution.py:93
  12.2 0.0 copy-start.1
  12.2 2.0 %copy-done.1 = bf16[8192,256]{1,0:T(8,128)(2,1)} copy-done((bf16[8192,256]{1,0:T(8,128)(2,1)}, bf16[8192,256]{1,0:T(8,128)(2,1)S(1)}, u32[]{:S(2)}) %copy-start.1) | copy-done | bytes 4194328
  14.2 1.6 %collective-permute-start.1 = (bf16[2,72,512]{2,1,0:T(8,128)(2,1)S(1)}, bf16[2,72,512]{2,1,0:T(8,128)(2,1)S(1)}, u32[]{:S(2)}, u32[]{:S(2)}) collective-permute-start(bf16[2,72,512]{2,1,0:T(8,128)(2,1)S(1)} %pad_maximum_fusion.1), channel_id=1, source_target_pairs={{0,4},{1,3},{2,6},{3,1},{4,0},{5,7},{6,2},{7,5},{8,12},{9,11},{10,... | collective-permute-start | bytes 442376 | tf_op jit(solution)/shard_map/ppermute | solution.py:248
  15.9 3.5 %collective-permute-done.1 = bf16[2,72,512]{2,1,0:T(8,128)(2,1)S(1)} collective-permute-done((bf16[2,72,512]{2,1,0:T(8,128)(2,1)S(1)}, bf16[2,72,512]{2,1,0:T(8,128)(2,1)S(1)}, u32[]{:S(2)}, u32[]{:S(2)}) %collective-permute-start.1) | collective-permute-done | bytes 147488 | tf_op jit(solution)/shard_map/ppermute | solution.py:248
  19.5 1.6 %collective-permute-start.2 = (bf16[4,72,512]{2,1,0:T(8,128)(2,1)S(1)}, bf16[4,72,512]{2,1,0:T(8,128)(2,1)S(1)}, u32[]{:S(2)}, u32[]{:S(2)}) collective-permute-start(bf16[4,72,512]{2,1,0:T(8,128)(2,1)S(1)} %pad_maximum_fusion.rest_0_), channel_id=1, source_target_pairs={{0,2},{1,5},{2,0},{3,7},{4,6},{5,1},{6,4},{7,3},{8,10},{9,13},{10,... | collective-permute-start | bytes 884744 | tf_op jit(solution)/shard_map/ppermute | solution.py:248
  21.1 0.1 collective-permute-start.5
  21.2 5.1 %collective-permute-done.2.rest_2_ = bf16[4,72,512]{2,1,0:T(8,128)(2,1)S(1)} collective-permute-done((bf16[4,72,512]{2,1,0:T(8,128)(2,1)S(1)}, bf16[4,72,512]{2,1,0:T(8,128)(2,1)S(1)}, u32[]{:S(2)}, u32[]{:S(2)}) %collective-permute-start.2) | collective-permute-done | bytes 294944 | tf_op jit(solution)/shard_map/ppermute | solution.py:248
  26.3 0.1 collective-permute-start.4
  26.4 0.1 convolution_convert_fusion
  26.6 2.2 %copy-done.2 = bf16[8192,256]{1,0:T(8,128)(2,1)S(1)} copy-done((bf16[8192,256]{1,0:T(8,128)(2,1)S(1)}, bf16[8192,256]{1,0:T(8,128)(2,1)}, u32[]{:S(2)}) %copy-start.2) | copy-done | bytes 4194328
  28.7 3.2 %fold_blocks.2 = (bf16[8192,256]{1,0:T(8,128)(2,1)}, f32[4,256]{1,0:T(4,128)S(1)}) custom-call(s32[16]{0:T(128)S(1)} %multiply_add_fusion.start_hbm, bf16[64,256]{1,0:T(8,128)(2,1)S(1)} %bitcast.14, bf16[4,8192]{1,0:T(4,128)(2,1)S(1)} %maximum_select_fusion.features_ref, bf16[8192,256]{1,0:T(8,128)(2,1)S(1)} %copy-done.2, ...), custom_call_target="tpu_custom_call" | custom-call | flops 213909504 | bytes 6291456 | tf_op jit(solution)/shard_map/fold_blocks/pallas_call | solution.py:206
  31.9 2.2 %fold_blocks.3 = (bf16[8192,256]{1,0:T(8,128)(2,1)}, bf16[4,256]{1,0:T(4,128)(2,1)}, bf16[4,2048]{1,0:T(4,128)(2,1)}) custom-call(s32[16]{0:T(128)S(1)} %multiply_add_fusion.start_hbm, bf16[64,256]{1,0:T(8,128)(2,1)S(1)} %bitcast.15, bf16[4,8192]{1,0:T(4,128)(2,1)S(1)} %maximum_select_fusion.features_ref, ...), custom_call_target="tpu_custom_call", output_to_operand_aliasing={{0}: (5, {})} | custom-call | flops 71303168 | bytes 2097152 | tf_op jit(solution)/shard_map/fold_blocks/pallas_call | solution.py:206
  (23 shorter events, 0.2 us)
Async XLA Ops:
  0.6 0.9 %copy-start = (bf16[64,1024]{1,0:T(8,128)(2,1)S(1)}, bf16[64,1024]{1,0:T(8,128)(2,1)}, u32[]{:S(2)}) copy-start(bf16[64,1024]{1,0:T(8,128)(2,1)} %param.17) | copy-start | bytes 393220
  1.6 12.5 %collective-permute-start = (bf16[1,72,512]{2,1,0:T(8,128)(2,1)S(1)}, bf16[1,72,512]{2,1,0:T(8,128)(2,1)S(1)}, u32[]{:S(2)}, u32[]{:S(2)}) collective-permute-start(bf16[1,72,512]{2,1,0:T(8,128)(2,1)S(1)} %maximum_bitcast_fusion), channel_id=1, source_target_pairs={{0,8},{1,9},{2,10},{3,11},{4,12},{5,13},{6,14},{7,15},{8,0},{9,1},... | collective-permute-start | bytes 221192 | tf_op jit(solution)/shard_map/ppermute | solution.py:248
  6.6 0.7 %copy-start.3 = (bf16[4,2048]{1,0:T(4,128)(2,1)S(1)}, bf16[4,2048]{1,0:T(4,128)(2,1)}, u32[]{:S(2)}) copy-start(bf16[4,2048]{1,0:T(4,128)(2,1)} %q_ref.1) | copy-start | bytes 49156
  7.3 0.7 %copy-start.4 = (bf16[4,256]{1,0:T(4,128)(2,1)S(1)}, bf16[4,256]{1,0:T(4,128)(2,1)}, u32[]{:S(2)}) copy-start(bf16[4,256]{1,0:T(4,128)(2,1)} %own_k_ref.1) | copy-start | bytes 6148
  8.0 6.2 %copy-start.5 = (bf16[4,4096]{1,0:T(4,128)(2,1)S(1)}, bf16[4,4096]{1,0:T(4,128)(2,1)}, u32[]{:S(2)}) copy-start(bf16[4,4096]{1,0:T(4,128)(2,1)} %param.10) | copy-start | bytes 98308
  12.2 2.0 %copy-start.1 = (bf16[8192,256]{1,0:T(8,128)(2,1)}, bf16[8192,256]{1,0:T(8,128)(2,1)S(1)}, u32[]{:S(2)}) copy-start(bf16[8192,256]{1,0:T(8,128)(2,1)S(1)} %get-tuple-element.18.served_ref) | copy-start | bytes 12582916
  14.2 6.9 %collective-permute-start.3 = (bf16[4,4096]{1,0:T(4,128)(2,1)S(1)}, bf16[4,4096]{1,0:T(4,128)(2,1)S(1)}, u32[]{:S(2)}, u32[]{:S(2)}) collective-permute-start(bf16[4,4096]{1,0:T(4,128)(2,1)S(1)} %copy-done.5), channel_id=1, source_target_pairs={{0,1},{1,0},{2,3},{3,2},{4,5},{5,4},{6,7},{7,6},{8,9},{9,8},{10,11... | collective-permute-start | bytes 98312 | tf_op jit(solution)/shard_map/ppermute | solution.py:286
  14.2 5.2 %collective-permute-start.1 = (bf16[2,72,512]{2,1,0:T(8,128)(2,1)S(1)}, bf16[2,72,512]{2,1,0:T(8,128)(2,1)S(1)}, u32[]{:S(2)}, u32[]{:S(2)}) collective-permute-start(bf16[2,72,512]{2,1,0:T(8,128)(2,1)S(1)} %pad_maximum_fusion.1), channel_id=1, source_target_pairs={{0,4},{1,3},{2,6},{3,1},{4,0},{5,7},{6,2},{7,5},{8,12},{9,11},{10,... | collective-permute-start | bytes 442376 | tf_op jit(solution)/shard_map/ppermute | solution.py:248
  19.5 6.8 %collective-permute-start.2 = (bf16[4,72,512]{2,1,0:T(8,128)(2,1)S(1)}, bf16[4,72,512]{2,1,0:T(8,128)(2,1)S(1)}, u32[]{:S(2)}, u32[]{:S(2)}) collective-permute-start(bf16[4,72,512]{2,1,0:T(8,128)(2,1)S(1)} %pad_maximum_fusion.rest_0_), channel_id=1, source_target_pairs={{0,2},{1,5},{2,0},{3,7},{4,6},{5,1},{6,4},{7,3},{8,10},{9,13},{10,... | collective-permute-start | bytes 884744 | tf_op jit(solution)/shard_map/ppermute | solution.py:248
  21.1 5.4 %collective-permute-start.5 = (bf16[4,72,512]{2,1,0:T(8,128)(2,1)S(1)}, bf16[4,72,512]{2,1,0:T(8,128)(2,1)S(1)}, u32[]{:S(2)}, u32[]{:S(2)}) collective-permute-start(bf16[4,72,512]{2,1,0:T(8,128)(2,1)S(1)} %pad_maximum_fusion.rest_0_), channel_id=1, source_target_pairs={{0,1},{1,0},{2,3},{3,2},{4,5},{5,4},{6,7},{7,6},{8,9},{9,8},{10,11... | collective-permute-start | bytes 884744 | tf_op jit(solution)/shard_map/ppermute | solution.py:289
  26.3 5.7 %collective-permute-start.4 = (bf16[4,72,512]{2,1,0:T(8,128)(2,1)S(1)}, bf16[4,72,512]{2,1,0:T(8,128)(2,1)S(1)}, u32[]{:S(2)}, u32[]{:S(2)}) collective-permute-start(bf16[4,72,512]{2,1,0:T(8,128)(2,1)S(1)} %collective-permute-done.2.rest_2_), channel_id=1, source_target_pairs={{0,1},{1,0},{2,3},{3,2},{4,5},{5,4},{6,7},{7,6},{8,9},{9,8},{10,11... | collective-permute-start | bytes 884744 | tf_op jit(solution)/shard_map/ppermute | solution.py:290
  26.6 2.2 %copy-start.2 = (bf16[8192,256]{1,0:T(8,128)(2,1)S(1)}, bf16[8192,256]{1,0:T(8,128)(2,1)}, u32[]{:S(2)}) copy-start(bf16[8192,256]{1,0:T(8,128)(2,1)} %copy-done.1) | copy-start | bytes 12582916

commit v6 on v5

v6 whole, which is shorter than its diff:
```python
import functools

import jax
import jax.numpy as jnp
from jax import lax
from jax.experimental import pallas as pl
from jax.experimental.pallas import tpu as pltpu
from jax.sharding import PartitionSpec as P

HEAD_SIZE = 128
ADAPTER_SCALE = 2.0

SMEM = pl.BlockSpec(memory_space=pltpu.SMEM)
VMEM = pl.BlockSpec(memory_space=pltpu.VMEM)
HBM = pl.BlockSpec(memory_space=pltpu.HBM)


def in_hbm(*arrays):
    return [pltpu.with_memory_space_constraint(x, pltpu.HBM) for x in arrays]


def attend_kernel(rows, lengths_hbm, q_hbm, own_k_hbm, k_hbm, v_hbm, *rest):
    context_ref, own_weight_ref, lengths, q_ref, own_k_ref, k_buf, v_buf, small_sem, k_sem, v_sem = (
        rest[-10:]
    )
    smalls = [
        pltpu.make_async_copy(source, into, small_sem.at[i])
        for i, (source, into) in enumerate(
            [(lengths_hbm, lengths), (q_hbm, q_ref), (own_k_hbm, own_k_ref)]
        )
    ]
    for copy in smalls:
        copy.start()

    def copies(i, row):
        return (
            pltpu.make_async_copy(k_hbm.at[row], k_buf.at[i], k_sem.at[i]),
            pltpu.make_async_copy(v_hbm.at[row], v_buf.at[i], v_sem.at[i]),
        )

    for i, row in enumerate(rows):
        for copy in copies(i, row):
            copy.start()
    for copy in smalls:
        copy.wait()
    queries = q_ref[...].astype(jnp.float32)
    own_keys = own_k_ref[...].astype(jnp.float32)
    heads = queries.shape[1] // HEAD_SIZE
    cache_len, width = k_buf.shape[1:]
    local_heads = width // HEAD_SIZE
    group = heads // local_heads
    scaling = 1.0 / HEAD_SIZE**0.5
    head_of = lax.broadcasted_iota(jnp.int32, (heads, HEAD_SIZE), 0) // group
    position = lax.broadcasted_iota(jnp.int32, (heads, cache_len), 1)
    for i, row in enumerate(rows):
        q = jnp.concatenate(
            [
                queries[row : row + 1, h * HEAD_SIZE : (h + 1) * HEAD_SIZE]
                for h in range(heads)
            ],
            axis=0,
        )
        spread = jnp.concatenate(
            [jnp.where(head_of == h, q, 0.0) for h in range(local_heads)], axis=1
        )
        own = jnp.sum(spread * own_keys[row : row + 1], axis=1, keepdims=True) * scaling
        get_keys, get_values = copies(i, row)
        get_keys.wait()
        scores = (
            lax.dot_general(
                spread.astype(jnp.bfloat16), k_buf[i], (((1,), (1,)), ((), ())),
                preferred_element_type=jnp.float32,
            )
            * scaling
        )
        valid = position < lengths[row]
        masked = jnp.where(valid, scores, -1e30)
        largest = jnp.maximum(jnp.max(masked, axis=1, keepdims=True), own)
        cached_exp = jnp.where(valid, jnp.exp(masked - largest), 0.0)
        own_exp = jnp.exp(own - largest)
        normaliser = jnp.sum(cached_exp, axis=1, keepdims=True) + own_exp
        weights = (cached_exp / normaliser).astype(jnp.bfloat16)
        weight_own = (own_exp / normaliser).astype(jnp.bfloat16).astype(jnp.float32)
        get_values.wait()
        wide = jnp.dot(weights, v_buf[i], preferred_element_type=jnp.float32)
        context = wide[:, :HEAD_SIZE]
        for h in range(1, local_heads):
            context = jnp.where(
                head_of == h, wide[:, h * HEAD_SIZE : (h + 1) * HEAD_SIZE], context
            )
        context_ref[i] = context
        own_weight_ref[i] = jnp.broadcast_to(weight_own, (heads, HEAD_SIZE))


def attend(rows, lengths, queries, own_key, stored_keys, stored_values, *after):
    cache_len, width = stored_keys.shape[1:]
    heads = queries.shape[1] // HEAD_SIZE
    count = len(rows)
    out = jax.ShapeDtypeStruct((count, heads, HEAD_SIZE), jnp.float32)
    return pl.pallas_call(
        functools.partial(attend_kernel, rows),
        out_shape=(out, out),
        in_specs=[HBM] * 5 + [pl.BlockSpec(memory_space=pl.ANY)] * len(after),
        out_specs=(VMEM, VMEM),
        scratch_shapes=[
            pltpu.SMEM(lengths.shape, jnp.int32),
            pltpu.VMEM(queries.shape, jnp.bfloat16),
            pltpu.VMEM(own_key.shape, jnp.bfloat16),
            pltpu.VMEM((count, cache_len, width), jnp.bfloat16),
            pltpu.VMEM((count, cache_len, width), jnp.bfloat16),
            pltpu.SemaphoreType.DMA((3,)),
            pltpu.SemaphoreType.DMA((count,)),
            pltpu.SemaphoreType.DMA((count,)),
        ],
        compiler_params=pltpu.CompilerParams(vmem_limit_bytes=16 * 2**20),
        cost_estimate=pl.CostEstimate(
            flops=4 * count * heads * cache_len * width,
            bytes_accessed=4 * count * cache_len * width,
            transcendentals=count * heads * cache_len,
        ),
        name="attend_cache",
    )(lengths, queries, own_key, stored_keys, stored_values, *after)


def fold_kernel(sizes, entry, ahead_from, stage, start_hbm, up_ref, features_ref, *rest):
    rest = list(rest)
    first, last = stage == 0, stage == 2
    served = rest.pop(0)
    arrays = [rest.pop(0) for _ in sizes]
    if not first:
        rest.pop(0)
        total = rest.pop(0)[...]
    if last:
        context_ref, own_weight_ref = rest[:2]
        merged, fresh_hbm, attended_hbm = rest[2:5]
        start, start_sem, m_buf, out_sem, fresh_ref, attended_ref, small_sem = rest[5:]
    elif first:
        merged, total_ref, ahead_ref, start, start_sem, m_buf, out_sem, w_buf, in_sem = rest
        total = jnp.zeros(total_ref.shape, jnp.float32)
    else:
        merged, total_ref, start, start_sem, m_buf, out_sem = rest
    width = arrays[0].shape[2]
    count = sum(sizes)

    def rows_of(i):
        return pl.ds(pl.multiple_of(start[entry + i], width), width)

    def fetch(i):
        into = w_buf.at[i] if i < count else ahead_ref.at[i - count]
        return pltpu.make_async_copy(served.at[rows_of(i)], into, in_sem.at[i])

    def store(i):
        return pltpu.make_async_copy(m_buf.at[i], merged.at[rows_of(i)], out_sem.at[i])

    get_start = pltpu.make_async_copy(start_hbm, start, start_sem)
    get_start.start()
    up = (up_ref[...].astype(jnp.float32) * ADAPTER_SCALE).astype(jnp.bfloat16)
    if first:
        get_start.wait()
        for i in range(start.shape[0]):
            fetch(i).start()
    slabs = [array.at[k] for array, size in zip(arrays, sizes) for k in range(size)]
    for i, slab in enumerate(slabs):
        update = lax.dot_general(
            slab[...], up, (((0,), (0,)), ((), ())), preferred_element_type=jnp.float32
        )
        if first:
            fetch(i).wait()
            rows = w_buf[i]
        else:
            rows = served[ahead_from + i]
        fold = (rows.astype(jnp.float32) + update).astype(jnp.bfloat16)
        m_buf[i] = fold
        if i == 0 and not first:
            get_start.wait()
        store(i).start()
        total = total + jnp.dot(
            features_ref[:, rows_of(i)], fold, preferred_element_type=jnp.float32
        )
    if last:
        fresh = total.astype(jnp.bfloat16)
        fresh_ref[...] = fresh
        put_fresh = pltpu.make_async_copy(fresh_ref, fresh_hbm, small_sem.at[0])
        put_fresh.start()
        value = fresh.astype(jnp.float32)
        heads = attended_ref.shape[1] // HEAD_SIZE
        group = heads // (fresh_ref.shape[1] // HEAD_SIZE)
        for h in range(heads):
            cols = slice(h * HEAD_SIZE, (h + 1) * HEAD_SIZE)
            at = (h // group) * HEAD_SIZE
            attended_ref[:, cols] = (
                context_ref[:, cols] + own_weight_ref[:, cols] * value[:, at : at + HEAD_SIZE]
            ).astype(jnp.bfloat16)
        put_attended = pltpu.make_async_copy(attended_ref, attended_hbm, small_sem.at[1])
        put_attended.start()
        put_fresh.wait()
        put_attended.wait()
    else:
        total_ref[...] = total
    if first:
        for i in range(count, start.shape[0]):
            fetch(i).wait()
    for i in range(count):
        store(i).wait()


def fold(stage, entry, start, up, features, served, arrays, ahead_from=0, state=(), finish=()):
    first, last = stage == 0, stage == 2
    sizes = [array.shape[0] for array in arrays]
    count = sum(sizes)
    ahead = start.shape[0] - count
    rank, cols = up.shape
    width = arrays[0].shape[2]
    rows, depth = features.shape
    in_specs = [HBM, VMEM, VMEM, HBM if first else VMEM] + [VMEM] * len(arrays)
    operands = [start, up, features, served, *arrays]
    aliases = {}
    out_shape = [jax.ShapeDtypeStruct((depth, cols), jnp.bfloat16)]
    out_specs = [HBM]
    scratch = [
        pltpu.SMEM(start.shape, jnp.int32),
        pltpu.SemaphoreType.DMA,
        pltpu.VMEM((count, width, cols), jnp.bfloat16),
        pltpu.SemaphoreType.DMA((count,)),
    ]
    if not first:
        aliases = {len(operands): 0}
        in_specs += [HBM, VMEM] + [VMEM] * len(finish)
        operands += [*state, *finish]
    if last:
        smalls = [(rows, cols), finish[0].shape]
        out_shape += [jax.ShapeDtypeStruct(shape, jnp.bfloat16) for shape in smalls]
        out_specs += [HBM, HBM]
        scratch += [pltpu.VMEM(shape, jnp.bfloat16) for shape in smalls]
        scratch += [pltpu.SemaphoreType.DMA((2,))]
    else:
        out_shape += [jax.ShapeDtypeStruct((rows, cols), jnp.float32)]
        out_specs += [VMEM]
    if first:
        out_shape += [jax.ShapeDtypeStruct((ahead, width, cols), jnp.bfloat16)]
        out_specs += [VMEM]
        scratch += [
            pltpu.VMEM((count, width, cols), jnp.bfloat16),
            pltpu.SemaphoreType.DMA((count + ahead,)),
        ]
    return pl.pallas_call(
        functools.partial(fold_kernel, sizes, entry, ahead_from, stage),
        out_shape=out_shape,
        in_specs=in_specs,
        out_specs=out_specs,
        input_output_aliases=aliases,
        scratch_shapes=scratch,
        compiler_params=pltpu.CompilerParams(vmem_limit_bytes=24 * 2**20),
        cost_estimate=pl.CostEstimate(
            flops=2 * count * width * cols * (rank + rows),
            bytes_accessed=4 * count * width * cols,
            transcendentals=0,
        ),
        name="fold_blocks",
    )(*operands)


def body(
    hidden_in,
    queries,
    stored_keys,
    stored_values,
    fresh_token_key,
    lengths,
    served_value_weight,
    adapter_in,
    adapter_out,
    owner_rank,
):
    n = lax.axis_size("replica")
    replica = lax.axis_index("replica")
    core = lax.axis_index("tensor")
    swap = [(0, 1), (1, 0)]
    full = adapter_in.shape[1]
    width = full // 2
    rows = queries.shape[0]

    bits = [n >> i for i in range(1, n.bit_length())]
    ways = [bits, bits[:-2] + bits[:-3:-1]]

    def exchange(x, step):
        pairs = [(2 * i + c, 2 * (i ^ ways[c][step]) + c) for i in range(n) for c in range(2)]
        return lax.ppermute(x, ("replica", "tensor"), pairs)

    def grown(up, bit):
        came = lax.ppermute(up, "replica", [(i, i ^ bit) for i in range(n)])
        above, below = jnp.concatenate([up, came], axis=0), jnp.concatenate([came, up], axis=0)
        return jnp.where((replica & bit) == 0, above, below)

    given = (
        *in_hbm(lengths, queries, fresh_token_key, stored_keys, stored_values),
    )
    slabs = lax.dynamic_slice_in_dim(adapter_in, core * width, width, axis=1)[None]
    up, hid_other = adapter_out, hidden_in
    *early, final = range(len(bits))
    parts = []
    split = rows // 2
    for step in early:
        came = exchange(slabs, step)
        if step == 0:
            grown_up = grown(up, 1)
            parts.append(attend(range(split), *given))
            up, parts[0], hid_other, owner_rank = lax.optimization_barrier(
                (grown_up, parts[0], hid_other, owner_rank)
            )
            grown_up = grown(up, 2)
            hid_other = lax.ppermute(hid_other, "tensor", swap)
            came, up = lax.optimization_barrier((came, grown_up))
        elif step == 1:
            grown_up = grown(up, 4)
            parts.append(attend(range(split, rows), *given, slabs, up))
            came, up, parts[1] = lax.optimization_barrier((came, grown_up, parts[1]))
        slabs = jnp.concatenate([slabs, came], axis=0)
    for step in range(3, len(bits)):
        up = grown(up, 1 << step)
    last = exchange(slabs, final)
    crossed = lax.ppermute(slabs, "tensor", swap)

    features = jnp.concatenate([hidden_in, hid_other], axis=1)
    features = jnp.where(core == 0, features, jnp.concatenate([hid_other, hidden_in], axis=1))

    slab = jnp.arange(n, dtype=jnp.int32)
    sources = []
    for way in ways:
        source = replica
        for step, bit in enumerate(way):
            source = source ^ (((slab >> step) & 1) * bit)
        sources.append(source)
    mine = jnp.where(core == 0, sources[0], sources[1])
    theirs = jnp.where(core == 0, sources[1], sources[0])
    count = slabs.shape[0]
    source = jnp.concatenate([mine[:count], theirs[:count], mine[count:], theirs[count:]])
    half = jnp.where((jnp.arange(2 * n) // count) % 2 == 0, core, 1 - core)
    place = jnp.sum(jnp.where(owner_rank[None, :] == source[:, None], slab[None, :], 0), axis=1)
    start = (place * full + half * width).astype(jnp.int32)

    merged, total, ahead = fold(
        0, 0, start, up, features, *in_hbm(served_value_weight), [slabs, crossed]
    )
    last, total = lax.optimization_barrier((last, total))
    last_crossed = lax.ppermute(last, "tensor", swap)
    merged, total = fold(
        1, 2 * count, start, up, features, ahead, [last], state=[merged, total]
    )
    context, own_weight = (
        jnp.concatenate(pair, axis=0).reshape(queries.shape) for pair in zip(*parts)
    )
    merged, fresh_token_value, attended = fold(
        2, 3 * count, start, up, features, ahead, [last_crossed], ahead_from=count,
        state=[merged, total], finish=[context, own_weight],
    )
    return (merged, fresh_token_value, attended)


def solution(mesh):
    in_specs = (
        P(("groups", "replica"), "tensor"),
        P(("groups", "replica"), "tensor"),
        P(("groups", "replica"), None, "tensor"),
        P(("groups", "replica"), None, "tensor"),
        P(("groups", "replica"), "tensor"),
        P(("groups", "replica")),
        P(None, "tensor"),
        P("groups", "replica"),
        P(("groups", "replica"), "tensor"),
        P("groups"),
    )
    out_specs = (
        P("groups", "tensor"),
        P(("groups", "replica"), "tensor"),
        P(("groups", "replica"), "tensor"),
    )
    return jax.shard_map(body, mesh=mesh, in_specs=in_specs, out_specs=out_specs, check_vma=False)
```

time: 34.5 us -> 30.6 us (0.89)
  local copies, waits for them, and re-layouts: 6.58 us -> 0.2 us
  Pallas kernels: 9.54 us -> 14.5 us
  waiting for transfers between devices: 8.61 us -> 4.53 us
  starting transfers between devices: 7.47 us -> 10.1 us
  other arithmetic: 1.03 us -> 0.3 us
    ppermute x3, waiting for transfers between devices: 8.6 us -> 1.05 us  [exchange(): return lax.ppermute(x, ('replica', 'tensor'), pairs)]
    unnamed x12 -> x10, local copies, waits for them, and re-layouts: 5.69 us -> 0.05 us
    ppermute x1 -> x4, starting transfers between devices: 0.01 us -> 5.08 us  [the longest x3 5.07 us: grown(): came = lax.ppermute(up, 'replica', [(i, i ^ bit) for i in range(n)])]
    pallas_call x3 -> x5, Pallas kernels: 9.54 us -> 14.5 us  [the longest x3 9 us: fold(): pl.pallas_call(functools.partial(fold_kernel, sizes, entry, ahead_from, s...]
    ppermute x3, starting transfers between devices: 7.33 us -> 4.83 us  [exchange(): return lax.ppermute(x, ('replica', 'tensor'), pairs)]
    ppermute x1 -> x4, waiting for transfers between devices: 0.01 us -> 1.99 us  [the longest x3 1.99 us: grown(): came = lax.ppermute(up, 'replica', [(i, i ^ bit) for i in range(n)])]
    ppermute x1, waiting for transfers between devices: 0.01 us -> 1.48 us  [body(): crossed = lax.ppermute(slabs, 'tensor', swap)]
    reshape x3 -> x0, local copies, waits for them, and re-layouts: 0.77 us -> none  [the longest x1 0.73 us: body(): adapter_out.reshape(up_rows, width)]
  transfers between devices with their start and end apart: 6 -> 9, of which waited for: 2 -> 3; matrix products, arithmetic and copies ran while one was open for 3% -> 2% of each run, Pallas kernels for 22% -> 40%
where the time goes in v6:
time: 30.6 us; the launch traced here: 30.4 us
  Pallas kernels  14.5 us (47%)
  starting transfers between devices  10.1 us (33%)
  waiting for transfers between devices  4.53 us (15%)
  between operations  0.79 us (3%)
    pallas_call x3, Pallas kernels, fold(): pl.pallas_call(functools.partial(fold_kernel, sizes, entry, ahead_from, s...  9 us
    pallas_call x2, Pallas kernels, attend(): pl.pallas_call(functools.partial(attend_kernel, rows), out_shape=(out, ou...  5.48 us
    ppermute x3, starting transfers between devices, grown(): came = lax.ppermute(up, 'replica', [(i, i ^ bit) for i in range(n)])  5.07 us
    ppermute x3, starting transfers between devices, exchange(): return lax.ppermute(x, ('replica', 'tensor'), pairs)  4.83 us
    ppermute x3, waiting for transfers between devices, grown(): came = lax.ppermute(up, 'replica', [(i, i ^ bit) for i in range(n)])  1.99 us
    ppermute x1, waiting for transfers between devices, body(): crossed = lax.ppermute(slabs, 'tensor', swap)  1.48 us
    ppermute x3, waiting for transfers between devices, exchange(): return lax.ppermute(x, ('replica', 'tensor'), pairs)  1.05 us
  transfers between devices with their start and end apart: 9, of which 3 were waited for; matrix products, arithmetic and copies ran while one was open for 2% of the time, Pallas kernels for 40%

profile of v6, /device:TPU:0, one launch (start us, length us, event | category | flops | bytes accessed | tf_op | source)
XLA Modules:
  0.0 30.4 jit_solution(6947436078659121355)
XLA Ops:
  0.6 0.0 copy-start
  0.7 3.0 %collective-permute-start = (bf16[8,256]{1,0:T(8,128)(2,1)}, bf16[8,256]{1,0:T(8,128)(2,1)S(1)}, u32[]{:S(2)}, u32[]{:S(2)}) collective-permute-start(bf16[8,256]{1,0:T(8,128)(2,1)} %param.18), channel_id=1, source_target_pairs={{0,2},{2,0},{4,6},{6,4},{8,10},{10,8},{12,14},{14,12},{1,3},{3,1},... | collective-permute-start | bytes 12296 | tf_op jit(solution)/shard_map/ppermute | solution.py:291
  3.7 2.7 %collective-permute-start.1 = (bf16[1,64,512]{2,1,0:T(8,128)(2,1)S(1)}, bf16[1,64,512]{2,1,0:T(8,128)(2,1)S(1)}, u32[]{:S(2)}, u32[]{:S(2)}) collective-permute-start(bf16[1,64,512]{2,1,0:T(8,128)(2,1)S(1)} %dynamic-slice_bitcast_fusion), channel_id=1, source_target_pairs={{0,8},{1,9},{2,10},{3,11},{4,12},{5,13},{6,14},{7,15},{8,0},{9,1},... | collective-permute-start | bytes 196616 | tf_op jit(solution)/shard_map/ppermute | solution.py:288
  6.4 0.1 fusion.4
  6.5 0.1 fusion.3
  6.5 0.1 pad_add_fusion
  6.6 2.8 %attend_cache.2 = (f32[2,16,128]{2,1,0:T(8,128)S(1)}, f32[2,16,128]{2,1,0:T(8,128)S(1)}) custom-call(s32[4]{0:T(128)} %lengths_hbm.3, bf16[4,2048]{1,0:T(4,128)(2,1)} %q_hbm.3, bf16[4,256]{1,0:T(4,128)(2,1)} %own_k_hbm.3, bf16[4,1024,256]{2,1,0:T(8,128)(2,1)} %k_hbm.3, bf16[4,1024,256]{2,1,0:T(8,128)(2,1)} %v_hbm.3), custom_call_target="tpu_custom_call" | custom-call | flops 33554432 | bytes 2097152 | tf_op jit(solution)/shard_map/attend_cache/pallas_call | solution.py:100
  9.4 1.6 %collective-permute-start.2 = (bf16[16,256]{1,0:T(8,128)(2,1)S(1)}, bf16[16,256]{1,0:T(8,128)(2,1)S(1)}, u32[]{:S(2)}, u32[]{:S(2)}) collective-permute-start(bf16[16,256]{1,0:T(8,128)(2,1)S(1)} %maximum_select_fusion.3), channel_id=1, source_target_pairs={{0,4},{2,6},{4,0},{6,2},{8,12},{10,14},{12,8},{14,10},{1,5},{3,7},... | collective-permute-start | bytes 24584 | tf_op jit(solution)/shard_map/ppermute | solution.py:291
  11.1 0.1 select_reduce_fusion
  11.2 2.0 %collective-permute-done.2 = bf16[16,256]{1,0:T(8,128)(2,1)S(1)} collective-permute-done((bf16[16,256]{1,0:T(8,128)(2,1)S(1)}, bf16[16,256]{1,0:T(8,128)(2,1)S(1)}, u32[]{:S(2)}, u32[]{:S(2)}) %collective-permute-start.2) | collective-permute-done | bytes 8224 | tf_op jit(solution)/shard_map/ppermute | solution.py:291
  13.1 0.4 %collective-permute-start.4 = (bf16[32,256]{1,0:T(8,128)(2,1)S(1)}, bf16[32,256]{1,0:T(8,128)(2,1)S(1)}, u32[]{:S(2)}, u32[]{:S(2)}) collective-permute-start(bf16[32,256]{1,0:T(8,128)(2,1)S(1)} %maximum_select_fusion.2.rest_1_), channel_id=1, source_target_pairs={{0,8},{2,10},{4,12},{6,14},{8,0},{10,2},{12,4},{14,6},{1,9},{3,11}... | collective-permute-start | bytes 49160 | tf_op jit(solution)/shard_map/ppermute | solution.py:291
  13.6 1.6 %collective-permute-start.3 = (bf16[2,64,512]{2,1,0:T(8,128)(2,1)S(1)}, bf16[2,64,512]{2,1,0:T(8,128)(2,1)S(1)}, u32[]{:S(2)}, u32[]{:S(2)}) collective-permute-start(bf16[2,64,512]{2,1,0:T(8,128)(2,1)S(1)} %pad_maximum_fusion.1.rest_0_), channel_id=1, source_target_pairs={{0,4},{1,3},{2,6},{3,1},{4,0},{5,7},{6,2},{7,5},{8,12},{9,11},{10,... | collective-permute-start | bytes 393224 | tf_op jit(solution)/shard_map/ppermute | solution.py:288
  15.2 2.7 %attend_cache.3 = (f32[2,16,128]{2,1,0:T(8,128)S(1)}, f32[2,16,128]{2,1,0:T(8,128)S(1)}) custom-call(s32[4]{0:T(128)} %lengths_hbm.3, bf16[4,2048]{1,0:T(4,128)(2,1)} %q_hbm.3, bf16[4,256]{1,0:T(4,128)(2,1)} %own_k_hbm.3, bf16[4,1024,256]{2,1,0:T(8,128)(2,1)} %k_hbm.3, bf16[4,1024,256]{2,1,0:T(8,128)(2,1)} %v_hbm.3, ...), custom_call_target="tpu_custom_call" | custom-call | flops 33554432 | bytes 2097152 | tf_op jit(solution)/shard_map/attend_cache/pallas_call | solution.py:100
  17.9 0.0 collective-permute-done.4
  18.0 1.0 %collective-permute-done.3 = bf16[2,64,512]{2,1,0:T(8,128)(2,1)S(1)} collective-permute-done((bf16[2,64,512]{2,1,0:T(8,128)(2,1)S(1)}, bf16[2,64,512]{2,1,0:T(8,128)(2,1)S(1)}, u32[]{:S(2)}, u32[]{:S(2)}) %collective-permute-start.3) | collective-permute-done | bytes 131104 | tf_op jit(solution)/shard_map/ppermute | solution.py:288
  19.1 0.5 %collective-permute-start.7 = (bf16[4,64,512]{2,1,0:T(8,128)(2,1)S(1)}, bf16[4,64,512]{2,1,0:T(8,128)(2,1)S(1)}, u32[]{:S(2)}, u32[]{:S(2)}) collective-permute-start(bf16[4,64,512]{2,1,0:T(8,128)(2,1)S(1)} %pad_maximum_fusion.rest_1_), channel_id=1, source_target_pairs={{0,2},{1,5},{2,0},{3,7},{4,6},{5,1},{6,4},{7,3},{8,10},{9,13},{10,... | collective-permute-start | bytes 786440 | tf_op jit(solution)/shard_map/ppermute | solution.py:288
  19.6 0.0 collective-permute-start.6
  19.6 0.0 collective-permute-done.5
  19.6 1.5 %collective-permute-done.6.rest_2_ = bf16[4,64,512]{2,1,0:T(8,128)(2,1)S(1)} collective-permute-done((bf16[4,64,512]{2,1,0:T(8,128)(2,1)S(1)}, bf16[4,64,512]{2,1,0:T(8,128)(2,1)S(1)}, u32[]{:S(2)}, u32[]{:S(2)}) %collective-permute-start.6) | collective-permute-done | bytes 262176 | tf_op jit(solution)/shard_map/ppermute | solution.py:322
  21.1 4.7 %fold_blocks.3 = (bf16[8192,256]{1,0:T(8,128)(2,1)}, f32[4,256]{1,0:T(4,128)S(1)}, bf16[8,512,256]{2,1,0:T(8,128)(2,1)S(1)}) custom-call(s32[16]{0:T(128)S(1)} %fusion.1.start_hbm, bf16[64,256]{1,0:T(8,128)(2,1)S(1)} %maximum_select_fusion.1.up_ref, bf16[4,8192]{1,0:T(4,128)(2,1)S(1)} %maximum_select_fusion.features_ref, bf16[8192,256]{1,0:T(8,128)(2,1)} %rest_0_.1, ...), custom_call_target="tpu_custom_call" | custom-call | flops 142606336 | bytes 4194304 | tf_op jit(solution)/shard_map/fold_blocks/pallas_call | solution.py:246
  25.8 0.2 collective-permute-start.8
  26.1 2.1 %fold_blocks.4 = (bf16[8192,256]{1,0:T(8,128)(2,1)}, f32[4,256]{1,0:T(4,128)S(1)}) custom-call(s32[16]{0:T(128)S(1)} %fusion.1.start_hbm, bf16[64,256]{1,0:T(8,128)(2,1)S(1)} %maximum_select_fusion.1.up_ref, bf16[4,8192]{1,0:T(4,128)(2,1)S(1)} %maximum_select_fusion.features_ref, ...), custom_call_target="tpu_custom_call", output_to_operand_aliasing={{0}: (5, {})} | custom-call | flops 71303168 | bytes 2097152 | tf_op jit(solution)/shard_map/fold_blocks/pallas_call | solution.py:246
  28.2 0.0 collective-permute-done.8.rest_1_
  28.2 2.2 %fold_blocks.5 = (bf16[8192,256]{1,0:T(8,128)(2,1)}, bf16[4,256]{1,0:T(4,128)(2,1)}, bf16[4,2048]{1,0:T(4,128)(2,1)}) custom-call(s32[16]{0:T(128)S(1)} %fusion.1.start_hbm, bf16[64,256]{1,0:T(8,128)(2,1)S(1)} %maximum_select_fusion.1.up_ref, bf16[4,8192]{1,0:T(4,128)(2,1)S(1)} %maximum_select_fusion.features_ref, ...), custom_call_target="tpu_custom_call", output_to_operand_aliasing={{0}: (5, {})} | custom-call | flops 71303168 | bytes 2097152 | tf_op jit(solution)/shard_map/fold_blocks/pallas_call | solution.py:246
  (23 shorter events, 0.2 us)
Async XLA Ops:
  0.6 3.1 %copy-start = (bf16[64,1024]{1,0:T(8,128)(2,1)S(1)}, bf16[64,1024]{1,0:T(8,128)(2,1)}, u32[]{:S(2)}) copy-start(bf16[64,1024]{1,0:T(8,128)(2,1)} %param.17) | copy-start | bytes 393220
  0.6 8.7 %copy-start.2 = (bf16[8,256]{1,0:T(8,128)(2,1)S(1)}, bf16[8,256]{1,0:T(8,128)(2,1)}, u32[]{:S(2)}) copy-start(bf16[8,256]{1,0:T(8,128)(2,1)} %param.18) | copy-start | bytes 12292
  0.7 10.4 %copy-start.1 = (bf16[4,4096]{1,0:T(4,128)(2,1)S(1)}, bf16[4,4096]{1,0:T(4,128)(2,1)}, u32[]{:S(2)}) copy-start(bf16[4,4096]{1,0:T(4,128)(2,1)} %param.10) | copy-start | bytes 98308
  0.7 10.4 %copy-start.3 = (s32[8]{0:T(128)S(1)}, s32[8]{0:T(128)}, u32[]{:S(2)}) copy-start(s32[8]{0:T(128)} %param.19) | copy-start | bytes 100
  0.7 8.7 %collective-permute-start = (bf16[8,256]{1,0:T(8,128)(2,1)}, bf16[8,256]{1,0:T(8,128)(2,1)S(1)}, u32[]{:S(2)}, u32[]{:S(2)}) collective-permute-start(bf16[8,256]{1,0:T(8,128)(2,1)} %param.18), channel_id=1, source_target_pairs={{0,2},{2,0},{4,6},{6,4},{8,10},{10,8},{12,14},{14,12},{1,3},{3,1},... | collective-permute-start | bytes 12296 | tf_op jit(solution)/shard_map/ppermute | solution.py:291
  3.7 9.4 %collective-permute-start.1 = (bf16[1,64,512]{2,1,0:T(8,128)(2,1)S(1)}, bf16[1,64,512]{2,1,0:T(8,128)(2,1)S(1)}, u32[]{:S(2)}, u32[]{:S(2)}) collective-permute-start(bf16[1,64,512]{2,1,0:T(8,128)(2,1)S(1)} %dynamic-slice_bitcast_fusion), channel_id=1, source_target_pairs={{0,8},{1,9},{2,10},{3,11},{4,12},{5,13},{6,14},{7,15},{8,0},{9,1},... | collective-permute-start | bytes 196616 | tf_op jit(solution)/shard_map/ppermute | solution.py:288
  9.4 3.7 %collective-permute-start.2 = (bf16[16,256]{1,0:T(8,128)(2,1)S(1)}, bf16[16,256]{1,0:T(8,128)(2,1)S(1)}, u32[]{:S(2)}, u32[]{:S(2)}) collective-permute-start(bf16[16,256]{1,0:T(8,128)(2,1)S(1)} %maximum_select_fusion.3), channel_id=1, source_target_pairs={{0,4},{2,6},{4,0},{6,2},{8,12},{10,14},{12,8},{14,10},{1,5},{3,7},... | collective-permute-start | bytes 24584 | tf_op jit(solution)/shard_map/ppermute | solution.py:291
  11.1 8.5 %collective-permute-start.5 = (bf16[4,4096]{1,0:T(4,128)(2,1)S(1)}, bf16[4,4096]{1,0:T(4,128)(2,1)S(1)}, u32[]{:S(2)}, u32[]{:S(2)}) collective-permute-start(bf16[4,4096]{1,0:T(4,128)(2,1)S(1)} %copy-done.1), channel_id=1, source_target_pairs={{0,1},{1,0},{2,3},{3,2},{4,5},{5,4},{6,7},{7,6},{8,9},{9,8},{10,11... | collective-permute-start | bytes 98312 | tf_op jit(solution)/shard_map/ppermute | solution.py:312
  13.1 4.8 %collective-permute-start.4 = (bf16[32,256]{1,0:T(8,128)(2,1)S(1)}, bf16[32,256]{1,0:T(8,128)(2,1)S(1)}, u32[]{:S(2)}, u32[]{:S(2)}) collective-permute-start(bf16[32,256]{1,0:T(8,128)(2,1)S(1)} %maximum_select_fusion.2.rest_1_), channel_id=1, source_target_pairs={{0,8},{2,10},{4,12},{6,14},{8,0},{10,2},{12,4},{14,6},{1,9},{3,11}... | collective-permute-start | bytes 49160 | tf_op jit(solution)/shard_map/ppermute | solution.py:291
  13.6 5.5 %collective-permute-start.3 = (bf16[2,64,512]{2,1,0:T(8,128)(2,1)S(1)}, bf16[2,64,512]{2,1,0:T(8,128)(2,1)S(1)}, u32[]{:S(2)}, u32[]{:S(2)}) collective-permute-start(bf16[2,64,512]{2,1,0:T(8,128)(2,1)S(1)} %pad_maximum_fusion.1.rest_0_), channel_id=1, source_target_pairs={{0,4},{1,3},{2,6},{3,1},{4,0},{5,7},{6,2},{7,5},{8,12},{9,11},{10,... | collective-permute-start | bytes 393224 | tf_op jit(solution)/shard_map/ppermute | solution.py:288
  19.1 6.7 %collective-permute-start.7 = (bf16[4,64,512]{2,1,0:T(8,128)(2,1)S(1)}, bf16[4,64,512]{2,1,0:T(8,128)(2,1)S(1)}, u32[]{:S(2)}, u32[]{:S(2)}) collective-permute-start(bf16[4,64,512]{2,1,0:T(8,128)(2,1)S(1)} %pad_maximum_fusion.rest_1_), channel_id=1, source_target_pairs={{0,2},{1,5},{2,0},{3,7},{4,6},{5,1},{6,4},{7,3},{8,10},{9,13},{10,... | collective-permute-start | bytes 786440 | tf_op jit(solution)/shard_map/ppermute | solution.py:288
  19.6 1.5 %collective-permute-start.6 = (bf16[4,64,512]{2,1,0:T(8,128)(2,1)S(1)}, bf16[4,64,512]{2,1,0:T(8,128)(2,1)S(1)}, u32[]{:S(2)}, u32[]{:S(2)}) collective-permute-start(bf16[4,64,512]{2,1,0:T(8,128)(2,1)S(1)} %pad_maximum_fusion.rest_1_), channel_id=1, source_target_pairs={{0,1},{1,0},{2,3},{3,2},{4,5},{5,4},{6,7},{7,6},{8,9},{9,8},{10,11... | collective-permute-start | bytes 786440 | tf_op jit(solution)/shard_map/ppermute | solution.py:322
  25.8 2.4 %collective-permute-start.8 = (bf16[4,64,512]{2,1,0:T(8,128)(2,1)S(1)}, bf16[4,64,512]{2,1,0:T(8,128)(2,1)S(1)}, u32[]{:S(2)}, u32[]{:S(2)}) collective-permute-start(bf16[4,64,512]{2,1,0:T(8,128)(2,1)S(1)} %collective-permute-done.7.rest_1_), channel_id=1, source_target_pairs={{0,1},{1,0},{2,3},{3,2},{4,5},{5,4},{6,7},{7,6},{8,9},{9,8},{10,11... | collective-permute-start | bytes 786440 | tf_op jit(solution)/shard_map/ppermute | solution.py:346

commit v7 on v6

--- a/solution.py
+++ b/solution.py
@@ -19,7 +19,10 @@
     return [pltpu.with_memory_space_constraint(x, pltpu.HBM) for x in arrays]
 
 
-def attend_kernel(rows, lengths_hbm, q_hbm, own_k_hbm, k_hbm, v_hbm, *rest):
+def attend_kernel(rows, fetch, lengths_hbm, q_hbm, own_k_hbm, k_hbm, v_hbm, *rest):
+    rest = list(rest)
+    if fetch:
+        served_hbm, served_ref, served_sem = rest.pop(0), rest.pop(-10), rest.pop(-1)
     context_ref, own_weight_ref, lengths, q_ref, own_k_ref, k_buf, v_buf, small_sem, k_sem, v_sem = (
         rest[-10:]
     )
@@ -41,6 +44,9 @@
     for i, row in enumerate(rows):
         for copy in copies(i, row):
             copy.start()
+    if fetch:
+        get_served = pltpu.make_async_copy(served_hbm, served_ref, served_sem)
+        get_served.start()
     for copy in smalls:
         copy.wait()
     queries = q_ref[...].astype(jnp.float32)
@@ -90,18 +96,24 @@
             )
         context_ref[i] = context
         own_weight_ref[i] = jnp.broadcast_to(weight_own, (heads, HEAD_SIZE))
-
-
-def attend(rows, lengths, queries, own_key, stored_keys, stored_values, *after):
+    if fetch:
+        get_served.wait()
+
+
+def attend(rows, given, served=None, after=()):
+    lengths, queries, own_key, stored_keys, stored_values = given
+    fetch = served is not None
     cache_len, width = stored_keys.shape[1:]
     heads = queries.shape[1] // HEAD_SIZE
     count = len(rows)
-    out = jax.ShapeDtypeStruct((count, heads, HEAD_SIZE), jnp.float32)
+    out_shape = [jax.ShapeDtypeStruct((count, heads, HEAD_SIZE), jnp.float32)] * 2
+    if fetch:
+        out_shape += [jax.ShapeDtypeStruct(served.shape, served.dtype)]
     return pl.pallas_call(
-        functools.partial(attend_kernel, rows),
-        out_shape=(out, out),
-        in_specs=[HBM] * 5 + [pl.BlockSpec(memory_space=pl.ANY)] * len(after),
-        out_specs=(VMEM, VMEM),
+        functools.partial(attend_kernel, rows, fetch),
+        out_shape=out_shape,
+        in_specs=[HBM] * (5 + fetch) + [pl.BlockSpec(memory_space=pl.ANY)] * len(after),
+        out_specs=[VMEM] * len(out_shape),
         scratch_shapes=[
             pltpu.SMEM(lengths.shape, jnp.int32),
             pltpu.VMEM(queries.shape, jnp.bfloat16),
@@ -111,21 +123,21 @@
             pltpu.SemaphoreType.DMA((3,)),
             pltpu.SemaphoreType.DMA((count,)),
             pltpu.SemaphoreType.DMA((count,)),
-        ],
-        compiler_params=pltpu.CompilerParams(vmem_limit_bytes=16 * 2**20),
+        ]
+        + [pltpu.SemaphoreType.DMA] * fetch,
+        compiler_params=pltpu.CompilerParams(vmem_limit_bytes=12 * 2**20),
         cost_estimate=pl.CostEstimate(
             flops=4 * count * heads * cache_len * width,
             bytes_accessed=4 * count * cache_len * width,
             transcendentals=count * heads * cache_len,
         ),
         name="attend_cache",
-    )(lengths, queries, own_key, stored_keys, stored_values, *after)
-
-
-def fold_kernel(sizes, entry, ahead_from, stage, start_hbm, up_ref, features_ref, *rest):
+    )(*given, *([served] if fetch else []), *after)
+
+
+def fold_kernel(sizes, entry, stage, start_hbm, up_ref, features_ref, served_ref, *rest):
     rest = list(rest)
     first, last = stage == 0, stage == 2
-    served = rest.pop(0)
     arrays = [rest.pop(0) for _ in sizes]
     if not first:
         rest.pop(0)
@@ -134,20 +146,15 @@
         context_ref, own_weight_ref = rest[:2]
         merged, fresh_hbm, attended_hbm = rest[2:5]
         start, start_sem, m_buf, out_sem, fresh_ref, attended_ref, small_sem = rest[5:]
-    elif first:
-        merged, total_ref, ahead_ref, start, start_sem, m_buf, out_sem, w_buf, in_sem = rest
-        total = jnp.zeros(total_ref.shape, jnp.float32)
     else:
         merged, total_ref, start, start_sem, m_buf, out_sem = rest
+    if first:
+        total = jnp.zeros(total_ref.shape, jnp.float32)
     width = arrays[0].shape[2]
     count = sum(sizes)
 
     def rows_of(i):
         return pl.ds(pl.multiple_of(start[entry + i], width), width)
-
-    def fetch(i):
-        into = w_buf.at[i] if i < count else ahead_ref.at[i - count]
-        return pltpu.make_async_copy(served.at[rows_of(i)], into, in_sem.at[i])
 
     def store(i):
         return pltpu.make_async_copy(m_buf.at[i], merged.at[rows_of(i)], out_sem.at[i])
@@ -155,24 +162,15 @@
     get_start = pltpu.make_async_copy(start_hbm, start, start_sem)
     get_start.start()
     up = (up_ref[...].astype(jnp.float32) * ADAPTER_SCALE).astype(jnp.bfloat16)
-    if first:
-        get_start.wait()
-        for i in range(start.shape[0]):
-            fetch(i).start()
     slabs = [array.at[k] for array, size in zip(arrays, sizes) for k in range(size)]
     for i, slab in enumerate(slabs):
         update = lax.dot_general(
             slab[...], up, (((0,), (0,)), ((), ())), preferred_element_type=jnp.float32
         )
-        if first:
-            fetch(i).wait()
-            rows = w_buf[i]
-        else:
-            rows = served[ahead_from + i]
-        fold = (rows.astype(jnp.float32) + update).astype(jnp.bfloat16)
+        if i == 0:
+            get_start.wait()
+        fold = (served_ref[rows_of(i), :].astype(jnp.float32) + update).astype(jnp.bfloat16)
         m_buf[i] = fold
-        if i == 0 and not first:
-            get_start.wait()
         store(i).start()
         total = total + jnp.dot(
             features_ref[:, rows_of(i)], fold, preferred_element_type=jnp.float32
@@ -197,22 +195,18 @@
         put_attended.wait()
     else:
         total_ref[...] = total
-    if first:
-        for i in range(count, start.shape[0]):
-            fetch(i).wait()
     for i in range(count):
         store(i).wait()
 
 
-def fold(stage, entry, start, up, features, served, arrays, ahead_from=0, state=(), finish=()):
+def fold(stage, entry, start, up, features, served, arrays, state=(), finish=()):
     first, last = stage == 0, stage == 2
     sizes = [array.shape[0] for array in arrays]
     count = sum(sizes)
-    ahead = start.shape[0] - count
     rank, cols = up.shape
     width = arrays[0].shape[2]
     rows, depth = features.shape
-    in_specs = [HBM, VMEM, VMEM, HBM if first else VMEM] + [VMEM] * len(arrays)
+    in_specs = [HBM, VMEM, VMEM, VMEM] + [VMEM] * len(arrays)
     operands = [start, up, features, served, *arrays]
     aliases = {}
     out_shape = [jax.ShapeDtypeStruct((depth, cols), jnp.bfloat16)]
@@ -236,21 +230,14 @@
     else:
         out_shape += [jax.ShapeDtypeStruct((rows, cols), jnp.float32)]
         out_specs += [VMEM]
-    if first:
-        out_shape += [jax.ShapeDtypeStruct((ahead, width, cols), jnp.bfloat16)]
-        out_specs += [VMEM]
-        scratch += [
-            pltpu.VMEM((count, width, cols), jnp.bfloat16),
-            pltpu.SemaphoreType.DMA((count + ahead,)),
-        ]
     return pl.pallas_call(
-        functools.partial(fold_kernel, sizes, entry, ahead_from, stage),
+        functools.partial(fold_kernel, sizes, entry, stage),
         out_shape=out_shape,
         in_specs=in_specs,
         out_specs=out_specs,
         input_output_aliases=aliases,
         scratch_shapes=scratch,
-        compiler_params=pltpu.CompilerParams(vmem_limit_bytes=24 * 2**20),
+        compiler_params=pltpu.CompilerParams(vmem_limit_bytes=12 * 2**20),
         cost_estimate=pl.CostEstimate(
             flops=2 * count * width * cols * (rank + rows),
             bytes_accessed=4 * count * width * cols,
@@ -304,17 +291,20 @@
         came = exchange(slabs, step)
         if step == 0:
             grown_up = grown(up, 1)
-            parts.append(attend(range(split), *given))
+            parts.append(attend(range(split), given))
             up, parts[0], hid_other, owner_rank = lax.optimization_barrier(
                 (grown_up, parts[0], hid_other, owner_rank)
             )
             grown_up = grown(up, 2)
             hid_other = lax.ppermute(hid_other, "tensor", swap)
-            came, up = lax.optimization_barrier((came, grown_up))
         elif step == 1:
-            grown_up = grown(up, 4)
-            parts.append(attend(range(split, rows), *given, slabs, up))
-            came, up, parts[1] = lax.optimization_barrier((came, grown_up, parts[1]))
+            *part, served = attend(
+                range(split, rows), given, *in_hbm(served_value_weight), [slabs]
+            )
+            up, part = lax.optimization_barrier((grown_up, part))
+            up = grown(up, 4)
+            came, part = lax.optimization_barrier((came, part))
+            parts.append(part)
         slabs = jnp.concatenate([slabs, came], axis=0)
     for step in range(3, len(bits)):
         up = grown(up, 1 << step)
@@ -339,20 +329,20 @@
     place = jnp.sum(jnp.where(owner_rank[None, :] == source[:, None], slab[None, :], 0), axis=1)
     start = (place * full + half * width).astype(jnp.int32)
 
-    merged, total, ahead = fold(
-        0, 0, start, up, features, *in_hbm(served_value_weight), [slabs, crossed]
+    merged, total = fold(
+        0, 0, start, up, features, served, [slabs, crossed]
     )
     last, total = lax.optimization_barrier((last, total))
     last_crossed = lax.ppermute(last, "tensor", swap)
     merged, total = fold(
-        1, 2 * count, start, up, features, ahead, [last], state=[merged, total]
+        1, 2 * count, start, up, features, served, [last], state=[merged, total]
     )
     context, own_weight = (
         jnp.concatenate(pair, axis=0).reshape(queries.shape) for pair in zip(*parts)
     )
     merged, fresh_token_value, attended = fold(
-        2, 3 * count, start, up, features, ahead, [last_crossed], ahead_from=count,
-        state=[merged, total], finish=[context, own_weight],
+        2, 3 * count, start, up, features, served, [last_crossed], state=[merged, total],
+        finish=[context, own_weight],
     )
     return (merged, fresh_token_value, attended)
 

time: 30.6 us -> 28.2 us (0.922)
  Pallas kernels: 14.5 us -> 12.6 us
    ppermute x3, waiting for transfers between devices: 1.99 us -> 4.22 us  [grown(): came = lax.ppermute(up, 'replica', [(i, i ^ bit) for i in range(n)])]
    pallas_call x5, Pallas kernels: 14.5 us -> 12.6 us  [the longest x3 6.93 us: fold(): pl.pallas_call(functools.partial(fold_kernel, sizes, entry, stage), out_s...]
    ppermute x1, waiting for transfers between devices: 1.48 us -> 0.01 us  [body(): crossed = lax.ppermute(slabs, 'tensor', swap)]
    ppermute x3, waiting for transfers between devices: 1.05 us -> 0.01 us  [exchange(): return lax.ppermute(x, ('replica', 'tensor'), pairs)]
    ppermute x3, starting transfers between devices: 4.83 us -> 4.23 us  [exchange(): return lax.ppermute(x, ('replica', 'tensor'), pairs)]
    ppermute x3, starting transfers between devices: 5.07 us -> 5.47 us  [grown(): came = lax.ppermute(up, 'replica', [(i, i ^ bit) for i in range(n)])]
  transfers between devices with their start and end apart: 9 -> 9, of which waited for: 3 -> 2; matrix products, arithmetic and copies ran while one was open for 2% -> 2% of each run, Pallas kernels for 40% -> 37%
where the time goes in v7:
time: 28.2 us; the launch traced here: 28 us
  Pallas kernels  12.6 us (45%)
  starting transfers between devices  9.85 us (35%)
  waiting for transfers between devices  4.24 us (15%)
  between operations  0.81 us (3%)
  other arithmetic  0.29 us (1%)
    pallas_call x3, Pallas kernels, fold(): pl.pallas_call(functools.partial(fold_kernel, sizes, entry, stage), out_s...  6.93 us
    pallas_call x2, Pallas kernels, attend(): pl.pallas_call(functools.partial(attend_kernel, rows, fetch), out_shape=o...  5.7 us
    ppermute x3, starting transfers between devices, grown(): came = lax.ppermute(up, 'replica', [(i, i ^ bit) for i in range(n)])  5.47 us
    ppermute x3, starting transfers between devices, exchange(): return lax.ppermute(x, ('replica', 'tensor'), pairs)  4.23 us
    ppermute x3, waiting for transfers between devices, grown(): came = lax.ppermute(up, 'replica', [(i, i ^ bit) for i in range(n)])  4.22 us
  transfers between devices with their start and end apart: 9, of which 2 were waited for; matrix products, arithmetic and copies ran while one was open for 2% of the time, Pallas kernels for 37%

profile of v7, /device:TPU:0, one launch (start us, length us, event | category | flops | bytes accessed | tf_op | source)
XLA Modules:
  0.0 28.0 jit_solution(4431286975764667825)
XLA Ops:
  0.6 0.0 copy-start
  0.7 3.0 %collective-permute-start = (bf16[8,256]{1,0:T(8,128)(2,1)}, bf16[8,256]{1,0:T(8,128)(2,1)S(1)}, u32[]{:S(2)}, u32[]{:S(2)}) collective-permute-start(bf16[8,256]{1,0:T(8,128)(2,1)} %param.18), channel_id=1, source_target_pairs={{0,2},{2,0},{4,6},{6,4},{8,10},{10,8},{12,14},{14,12},{1,3},{3,1},... | collective-permute-start | bytes 12296 | tf_op jit(solution)/shard_map/ppermute | solution.py:278
  3.7 2.7 %collective-permute-start.2 = (bf16[1,64,512]{2,1,0:T(8,128)(2,1)S(1)}, bf16[1,64,512]{2,1,0:T(8,128)(2,1)S(1)}, u32[]{:S(2)}, u32[]{:S(2)}) collective-permute-start(bf16[1,64,512]{2,1,0:T(8,128)(2,1)S(1)} %dynamic-slice_bitcast_fusion), channel_id=1, source_target_pairs={{0,8},{1,9},{2,10},{3,11},{4,12},{5,13},{6,14},{7,15},{8,0},{9,1},... | collective-permute-start | bytes 196616 | tf_op jit(solution)/shard_map/ppermute | solution.py:275
  6.4 0.1 fusion.4
  6.5 0.1 fusion.3
  6.5 0.1 pad_add_fusion
  6.6 2.8 %attend_cache.2 = (f32[2,16,128]{2,1,0:T(8,128)S(1)}, f32[2,16,128]{2,1,0:T(8,128)S(1)}) custom-call(s32[4]{0:T(128)} %lengths_hbm.3, bf16[4,2048]{1,0:T(4,128)(2,1)} %q_hbm.3, bf16[4,256]{1,0:T(4,128)(2,1)} %own_k_hbm.3, bf16[4,1024,256]{2,1,0:T(8,128)(2,1)} %k_hbm.3, bf16[4,1024,256]{2,1,0:T(8,128)(2,1)} %v_hbm.3), custom_call_target="tpu_custom_call" | custom-call | flops 33554432 | bytes 2097152 | tf_op jit(solution)/shard_map/attend_cache/pallas_call | solution.py:112
  9.4 0.0 collective-permute-done
  9.4 1.6 %collective-permute-start.1 = (bf16[16,256]{1,0:T(8,128)(2,1)S(1)}, bf16[16,256]{1,0:T(8,128)(2,1)S(1)}, u32[]{:S(2)}, u32[]{:S(2)}) collective-permute-start(bf16[16,256]{1,0:T(8,128)(2,1)S(1)} %maximum_select_fusion.3), channel_id=1, source_target_pairs={{0,4},{2,6},{4,0},{6,2},{8,12},{10,14},{12,8},{14,10},{1,5},{3,7},... | collective-permute-start | bytes 24584 | tf_op jit(solution)/shard_map/ppermute | solution.py:278
  11.1 0.0 collective-permute-start.4
  11.1 0.1 select_reduce_fusion
  11.2 0.5 %collective-permute-start.5 = (bf16[2,64,512]{2,1,0:T(8,128)(2,1)S(1)}, bf16[2,64,512]{2,1,0:T(8,128)(2,1)S(1)}, u32[]{:S(2)}, u32[]{:S(2)}) collective-permute-start(bf16[2,64,512]{2,1,0:T(8,128)(2,1)S(1)} %pad_maximum_fusion.1.rest_1_), channel_id=1, source_target_pairs={{0,4},{1,3},{2,6},{3,1},{4,0},{5,7},{6,2},{7,5},{8,12},{9,11},{10,... | collective-permute-start | bytes 393224 | tf_op jit(solution)/shard_map/ppermute | solution.py:275
  11.7 1.4 %collective-permute-done.1 = bf16[16,256]{1,0:T(8,128)(2,1)S(1)} collective-permute-done((bf16[16,256]{1,0:T(8,128)(2,1)S(1)}, bf16[16,256]{1,0:T(8,128)(2,1)S(1)}, u32[]{:S(2)}, u32[]{:S(2)}) %collective-permute-start.1) | collective-permute-done | bytes 8224 | tf_op jit(solution)/shard_map/ppermute | solution.py:278
  13.1 2.9 %attend_cache.3 = (f32[2,16,128]{2,1,0:T(8,128)S(1)}, f32[2,16,128]{2,1,0:T(8,128)S(1)}, bf16[8192,256]{1,0:T(8,128)(2,1)S(1)}) custom-call(s32[4]{0:T(128)} %lengths_hbm.3, bf16[4,2048]{1,0:T(4,128)(2,1)} %q_hbm.3, bf16[4,256]{1,0:T(4,128)(2,1)} %own_k_hbm.3, bf16[4,1024,256]{2,1,0:T(8,128)(2,1)} %k_hbm.3, bf16[4,1024,256]{2,1,0:T(8,128)(2,1)} %v_hbm.3, ...), custom_call_target="tpu_custom_call" | custom-call | flops 33554432 | bytes 2097152 | tf_op jit(solution)/shard_map/attend_cache/pallas_call | solution.py:112
  16.1 0.8 %collective-permute-start.3 = (bf16[32,256]{1,0:T(8,128)(2,1)S(1)}, bf16[32,256]{1,0:T(8,128)(2,1)S(1)}, u32[]{:S(2)}, u32[]{:S(2)}) collective-permute-start(bf16[32,256]{1,0:T(8,128)(2,1)S(1)} %maximum_select_fusion.2), channel_id=1, source_target_pairs={{0,8},{2,10},{4,12},{6,14},{8,0},{10,2},{12,4},{14,6},{1,9},{3,11}... | collective-permute-start | bytes 49160 | tf_op jit(solution)/shard_map/ppermute | solution.py:278
  16.9 0.0 collective-permute-done.5
  16.9 0.1 collective-permute-start.7
  17.0 1.1 %collective-permute-start.6 = (bf16[4,64,512]{2,1,0:T(8,128)(2,1)S(1)}, bf16[4,64,512]{2,1,0:T(8,128)(2,1)S(1)}, u32[]{:S(2)}, u32[]{:S(2)}) collective-permute-start(bf16[4,64,512]{2,1,0:T(8,128)(2,1)S(1)} %pad_maximum_fusion.rest_0_), channel_id=1, source_target_pairs={{0,2},{1,5},{2,0},{3,7},{4,6},{5,1},{6,4},{7,3},{8,10},{9,13},{10,... | collective-permute-start | bytes 786440 | tf_op jit(solution)/shard_map/ppermute | solution.py:275
  18.1 0.0 collective-permute-done.4
  18.1 2.8 %collective-permute-done.3 = bf16[32,256]{1,0:T(8,128)(2,1)S(1)} collective-permute-done((bf16[32,256]{1,0:T(8,128)(2,1)S(1)}, bf16[32,256]{1,0:T(8,128)(2,1)S(1)}, u32[]{:S(2)}, u32[]{:S(2)}) %collective-permute-start.3) | collective-permute-done | bytes 16416 | tf_op jit(solution)/shard_map/ppermute | solution.py:278
  20.9 2.6 %fold_blocks.3 = (bf16[8192,256]{1,0:T(8,128)(2,1)}, f32[4,256]{1,0:T(4,128)S(1)}) custom-call(s32[16]{0:T(128)S(1)} %fusion.1.start_hbm, bf16[64,256]{1,0:T(8,128)(2,1)S(1)} %maximum_select_fusion.1.up_ref, bf16[4,8192]{1,0:T(4,128)(2,1)S(1)} %maximum_select_fusion.features_ref, bf16[8192,256]{1,0:T(8,128)(2,1)S(1)} %get-tuple-element.33.served_ref, ...), custom_call_target="tpu_custom_call" | custom-call | flops 142606336 | bytes 4194304 | tf_op jit(solution)/shard_map/fold_blocks/pallas_call | solution.py:233
  23.5 0.1 collective-permute-start.8
  23.6 2.2 %fold_blocks.4 = (bf16[8192,256]{1,0:T(8,128)(2,1)}, f32[4,256]{1,0:T(4,128)S(1)}) custom-call(s32[16]{0:T(128)S(1)} %fusion.1.start_hbm, bf16[64,256]{1,0:T(8,128)(2,1)S(1)} %maximum_select_fusion.1.up_ref, bf16[4,8192]{1,0:T(4,128)(2,1)S(1)} %maximum_select_fusion.features_ref, ...), custom_call_target="tpu_custom_call", output_to_operand_aliasing={{0}: (5, {})} | custom-call | flops 71303168 | bytes 2097152 | tf_op jit(solution)/shard_map/fold_blocks/pallas_call | solution.py:233
  25.8 2.2 %fold_blocks.5 = (bf16[8192,256]{1,0:T(8,128)(2,1)}, bf16[4,256]{1,0:T(4,128)(2,1)}, bf16[4,2048]{1,0:T(4,128)(2,1)}) custom-call(s32[16]{0:T(128)S(1)} %fusion.1.start_hbm, bf16[64,256]{1,0:T(8,128)(2,1)S(1)} %maximum_select_fusion.1.up_ref, bf16[4,8192]{1,0:T(4,128)(2,1)S(1)} %maximum_select_fusion.features_ref, ...), custom_call_target="tpu_custom_call", output_to_operand_aliasing={{0}: (5, {})} | custom-call | flops 71303168 | bytes 2097152 | tf_op jit(solution)/shard_map/fold_blocks/pallas_call | solution.py:233
  (23 shorter events, 0.2 us)
Async XLA Ops:
  0.6 3.1 %copy-start = (bf16[64,1024]{1,0:T(8,128)(2,1)S(1)}, bf16[64,1024]{1,0:T(8,128)(2,1)}, u32[]{:S(2)}) copy-start(bf16[64,1024]{1,0:T(8,128)(2,1)} %param.17) | copy-start | bytes 393220
  0.6 8.7 %copy-start.2 = (bf16[8,256]{1,0:T(8,128)(2,1)S(1)}, bf16[8,256]{1,0:T(8,128)(2,1)}, u32[]{:S(2)}) copy-start(bf16[8,256]{1,0:T(8,128)(2,1)} %param.18) | copy-start | bytes 12292
  0.7 10.4 %copy-start.1 = (bf16[4,4096]{1,0:T(4,128)(2,1)S(1)}, bf16[4,4096]{1,0:T(4,128)(2,1)}, u32[]{:S(2)}) copy-start(bf16[4,4096]{1,0:T(4,128)(2,1)} %param.10) | copy-start | bytes 98308
  0.7 10.4 %copy-start.3 = (s32[8]{0:T(128)S(1)}, s32[8]{0:T(128)}, u32[]{:S(2)}) copy-start(s32[8]{0:T(128)} %param.19) | copy-start | bytes 100
  0.7 8.7 %collective-permute-start = (bf16[8,256]{1,0:T(8,128)(2,1)}, bf16[8,256]{1,0:T(8,128)(2,1)S(1)}, u32[]{:S(2)}, u32[]{:S(2)}) collective-permute-start(bf16[8,256]{1,0:T(8,128)(2,1)} %param.18), channel_id=1, source_target_pairs={{0,2},{2,0},{4,6},{6,4},{8,10},{10,8},{12,14},{14,12},{1,3},{3,1},... | collective-permute-start | bytes 12296 | tf_op jit(solution)/shard_map/ppermute | solution.py:278
  3.7 7.4 %collective-permute-start.2 = (bf16[1,64,512]{2,1,0:T(8,128)(2,1)S(1)}, bf16[1,64,512]{2,1,0:T(8,128)(2,1)S(1)}, u32[]{:S(2)}, u32[]{:S(2)}) collective-permute-start(bf16[1,64,512]{2,1,0:T(8,128)(2,1)S(1)} %dynamic-slice_bitcast_fusion), channel_id=1, source_target_pairs={{0,8},{1,9},{2,10},{3,11},{4,12},{5,13},{6,14},{7,15},{8,0},{9,1},... | collective-permute-start | bytes 196616 | tf_op jit(solution)/shard_map/ppermute | solution.py:275
  9.4 3.7 %collective-permute-start.1 = (bf16[16,256]{1,0:T(8,128)(2,1)S(1)}, bf16[16,256]{1,0:T(8,128)(2,1)S(1)}, u32[]{:S(2)}, u32[]{:S(2)}) collective-permute-start(bf16[16,256]{1,0:T(8,128)(2,1)S(1)} %maximum_select_fusion.3), channel_id=1, source_target_pairs={{0,4},{2,6},{4,0},{6,2},{8,12},{10,14},{12,8},{14,10},{1,5},{3,7},... | collective-permute-start | bytes 24584 | tf_op jit(solution)/shard_map/ppermute | solution.py:278
  11.1 7.0 %collective-permute-start.4 = (bf16[4,4096]{1,0:T(4,128)(2,1)S(1)}, bf16[4,4096]{1,0:T(4,128)(2,1)S(1)}, u32[]{:S(2)}, u32[]{:S(2)}) collective-permute-start(bf16[4,4096]{1,0:T(4,128)(2,1)S(1)} %copy-done.1), channel_id=1, source_target_pairs={{0,1},{1,0},{2,3},{3,2},{4,5},{5,4},{6,7},{7,6},{8,9},{9,8},{10,11... | collective-permute-start | bytes 98312 | tf_op jit(solution)/shard_map/ppermute | solution.py:299
  11.2 5.7 %collective-permute-start.5 = (bf16[2,64,512]{2,1,0:T(8,128)(2,1)S(1)}, bf16[2,64,512]{2,1,0:T(8,128)(2,1)S(1)}, u32[]{:S(2)}, u32[]{:S(2)}) collective-permute-start(bf16[2,64,512]{2,1,0:T(8,128)(2,1)S(1)} %pad_maximum_fusion.1.rest_1_), channel_id=1, source_target_pairs={{0,4},{1,3},{2,6},{3,1},{4,0},{5,7},{6,2},{7,5},{8,12},{9,11},{10,... | collective-permute-start | bytes 393224 | tf_op jit(solution)/shard_map/ppermute | solution.py:275
  16.1 4.8 %collective-permute-start.3 = (bf16[32,256]{1,0:T(8,128)(2,1)S(1)}, bf16[32,256]{1,0:T(8,128)(2,1)S(1)}, u32[]{:S(2)}, u32[]{:S(2)}) collective-permute-start(bf16[32,256]{1,0:T(8,128)(2,1)S(1)} %maximum_select_fusion.2), channel_id=1, source_target_pairs={{0,8},{2,10},{4,12},{6,14},{8,0},{10,2},{12,4},{14,6},{1,9},{3,11}... | collective-permute-start | bytes 49160 | tf_op jit(solution)/shard_map/ppermute | solution.py:278
  16.9 4.0 %collective-permute-start.7 = (bf16[4,64,512]{2,1,0:T(8,128)(2,1)S(1)}, bf16[4,64,512]{2,1,0:T(8,128)(2,1)S(1)}, u32[]{:S(2)}, u32[]{:S(2)}) collective-permute-start(bf16[4,64,512]{2,1,0:T(8,128)(2,1)S(1)} %pad_maximum_fusion.rest_0_), channel_id=1, source_target_pairs={{0,1},{1,0},{2,3},{3,2},{4,5},{5,4},{6,7},{7,6},{8,9},{9,8},{10,11... | collective-permute-start | bytes 786440 | tf_op jit(solution)/shard_map/ppermute | solution.py:312
  17.0 6.5 %collective-permute-start.6 = (bf16[4,64,512]{2,1,0:T(8,128)(2,1)S(1)}, bf16[4,64,512]{2,1,0:T(8,128)(2,1)S(1)}, u32[]{:S(2)}, u32[]{:S(2)}) collective-permute-start(bf16[4,64,512]{2,1,0:T(8,128)(2,1)S(1)} %pad_maximum_fusion.rest_0_), channel_id=1, source_target_pairs={{0,2},{1,5},{2,0},{3,7},{4,6},{5,1},{6,4},{7,3},{8,10},{9,13},{10,... | collective-permute-start | bytes 786440 | tf_op jit(solution)/shard_map/ppermute | solution.py:275
  23.5 2.3 %collective-permute-start.8 = (bf16[4,64,512]{2,1,0:T(8,128)(2,1)S(1)}, bf16[4,64,512]{2,1,0:T(8,128)(2,1)S(1)}, u32[]{:S(2)}, u32[]{:S(2)}) collective-permute-start(bf16[4,64,512]{2,1,0:T(8,128)(2,1)S(1)} %collective-permute-done.6.rest_0_), channel_id=1, source_target_pairs={{0,1},{1,0},{2,3},{3,2},{4,5},{5,4},{6,7},{7,6},{8,9},{9,8},{10,11... | collective-permute-start | bytes 786440 | tf_op jit(solution)/shard_map/ppermute | solution.py:336

commit v8 on v7

--- a/solution.py
+++ b/solution.py
@@ -19,10 +19,7 @@
     return [pltpu.with_memory_space_constraint(x, pltpu.HBM) for x in arrays]
 
 
-def attend_kernel(rows, fetch, lengths_hbm, q_hbm, own_k_hbm, k_hbm, v_hbm, *rest):
-    rest = list(rest)
-    if fetch:
-        served_hbm, served_ref, served_sem = rest.pop(0), rest.pop(-10), rest.pop(-1)
+def attend_kernel(lengths_hbm, q_hbm, own_k_hbm, k_hbm, v_hbm, *rest):
     context_ref, own_weight_ref, lengths, q_ref, own_k_ref, k_buf, v_buf, small_sem, k_sem, v_sem = (
         rest[-10:]
     )
@@ -35,18 +32,15 @@
     for copy in smalls:
         copy.start()
 
-    def copies(i, row):
+    def copies(row):
         return (
-            pltpu.make_async_copy(k_hbm.at[row], k_buf.at[i], k_sem.at[i]),
-            pltpu.make_async_copy(v_hbm.at[row], v_buf.at[i], v_sem.at[i]),
-        )
-
-    for i, row in enumerate(rows):
-        for copy in copies(i, row):
+            pltpu.make_async_copy(k_hbm.at[row], k_buf.at[row], k_sem.at[row]),
+            pltpu.make_async_copy(v_hbm.at[row], v_buf.at[row], v_sem.at[row]),
+        )
+
+    for row in range(k_buf.shape[0]):
+        for copy in copies(row):
             copy.start()
-    if fetch:
-        get_served = pltpu.make_async_copy(served_hbm, served_ref, served_sem)
-        get_served.start()
     for copy in smalls:
         copy.wait()
     queries = q_ref[...].astype(jnp.float32)
@@ -58,7 +52,7 @@
     scaling = 1.0 / HEAD_SIZE**0.5
     head_of = lax.broadcasted_iota(jnp.int32, (heads, HEAD_SIZE), 0) // group
     position = lax.broadcasted_iota(jnp.int32, (heads, cache_len), 1)
-    for i, row in enumerate(rows):
+    for row in range(k_buf.shape[0]):
         q = jnp.concatenate(
             [
                 queries[row : row + 1, h * HEAD_SIZE : (h + 1) * HEAD_SIZE]
@@ -70,11 +64,11 @@
             [jnp.where(head_of == h, q, 0.0) for h in range(local_heads)], axis=1
         )
         own = jnp.sum(spread * own_keys[row : row + 1], axis=1, keepdims=True) * scaling
-        get_keys, get_values = copies(i, row)
+        get_keys, get_values = copies(row)
         get_keys.wait()
         scores = (
             lax.dot_general(
-                spread.astype(jnp.bfloat16), k_buf[i], (((1,), (1,)), ((), ())),
+                spread.astype(jnp.bfloat16), k_buf[row], (((1,), (1,)), ((), ())),
                 preferred_element_type=jnp.float32,
             )
             * scaling
@@ -88,32 +82,25 @@
         weights = (cached_exp / normaliser).astype(jnp.bfloat16)
         weight_own = (own_exp / normaliser).astype(jnp.bfloat16).astype(jnp.float32)
         get_values.wait()
-        wide = jnp.dot(weights, v_buf[i], preferred_element_type=jnp.float32)
+        wide = jnp.dot(weights, v_buf[row], preferred_element_type=jnp.float32)
         context = wide[:, :HEAD_SIZE]
         for h in range(1, local_heads):
             context = jnp.where(
                 head_of == h, wide[:, h * HEAD_SIZE : (h + 1) * HEAD_SIZE], context
             )
-        context_ref[i] = context
-        own_weight_ref[i] = jnp.broadcast_to(weight_own, (heads, HEAD_SIZE))
-    if fetch:
-        get_served.wait()
-
-
-def attend(rows, given, served=None, after=()):
-    lengths, queries, own_key, stored_keys, stored_values = given
-    fetch = served is not None
-    cache_len, width = stored_keys.shape[1:]
+        context_ref[row] = context
+        own_weight_ref[row] = jnp.broadcast_to(weight_own, (heads, HEAD_SIZE))
+
+
+def attend(lengths, queries, own_key, stored_keys, stored_values, after):
+    count, cache_len, width = stored_keys.shape
     heads = queries.shape[1] // HEAD_SIZE
-    count = len(rows)
-    out_shape = [jax.ShapeDtypeStruct((count, heads, HEAD_SIZE), jnp.float32)] * 2
-    if fetch:
-        out_shape += [jax.ShapeDtypeStruct(served.shape, served.dtype)]
+    out = jax.ShapeDtypeStruct((count, heads, HEAD_SIZE), jnp.float32)
     return pl.pallas_call(
-        functools.partial(attend_kernel, rows, fetch),
-        out_shape=out_shape,
-        in_specs=[HBM] * (5 + fetch) + [pl.BlockSpec(memory_space=pl.ANY)] * len(after),
-        out_specs=[VMEM] * len(out_shape),
+        attend_kernel,
+        out_shape=(out, out),
+        in_specs=[HBM] * 5 + [pl.BlockSpec(memory_space=pl.ANY)],
+        out_specs=(VMEM, VMEM),
         scratch_shapes=[
             pltpu.SMEM(lengths.shape, jnp.int32),
             pltpu.VMEM(queries.shape, jnp.bfloat16),
@@ -123,8 +110,7 @@
             pltpu.SemaphoreType.DMA((3,)),
             pltpu.SemaphoreType.DMA((count,)),
             pltpu.SemaphoreType.DMA((count,)),
-        ]
-        + [pltpu.SemaphoreType.DMA] * fetch,
+        ],
         compiler_params=pltpu.CompilerParams(vmem_limit_bytes=12 * 2**20),
         cost_estimate=pl.CostEstimate(
             flops=4 * count * heads * cache_len * width,
@@ -132,7 +118,36 @@
             transcendentals=count * heads * cache_len,
         ),
         name="attend_cache",
-    )(*given, *([served] if fetch else []), *after)
+    )(lengths, queries, own_key, stored_keys, stored_values, after)
+
+
+def fetch_kernel(pieces, source, after, into, sem):
+    del after
+    size = source.shape[0] // pieces
+    copies = [
+        pltpu.make_async_copy(
+            source.at[pl.ds(i * size, size)], into.at[pl.ds(i * size, size)], sem.at[i]
+        )
+        for i in range(pieces)
+    ]
+    for copy in copies:
+        copy.start()
+    for copy in copies:
+        copy.wait()
+
+
+def fetch(served, after):
+    pieces = 8
+    return pl.pallas_call(
+        functools.partial(fetch_kernel, pieces),
+        out_shape=jax.ShapeDtypeStruct(served.shape, served.dtype),
+        in_specs=[HBM, pl.BlockSpec(memory_space=pl.ANY)],
+        out_specs=VMEM,
+        scratch_shapes=[pltpu.SemaphoreType.DMA((pieces,))],
+        compiler_params=pltpu.CompilerParams(vmem_limit_bytes=12 * 2**20),
+        cost_estimate=pl.CostEstimate(flops=1, bytes_accessed=1, transcendentals=0),
+        name="fetch_served",
+    )(served, after)
 
 
 def fold_kernel(sizes, entry, stage, start_hbm, up_ref, features_ref, served_ref, *rest):
@@ -265,7 +280,6 @@
     swap = [(0, 1), (1, 0)]
     full = adapter_in.shape[1]
     width = full // 2
-    rows = queries.shape[0]
 
     bits = [n >> i for i in range(1, n.bit_length())]
     ways = [bits, bits[:-2] + bits[:-3:-1]]
@@ -282,37 +296,39 @@
     given = (
         *in_hbm(lengths, queries, fresh_token_key, stored_keys, stored_values),
     )
+    hid_other = lax.ppermute(hidden_in, "tensor", swap)
+    near = [adapter_out] + [
+        lax.ppermute(adapter_out, "replica", [(i, i ^ b) for i in range(n)]) for b in (1, 2, 3)
+    ]
+    odd = (replica & 1) == 1
+    pairs = [
+        jnp.where(odd, jnp.concatenate([b, a], axis=0), jnp.concatenate([a, b], axis=0))
+        for a, b in (near[:2], near[2:])
+    ]
+    up = jnp.where(
+        (replica & 2) == 0, jnp.concatenate(pairs, axis=0), jnp.concatenate(pairs[::-1], axis=0)
+    )
     slabs = lax.dynamic_slice_in_dim(adapter_in, core * width, width, axis=1)[None]
-    up, hid_other = adapter_out, hidden_in
     *early, final = range(len(bits))
-    parts = []
-    split = rows // 2
     for step in early:
         came = exchange(slabs, step)
         if step == 0:
-            grown_up = grown(up, 1)
-            parts.append(attend(range(split), given))
-            up, parts[0], hid_other, owner_rank = lax.optimization_barrier(
-                (grown_up, parts[0], hid_other, owner_rank)
-            )
-            grown_up = grown(up, 2)
-            hid_other = lax.ppermute(hid_other, "tensor", swap)
+            attention = attend(*given, slabs)
+            came, attention, owner_rank = lax.optimization_barrier((came, attention, owner_rank))
         elif step == 1:
-            *part, served = attend(
-                range(split, rows), given, *in_hbm(served_value_weight), [slabs]
-            )
-            up, part = lax.optimization_barrier((grown_up, part))
+            served = fetch(*in_hbm(served_value_weight), slabs)
+            up, served = lax.optimization_barrier((up, served))
             up = grown(up, 4)
-            came, part = lax.optimization_barrier((came, part))
-            parts.append(part)
+            came, served = lax.optimization_barrier((came, served))
         slabs = jnp.concatenate([slabs, came], axis=0)
     for step in range(3, len(bits)):
         up = grown(up, 1 << step)
     last = exchange(slabs, final)
-    crossed = lax.ppermute(slabs, "tensor", swap)
 
     features = jnp.concatenate([hidden_in, hid_other], axis=1)
     features = jnp.where(core == 0, features, jnp.concatenate([hid_other, hidden_in], axis=1))
+    crossed, features = lax.optimization_barrier((slabs, features))
+    crossed = lax.ppermute(crossed, "tensor", swap)
 
     slab = jnp.arange(n, dtype=jnp.int32)
     sources = []
@@ -337,9 +353,7 @@
     merged, total = fold(
         1, 2 * count, start, up, features, served, [last], state=[merged, total]
     )
-    context, own_weight = (
-        jnp.concatenate(pair, axis=0).reshape(queries.shape) for pair in zip(*parts)
-    )
+    context, own_weight = (x.reshape(queries.shape) for x in attention)
     merged, fresh_token_value, attended = fold(
         2, 3 * count, start, up, features, served, [last_crossed], state=[merged, total],
         finish=[context, own_weight],

time: 28.2 us -> 30.2 us (1.071)
  starting transfers between devices: 9.85 us -> 12.4 us
  waiting for transfers between devices: 4.24 us -> 2.27 us
  Pallas kernels: 12.6 us -> 14 us
    ppermute x2 -> x5, starting transfers between devices: 0.07 us -> 4.62 us  [the longest x3 4.61 us: body(): lax.ppermute(adapter_out, 'replica', [(i, i ^ b) for i in range(n)])]
    ppermute x3 -> x1, starting transfers between devices: 5.47 us -> 1.54 us  [grown(): came = lax.ppermute(up, 'replica', [(i, i ^ bit) for i in range(n)])]
    ppermute x3 -> x1, waiting for transfers between devices: 4.22 us -> 1.78 us  [grown(): came = lax.ppermute(up, 'replica', [(i, i ^ bit) for i in range(n)])]
    ppermute x3, starting transfers between devices: 4.23 us -> 6.26 us  [exchange(): return lax.ppermute(x, ('replica', 'tensor'), pairs)]
    pallas_call x2, Pallas kernels: 5.7 us -> 7.08 us  [the longest x1 4.86 us: attend(): pl.pallas_call(attend_kernel, out_shape=(out, out), in_specs=[HBM] * 5 +...]
    ppermute x3, waiting for transfers between devices: 0.01 us -> 0.48 us  [exchange(): return lax.ppermute(x, ('replica', 'tensor'), pairs)]
  transfers between devices with their start and end apart: 9 -> 10, of which waited for: 2 -> 2; matrix products, arithmetic and copies ran while one was open for 2% -> 2% of each run, Pallas kernels for 37% -> 39%
where the time goes in v8:
time: 30.2 us; the launch traced here: 30 us
  Pallas kernels  14 us (46%)
  starting transfers between devices  12.4 us (41%)
  waiting for transfers between devices  2.27 us (8%)
  between operations  0.82 us (3%)
    pallas_call x3, Pallas kernels, fold(): pl.pallas_call(functools.partial(fold_kernel, sizes, entry, stage), out_s...  6.92 us
    ppermute x3, starting transfers between devices, exchange(): return lax.ppermute(x, ('replica', 'tensor'), pairs)  6.26 us
    pallas_call x1, Pallas kernels, attend(): pl.pallas_call(attend_kernel, out_shape=(out, out), in_specs=[HBM] * 5 +...  4.86 us
    ppermute x3, starting transfers between devices, body(): lax.ppermute(adapter_out, 'replica', [(i, i ^ b) for i in range(n)])  4.61 us
    pallas_call x1, Pallas kernels, fetch(): pl.pallas_call(functools.partial(fetch_kernel, pieces), out_shape=jax.Sha...  2.22 us
    ppermute x1, waiting for transfers between devices, grown(): came = lax.ppermute(up, 'replica', [(i, i ^ bit) for i in range(n)])  1.78 us
    ppermute x1, starting transfers between devices, grown(): came = lax.ppermute(up, 'replica', [(i, i ^ bit) for i in range(n)])  1.54 us
  transfers between devices with their start and end apart: 10, of which 2 were waited for; matrix products, arithmetic and copies ran while one was open for 2% of the time, Pallas kernels for 39%

profile of v8, /device:TPU:0, one launch (start us, length us, event | category | flops | bytes accessed | tf_op | source)
XLA Modules:
  0.0 30.0 jit_solution(12734790381937984334)
XLA Ops:
  0.6 0.0 copy-start
  0.7 3.0 %collective-permute-start.1 = (bf16[8,256]{1,0:T(8,128)(2,1)}, bf16[8,256]{1,0:T(8,128)(2,1)S(1)}, u32[]{:S(2)}, u32[]{:S(2)}) collective-permute-start(bf16[8,256]{1,0:T(8,128)(2,1)} %param.18), channel_id=1, source_target_pairs={{0,2},{2,0},{4,6},{6,4},{8,10},{10,8},{12,14},{14,12},{1,3},{3,1},... | collective-permute-start | bytes 12296 | tf_op jit(solution)/shard_map/ppermute | solution.py:301
  3.7 1.6 %collective-permute-start.3 = (bf16[8,256]{1,0:T(8,128)(2,1)}, bf16[8,256]{1,0:T(8,128)(2,1)S(1)}, u32[]{:S(2)}, u32[]{:S(2)}) collective-permute-start(bf16[8,256]{1,0:T(8,128)(2,1)} %param.18), channel_id=1, source_target_pairs={{0,4},{2,6},{4,0},{6,2},{8,12},{10,14},{12,8},{14,10},{1,5},{3,7},... | collective-permute-start | bytes 12296 | tf_op jit(solution)/shard_map/ppermute | solution.py:301
  5.3 3.0 %collective-permute-start = (bf16[1,64,512]{2,1,0:T(8,128)(2,1)S(1)}, bf16[1,64,512]{2,1,0:T(8,128)(2,1)S(1)}, u32[]{:S(2)}, u32[]{:S(2)}) collective-permute-start(bf16[1,64,512]{2,1,0:T(8,128)(2,1)S(1)} %dynamic-slice_bitcast_fusion.rest_0_), channel_id=1, source_target_pairs={{0,8},{1,9},{2,10},{3,11},{4,12},{5,13},{6,14},{7,15},{8,0},{9,1},... | collective-permute-start | bytes 196616 | tf_op jit(solution)/shard_map/ppermute | solution.py:289
  8.3 0.1 fusion.4
  8.4 0.1 fusion.3
  8.5 0.1 pad_add_fusion
  8.6 4.9 %attend_cache.1 = (f32[4,16,128]{2,1,0:T(8,128)S(1)}, f32[4,16,128]{2,1,0:T(8,128)S(1)}) custom-call(s32[4]{0:T(128)} %lengths_hbm.1, bf16[4,2048]{1,0:T(4,128)(2,1)} %q_hbm.1, bf16[4,256]{1,0:T(4,128)(2,1)} %own_k_hbm.1, bf16[4,1024,256]{2,1,0:T(8,128)(2,1)} %k_hbm.1, bf16[4,1024,256]{2,1,0:T(8,128)(2,1)} %v_hbm.1, ...), custom_call_target="tpu_custom_call" | custom-call | flops 67108864 | bytes 4194304 | tf_op jit(solution)/shard_map/attend_cache/pallas_call | solution.py:99
  13.4 0.0 collective-permute-done.1
  13.5 0.0 collective-permute-done.2
  13.5 0.0 collective-permute-done
  13.6 1.6 %collective-permute-start.5 = (bf16[2,64,512]{2,1,0:T(8,128)(2,1)S(1)}, bf16[2,64,512]{2,1,0:T(8,128)(2,1)S(1)}, u32[]{:S(2)}, u32[]{:S(2)}) collective-permute-start(bf16[2,64,512]{2,1,0:T(8,128)(2,1)S(1)} %pad_maximum_fusion.1.after), channel_id=1, source_target_pairs={{0,4},{1,3},{2,6},{3,1},{4,0},{5,7},{6,2},{7,5},{8,12},{9,11},{10,... | collective-permute-start | bytes 393224 | tf_op jit(solution)/shard_map/ppermute | solution.py:289
  15.2 0.0 collective-permute-done.6
  15.3 0.0 copy-start.3
  15.3 2.2 %fetch_served.1.served_ref = bf16[8192,256]{1,0:T(8,128)(2,1)S(1)} custom-call(bf16[8192,256]{1,0:T(8,128)(2,1)} %source.1, bf16[2,64,512]{2,1,0:T(8,128)(2,1)S(1)} %pad_maximum_fusion.1.after), custom_call_target="tpu_custom_call" | custom-call | flops 1 | bytes 1 | tf_op jit(solution)/shard_map/fetch_served/pallas_call | solution.py:141
  17.5 1.5 %collective-permute-start.4 = (bf16[32,256]{1,0:T(8,128)(2,1)S(1)}, bf16[32,256]{1,0:T(8,128)(2,1)S(1)}, u32[]{:S(2)}, u32[]{:S(2)}) collective-permute-start(bf16[32,256]{1,0:T(8,128)(2,1)S(1)} %maximum_select_fusion.2), channel_id=1, source_target_pairs={{0,8},{2,10},{4,12},{6,14},{8,0},{10,2},{12,4},{14,6},{1,9},{3,11}... | collective-permute-start | bytes 49160 | tf_op jit(solution)/shard_map/ppermute | solution.py:292
  19.1 0.1 select_reduce_fusion
  19.2 1.6 %collective-permute-start.7 = (bf16[4,64,512]{2,1,0:T(8,128)(2,1)S(1)}, bf16[4,64,512]{2,1,0:T(8,128)(2,1)S(1)}, u32[]{:S(2)}, u32[]{:S(2)}) collective-permute-start(bf16[4,64,512]{2,1,0:T(8,128)(2,1)S(1)} %pad_maximum_fusion.rest_0_), channel_id=1, source_target_pairs={{0,2},{1,5},{2,0},{3,7},{4,6},{5,1},{6,4},{7,3},{8,10},{9,13},{10,... | collective-permute-start | bytes 786440 | tf_op jit(solution)/shard_map/ppermute | solution.py:289
  20.8 0.0 collective-permute-start.8
  20.8 1.8 %collective-permute-done.4 = bf16[32,256]{1,0:T(8,128)(2,1)S(1)} collective-permute-done((bf16[32,256]{1,0:T(8,128)(2,1)S(1)}, bf16[32,256]{1,0:T(8,128)(2,1)S(1)}, u32[]{:S(2)}, u32[]{:S(2)}) %collective-permute-start.4) | collective-permute-done | bytes 16416 | tf_op jit(solution)/shard_map/ppermute | solution.py:292
  22.6 2.6 %fold_blocks.3 = (bf16[8192,256]{1,0:T(8,128)(2,1)}, f32[4,256]{1,0:T(4,128)S(1)}) custom-call(s32[16]{0:T(128)S(1)} %fusion.1.start_hbm, bf16[64,256]{1,0:T(8,128)(2,1)S(1)} %maximum_select_fusion.1.up_ref, bf16[4,8192]{1,0:T(4,128)(2,1)S(1)} %maximum_select_fusion.features_ref, bf16[8192,256]{1,0:T(8,128)(2,1)S(1)} %fetch_served.1.served_ref, ...), custom_call_target="tpu_custom_call" | custom-call | flops 142606336 | bytes 4194304 | tf_op jit(solution)/shard_map/fold_blocks/pallas_call | solution.py:248
  25.1 0.5 %collective-permute-done.7.rest_0_ = bf16[4,64,512]{2,1,0:T(8,128)(2,1)S(1)} collective-permute-done((bf16[4,64,512]{2,1,0:T(8,128)(2,1)S(1)}, bf16[4,64,512]{2,1,0:T(8,128)(2,1)S(1)}, u32[]{:S(2)}, u32[]{:S(2)}) %collective-permute-start.7) | collective-permute-done | bytes 262176 | tf_op jit(solution)/shard_map/ppermute | solution.py:289
  25.6 2.1 %fold_blocks.4 = (bf16[8192,256]{1,0:T(8,128)(2,1)}, f32[4,256]{1,0:T(4,128)S(1)}) custom-call(s32[16]{0:T(128)S(1)} %fusion.1.start_hbm, bf16[64,256]{1,0:T(8,128)(2,1)S(1)} %maximum_select_fusion.1.up_ref, bf16[4,8192]{1,0:T(4,128)(2,1)S(1)} %maximum_select_fusion.features_ref, ...), custom_call_target="tpu_custom_call", output_to_operand_aliasing={{0}: (5, {})} | custom-call | flops 71303168 | bytes 2097152 | tf_op jit(solution)/shard_map/fold_blocks/pallas_call | solution.py:248
  27.8 2.2 %fold_blocks.5 = (bf16[8192,256]{1,0:T(8,128)(2,1)}, bf16[4,256]{1,0:T(4,128)(2,1)}, bf16[4,2048]{1,0:T(4,128)(2,1)}) custom-call(s32[16]{0:T(128)S(1)} %fusion.1.start_hbm, bf16[64,256]{1,0:T(8,128)(2,1)S(1)} %maximum_select_fusion.1.up_ref, bf16[4,8192]{1,0:T(4,128)(2,1)S(1)} %maximum_select_fusion.features_ref, ...), custom_call_target="tpu_custom_call", output_to_operand_aliasing={{0}: (5, {})} | custom-call | flops 71303168 | bytes 2097152 | tf_op jit(solution)/shard_map/fold_blocks/pallas_call | solution.py:248
  (24 shorter events, 0.2 us)
Async XLA Ops:
  0.6 4.7 %copy-start = (bf16[64,1024]{1,0:T(8,128)(2,1)S(1)}, bf16[64,1024]{1,0:T(8,128)(2,1)}, u32[]{:S(2)}) copy-start(bf16[64,1024]{1,0:T(8,128)(2,1)} %param.17) | copy-start | bytes 393220
  0.6 12.8 %copy-start.2 = (bf16[8,256]{1,0:T(8,128)(2,1)S(1)}, bf16[8,256]{1,0:T(8,128)(2,1)}, u32[]{:S(2)}) copy-start(bf16[8,256]{1,0:T(8,128)(2,1)} %param.18) | copy-start | bytes 12292
  0.7 14.6 %copy-start.1 = (bf16[4,4096]{1,0:T(4,128)(2,1)S(1)}, bf16[4,4096]{1,0:T(4,128)(2,1)}, u32[]{:S(2)}) copy-start(bf16[4,4096]{1,0:T(4,128)(2,1)} %param.10) | copy-start | bytes 98308
  0.7 12.8 %collective-permute-start.1 = (bf16[8,256]{1,0:T(8,128)(2,1)}, bf16[8,256]{1,0:T(8,128)(2,1)S(1)}, u32[]{:S(2)}, u32[]{:S(2)}) collective-permute-start(bf16[8,256]{1,0:T(8,128)(2,1)} %param.18), channel_id=1, source_target_pairs={{0,2},{2,0},{4,6},{6,4},{8,10},{10,8},{12,14},{14,12},{1,3},{3,1},... | collective-permute-start | bytes 12296 | tf_op jit(solution)/shard_map/ppermute | solution.py:301
  3.7 9.8 %collective-permute-start.3 = (bf16[8,256]{1,0:T(8,128)(2,1)}, bf16[8,256]{1,0:T(8,128)(2,1)S(1)}, u32[]{:S(2)}, u32[]{:S(2)}) collective-permute-start(bf16[8,256]{1,0:T(8,128)(2,1)} %param.18), channel_id=1, source_target_pairs={{0,4},{2,6},{4,0},{6,2},{8,12},{10,14},{12,8},{14,10},{1,5},{3,7},... | collective-permute-start | bytes 12296 | tf_op jit(solution)/shard_map/ppermute | solution.py:301
  5.3 8.2 %collective-permute-start.2 = (bf16[8,256]{1,0:T(8,128)(2,1)}, bf16[8,256]{1,0:T(8,128)(2,1)S(1)}, u32[]{:S(2)}, u32[]{:S(2)}) collective-permute-start(bf16[8,256]{1,0:T(8,128)(2,1)} %param.18), channel_id=1, source_target_pairs={{0,6},{2,4},{4,2},{6,0},{8,14},{10,12},{12,10},{14,8},{1,7},{3,5},... | collective-permute-start | bytes 12296 | tf_op jit(solution)/shard_map/ppermute | solution.py:301
  5.3 9.9 %collective-permute-start.6 = (bf16[4,4096]{1,0:T(4,128)(2,1)}, bf16[4,4096]{1,0:T(4,128)(2,1)S(1)}, u32[]{:S(2)}, u32[]{:S(2)}) collective-permute-start(bf16[4,4096]{1,0:T(4,128)(2,1)} %param.10), channel_id=1, source_target_pairs={{0,1},{1,0},{2,3},{3,2},{4,5},{5,4},{6,7},{7,6},{8,9},{9,8},{10,11... | collective-permute-start | bytes 98312 | tf_op jit(solution)/shard_map/ppermute | solution.py:299
  5.3 8.2 %collective-permute-start = (bf16[1,64,512]{2,1,0:T(8,128)(2,1)S(1)}, bf16[1,64,512]{2,1,0:T(8,128)(2,1)S(1)}, u32[]{:S(2)}, u32[]{:S(2)}) collective-permute-start(bf16[1,64,512]{2,1,0:T(8,128)(2,1)S(1)} %dynamic-slice_bitcast_fusion.rest_0_), channel_id=1, source_target_pairs={{0,8},{1,9},{2,10},{3,11},{4,12},{5,13},{6,14},{7,15},{8,0},{9,1},... | collective-permute-start | bytes 196616 | tf_op jit(solution)/shard_map/ppermute | solution.py:289
  13.6 5.6 %collective-permute-start.5 = (bf16[2,64,512]{2,1,0:T(8,128)(2,1)S(1)}, bf16[2,64,512]{2,1,0:T(8,128)(2,1)S(1)}, u32[]{:S(2)}, u32[]{:S(2)}) collective-permute-start(bf16[2,64,512]{2,1,0:T(8,128)(2,1)S(1)} %pad_maximum_fusion.1.after), channel_id=1, source_target_pairs={{0,4},{1,3},{2,6},{3,1},{4,0},{5,7},{6,2},{7,5},{8,12},{9,11},{10,... | collective-permute-start | bytes 393224 | tf_op jit(solution)/shard_map/ppermute | solution.py:289
  15.3 3.8 %copy-start.3 = (s32[8]{0:T(128)S(1)}, s32[8]{0:T(128)}, u32[]{:S(2)}) copy-start(s32[8]{0:T(128)} %param.19) | copy-start | bytes 100
  17.5 5.0 %collective-permute-start.4 = (bf16[32,256]{1,0:T(8,128)(2,1)S(1)}, bf16[32,256]{1,0:T(8,128)(2,1)S(1)}, u32[]{:S(2)}, u32[]{:S(2)}) collective-permute-start(bf16[32,256]{1,0:T(8,128)(2,1)S(1)} %maximum_select_fusion.2), channel_id=1, source_target_pairs={{0,8},{2,10},{4,12},{6,14},{8,0},{10,2},{12,4},{14,6},{1,9},{3,11}... | collective-permute-start | bytes 49160 | tf_op jit(solution)/shard_map/ppermute | solution.py:292
  19.2 6.4 %collective-permute-start.7 = (bf16[4,64,512]{2,1,0:T(8,128)(2,1)S(1)}, bf16[4,64,512]{2,1,0:T(8,128)(2,1)S(1)}, u32[]{:S(2)}, u32[]{:S(2)}) collective-permute-start(bf16[4,64,512]{2,1,0:T(8,128)(2,1)S(1)} %pad_maximum_fusion.rest_0_), channel_id=1, source_target_pairs={{0,2},{1,5},{2,0},{3,7},{4,6},{5,1},{6,4},{7,3},{8,10},{9,13},{10,... | collective-permute-start | bytes 786440 | tf_op jit(solution)/shard_map/ppermute | solution.py:289
  20.8 1.8 %collective-permute-start.8 = (bf16[4,64,512]{2,1,0:T(8,128)(2,1)S(1)}, bf16[4,64,512]{2,1,0:T(8,128)(2,1)S(1)}, u32[]{:S(2)}, u32[]{:S(2)}) collective-permute-start(bf16[4,64,512]{2,1,0:T(8,128)(2,1)S(1)} %pad_maximum_fusion.rest_0_), channel_id=1, source_target_pairs={{0,1},{1,0},{2,3},{3,2},{4,5},{5,4},{6,7},{7,6},{8,9},{9,8},{10,11... | collective-permute-start | bytes 786440 | tf_op jit(solution)/shard_map/ppermute | solution.py:331
  25.6 2.2 %collective-permute-start.9 = (bf16[4,64,512]{2,1,0:T(8,128)(2,1)S(1)}, bf16[4,64,512]{2,1,0:T(8,128)(2,1)S(1)}, u32[]{:S(2)}, u32[]{:S(2)}) collective-permute-start(bf16[4,64,512]{2,1,0:T(8,128)(2,1)S(1)} %collective-permute-done.7.rest_0_), channel_id=1, source_target_pairs={{0,1},{1,0},{2,3},{3,2},{4,5},{5,4},{6,7},{7,6},{8,9},{9,8},{10,11... | collective-permute-start | bytes 786440 | tf_op jit(solution)/shard_map/ppermute | solution.py:352

commit v9 on v7

--- a/solution.py
+++ b/solution.py
@@ -135,116 +135,170 @@
     )(*given, *([served] if fetch else []), *after)
 
 
-def fold_kernel(sizes, entry, stage, start_hbm, up_ref, features_ref, served_ref, *rest):
-    rest = list(rest)
-    first, last = stage == 0, stage == 2
-    arrays = [rest.pop(0) for _ in sizes]
-    if not first:
-        rest.pop(0)
-        total = rest.pop(0)[...]
-    if last:
-        context_ref, own_weight_ref = rest[:2]
-        merged, fresh_hbm, attended_hbm = rest[2:5]
-        start, start_sem, m_buf, out_sem, fresh_ref, attended_ref, small_sem = rest[5:]
-    else:
-        merged, total_ref, start, start_sem, m_buf, out_sem = rest
-    if first:
-        total = jnp.zeros(total_ref.shape, jnp.float32)
-    width = arrays[0].shape[2]
-    count = sum(sizes)
-
-    def rows_of(i):
-        return pl.ds(pl.multiple_of(start[entry + i], width), width)
-
-    def store(i):
-        return pltpu.make_async_copy(m_buf.at[i], merged.at[rows_of(i)], out_sem.at[i])
-
-    get_start = pltpu.make_async_copy(start_hbm, start, start_sem)
-    get_start.start()
-    up = (up_ref[...].astype(jnp.float32) * ADAPTER_SCALE).astype(jnp.bfloat16)
-    slabs = [array.at[k] for array, size in zip(arrays, sizes) for k in range(size)]
+class Merge:
+    def __init__(self, start_hbm, start, start_sem, merged, out_sem, width):
+        self.start, self.merged, self.out_sem, self.width = start, merged, out_sem, width
+        self.get_start = pltpu.make_async_copy(start_hbm, start, start_sem)
+        self.get_start.start()
+
+    def rows_of(self, entry):
+        return pl.ds(pl.multiple_of(self.start[entry], self.width), self.width)
+
+    def store(self, source, entry, at):
+        return pltpu.make_async_copy(source, self.merged.at[self.rows_of(entry)], self.out_sem.at[at])
+
+    def rows(self, slab, up, served_ref, features_ref, entry, total):
+        update = lax.dot_general(
+            slab[: up.shape[0]], up, (((0,), (0,)), ((), ())), preferred_element_type=jnp.float32
+        )
+        if self.get_start is not None:
+            self.get_start.wait()
+            self.get_start = None
+        rows = self.rows_of(entry)
+        fold = (served_ref[rows, :].astype(jnp.float32) + update).astype(jnp.bfloat16)
+        part = jnp.dot(features_ref[:, rows], fold, preferred_element_type=jnp.float32)
+        return fold, total + part
+
+
+def merge_kernel(per, left, start_hbm, pick_ref, features_ref, served_ref, slabs_ref, crossed_ref,
+                 last_ref, merged, total_ref, up_ref, left_ref, start, start_sem, m_buf, out_sem):
+    width = slabs_ref.shape[2]
+    rank, cols = up_ref.shape
+    merge = Merge(start_hbm, start, start_sem, merged, out_sem, width)
+    ups = []
+    for ref in (slabs_ref, last_ref):
+        for k in range(ref.shape[0]):
+            below = ref[k, rank:].astype(jnp.float32)
+            if cols <= width:
+                ups.append(below[:per, :cols])
+            else:
+                ups.append(
+                    jnp.concatenate(
+                        [below[i * per : (i + 1) * per] for i in range(cols // width)], axis=1
+                    )
+                )
+    ups = jnp.concatenate(ups, axis=0).astype(jnp.bfloat16)
+    up = jnp.dot(pick_ref[...], ups, preferred_element_type=jnp.float32).astype(jnp.bfloat16)
+    up_ref[...] = up
+    total = jnp.zeros(total_ref.shape, jnp.float32)
+    slabs = [ref.at[k] for ref in (slabs_ref, crossed_ref, last_ref) for k in range(ref.shape[0])]
+    keep = len(slabs) - left
     for i, slab in enumerate(slabs):
-        update = lax.dot_general(
-            slab[...], up, (((0,), (0,)), ((), ())), preferred_element_type=jnp.float32
+        fold, total = merge.rows(slab, up, served_ref, features_ref, i, total)
+        if i < keep:
+            m_buf[i] = fold
+            merge.store(m_buf.at[i], i, i).start()
+        else:
+            left_ref[i - keep] = fold
+    total_ref[...] = total
+    for i in range(keep):
+        merge.store(m_buf.at[i], i, i).wait()
+
+
+def final_kernel(start_hbm, up_ref, features_ref, served_ref, left_ref, last_ref, merged_in,
+                 total_ref, context_ref, own_weight_ref, merged, fresh_hbm, attended_hbm, start,
+                 start_sem, m_buf, out_sem, fresh_ref, attended_ref, small_sem):
+    del merged_in
+    count, _, width = last_ref.shape
+    left = left_ref.shape[0]
+    merge = Merge(start_hbm, start, start_sem, merged, out_sem, width)
+    first = start.shape[0] - count
+    total = total_ref[...]
+    stores = []
+    for i in range(count):
+        fold, total = merge.rows(
+            last_ref.at[i], up_ref[...], served_ref, features_ref, first + i, total
         )
         if i == 0:
-            get_start.wait()
-        fold = (served_ref[rows_of(i), :].astype(jnp.float32) + update).astype(jnp.bfloat16)
+            stores += [
+                merge.store(left_ref.at[k], first - left + k, count + k) for k in range(left)
+            ]
+            for store in stores:
+                store.start()
         m_buf[i] = fold
-        store(i).start()
-        total = total + jnp.dot(
-            features_ref[:, rows_of(i)], fold, preferred_element_type=jnp.float32
-        )
-    if last:
-        fresh = total.astype(jnp.bfloat16)
-        fresh_ref[...] = fresh
-        put_fresh = pltpu.make_async_copy(fresh_ref, fresh_hbm, small_sem.at[0])
-        put_fresh.start()
-        value = fresh.astype(jnp.float32)
-        heads = attended_ref.shape[1] // HEAD_SIZE
-        group = heads // (fresh_ref.shape[1] // HEAD_SIZE)
-        for h in range(heads):
-            cols = slice(h * HEAD_SIZE, (h + 1) * HEAD_SIZE)
-            at = (h // group) * HEAD_SIZE
-            attended_ref[:, cols] = (
-                context_ref[:, cols] + own_weight_ref[:, cols] * value[:, at : at + HEAD_SIZE]
-            ).astype(jnp.bfloat16)
-        put_attended = pltpu.make_async_copy(attended_ref, attended_hbm, small_sem.at[1])
-        put_attended.start()
-        put_fresh.wait()
-        put_attended.wait()
-    else:
-        total_ref[...] = total
-    for i in range(count):
-        store(i).wait()
-
-
-def fold(stage, entry, start, up, features, served, arrays, state=(), finish=()):
-    first, last = stage == 0, stage == 2
-    sizes = [array.shape[0] for array in arrays]
-    count = sum(sizes)
-    rank, cols = up.shape
-    width = arrays[0].shape[2]
-    rows, depth = features.shape
-    in_specs = [HBM, VMEM, VMEM, VMEM] + [VMEM] * len(arrays)
-    operands = [start, up, features, served, *arrays]
-    aliases = {}
-    out_shape = [jax.ShapeDtypeStruct((depth, cols), jnp.bfloat16)]
-    out_specs = [HBM]
-    scratch = [
-        pltpu.SMEM(start.shape, jnp.int32),
-        pltpu.SemaphoreType.DMA,
-        pltpu.VMEM((count, width, cols), jnp.bfloat16),
-        pltpu.SemaphoreType.DMA((count,)),
-    ]
-    if not first:
-        aliases = {len(operands): 0}
-        in_specs += [HBM, VMEM] + [VMEM] * len(finish)
-        operands += [*state, *finish]
-    if last:
-        smalls = [(rows, cols), finish[0].shape]
-        out_shape += [jax.ShapeDtypeStruct(shape, jnp.bfloat16) for shape in smalls]
-        out_specs += [HBM, HBM]
-        scratch += [pltpu.VMEM(shape, jnp.bfloat16) for shape in smalls]
-        scratch += [pltpu.SemaphoreType.DMA((2,))]
-    else:
-        out_shape += [jax.ShapeDtypeStruct((rows, cols), jnp.float32)]
-        out_specs += [VMEM]
+        stores.append(merge.store(m_buf.at[i], first + i, i))
+        stores[-1].start()
+    fresh = total.astype(jnp.bfloat16)
+    fresh_ref[...] = fresh
+    put_fresh = pltpu.make_async_copy(fresh_ref, fresh_hbm, small_sem.at[0])
+    put_fresh.start()
+    value = fresh.astype(jnp.float32)
+    heads = attended_ref.shape[1] // HEAD_SIZE
+    group = heads // (fresh_ref.shape[1] // HEAD_SIZE)
+    for h in range(heads):
+        cols = slice(h * HEAD_SIZE, (h + 1) * HEAD_SIZE)
+        at = (h // group) * HEAD_SIZE
+        attended_ref[:, cols] = (
+            context_ref[:, cols] + own_weight_ref[:, cols] * value[:, at : at + HEAD_SIZE]
+        ).astype(jnp.bfloat16)
+    put_attended = pltpu.make_async_copy(attended_ref, attended_hbm, small_sem.at[1])
+    put_attended.start()
+    for store in stores:
+        store.wait()
+    put_fresh.wait()
+    put_attended.wait()
+
+
+def merge(per, start, pick, features, served, slabs, crossed, last):
+    left = 3
+    count = slabs.shape[0] + crossed.shape[0] + last.shape[0]
+    width = slabs.shape[2]
+    rank = pick.shape[0]
+    depth, cols = served.shape
     return pl.pallas_call(
-        functools.partial(fold_kernel, sizes, entry, stage),
-        out_shape=out_shape,
-        in_specs=in_specs,
-        out_specs=out_specs,
-        input_output_aliases=aliases,
-        scratch_shapes=scratch,
+        functools.partial(merge_kernel, per, left),
+        out_shape=(
+            jax.ShapeDtypeStruct((depth, cols), jnp.bfloat16),
+            jax.ShapeDtypeStruct((features.shape[0], cols), jnp.float32),
+            jax.ShapeDtypeStruct((rank, cols), jnp.bfloat16),
+            jax.ShapeDtypeStruct((left, width, cols), jnp.bfloat16),
+        ),
+        in_specs=[HBM] + [VMEM] * 6,
+        out_specs=(HBM, VMEM, VMEM, VMEM),
+        scratch_shapes=[
+            pltpu.SMEM(start.shape, jnp.int32),
+            pltpu.SemaphoreType.DMA,
+            pltpu.VMEM((count - left, width, cols), jnp.bfloat16),
+            pltpu.SemaphoreType.DMA((count - left,)),
+        ],
         compiler_params=pltpu.CompilerParams(vmem_limit_bytes=12 * 2**20),
         cost_estimate=pl.CostEstimate(
-            flops=2 * count * width * cols * (rank + rows),
+            flops=2 * count * width * cols * rank,
             bytes_accessed=4 * count * width * cols,
             transcendentals=0,
         ),
-        name="fold_blocks",
-    )(*operands)
+        name="merge_blocks",
+    )(start, pick, features, served, slabs, crossed, last)
+
+
+def finish(start, up, features, served, left, last, merged, total, context, own_weight):
+    count, _, width = last.shape
+    depth, cols = served.shape
+    smalls = [total.shape, context.shape]
+    return pl.pallas_call(
+        final_kernel,
+        out_shape=[
+            jax.ShapeDtypeStruct(shape, jnp.bfloat16) for shape in [(depth, cols), *smalls]
+        ],
+        in_specs=[HBM] + [VMEM] * 5 + [HBM] + [VMEM] * 3,
+        out_specs=[HBM] * 3,
+        input_output_aliases={6: 0},
+        scratch_shapes=[
+            pltpu.SMEM(start.shape, jnp.int32),
+            pltpu.SemaphoreType.DMA,
+            pltpu.VMEM((count, width, cols), jnp.bfloat16),
+            pltpu.SemaphoreType.DMA((count + left.shape[0],)),
+        ]
+        + [pltpu.VMEM(shape, jnp.bfloat16) for shape in smalls]
+        + [pltpu.SemaphoreType.DMA((2,))],
+        compiler_params=pltpu.CompilerParams(vmem_limit_bytes=12 * 2**20),
+        cost_estimate=pl.CostEstimate(
+            flops=2 * count * width * cols * up.shape[0],
+            bytes_accessed=4 * count * width * cols,
+            transcendentals=0,
+        ),
+        name="finish_rows",
+    )(start, up, features, served, left, last, merged, total, context, own_weight)
 
 
 def body(
@@ -266,6 +320,8 @@
     full = adapter_in.shape[1]
     width = full // 2
     rows = queries.shape[0]
+    per, cols = adapter_out.shape
+    rank = n * per
 
     bits = [n >> i for i in range(1, n.bit_length())]
     ways = [bits, bits[:-2] + bits[:-3:-1]]
@@ -274,45 +330,41 @@
         pairs = [(2 * i + c, 2 * (i ^ ways[c][step]) + c) for i in range(n) for c in range(2)]
         return lax.ppermute(x, ("replica", "tensor"), pairs)
 
-    def grown(up, bit):
-        came = lax.ppermute(up, "replica", [(i, i ^ bit) for i in range(n)])
-        above, below = jnp.concatenate([up, came], axis=0), jnp.concatenate([came, up], axis=0)
-        return jnp.where((replica & bit) == 0, above, below)
-
-    given = (
-        *in_hbm(lengths, queries, fresh_token_key, stored_keys, stored_values),
-    )
-    slabs = lax.dynamic_slice_in_dim(adapter_in, core * width, width, axis=1)[None]
-    up, hid_other = adapter_out, hidden_in
+    if cols <= width:
+        below = jnp.pad(adapter_out, ((0, -per % 8), (0, width - cols)))
+    else:
+        below = jnp.concatenate(jnp.split(adapter_out, cols // width, axis=1), axis=0)
+        below = jnp.pad(below, ((0, -below.shape[0] % 8), (0, 0)))
+    slabs = jnp.concatenate(
+        [lax.dynamic_slice_in_dim(adapter_in, core * width, width, axis=1), below], axis=0
+    )[None]
+
+    given = in_hbm(lengths, queries, fresh_token_key, stored_keys, stored_values)
     *early, final = range(len(bits))
     parts = []
     split = rows // 2
     for step in early:
         came = exchange(slabs, step)
         if step == 0:
-            grown_up = grown(up, 1)
-            parts.append(attend(range(split), given))
-            up, parts[0], hid_other, owner_rank = lax.optimization_barrier(
-                (grown_up, parts[0], hid_other, owner_rank)
+            parts.append(attend(range(split), given, after=[slabs]))
+            parts[0], hid_other, owner_rank = lax.optimization_barrier(
+                (parts[0], hidden_in, owner_rank)
             )
-            grown_up = grown(up, 2)
             hid_other = lax.ppermute(hid_other, "tensor", swap)
+            came, parts[0] = lax.optimization_barrier((came, parts[0]))
         elif step == 1:
             *part, served = attend(
                 range(split, rows), given, *in_hbm(served_value_weight), [slabs]
             )
-            up, part = lax.optimization_barrier((grown_up, part))
-            up = grown(up, 4)
             came, part = lax.optimization_barrier((came, part))
             parts.append(part)
         slabs = jnp.concatenate([slabs, came], axis=0)
-    for step in range(3, len(bits)):
-        up = grown(up, 1 << step)
     last = exchange(slabs, final)
-    crossed = lax.ppermute(slabs, "tensor", swap)
 
     features = jnp.concatenate([hidden_in, hid_other], axis=1)
     features = jnp.where(core == 0, features, jnp.concatenate([hid_other, hidden_in], axis=1))
+    crossed, features = lax.optimization_barrier((slabs, features))
+    crossed = lax.ppermute(crossed, "tensor", swap)
 
     slab = jnp.arange(n, dtype=jnp.int32)
     sources = []
@@ -329,22 +381,28 @@
     place = jnp.sum(jnp.where(owner_rank[None, :] == source[:, None], slab[None, :], 0), axis=1)
     start = (place * full + half * width).astype(jnp.int32)
 
-    merged, total = fold(
-        0, 0, start, up, features, served, [slabs, crossed]
-    )
-    last, total = lax.optimization_barrier((last, total))
-    last_crossed = lax.ppermute(last, "tensor", swap)
-    merged, total = fold(
-        1, 2 * count, start, up, features, served, [last], state=[merged, total]
-    )
+    row = jnp.arange(rank, dtype=jnp.int32)
+    row_source = replica
+    for step in range(len(bits)):
+        bit = jnp.where(core == 0, ways[0][step], ways[1][step])
+        row_source = row_source ^ (((row // per >> step) & 1) * bit)
+    pick = jnp.where(
+        row[:, None] == (row_source * per + row % per)[None, :], ADAPTER_SCALE, 0.0
+    ).astype(jnp.bfloat16)
+
     context, own_weight = (
         jnp.concatenate(pair, axis=0).reshape(queries.shape) for pair in zip(*parts)
     )
-    merged, fresh_token_value, attended = fold(
-        2, 3 * count, start, up, features, served, [last_crossed], state=[merged, total],
-        finish=[context, own_weight],
-    )
-    return (merged, fresh_token_value, attended)
+    last, start, pick, context, own_weight = lax.optimization_barrier(
+        (last, start, pick, context, own_weight)
+    )
+    last_crossed = lax.ppermute(last, "tensor", swap)
+    merged, total, up, left = merge(per, start, pick, features, served, slabs, crossed, last)
+    return tuple(
+        finish(
+            start, up, features, served, left, last_crossed, merged, total, context, own_weight
+        )
+    )
 
 
 def solution(mesh):

time: 28.2 us -> 27.6 us (0.979)
  starting transfers between devices: 9.85 us -> 6.93 us
  waiting for transfers between devices: 4.24 us -> 6.8 us
  Pallas kernels: 12.6 us -> 10.8 us
  local copies, waits for them, and re-layouts: 0.2 us -> 1.07 us
  other arithmetic: 0.29 us -> 0.99 us
    ppermute x3, waiting for transfers between devices: 0.01 us -> 6.8 us  [exchange(): return lax.ppermute(x, ('replica', 'tensor'), pairs)]
    ppermute x4 -> x1, starting transfers between devices: 5.54 us -> 0.07 us  [body(): crossed = lax.ppermute(crossed, 'tensor', swap)]
    ppermute x4 -> x1, waiting for transfers between devices: 4.22 us -> 0.01 us  [body(): crossed = lax.ppermute(crossed, 'tensor', swap)]
    ppermute x3, starting transfers between devices: 4.23 us -> 6.79 us  [exchange(): return lax.ppermute(x, ('replica', 'tensor'), pairs)]
    pallas_call x3 -> x2, Pallas kernels: 6.93 us -> 5.07 us  [the longest x1 2.84 us: merge(): pl.pallas_call(functools.partial(merge_kernel, per, left), out_shape=(jax...]
    unnamed x10 -> x8, local copies, waits for them, and re-layouts: 0.05 us -> 0.92 us
    broadcast_in_dim x0 -> x1, other arithmetic: none -> 0.69 us  [body(): jnp.concatenate([lax.dynamic_slice_in_dim(adapter_in, core * width, width...]
  transfers between devices with their start and end apart: 9 -> 6, of which waited for: 2 -> 3; matrix products, arithmetic and copies ran while one was open for 2% -> 2% of each run, Pallas kernels for 37% -> 31%
where the time goes in v9:
time: 27.6 us; the launch traced here: 27.3 us
  Pallas kernels  10.8 us (39%)
  starting transfers between devices  6.93 us (25%)
  waiting for transfers between devices  6.8 us (25%)
  local copies, waits for them, and re-layouts  1.07 us (4%)
  other arithmetic  0.99 us (4%)
  between operations  0.78 us (3%)
    ppermute x3, waiting for transfers between devices, exchange(): return lax.ppermute(x, ('replica', 'tensor'), pairs)  6.8 us
    ppermute x3, starting transfers between devices, exchange(): return lax.ppermute(x, ('replica', 'tensor'), pairs)  6.79 us
    pallas_call x2, Pallas kernels, attend(): pl.pallas_call(functools.partial(attend_kernel, rows, fetch), out_shape=o...  5.7 us
    pallas_call x1, Pallas kernels, merge(): pl.pallas_call(functools.partial(merge_kernel, per, left), out_shape=(jax...  2.84 us
    pallas_call x1, Pallas kernels, finish(): pl.pallas_call(final_kernel, out_shape=[jax.ShapeDtypeStruct(shape, jnp.b...  2.23 us
    unnamed x8, local copies, waits for them, and re-layouts  0.92 us
    broadcast_in_dim x1, other arithmetic, body(): jnp.concatenate([lax.dynamic_slice_in_dim(adapter_in, core * width, width...  0.69 us
  transfers between devices with their start and end apart: 6, of which 3 were waited for; matrix products, arithmetic and copies ran while one was open for 2% of the time, Pallas kernels for 31%

profile of v9, /device:TPU:0, one launch (start us, length us, event | category | flops | bytes accessed | tf_op | source)
XLA Modules:
  0.0 27.3 jit_solution(12597811597375101875)
XLA Ops:
  0.6 0.0 copy-start
  0.6 0.0 copy-start.1
  0.7 0.9 %copy-done = bf16[64,1024]{1,0:T(8,128)(2,1)S(1)} copy-done((bf16[64,1024]{1,0:T(8,128)(2,1)S(1)}, bf16[64,1024]{1,0:T(8,128)(2,1)}, u32[]{:S(2)}) %copy-start) | copy-done | bytes 131096
  1.5 0.7 %fusion.2.rest_0_ = bf16[1,72,512]{2,1,0:T(8,128)(2,1)S(1)} fusion(bf16[8,256]{1,0:T(8,128)(2,1)} %param.18, bf16[64,512]{1,0:T(8,128)(2,1)S(1)} %constant_dynamic-slice_fusion), kind=kLoop, calls=%fused_computation.5 | loop fusion | flops 221184 | bytes 143360 | tf_op jit(solution)/shard_map/broadcast_in_dim | solution.py:338
  2.2 4.0 %collective-permute-start = (bf16[1,72,512]{2,1,0:T(8,128)(2,1)S(1)}, bf16[1,72,512]{2,1,0:T(8,128)(2,1)S(1)}, u32[]{:S(2)}, u32[]{:S(2)}) collective-permute-start(bf16[1,72,512]{2,1,0:T(8,128)(2,1)S(1)} %fusion.2.rest_0_), channel_id=1, source_target_pairs={{0,8},{1,9},{2,10},{3,11},{4,12},{5,13},{6,14},{7,15},{8,0},{9,1},... | collective-permute-start | bytes 221192 | tf_op jit(solution)/shard_map/ppermute | solution.py:331
  6.3 2.8 %attend_cache.2 = (f32[2,16,128]{2,1,0:T(8,128)S(1)}, f32[2,16,128]{2,1,0:T(8,128)S(1)}) custom-call(s32[4]{0:T(128)} %lengths_hbm.3, bf16[4,2048]{1,0:T(4,128)(2,1)} %q_hbm.3, bf16[4,256]{1,0:T(4,128)(2,1)} %own_k_hbm.3, bf16[4,1024,256]{2,1,0:T(8,128)(2,1)} %k_hbm.3, bf16[4,1024,256]{2,1,0:T(8,128)(2,1)} %v_hbm.3, bf16[1,72,512]{2,1,0:T(8,128)(2,1)S(1)} %fusion.2.rest_0_), custom_call_target="tpu_custom_call" | custom-call | flops 33554432 | bytes 2097152 | tf_op jit(solution)/shard_map/attend_cache/pallas_call | solution.py:112
  9.0 0.1 collective-permute-start.3
  9.2 0.1 fusion.8
  9.2 0.1 fusion.7
  9.3 0.1 pad_add_fusion
  9.4 0.1 select_reduce_fusion
  9.5 0.7 %collective-permute-done = bf16[1,72,512]{2,1,0:T(8,128)(2,1)S(1)} collective-permute-done((bf16[1,72,512]{2,1,0:T(8,128)(2,1)S(1)}, bf16[1,72,512]{2,1,0:T(8,128)(2,1)S(1)}, u32[]{:S(2)}, u32[]{:S(2)}) %collective-permute-start) | collective-permute-done | bytes 73760 | tf_op jit(solution)/shard_map/ppermute | solution.py:331
  10.2 1.0 %collective-permute-start.1 = (bf16[2,72,512]{2,1,0:T(8,128)(2,1)S(1)}, bf16[2,72,512]{2,1,0:T(8,128)(2,1)S(1)}, u32[]{:S(2)}, u32[]{:S(2)}) collective-permute-start(bf16[2,72,512]{2,1,0:T(8,128)(2,1)S(1)} %pad_maximum_fusion.1.rest_1_), channel_id=1, source_target_pairs={{0,4},{1,3},{2,6},{3,1},{4,0},{5,7},{6,2},{7,5},{8,12},{9,11},{10,... | collective-permute-start | bytes 442376 | tf_op jit(solution)/shard_map/ppermute | solution.py:331
  11.2 2.9 %attend_cache.3 = (f32[2,16,128]{2,1,0:T(8,128)S(1)}, f32[2,16,128]{2,1,0:T(8,128)S(1)}, bf16[8192,256]{1,0:T(8,128)(2,1)S(1)}) custom-call(s32[4]{0:T(128)} %lengths_hbm.3, bf16[4,2048]{1,0:T(4,128)(2,1)} %q_hbm.3, bf16[4,256]{1,0:T(4,128)(2,1)} %own_k_hbm.3, bf16[4,1024,256]{2,1,0:T(8,128)(2,1)} %k_hbm.3, bf16[4,1024,256]{2,1,0:T(8,128)(2,1)} %v_hbm.3, ...), custom_call_target="tpu_custom_call" | custom-call | flops 33554432 | bytes 2097152 | tf_op jit(solution)/shard_map/attend_cache/pallas_call | solution.py:112
  14.1 1.3 %collective-permute-done.1 = bf16[2,72,512]{2,1,0:T(8,128)(2,1)S(1)} collective-permute-done((bf16[2,72,512]{2,1,0:T(8,128)(2,1)S(1)}, bf16[2,72,512]{2,1,0:T(8,128)(2,1)S(1)}, u32[]{:S(2)}, u32[]{:S(2)}) %collective-permute-start.1) | collective-permute-done | bytes 147488 | tf_op jit(solution)/shard_map/ppermute | solution.py:331
  15.4 1.8 %collective-permute-start.2 = (bf16[4,72,512]{2,1,0:T(8,128)(2,1)S(1)}, bf16[4,72,512]{2,1,0:T(8,128)(2,1)S(1)}, u32[]{:S(2)}, u32[]{:S(2)}) collective-permute-start(bf16[4,72,512]{2,1,0:T(8,128)(2,1)S(1)} %pad_maximum_fusion.slabs_ref), channel_id=1, source_target_pairs={{0,2},{1,5},{2,0},{3,7},{4,6},{5,1},{6,4},{7,3},{8,10},{9,13},{10,... | collective-permute-start | bytes 884744 | tf_op jit(solution)/shard_map/ppermute | solution.py:331
  17.2 0.0 collective-permute-done.3
  17.3 0.1 collective-permute-start.4
  17.4 4.8 %collective-permute-done.2.last_ref = bf16[4,72,512]{2,1,0:T(8,128)(2,1)S(1)} collective-permute-done((bf16[4,72,512]{2,1,0:T(8,128)(2,1)S(1)}, bf16[4,72,512]{2,1,0:T(8,128)(2,1)S(1)}, u32[]{:S(2)}, u32[]{:S(2)}) %collective-permute-start.2) | collective-permute-done | bytes 294944 | tf_op jit(solution)/shard_map/ppermute | solution.py:331
  22.2 0.0 collective-permute-start.5
  22.2 0.0 collective-permute-done.4.crossed_ref
  22.2 2.8 %merge_blocks.1 = (bf16[8192,256]{1,0:T(8,128)(2,1)}, f32[4,256]{1,0:T(4,128)S(1)}, bf16[64,256]{1,0:T(8,128)(2,1)S(1)}, bf16[3,512,256]{2,1,0:T(8,128)(2,1)S(1)}) custom-call(s32[16]{0:T(128)S(1)} %fusion.5.start_hbm, bf16[64,64]{1,0:T(8,128)(2,1)S(1)} %select_convert_fusion.pick_ref, bf16[4,8192]{1,0:T(4,128)(2,1)S(1)} %maximum_select_fusion.features_ref, ...), custom_call_target="tpu_custom_call" | custom-call | flops 201326592 | bytes 6291456 | tf_op jit(solution)/shard_map/merge_blocks/pallas_call | solution.py:248
  25.1 0.0 collective-permute-done.5.last_ref
  25.1 2.2 %finish_rows.1 = (bf16[8192,256]{1,0:T(8,128)(2,1)}, bf16[4,256]{1,0:T(4,128)(2,1)}, bf16[4,2048]{1,0:T(4,128)(2,1)}) custom-call(s32[16]{0:T(128)S(1)} %fusion.5.start_hbm, bf16[64,256]{1,0:T(8,128)(2,1)S(1)} %get-tuple-element.49.up_ref, bf16[4,8192]{1,0:T(4,128)(2,1)S(1)} %maximum_select_fusion.features_ref, ...), custom_call_target="tpu_custom_call", output_to_operand_aliasing={{0}: (6, {})} | custom-call | flops 67108864 | bytes 2097152 | tf_op jit(solution)/shard_map/finish_rows/pallas_call | solution.py:278
  (14 shorter events, 0.2 us)
Async XLA Ops:
  0.6 0.9 %copy-start = (bf16[64,1024]{1,0:T(8,128)(2,1)S(1)}, bf16[64,1024]{1,0:T(8,128)(2,1)}, u32[]{:S(2)}) copy-start(bf16[64,1024]{1,0:T(8,128)(2,1)} %param.17) | copy-start | bytes 393220
  0.6 8.4 %copy-start.1 = (bf16[4,4096]{1,0:T(4,128)(2,1)S(1)}, bf16[4,4096]{1,0:T(4,128)(2,1)}, u32[]{:S(2)}) copy-start(bf16[4,4096]{1,0:T(4,128)(2,1)} %param.10) | copy-start | bytes 98308
  0.7 8.8 %copy-start.2 = (s32[8]{0:T(128)S(1)}, s32[8]{0:T(128)}, u32[]{:S(2)}) copy-start(s32[8]{0:T(128)} %param.19) | copy-start | bytes 100
  2.2 7.9 %collective-permute-start = (bf16[1,72,512]{2,1,0:T(8,128)(2,1)S(1)}, bf16[1,72,512]{2,1,0:T(8,128)(2,1)S(1)}, u32[]{:S(2)}, u32[]{:S(2)}) collective-permute-start(bf16[1,72,512]{2,1,0:T(8,128)(2,1)S(1)} %fusion.2.rest_0_), channel_id=1, source_target_pairs={{0,8},{1,9},{2,10},{3,11},{4,12},{5,13},{6,14},{7,15},{8,0},{9,1},... | collective-permute-start | bytes 221192 | tf_op jit(solution)/shard_map/ppermute | solution.py:331
  9.0 8.2 %collective-permute-start.3 = (bf16[4,4096]{1,0:T(4,128)(2,1)S(1)}, bf16[4,4096]{1,0:T(4,128)(2,1)S(1)}, u32[]{:S(2)}, u32[]{:S(2)}) collective-permute-start(bf16[4,4096]{1,0:T(4,128)(2,1)S(1)} %copy-done.1), channel_id=1, source_target_pairs={{0,1},{1,0},{2,3},{3,2},{4,5},{5,4},{6,7},{7,6},{8,9},{9,8},{10,11... | collective-permute-start | bytes 98312 | tf_op jit(solution)/shard_map/ppermute | solution.py:353
  10.2 5.2 %collective-permute-start.1 = (bf16[2,72,512]{2,1,0:T(8,128)(2,1)S(1)}, bf16[2,72,512]{2,1,0:T(8,128)(2,1)S(1)}, u32[]{:S(2)}, u32[]{:S(2)}) collective-permute-start(bf16[2,72,512]{2,1,0:T(8,128)(2,1)S(1)} %pad_maximum_fusion.1.rest_1_), channel_id=1, source_target_pairs={{0,4},{1,3},{2,6},{3,1},{4,0},{5,7},{6,2},{7,5},{8,12},{9,11},{10,... | collective-permute-start | bytes 442376 | tf_op jit(solution)/shard_map/ppermute | solution.py:331
  15.4 6.8 %collective-permute-start.2 = (bf16[4,72,512]{2,1,0:T(8,128)(2,1)S(1)}, bf16[4,72,512]{2,1,0:T(8,128)(2,1)S(1)}, u32[]{:S(2)}, u32[]{:S(2)}) collective-permute-start(bf16[4,72,512]{2,1,0:T(8,128)(2,1)S(1)} %pad_maximum_fusion.slabs_ref), channel_id=1, source_target_pairs={{0,2},{1,5},{2,0},{3,7},{4,6},{5,1},{6,4},{7,3},{8,10},{9,13},{10,... | collective-permute-start | bytes 884744 | tf_op jit(solution)/shard_map/ppermute | solution.py:331
  17.3 5.0 %collective-permute-start.4 = (bf16[4,72,512]{2,1,0:T(8,128)(2,1)S(1)}, bf16[4,72,512]{2,1,0:T(8,128)(2,1)S(1)}, u32[]{:S(2)}, u32[]{:S(2)}) collective-permute-start(bf16[4,72,512]{2,1,0:T(8,128)(2,1)S(1)} %pad_maximum_fusion.slabs_ref), channel_id=1, source_target_pairs={{0,1},{1,0},{2,3},{3,2},{4,5},{5,4},{6,7},{7,6},{8,9},{9,8},{10,11... | collective-permute-start | bytes 884744 | tf_op jit(solution)/shard_map/ppermute | solution.py:367
  22.2 2.9 %collective-permute-start.5 = (bf16[4,72,512]{2,1,0:T(8,128)(2,1)S(1)}, bf16[4,72,512]{2,1,0:T(8,128)(2,1)S(1)}, u32[]{:S(2)}, u32[]{:S(2)}) collective-permute-start(bf16[4,72,512]{2,1,0:T(8,128)(2,1)S(1)} %collective-permute-done.2.last_ref), channel_id=1, source_target_pairs={{0,1},{1,0},{2,3},{3,2},{4,5},{5,4},{6,7},{7,6},{8,9},{9,8},{10,11... | collective-permute-start | bytes 884744 | tf_op jit(solution)/shard_map/ppermute | solution.py:399

commit v10 on v9

--- a/solution.py
+++ b/solution.py
@@ -135,36 +135,77 @@
     )(*given, *([served] if fetch else []), *after)
 
 
+def pack_kernel(per, block_hbm, up_hbm, slab_ref, half_ref, up_ref, sem):
+    rank, width = half_ref.shape
+    cols = up_ref.shape[1]
+    first = pl.multiple_of(lax.axis_index("tensor") * width, width)
+    copies = [
+        pltpu.make_async_copy(block_hbm.at[:, pl.ds(first, width)], half_ref, sem.at[0]),
+        pltpu.make_async_copy(up_hbm, up_ref, sem.at[1]),
+    ]
+    for copy in copies:
+        copy.start()
+    for copy in copies:
+        copy.wait()
+    slab_ref[0, :rank] = half_ref[...]
+    up = up_ref[...].astype(jnp.float32)
+    if cols <= width:
+        below = jnp.concatenate([up, jnp.zeros((per, width - cols), jnp.float32)], axis=1)
+    else:
+        below = jnp.concatenate(
+            [up[:, i * width : (i + 1) * width] for i in range(cols // width)], axis=0
+        )
+    spare = slab_ref.shape[1] - rank - below.shape[0]
+    if spare:
+        below = jnp.concatenate([below, jnp.zeros((spare, width), jnp.float32)], axis=0)
+    slab_ref[0, rank:] = below.astype(jnp.bfloat16)
+
+
+def pack(block, up):
+    rank, full = block.shape
+    per, cols = up.shape
+    width = full // 2
+    below = -(-per * max(cols // width, 1) // 8) * 8
+    return pl.pallas_call(
+        functools.partial(pack_kernel, per),
+        out_shape=jax.ShapeDtypeStruct((1, rank + below, width), block.dtype),
+        in_specs=[HBM, HBM],
+        out_specs=VMEM,
+        scratch_shapes=[
+            pltpu.VMEM((rank, width), block.dtype),
+            pltpu.VMEM(up.shape, up.dtype),
+            pltpu.SemaphoreType.DMA((2,)),
+        ],
+        name="pack_slab",
+    )(*in_hbm(block, up))
+
+
 class Merge:
-    def __init__(self, start_hbm, start, start_sem, merged, out_sem, width):
-        self.start, self.merged, self.out_sem, self.width = start, merged, out_sem, width
-        self.get_start = pltpu.make_async_copy(start_hbm, start, start_sem)
-        self.get_start.start()
+    def __init__(self, start_ref, merged, out_sem, width):
+        self.start, self.merged, self.out_sem, self.width = start_ref[...], merged, out_sem, width
+        self.entry = lax.broadcasted_iota(jnp.int32, self.start.shape, 1)
 
     def rows_of(self, entry):
-        return pl.ds(pl.multiple_of(self.start[entry], self.width), self.width)
-
-    def store(self, source, entry, at):
-        return pltpu.make_async_copy(source, self.merged.at[self.rows_of(entry)], self.out_sem.at[at])
-
-    def rows(self, slab, up, served_ref, features_ref, entry, total):
+        first = jnp.sum(jnp.where(self.entry == entry, self.start, 0))
+        return pl.ds(pl.multiple_of(first, self.width), self.width)
+
+    def store(self, source, rows, at):
+        return pltpu.make_async_copy(source, self.merged.at[rows], self.out_sem.at[at])
+
+    def rows(self, slab, up, served_ref, features_ref, rows, total):
         update = lax.dot_general(
             slab[: up.shape[0]], up, (((0,), (0,)), ((), ())), preferred_element_type=jnp.float32
         )
-        if self.get_start is not None:
-            self.get_start.wait()
-            self.get_start = None
-        rows = self.rows_of(entry)
         fold = (served_ref[rows, :].astype(jnp.float32) + update).astype(jnp.bfloat16)
         part = jnp.dot(features_ref[:, rows], fold, preferred_element_type=jnp.float32)
         return fold, total + part
 
 
-def merge_kernel(per, left, start_hbm, pick_ref, features_ref, served_ref, slabs_ref, crossed_ref,
-                 last_ref, merged, total_ref, up_ref, left_ref, start, start_sem, m_buf, out_sem):
+def merge_kernel(per, left, start_ref, pick_ref, features_ref, served_ref, slabs_ref, crossed_ref,
+                 last_ref, merged, total_ref, up_ref, left_ref, m_buf, out_sem):
     width = slabs_ref.shape[2]
     rank, cols = up_ref.shape
-    merge = Merge(start_hbm, start, start_sem, merged, out_sem, width)
+    merge = Merge(start_ref, merged, out_sem, width)
     ups = []
     for ref in (slabs_ref, last_ref):
         for k in range(ref.shape[0]):
@@ -183,40 +224,41 @@
     total = jnp.zeros(total_ref.shape, jnp.float32)
     slabs = [ref.at[k] for ref in (slabs_ref, crossed_ref, last_ref) for k in range(ref.shape[0])]
     keep = len(slabs) - left
+    stores = []
     for i, slab in enumerate(slabs):
-        fold, total = merge.rows(slab, up, served_ref, features_ref, i, total)
+        rows = merge.rows_of(i)
+        fold, total = merge.rows(slab, up, served_ref, features_ref, rows, total)
         if i < keep:
             m_buf[i] = fold
-            merge.store(m_buf.at[i], i, i).start()
+            stores.append(merge.store(m_buf.at[i], rows, i))
+            stores[-1].start()
         else:
             left_ref[i - keep] = fold
     total_ref[...] = total
-    for i in range(keep):
-        merge.store(m_buf.at[i], i, i).wait()
-
-
-def final_kernel(start_hbm, up_ref, features_ref, served_ref, left_ref, last_ref, merged_in,
-                 total_ref, context_ref, own_weight_ref, merged, fresh_hbm, attended_hbm, start,
-                 start_sem, m_buf, out_sem, fresh_ref, attended_ref, small_sem):
+    for store in stores:
+        store.wait()
+
+
+def final_kernel(start_ref, up_ref, features_ref, served_ref, left_ref, last_ref, merged_in,
+                 total_ref, context_ref, own_weight_ref, merged, fresh_hbm, attended_hbm, m_buf,
+                 out_sem, fresh_ref, attended_ref, small_sem):
     del merged_in
     count, _, width = last_ref.shape
     left = left_ref.shape[0]
-    merge = Merge(start_hbm, start, start_sem, merged, out_sem, width)
-    first = start.shape[0] - count
+    merge = Merge(start_ref, merged, out_sem, width)
+    first = start_ref.shape[1] - count
     total = total_ref[...]
-    stores = []
+    stores = [
+        merge.store(left_ref.at[k], merge.rows_of(first - left + k), count + k)
+        for k in range(left)
+    ]
+    for store in stores:
+        store.start()
     for i in range(count):
-        fold, total = merge.rows(
-            last_ref.at[i], up_ref[...], served_ref, features_ref, first + i, total
-        )
-        if i == 0:
-            stores += [
-                merge.store(left_ref.at[k], first - left + k, count + k) for k in range(left)
-            ]
-            for store in stores:
-                store.start()
+        rows = merge.rows_of(first + i)
+        fold, total = merge.rows(last_ref.at[i], up_ref[...], served_ref, features_ref, rows, total)
         m_buf[i] = fold
-        stores.append(merge.store(m_buf.at[i], first + i, i))
+        stores.append(merge.store(m_buf.at[i], rows, i))
         stores[-1].start()
     fresh = total.astype(jnp.bfloat16)
     fresh_ref[...] = fresh
@@ -253,11 +295,9 @@
             jax.ShapeDtypeStruct((rank, cols), jnp.bfloat16),
             jax.ShapeDtypeStruct((left, width, cols), jnp.bfloat16),
         ),
-        in_specs=[HBM] + [VMEM] * 6,
+        in_specs=[VMEM] * 7,
         out_specs=(HBM, VMEM, VMEM, VMEM),
         scratch_shapes=[
-            pltpu.SMEM(start.shape, jnp.int32),
-            pltpu.SemaphoreType.DMA,
             pltpu.VMEM((count - left, width, cols), jnp.bfloat16),
             pltpu.SemaphoreType.DMA((count - left,)),
         ],
@@ -280,12 +320,10 @@
         out_shape=[
             jax.ShapeDtypeStruct(shape, jnp.bfloat16) for shape in [(depth, cols), *smalls]
         ],
-        in_specs=[HBM] + [VMEM] * 5 + [HBM] + [VMEM] * 3,
+        in_specs=[VMEM] * 6 + [HBM] + [VMEM] * 3,
         out_specs=[HBM] * 3,
         input_output_aliases={6: 0},
         scratch_shapes=[
-            pltpu.SMEM(start.shape, jnp.int32),
-            pltpu.SemaphoreType.DMA,
             pltpu.VMEM((count, width, cols), jnp.bfloat16),
             pltpu.SemaphoreType.DMA((count + left.shape[0],)),
         ]
@@ -324,20 +362,13 @@
     rank = n * per
 
     bits = [n >> i for i in range(1, n.bit_length())]
-    ways = [bits, bits[:-2] + bits[:-3:-1]]
+    ways = [bits, bits[-1:] + bits[:-1]]
 
     def exchange(x, step):
         pairs = [(2 * i + c, 2 * (i ^ ways[c][step]) + c) for i in range(n) for c in range(2)]
         return lax.ppermute(x, ("replica", "tensor"), pairs)
 
-    if cols <= width:
-        below = jnp.pad(adapter_out, ((0, -per % 8), (0, width - cols)))
-    else:
-        below = jnp.concatenate(jnp.split(adapter_out, cols // width, axis=1), axis=0)
-        below = jnp.pad(below, ((0, -below.shape[0] % 8), (0, 0)))
-    slabs = jnp.concatenate(
-        [lax.dynamic_slice_in_dim(adapter_in, core * width, width, axis=1), below], axis=0
-    )[None]
+    slabs = pack(adapter_in, adapter_out)
 
     given = in_hbm(lengths, queries, fresh_token_key, stored_keys, stored_values)
     *early, final = range(len(bits))
@@ -379,7 +410,7 @@
     source = jnp.concatenate([mine[:count], theirs[:count], mine[count:], theirs[count:]])
     half = jnp.where((jnp.arange(2 * n) // count) % 2 == 0, core, 1 - core)
     place = jnp.sum(jnp.where(owner_rank[None, :] == source[:, None], slab[None, :], 0), axis=1)
-    start = (place * full + half * width).astype(jnp.int32)
+    start = (place * full + half * width).astype(jnp.int32)[None]
 
     row = jnp.arange(rank, dtype=jnp.int32)
     row_source = replica

time: 27.6 us -> 28.7 us (1.040)
  Pallas kernels: 10.8 us -> 11.5 us
  other arithmetic: 0.99 us -> 0.31 us
  starting transfers between devices: 6.93 us -> 7.47 us
  waiting for transfers between devices: 6.8 us -> 7.2 us
    pallas_call x0 -> x1, Pallas kernels: none -> 1.51 us  [pack(): pl.pallas_call(functools.partial(pack_kernel, per), out_shape=jax.ShapeDt...]
    broadcast_in_dim x1 -> x0, other arithmetic: 0.69 us -> none  [body(): jnp.concatenate([lax.dynamic_slice_in_dim(adapter_in, core * width, width...]
    ppermute x3, starting transfers between devices: 6.79 us -> 7.33 us  [exchange(): return lax.ppermute(x, ('replica', 'tensor'), pairs)]
    pallas_call x1, Pallas kernels: 2.84 us -> 2.39 us  [merge(): pl.pallas_call(functools.partial(merge_kernel, per, left), out_shape=(jax...]
    ppermute x3, waiting for transfers between devices: 6.8 us -> 7.19 us  [exchange(): return lax.ppermute(x, ('replica', 'tensor'), pairs)]
    pallas_call x1, Pallas kernels: 2.23 us -> 1.93 us  [finish(): pl.pallas_call(final_kernel, out_shape=[jax.ShapeDtypeStruct(shape, jnp.b...]
    unnamed x8 -> x10, local copies, waits for them, and re-layouts: 0.92 us -> 0.96 us
  transfers between devices with their start and end apart: 6 -> 6, of which waited for: 3 -> 2; matrix products, arithmetic and copies ran while one was open for 2% -> 2% of each run, Pallas kernels for 31% -> 28%
where the time goes in v10:
time: 28.7 us; the launch traced here: 28.4 us
  Pallas kernels  11.5 us (40%)
  starting transfers between devices  7.47 us (26%)
  waiting for transfers between devices  7.2 us (25%)
  local copies, waits for them, and re-layouts  1.1 us (4%)
  between operations  0.78 us (3%)
  other arithmetic  0.31 us (1%)
    ppermute x3, starting transfers between devices, exchange(): return lax.ppermute(x, ('replica', 'tensor'), pairs)  7.33 us
    ppermute x3, waiting for transfers between devices, exchange(): return lax.ppermute(x, ('replica', 'tensor'), pairs)  7.19 us
    pallas_call x2, Pallas kernels, attend(): pl.pallas_call(functools.partial(attend_kernel, rows, fetch), out_shape=o...  5.7 us
    pallas_call x1, Pallas kernels, merge(): pl.pallas_call(functools.partial(merge_kernel, per, left), out_shape=(jax...  2.39 us
    pallas_call x1, Pallas kernels, finish(): pl.pallas_call(final_kernel, out_shape=[jax.ShapeDtypeStruct(shape, jnp.b...  1.93 us
    pallas_call x1, Pallas kernels, pack(): pl.pallas_call(functools.partial(pack_kernel, per), out_shape=jax.ShapeDt...  1.51 us
    unnamed x10, local copies, waits for them, and re-layouts  0.96 us
  transfers between devices with their start and end apart: 6, of which 2 were waited for; matrix products, arithmetic and copies ran while one was open for 2% of the time, Pallas kernels for 28%

profile of v10, /device:TPU:0, one launch (start us, length us, event | category | flops | bytes accessed | tf_op | source)
XLA Modules:
  0.0 28.4 jit_solution(9593737843553022188)
XLA Ops:
  0.6 0.0 copy-start.2
  0.6 0.0 copy-start.3
  0.7 1.5 %pack_slab.1.rest_0_ = bf16[1,72,512]{2,1,0:T(8,128)(2,1)} custom-call(bf16[64,1024]{1,0:T(8,128)(2,1)} %block_hbm.1, bf16[8,256]{1,0:T(8,128)(2,1)} %up_hbm.1), custom_call_target="tpu_custom_call" | custom-call | tf_op jit(solution)/shard_map/pack_slab/pallas_call | solution.py:169
  2.2 4.1 %collective-permute-start = (bf16[1,72,512]{2,1,0:T(8,128)(2,1)}, bf16[1,72,512]{2,1,0:T(8,128)(2,1)S(1)}, u32[]{:S(2)}, u32[]{:S(2)}) collective-permute-start(bf16[1,72,512]{2,1,0:T(8,128)(2,1)} %pack_slab.1.rest_0_), channel_id=1, source_target_pairs={{0,8},{1,3},{2,10},{3,1},{4,12},{5,7},{6,14},{7,5},{8,0},{9,11},{1... | collective-permute-start | bytes 221192 | tf_op jit(solution)/shard_map/ppermute | solution.py:369
  6.3 0.9 %copy-done = bf16[1,72,512]{2,1,0:T(8,128)(2,1)S(1)} copy-done((bf16[1,72,512]{2,1,0:T(8,128)(2,1)S(1)}, bf16[1,72,512]{2,1,0:T(8,128)(2,1)}, u32[]{:S(2)}) %copy-start) | copy-done | bytes 73752
  7.2 2.8 %attend_cache.2 = (f32[2,16,128]{2,1,0:T(8,128)S(1)}, f32[2,16,128]{2,1,0:T(8,128)S(1)}) custom-call(s32[4]{0:T(128)} %lengths_hbm.3, bf16[4,2048]{1,0:T(4,128)(2,1)} %q_hbm.3, bf16[4,256]{1,0:T(4,128)(2,1)} %own_k_hbm.3, bf16[4,1024,256]{2,1,0:T(8,128)(2,1)} %k_hbm.3, bf16[4,1024,256]{2,1,0:T(8,128)(2,1)} %v_hbm.3, bf16[1,72,512]{2,1,0:T(8,128)(2,1)S(1)} %copy-done), custom_call_target="tpu_custom_call" | custom-call | flops 33554432 | bytes 2097152 | tf_op jit(solution)/shard_map/attend_cache/pallas_call | solution.py:112
  10.0 0.1 collective-permute-start.3
  10.1 0.1 fusion.5
  10.1 0.1 fusion.4
  10.2 0.1 pad_add_fusion
  10.3 0.1 select_reduce_fusion
  10.4 0.0 collective-permute-done
  10.4 1.6 %collective-permute-start.1 = (bf16[2,72,512]{2,1,0:T(8,128)(2,1)S(1)}, bf16[2,72,512]{2,1,0:T(8,128)(2,1)S(1)}, u32[]{:S(2)}, u32[]{:S(2)}) collective-permute-start(bf16[2,72,512]{2,1,0:T(8,128)(2,1)S(1)} %pad_maximum_fusion.1.rest_1_), channel_id=1, source_target_pairs={{0,4},{1,9},{2,6},{3,11},{4,0},{5,13},{6,2},{7,15},{8,12},{9,1},{1... | collective-permute-start | bytes 442376 | tf_op jit(solution)/shard_map/ppermute | solution.py:369
  12.1 2.9 %attend_cache.3 = (f32[2,16,128]{2,1,0:T(8,128)S(1)}, f32[2,16,128]{2,1,0:T(8,128)S(1)}, bf16[8192,256]{1,0:T(8,128)(2,1)S(1)}) custom-call(s32[4]{0:T(128)} %lengths_hbm.3, bf16[4,2048]{1,0:T(4,128)(2,1)} %q_hbm.3, bf16[4,256]{1,0:T(4,128)(2,1)} %own_k_hbm.3, bf16[4,1024,256]{2,1,0:T(8,128)(2,1)} %k_hbm.3, bf16[4,1024,256]{2,1,0:T(8,128)(2,1)} %v_hbm.3, ...), custom_call_target="tpu_custom_call" | custom-call | flops 33554432 | bytes 2097152 | tf_op jit(solution)/shard_map/attend_cache/pallas_call | solution.py:112
  15.1 2.2 %collective-permute-done.1 = bf16[2,72,512]{2,1,0:T(8,128)(2,1)S(1)} collective-permute-done((bf16[2,72,512]{2,1,0:T(8,128)(2,1)S(1)}, bf16[2,72,512]{2,1,0:T(8,128)(2,1)S(1)}, u32[]{:S(2)}, u32[]{:S(2)}) %collective-permute-start.1) | collective-permute-done | bytes 147488 | tf_op jit(solution)/shard_map/ppermute | solution.py:369
  17.3 1.6 %collective-permute-start.2 = (bf16[4,72,512]{2,1,0:T(8,128)(2,1)S(1)}, bf16[4,72,512]{2,1,0:T(8,128)(2,1)S(1)}, u32[]{:S(2)}, u32[]{:S(2)}) collective-permute-start(bf16[4,72,512]{2,1,0:T(8,128)(2,1)S(1)} %pad_maximum_fusion.slabs_ref), channel_id=1, source_target_pairs={{0,2},{1,5},{2,0},{3,7},{4,6},{5,1},{6,4},{7,3},{8,10},{9,13},{10,... | collective-permute-start | bytes 884744 | tf_op jit(solution)/shard_map/ppermute | solution.py:369
  18.8 0.0 collective-permute-done.3
  18.9 0.1 collective-permute-start.4
  19.0 5.0 %collective-permute-done.2.last_ref = bf16[4,72,512]{2,1,0:T(8,128)(2,1)S(1)} collective-permute-done((bf16[4,72,512]{2,1,0:T(8,128)(2,1)S(1)}, bf16[4,72,512]{2,1,0:T(8,128)(2,1)S(1)}, u32[]{:S(2)}, u32[]{:S(2)}) %collective-permute-start.2) | collective-permute-done | bytes 294944 | tf_op jit(solution)/shard_map/ppermute | solution.py:369
  24.1 0.0 collective-permute-start.5
  24.1 0.0 collective-permute-done.4.crossed_ref
  24.1 2.4 %merge_blocks.1 = (bf16[8192,256]{1,0:T(8,128)(2,1)}, f32[4,256]{1,0:T(4,128)S(1)}, bf16[64,256]{1,0:T(8,128)(2,1)S(1)}, bf16[3,512,256]{2,1,0:T(8,128)(2,1)S(1)}) custom-call(s32[1,16]{1,0:T(1,128)S(1)} %fusion.2.start_ref, bf16[64,64]{1,0:T(8,128)(2,1)S(1)} %select_convert_fusion.pick_ref, bf16[4,8192]{1,0:T(4,128)(2,1)S(1)} %maximum_select_fusion.features_ref, ...), custom_call_target="tpu_custom_call" | custom-call | flops 201326592 | bytes 6291456 | tf_op jit(solution)/shard_map/merge_blocks/pallas_call | solution.py:290
  26.5 0.0 collective-permute-done.5.last_ref
  26.5 1.9 %finish_rows.1 = (bf16[8192,256]{1,0:T(8,128)(2,1)}, bf16[4,256]{1,0:T(4,128)(2,1)}, bf16[4,2048]{1,0:T(4,128)(2,1)}) custom-call(s32[1,16]{1,0:T(1,128)S(1)} %fusion.2.start_ref, bf16[64,256]{1,0:T(8,128)(2,1)S(1)} %get-tuple-element.49.up_ref, bf16[4,8192]{1,0:T(4,128)(2,1)S(1)} %maximum_select_fusion.features_ref, ...), custom_call_target="tpu_custom_call", output_to_operand_aliasing={{0}: (6, {})} | custom-call | flops 67108864 | bytes 2097152 | tf_op jit(solution)/shard_map/finish_rows/pallas_call | solution.py:318
  (15 shorter events, 0.2 us)
Async XLA Ops:
  0.6 9.3 %copy-start.2 = (bf16[4,4096]{1,0:T(4,128)(2,1)S(1)}, bf16[4,4096]{1,0:T(4,128)(2,1)}, u32[]{:S(2)}) copy-start(bf16[4,4096]{1,0:T(4,128)(2,1)} %param.10) | copy-start | bytes 98308
  0.6 9.7 %copy-start.3 = (s32[8]{0:T(128)S(1)}, s32[8]{0:T(128)}, u32[]{:S(2)}) copy-start(s32[8]{0:T(128)} %param.19) | copy-start | bytes 100
  2.2 8.2 %collective-permute-start = (bf16[1,72,512]{2,1,0:T(8,128)(2,1)}, bf16[1,72,512]{2,1,0:T(8,128)(2,1)S(1)}, u32[]{:S(2)}, u32[]{:S(2)}) collective-permute-start(bf16[1,72,512]{2,1,0:T(8,128)(2,1)} %pack_slab.1.rest_0_), channel_id=1, source_target_pairs={{0,8},{1,3},{2,10},{3,1},{4,12},{5,7},{6,14},{7,5},{8,0},{9,11},{1... | collective-permute-start | bytes 221192 | tf_op jit(solution)/shard_map/ppermute | solution.py:369
  6.3 0.9 %copy-start = (bf16[1,72,512]{2,1,0:T(8,128)(2,1)S(1)}, bf16[1,72,512]{2,1,0:T(8,128)(2,1)}, u32[]{:S(2)}) copy-start(bf16[1,72,512]{2,1,0:T(8,128)(2,1)} %pack_slab.1.rest_0_) | copy-start | bytes 221188
  7.2 3.2 %copy-start.1 = (bf16[1,72,512]{2,1,0:T(8,128)(2,1)S(1)}, bf16[1,72,512]{2,1,0:T(8,128)(2,1)}, u32[]{:S(2)}) copy-start(bf16[1,72,512]{2,1,0:T(8,128)(2,1)} %pack_slab.1.rest_0_) | copy-start | bytes 221188
  10.0 8.9 %collective-permute-start.3 = (bf16[4,4096]{1,0:T(4,128)(2,1)S(1)}, bf16[4,4096]{1,0:T(4,128)(2,1)S(1)}, u32[]{:S(2)}, u32[]{:S(2)}) collective-permute-start(bf16[4,4096]{1,0:T(4,128)(2,1)S(1)} %copy-done.2), channel_id=1, source_target_pairs={{0,1},{1,0},{2,3},{3,2},{4,5},{5,4},{6,7},{7,6},{8,9},{9,8},{10,11... | collective-permute-start | bytes 98312 | tf_op jit(solution)/shard_map/ppermute | solution.py:384
  10.4 6.8 %collective-permute-start.1 = (bf16[2,72,512]{2,1,0:T(8,128)(2,1)S(1)}, bf16[2,72,512]{2,1,0:T(8,128)(2,1)S(1)}, u32[]{:S(2)}, u32[]{:S(2)}) collective-permute-start(bf16[2,72,512]{2,1,0:T(8,128)(2,1)S(1)} %pad_maximum_fusion.1.rest_1_), channel_id=1, source_target_pairs={{0,4},{1,9},{2,6},{3,11},{4,0},{5,13},{6,2},{7,15},{8,12},{9,1},{1... | collective-permute-start | bytes 442376 | tf_op jit(solution)/shard_map/ppermute | solution.py:369
  17.3 6.8 %collective-permute-start.2 = (bf16[4,72,512]{2,1,0:T(8,128)(2,1)S(1)}, bf16[4,72,512]{2,1,0:T(8,128)(2,1)S(1)}, u32[]{:S(2)}, u32[]{:S(2)}) collective-permute-start(bf16[4,72,512]{2,1,0:T(8,128)(2,1)S(1)} %pad_maximum_fusion.slabs_ref), channel_id=1, source_target_pairs={{0,2},{1,5},{2,0},{3,7},{4,6},{5,1},{6,4},{7,3},{8,10},{9,13},{10,... | collective-permute-start | bytes 884744 | tf_op jit(solution)/shard_map/ppermute | solution.py:369
  18.9 5.2 %collective-permute-start.4 = (bf16[4,72,512]{2,1,0:T(8,128)(2,1)S(1)}, bf16[4,72,512]{2,1,0:T(8,128)(2,1)S(1)}, u32[]{:S(2)}, u32[]{:S(2)}) collective-permute-start(bf16[4,72,512]{2,1,0:T(8,128)(2,1)S(1)} %pad_maximum_fusion.slabs_ref), channel_id=1, source_target_pairs={{0,1},{1,0},{2,3},{3,2},{4,5},{5,4},{6,7},{7,6},{8,9},{9,8},{10,11... | collective-permute-start | bytes 884744 | tf_op jit(solution)/shard_map/ppermute | solution.py:398
  24.1 2.4 %collective-permute-start.5 = (bf16[4,72,512]{2,1,0:T(8,128)(2,1)S(1)}, bf16[4,72,512]{2,1,0:T(8,128)(2,1)S(1)}, u32[]{:S(2)}, u32[]{:S(2)}) collective-permute-start(bf16[4,72,512]{2,1,0:T(8,128)(2,1)S(1)} %collective-permute-done.2.last_ref), channel_id=1, source_target_pairs={{0,1},{1,0},{2,3},{3,2},{4,5},{5,4},{6,7},{7,6},{8,9},{9,8},{10,11... | collective-permute-start | bytes 884744 | tf_op jit(solution)/shard_map/ppermute | solution.py:430

commit v11 on v10

--- a/solution.py
+++ b/solution.py
@@ -9,6 +9,7 @@
 
 HEAD_SIZE = 128
 ADAPTER_SCALE = 2.0
+PANEL = 128
 
 SMEM = pl.BlockSpec(memory_space=pltpu.SMEM)
 VMEM = pl.BlockSpec(memory_space=pltpu.VMEM)
@@ -135,51 +136,6 @@
     )(*given, *([served] if fetch else []), *after)
 
 
-def pack_kernel(per, block_hbm, up_hbm, slab_ref, half_ref, up_ref, sem):
-    rank, width = half_ref.shape
-    cols = up_ref.shape[1]
-    first = pl.multiple_of(lax.axis_index("tensor") * width, width)
-    copies = [
-        pltpu.make_async_copy(block_hbm.at[:, pl.ds(first, width)], half_ref, sem.at[0]),
-        pltpu.make_async_copy(up_hbm, up_ref, sem.at[1]),
-    ]
-    for copy in copies:
-        copy.start()
-    for copy in copies:
-        copy.wait()
-    slab_ref[0, :rank] = half_ref[...]
-    up = up_ref[...].astype(jnp.float32)
-    if cols <= width:
-        below = jnp.concatenate([up, jnp.zeros((per, width - cols), jnp.float32)], axis=1)
-    else:
-        below = jnp.concatenate(
-            [up[:, i * width : (i + 1) * width] for i in range(cols // width)], axis=0
-        )
-    spare = slab_ref.shape[1] - rank - below.shape[0]
-    if spare:
-        below = jnp.concatenate([below, jnp.zeros((spare, width), jnp.float32)], axis=0)
-    slab_ref[0, rank:] = below.astype(jnp.bfloat16)
-
-
-def pack(block, up):
-    rank, full = block.shape
-    per, cols = up.shape
-    width = full // 2
-    below = -(-per * max(cols // width, 1) // 8) * 8
-    return pl.pallas_call(
-        functools.partial(pack_kernel, per),
-        out_shape=jax.ShapeDtypeStruct((1, rank + below, width), block.dtype),
-        in_specs=[HBM, HBM],
-        out_specs=VMEM,
-        scratch_shapes=[
-            pltpu.VMEM((rank, width), block.dtype),
-            pltpu.VMEM(up.shape, up.dtype),
-            pltpu.SemaphoreType.DMA((2,)),
-        ],
-        name="pack_slab",
-    )(*in_hbm(block, up))
-
-
 class Merge:
     def __init__(self, start_ref, merged, out_sem, width):
         self.start, self.merged, self.out_sem, self.width = start_ref[...], merged, out_sem, width
@@ -193,8 +149,12 @@
         return pltpu.make_async_copy(source, self.merged.at[rows], self.out_sem.at[at])
 
     def rows(self, slab, up, served_ref, features_ref, rows, total):
+        rank = up.shape[0]
+        block = jnp.concatenate(
+            [slab[i * rank : (i + 1) * rank] for i in range(self.width // PANEL)], axis=1
+        )
         update = lax.dot_general(
-            slab[: up.shape[0]], up, (((0,), (0,)), ((), ())), preferred_element_type=jnp.float32
+            block, up, (((0,), (0,)), ((), ())), preferred_element_type=jnp.float32
         )
         fold = (served_ref[rows, :].astype(jnp.float32) + update).astype(jnp.bfloat16)
         part = jnp.dot(features_ref[:, rows], fold, preferred_element_type=jnp.float32)
@@ -203,21 +163,18 @@
 
 def merge_kernel(per, left, start_ref, pick_ref, features_ref, served_ref, slabs_ref, crossed_ref,
                  last_ref, merged, total_ref, up_ref, left_ref, m_buf, out_sem):
-    width = slabs_ref.shape[2]
+    width = m_buf.shape[1]
     rank, cols = up_ref.shape
     merge = Merge(start_ref, merged, out_sem, width)
     ups = []
     for ref in (slabs_ref, last_ref):
         for k in range(ref.shape[0]):
-            below = ref[k, rank:].astype(jnp.float32)
-            if cols <= width:
-                ups.append(below[:per, :cols])
-            else:
-                ups.append(
-                    jnp.concatenate(
-                        [below[i * per : (i + 1) * per] for i in range(cols // width)], axis=1
-                    )
+            below = ref[k, rank * (width // PANEL) :].astype(jnp.float32)
+            ups.append(
+                jnp.concatenate(
+                    [below[i * per : (i + 1) * per] for i in range(cols // PANEL)], axis=1
                 )
+            )
     ups = jnp.concatenate(ups, axis=0).astype(jnp.bfloat16)
     up = jnp.dot(pick_ref[...], ups, preferred_element_type=jnp.float32).astype(jnp.bfloat16)
     up_ref[...] = up
@@ -243,7 +200,7 @@
                  total_ref, context_ref, own_weight_ref, merged, fresh_hbm, attended_hbm, m_buf,
                  out_sem, fresh_ref, attended_ref, small_sem):
     del merged_in
-    count, _, width = last_ref.shape
+    count, width = last_ref.shape[0], m_buf.shape[1]
     left = left_ref.shape[0]
     merge = Merge(start_ref, merged, out_sem, width)
     first = start_ref.shape[1] - count
@@ -284,9 +241,9 @@
 def merge(per, start, pick, features, served, slabs, crossed, last):
     left = 3
     count = slabs.shape[0] + crossed.shape[0] + last.shape[0]
-    width = slabs.shape[2]
     rank = pick.shape[0]
     depth, cols = served.shape
+    width = depth // start.shape[1]
     return pl.pallas_call(
         functools.partial(merge_kernel, per, left),
         out_shape=(
@@ -312,8 +269,9 @@
 
 
 def finish(start, up, features, served, left, last, merged, total, context, own_weight):
-    count, _, width = last.shape
+    count = last.shape[0]
     depth, cols = served.shape
+    width = depth // start.shape[1]
     smalls = [total.shape, context.shape]
     return pl.pallas_call(
         final_kernel,
@@ -339,6 +297,10 @@
     )(start, up, features, served, left, last, merged, total, context, own_weight)
 
 
+def panels(x):
+    return [x[:, i : i + PANEL] for i in range(0, x.shape[1], PANEL)]
+
+
 def body(
     hidden_in,
     queries,
@@ -362,13 +324,17 @@
     rank = n * per
 
     bits = [n >> i for i in range(1, n.bit_length())]
-    ways = [bits, bits[-1:] + bits[:-1]]
+    ways = [bits, bits[:-2] + bits[:-3:-1]]
 
     def exchange(x, step):
         pairs = [(2 * i + c, 2 * (i ^ ways[c][step]) + c) for i in range(n) for c in range(2)]
         return lax.ppermute(x, ("replica", "tensor"), pairs)
 
-    slabs = pack(adapter_in, adapter_out)
+    below = jnp.concatenate(panels(adapter_out), axis=0)
+    below = jnp.pad(below, ((0, -below.shape[0] % 8), (0, 0)))
+    block = lax.dynamic_slice_in_dim(adapter_in, core * width, width, axis=1)
+    block, below = lax.optimization_barrier((block, below))
+    slabs = jnp.concatenate([*panels(block), below], axis=0)[None]
 
     given = in_hbm(lengths, queries, fresh_token_key, stored_keys, stored_values)
     *early, final = range(len(bits))

time: 28.7 us -> 25.9 us (0.902)
  Pallas kernels: 11.5 us -> 10 us
  waiting for transfers between devices: 7.2 us -> 6.27 us
  starting transfers between devices: 7.47 us -> 7.12 us
    pallas_call x1 -> x0, Pallas kernels: 1.51 us -> none  [pack(): pl.pallas_call(functools.partial(pack_kernel, per), out_shape=jax.ShapeDt...]
    ppermute x3, waiting for transfers between devices: 7.19 us -> 6.26 us  [exchange(): return lax.ppermute(x, ('replica', 'tensor'), pairs)]
    unnamed x10 -> x12, local copies, waits for them, and re-layouts: 0.96 us -> 0.19 us
    slice x0 -> x1, local copies, waits for them, and re-layouts: none -> 0.76 us  [panels(): return [x[:, i:i + PANEL] for i in range(0, x.shape[1], PANEL)]]
    ppermute x3, starting transfers between devices: 7.33 us -> 6.98 us  [exchange(): return lax.ppermute(x, ('replica', 'tensor'), pairs)]
  transfers between devices with their start and end apart: 6 -> 6, of which waited for: 2 -> 3; matrix products, arithmetic and copies ran while one was open for 2% -> 2% of each run, Pallas kernels for 28% -> 32%
where the time goes in v11:
time: 25.9 us; the launch traced here: 25.6 us
  Pallas kernels  10 us (39%)
  starting transfers between devices  7.12 us (27%)
  waiting for transfers between devices  6.27 us (24%)
  local copies, waits for them, and re-layouts  1.11 us (4%)
  between operations  0.8 us (3%)
  other arithmetic  0.31 us (1%)
    ppermute x3, starting transfers between devices, exchange(): return lax.ppermute(x, ('replica', 'tensor'), pairs)  6.98 us
    ppermute x3, waiting for transfers between devices, exchange(): return lax.ppermute(x, ('replica', 'tensor'), pairs)  6.26 us
    pallas_call x2, Pallas kernels, attend(): pl.pallas_call(functools.partial(attend_kernel, rows, fetch), out_shape=o...  5.7 us
    pallas_call x1, Pallas kernels, merge(): pl.pallas_call(functools.partial(merge_kernel, per, left), out_shape=(jax...  2.39 us
    pallas_call x1, Pallas kernels, finish(): pl.pallas_call(final_kernel, out_shape=[jax.ShapeDtypeStruct(shape, jnp.b...  1.93 us
    slice x1, local copies, waits for them, and re-layouts, panels(): return [x[:, i:i + PANEL] for i in range(0, x.shape[1], PANEL)]  0.76 us
  transfers between devices with their start and end apart: 6, of which 3 were waited for; matrix products, arithmetic and copies ran while one was open for 2% of the time, Pallas kernels for 32%

profile of v11, /device:TPU:0, one launch (start us, length us, event | category | flops | bytes accessed | tf_op | source)
XLA Modules:
  0.0 25.6 jit_solution(3764171345066961633)
XLA Ops:
  0.6 0.0 copy-start
  0.6 0.0 copy-start.1
  0.7 0.8 %fusion.4 = (bf16[8,128]{1,0:T(8,128)(2,1)S(1)}, bf16[8,128]{1,0:T(8,128)(2,1)S(1)}) fusion(bf16[8,256]{1,0:T(8,128)(2,1)} %param.18), kind=kLoop, calls=%fused_computation.42 | loop fusion | bytes 8192 | tf_op jit(solution)/shard_map/slice | solution.py:301
  1.4 0.1 copy-done
  1.6 4.1 %collective-permute-start = (bf16[1,272,128]{2,1,0:T(8,128)(2,1)S(1)}, bf16[1,272,128]{2,1,0:T(8,128)(2,1)S(1)}, u32[]{:S(2)}, u32[]{:S(2)}) collective-permute-start(bf16[1,272,128]{2,1,0:T(8,128)(2,1)S(1)} %bitcast.13), channel_id=1, source_target_pairs={{0,8},{1,9},{2,10},{3,11},{4,12},{5,13},{6,14},{7,15},{8,0},{9,1},... | collective-permute-start | bytes 208904 | tf_op jit(solution)/shard_map/ppermute | solution.py:331
  5.7 2.8 %attend_cache.2 = (f32[2,16,128]{2,1,0:T(8,128)S(1)}, f32[2,16,128]{2,1,0:T(8,128)S(1)}) custom-call(s32[4]{0:T(128)} %lengths_hbm.3, bf16[4,2048]{1,0:T(4,128)(2,1)} %q_hbm.3, bf16[4,256]{1,0:T(4,128)(2,1)} %own_k_hbm.3, bf16[4,1024,256]{2,1,0:T(8,128)(2,1)} %k_hbm.3, bf16[4,1024,256]{2,1,0:T(8,128)(2,1)} %v_hbm.3, bf16[1,272,128]{2,1,0:T(8,128)(2,1)S(1)} %bitcast.14), custom_call_target="tpu_custom_call" | custom-call | flops 33554432 | bytes 2097152 | tf_op jit(solution)/shard_map/attend_cache/pallas_call | solution.py:113
  8.5 0.1 collective-permute-start.3
  8.6 0.1 fusion.6
  8.7 0.1 fusion.5
  8.8 0.1 pad_add_fusion
  8.8 0.1 select_reduce_fusion
  8.9 0.6 %collective-permute-done = bf16[1,272,128]{2,1,0:T(8,128)(2,1)S(1)} collective-permute-done((bf16[1,272,128]{2,1,0:T(8,128)(2,1)S(1)}, bf16[1,272,128]{2,1,0:T(8,128)(2,1)S(1)}, u32[]{:S(2)}, u32[]{:S(2)}) %collective-permute-start) | collective-permute-done | bytes 69664 | tf_op jit(solution)/shard_map/ppermute | solution.py:331
  9.5 1.1 %collective-permute-start.1 = (bf16[2,272,128]{2,1,0:T(8,128)(2,1)S(1)}, bf16[2,272,128]{2,1,0:T(8,128)(2,1)S(1)}, u32[]{:S(2)}, u32[]{:S(2)}) collective-permute-start(bf16[2,272,128]{2,1,0:T(8,128)(2,1)S(1)} %pad_maximum_fusion.1.rest_1_), channel_id=1, source_target_pairs={{0,4},{1,3},{2,6},{3,1},{4,0},{5,7},{6,2},{7,5},{8,12},{9,11},{10,... | collective-permute-start | bytes 417800 | tf_op jit(solution)/shard_map/ppermute | solution.py:331
  10.6 2.9 %attend_cache.3 = (f32[2,16,128]{2,1,0:T(8,128)S(1)}, f32[2,16,128]{2,1,0:T(8,128)S(1)}, bf16[8192,256]{1,0:T(8,128)(2,1)S(1)}) custom-call(s32[4]{0:T(128)} %lengths_hbm.3, bf16[4,2048]{1,0:T(4,128)(2,1)} %q_hbm.3, bf16[4,256]{1,0:T(4,128)(2,1)} %own_k_hbm.3, bf16[4,1024,256]{2,1,0:T(8,128)(2,1)} %k_hbm.3, bf16[4,1024,256]{2,1,0:T(8,128)(2,1)} %v_hbm.3, ...), custom_call_target="tpu_custom_call" | custom-call | flops 33554432 | bytes 2097152 | tf_op jit(solution)/shard_map/attend_cache/pallas_call | solution.py:113
  13.6 1.1 %collective-permute-done.1 = bf16[2,272,128]{2,1,0:T(8,128)(2,1)S(1)} collective-permute-done((bf16[2,272,128]{2,1,0:T(8,128)(2,1)S(1)}, bf16[2,272,128]{2,1,0:T(8,128)(2,1)S(1)}, u32[]{:S(2)}, u32[]{:S(2)}) %collective-permute-start.1) | collective-permute-done | bytes 139296 | tf_op jit(solution)/shard_map/ppermute | solution.py:331
  14.7 1.8 %collective-permute-start.2 = (bf16[4,272,128]{2,1,0:T(8,128)(2,1)S(1)}, bf16[4,272,128]{2,1,0:T(8,128)(2,1)S(1)}, u32[]{:S(2)}, u32[]{:S(2)}) collective-permute-start(bf16[4,272,128]{2,1,0:T(8,128)(2,1)S(1)} %pad_maximum_fusion.slabs_ref), channel_id=1, source_target_pairs={{0,2},{1,5},{2,0},{3,7},{4,6},{5,1},{6,4},{7,3},{8,10},{9,13},{10,... | collective-permute-start | bytes 835592 | tf_op jit(solution)/shard_map/ppermute | solution.py:331
  16.5 0.0 collective-permute-done.3
  16.5 0.1 collective-permute-start.4
  16.6 4.6 %collective-permute-done.2.last_ref = bf16[4,272,128]{2,1,0:T(8,128)(2,1)S(1)} collective-permute-done((bf16[4,272,128]{2,1,0:T(8,128)(2,1)S(1)}, bf16[4,272,128]{2,1,0:T(8,128)(2,1)S(1)}, u32[]{:S(2)}, u32[]{:S(2)}) %collective-permute-start.2) | collective-permute-done | bytes 278560 | tf_op jit(solution)/shard_map/ppermute | solution.py:331
  21.3 0.0 collective-permute-start.5
  21.3 0.0 collective-permute-done.4.crossed_ref
  21.3 2.4 %merge_blocks.1 = (bf16[8192,256]{1,0:T(8,128)(2,1)}, f32[4,256]{1,0:T(4,128)S(1)}, bf16[64,256]{1,0:T(8,128)(2,1)S(1)}, bf16[3,512,256]{2,1,0:T(8,128)(2,1)S(1)}) custom-call(s32[1,16]{1,0:T(1,128)S(1)} %fusion.2.start_ref, bf16[64,64]{1,0:T(8,128)(2,1)S(1)} %select_convert_fusion.pick_ref, bf16[4,8192]{1,0:T(4,128)(2,1)S(1)} %maximum_select_fusion.features_ref, ...), custom_call_target="tpu_custom_call" | custom-call | flops 201326592 | bytes 6291456 | tf_op jit(solution)/shard_map/merge_blocks/pallas_call | solution.py:247
  23.7 0.0 collective-permute-done.5.last_ref
  23.7 1.9 %finish_rows.1 = (bf16[8192,256]{1,0:T(8,128)(2,1)}, bf16[4,256]{1,0:T(4,128)(2,1)}, bf16[4,2048]{1,0:T(4,128)(2,1)}) custom-call(s32[1,16]{1,0:T(1,128)S(1)} %fusion.2.start_ref, bf16[64,256]{1,0:T(8,128)(2,1)S(1)} %get-tuple-element.53.up_ref, bf16[4,8192]{1,0:T(4,128)(2,1)S(1)} %maximum_select_fusion.features_ref, ...), custom_call_target="tpu_custom_call", output_to_operand_aliasing={{0}: (6, {})} | custom-call | flops 67108864 | bytes 2097152 | tf_op jit(solution)/shard_map/finish_rows/pallas_call | solution.py:276
  (20 shorter events, 0.2 us)
Async XLA Ops:
  0.6 0.9 %copy-start = (bf16[64,1024]{1,0:T(8,128)(2,1)S(1)}, bf16[64,1024]{1,0:T(8,128)(2,1)}, u32[]{:S(2)}) copy-start(bf16[64,1024]{1,0:T(8,128)(2,1)} %param.17) | copy-start | bytes 393220
  0.6 7.8 %copy-start.1 = (bf16[4,4096]{1,0:T(4,128)(2,1)S(1)}, bf16[4,4096]{1,0:T(4,128)(2,1)}, u32[]{:S(2)}) copy-start(bf16[4,4096]{1,0:T(4,128)(2,1)} %param.10) | copy-start | bytes 98308
  0.7 8.2 %copy-start.2 = (s32[8]{0:T(128)S(1)}, s32[8]{0:T(128)}, u32[]{:S(2)}) copy-start(s32[8]{0:T(128)} %param.19) | copy-start | bytes 100
  1.6 7.9 %collective-permute-start = (bf16[1,272,128]{2,1,0:T(8,128)(2,1)S(1)}, bf16[1,272,128]{2,1,0:T(8,128)(2,1)S(1)}, u32[]{:S(2)}, u32[]{:S(2)}) collective-permute-start(bf16[1,272,128]{2,1,0:T(8,128)(2,1)S(1)} %bitcast.13), channel_id=1, source_target_pairs={{0,8},{1,9},{2,10},{3,11},{4,12},{5,13},{6,14},{7,15},{8,0},{9,1},... | collective-permute-start | bytes 208904 | tf_op jit(solution)/shard_map/ppermute | solution.py:331
  8.5 8.0 %collective-permute-start.3 = (bf16[4,4096]{1,0:T(4,128)(2,1)S(1)}, bf16[4,4096]{1,0:T(4,128)(2,1)S(1)}, u32[]{:S(2)}, u32[]{:S(2)}) collective-permute-start(bf16[4,4096]{1,0:T(4,128)(2,1)S(1)} %copy-done.1), channel_id=1, source_target_pairs={{0,1},{1,0},{2,3},{3,2},{4,5},{5,4},{6,7},{7,6},{8,9},{9,8},{10,11... | collective-permute-start | bytes 98312 | tf_op jit(solution)/shard_map/ppermute | solution.py:350
  9.5 5.1 %collective-permute-start.1 = (bf16[2,272,128]{2,1,0:T(8,128)(2,1)S(1)}, bf16[2,272,128]{2,1,0:T(8,128)(2,1)S(1)}, u32[]{:S(2)}, u32[]{:S(2)}) collective-permute-start(bf16[2,272,128]{2,1,0:T(8,128)(2,1)S(1)} %pad_maximum_fusion.1.rest_1_), channel_id=1, source_target_pairs={{0,4},{1,3},{2,6},{3,1},{4,0},{5,7},{6,2},{7,5},{8,12},{9,11},{10,... | collective-permute-start | bytes 417800 | tf_op jit(solution)/shard_map/ppermute | solution.py:331
  14.7 6.6 %collective-permute-start.2 = (bf16[4,272,128]{2,1,0:T(8,128)(2,1)S(1)}, bf16[4,272,128]{2,1,0:T(8,128)(2,1)S(1)}, u32[]{:S(2)}, u32[]{:S(2)}) collective-permute-start(bf16[4,272,128]{2,1,0:T(8,128)(2,1)S(1)} %pad_maximum_fusion.slabs_ref), channel_id=1, source_target_pairs={{0,2},{1,5},{2,0},{3,7},{4,6},{5,1},{6,4},{7,3},{8,10},{9,13},{10,... | collective-permute-start | bytes 835592 | tf_op jit(solution)/shard_map/ppermute | solution.py:331
  16.5 4.8 %collective-permute-start.4 = (bf16[4,272,128]{2,1,0:T(8,128)(2,1)S(1)}, bf16[4,272,128]{2,1,0:T(8,128)(2,1)S(1)}, u32[]{:S(2)}, u32[]{:S(2)}) collective-permute-start(bf16[4,272,128]{2,1,0:T(8,128)(2,1)S(1)} %pad_maximum_fusion.slabs_ref), channel_id=1, source_target_pairs={{0,1},{1,0},{2,3},{3,2},{4,5},{5,4},{6,7},{7,6},{8,9},{9,8},{10,11... | collective-permute-start | bytes 835592 | tf_op jit(solution)/shard_map/ppermute | solution.py:364
  21.3 2.4 %collective-permute-start.5 = (bf16[4,272,128]{2,1,0:T(8,128)(2,1)S(1)}, bf16[4,272,128]{2,1,0:T(8,128)(2,1)S(1)}, u32[]{:S(2)}, u32[]{:S(2)}) collective-permute-start(bf16[4,272,128]{2,1,0:T(8,128)(2,1)S(1)} %collective-permute-done.2.last_ref), channel_id=1, source_target_pairs={{0,1},{1,0},{2,3},{3,2},{4,5},{5,4},{6,7},{7,6},{8,9},{9,8},{10,11... | collective-permute-start | bytes 835592 | tf_op jit(solution)/shard_map/ppermute | solution.py:396

commit v12 on v11

--- a/solution.py
+++ b/solution.py
@@ -338,14 +338,15 @@
 
     given = in_hbm(lengths, queries, fresh_token_key, stored_keys, stored_values)
     *early, final = range(len(bits))
-    parts = []
+    parts, images = [], []
     split = rows // 2
+    came = slabs
     for step in early:
-        came = exchange(slabs, step)
+        piece, came = came, exchange(slabs, step)
         if step == 0:
             parts.append(attend(range(split), given, after=[slabs]))
-            parts[0], hid_other, owner_rank = lax.optimization_barrier(
-                (parts[0], hidden_in, owner_rank)
+            parts[0], hid_other, owner_rank, piece = lax.optimization_barrier(
+                (parts[0], hidden_in, owner_rank, piece)
             )
             hid_other = lax.ppermute(hid_other, "tensor", swap)
             came, parts[0] = lax.optimization_barrier((came, parts[0]))
@@ -353,10 +354,13 @@
             *part, served = attend(
                 range(split, rows), given, *in_hbm(served_value_weight), [slabs]
             )
+            part, piece = lax.optimization_barrier((part, piece))
             came, part = lax.optimization_barrier((came, part))
             parts.append(part)
+        images.append(exchange(piece, final))
         slabs = jnp.concatenate([slabs, came], axis=0)
-    last = exchange(slabs, final)
+    last = exchange(came, final)
+    slabs = jnp.concatenate([slabs, *images], axis=0)
 
     features = jnp.concatenate([hidden_in, hid_other], axis=1)
     features = jnp.where(core == 0, features, jnp.concatenate([hid_other, hidden_in], axis=1))
@@ -374,7 +378,9 @@
     theirs = jnp.where(core == 0, sources[1], sources[0])
     count = slabs.shape[0]
     source = jnp.concatenate([mine[:count], theirs[:count], mine[count:], theirs[count:]])
-    half = jnp.where((jnp.arange(2 * n) // count) % 2 == 0, core, 1 - core)
+    half = jnp.concatenate(
+        [jnp.full((size,), c) for size in (count, n - count) for c in (core, 1 - core)]
+    )
     place = jnp.sum(jnp.where(owner_rank[None, :] == source[:, None], slab[None, :], 0), axis=1)
     start = (place * full + half * width).astype(jnp.int32)[None]
 

time: 25.9 us -> 25.5 us (0.985)
  waiting for transfers between devices: 6.27 us -> 3.71 us
  starting transfers between devices: 7.12 us -> 9.63 us
  Pallas kernels: 10 us -> 9.59 us
    ppermute x3 -> x5, waiting for transfers between devices: 6.26 us -> 3.37 us  [exchange(): return lax.ppermute(x, ('replica', 'tensor'), pairs)]
    ppermute x3 -> x5, starting transfers between devices: 6.98 us -> 9.48 us  [exchange(): return lax.ppermute(x, ('replica', 'tensor'), pairs)]
    pallas_call x1, Pallas kernels: 1.93 us -> 1.38 us  [finish(): pl.pallas_call(final_kernel, out_shape=[jax.ShapeDtypeStruct(shape, jnp.b...]
    ppermute x1, waiting for transfers between devices: 0.01 us -> 0.34 us  [body(): crossed = lax.ppermute(crossed, 'tensor', swap)]
  transfers between devices with their start and end apart: 6 -> 8, of which waited for: 3 -> 3; matrix products, arithmetic and copies ran while one was open for 2% -> 2% of each run, Pallas kernels for 32% -> 32%
where the time goes in v12:
time: 25.5 us; the launch traced here: 25.3 us
  starting transfers between devices  9.63 us (38%)
  Pallas kernels  9.59 us (38%)
  waiting for transfers between devices  3.71 us (15%)
  local copies, waits for them, and re-layouts  1.19 us (5%)
  between operations  0.83 us (3%)
  other arithmetic  0.34 us (1%)
    ppermute x5, starting transfers between devices, exchange(): return lax.ppermute(x, ('replica', 'tensor'), pairs)  9.48 us
    pallas_call x2, Pallas kernels, attend(): pl.pallas_call(functools.partial(attend_kernel, rows, fetch), out_shape=o...  5.7 us
    ppermute x5, waiting for transfers between devices, exchange(): return lax.ppermute(x, ('replica', 'tensor'), pairs)  3.37 us
    pallas_call x1, Pallas kernels, merge(): pl.pallas_call(functools.partial(merge_kernel, per, left), out_shape=(jax...  2.51 us
    pallas_call x1, Pallas kernels, finish(): pl.pallas_call(final_kernel, out_shape=[jax.ShapeDtypeStruct(shape, jnp.b...  1.38 us
    slice x1, local copies, waits for them, and re-layouts, panels(): return [x[:, i:i + PANEL] for i in range(0, x.shape[1], PANEL)]  0.76 us
  transfers between devices with their start and end apart: 8, of which 3 were waited for; matrix products, arithmetic and copies ran while one was open for 2% of the time, Pallas kernels for 32%

profile of v12, /device:TPU:0, one launch (start us, length us, event | category | flops | bytes accessed | tf_op | source)
XLA Modules:
  0.0 25.3 jit_solution(7538358393270208236)
XLA Ops:
  0.6 0.0 copy-start
  0.7 0.8 %fusion.3 = (bf16[8,128]{1,0:T(8,128)(2,1)S(1)}, bf16[8,128]{1,0:T(8,128)(2,1)S(1)}) fusion(bf16[8,256]{1,0:T(8,128)(2,1)} %param.18), kind=kLoop, calls=%fused_computation.40 | loop fusion | bytes 8192 | tf_op jit(solution)/shard_map/slice | solution.py:301
  1.4 0.1 copy-done
  1.6 4.1 %collective-permute-start = (bf16[1,272,128]{2,1,0:T(8,128)(2,1)S(1)}, bf16[1,272,128]{2,1,0:T(8,128)(2,1)S(1)}, u32[]{:S(2)}, u32[]{:S(2)}) collective-permute-start(bf16[1,272,128]{2,1,0:T(8,128)(2,1)S(1)} %bitcast.32), channel_id=1, source_target_pairs={{0,8},{1,9},{2,10},{3,11},{4,12},{5,13},{6,14},{7,15},{8,0},{9,1},... | collective-permute-start | bytes 208904 | tf_op jit(solution)/shard_map/ppermute | solution.py:331
  5.7 2.8 %attend_cache.2 = (f32[2,16,128]{2,1,0:T(8,128)S(1)}, f32[2,16,128]{2,1,0:T(8,128)S(1)}) custom-call(s32[4]{0:T(128)} %lengths_hbm.3, bf16[4,2048]{1,0:T(4,128)(2,1)} %q_hbm.3, bf16[4,256]{1,0:T(4,128)(2,1)} %own_k_hbm.3, bf16[4,1024,256]{2,1,0:T(8,128)(2,1)} %k_hbm.3, bf16[4,1024,256]{2,1,0:T(8,128)(2,1)} %v_hbm.3, bf16[1,272,128]{2,1,0:T(8,128)(2,1)S(1)} %bitcast.33), custom_call_target="tpu_custom_call" | custom-call | flops 33554432 | bytes 2097152 | tf_op jit(solution)/shard_map/attend_cache/pallas_call | solution.py:113
  8.5 0.1 collective-permute-start.5
  8.6 1.6 %collective-permute-start.3 = (bf16[1,272,128]{2,1,0:T(8,128)(2,1)S(1)}, bf16[1,272,128]{2,1,0:T(8,128)(2,1)S(1)}, u32[]{:S(2)}, u32[]{:S(2)}) collective-permute-start(bf16[1,272,128]{2,1,0:T(8,128)(2,1)S(1)} %bitcast.34), channel_id=1, source_target_pairs={{0,2},{1,5},{2,0},{3,7},{4,6},{5,1},{6,4},{7,3},{8,10},{9,13},{10,... | collective-permute-start | bytes 208904 | tf_op jit(solution)/shard_map/ppermute | solution.py:331
  10.2 0.1 slice.39
  10.2 0.1 slice.38
  10.3 0.1 pad_add_fusion
  10.4 0.1 select_reduce_fusion
  10.5 0.0 collective-permute-done
  10.5 1.6 %collective-permute-start.1 = (bf16[2,272,128]{2,1,0:T(8,128)(2,1)S(1)}, bf16[2,272,128]{2,1,0:T(8,128)(2,1)S(1)}, u32[]{:S(2)}, u32[]{:S(2)}) collective-permute-start(bf16[2,272,128]{2,1,0:T(8,128)(2,1)S(1)} %pad_maximum_fusion.rest_1_), channel_id=1, source_target_pairs={{0,4},{1,3},{2,6},{3,1},{4,0},{5,7},{6,2},{7,5},{8,12},{9,11},{10,... | collective-permute-start | bytes 417800 | tf_op jit(solution)/shard_map/ppermute | solution.py:331
  12.2 0.0 collective-permute-done.5
  12.2 2.9 %attend_cache.3 = (f32[2,16,128]{2,1,0:T(8,128)S(1)}, f32[2,16,128]{2,1,0:T(8,128)S(1)}, bf16[8192,256]{1,0:T(8,128)(2,1)S(1)}) custom-call(s32[4]{0:T(128)} %lengths_hbm.3, bf16[4,2048]{1,0:T(4,128)(2,1)} %q_hbm.3, bf16[4,256]{1,0:T(4,128)(2,1)} %own_k_hbm.3, bf16[4,1024,256]{2,1,0:T(8,128)(2,1)} %k_hbm.3, bf16[4,1024,256]{2,1,0:T(8,128)(2,1)} %v_hbm.3, ...), custom_call_target="tpu_custom_call" | custom-call | flops 33554432 | bytes 2097152 | tf_op jit(solution)/shard_map/attend_cache/pallas_call | solution.py:113
  15.2 0.6 %collective-permute-start.4 = (bf16[1,272,128]{2,1,0:T(8,128)(2,1)S(1)}, bf16[1,272,128]{2,1,0:T(8,128)(2,1)S(1)}, u32[]{:S(2)}, u32[]{:S(2)}) collective-permute-start(bf16[1,272,128]{2,1,0:T(8,128)(2,1)S(1)} %collective-permute-done), channel_id=1, source_target_pairs={{0,2},{1,5},{2,0},{3,7},{4,6},{5,1},{6,4},{7,3},{8,10},{9,13},{10,... | collective-permute-start | bytes 208904 | tf_op jit(solution)/shard_map/ppermute | solution.py:331
  15.8 1.6 %collective-permute-start.2 = (bf16[2,272,128]{2,1,0:T(8,128)(2,1)S(1)}, bf16[2,272,128]{2,1,0:T(8,128)(2,1)S(1)}, u32[]{:S(2)}, u32[]{:S(2)}) collective-permute-start(bf16[2,272,128]{2,1,0:T(8,128)(2,1)S(1)} %collective-permute-done.1), channel_id=1, source_target_pairs={{0,2},{1,5},{2,0},{3,7},{4,6},{5,1},{6,4},{7,3},{8,10},{9,13},{10,... | collective-permute-start | bytes 417800 | tf_op jit(solution)/shard_map/ppermute | solution.py:331
  17.4 2.1 %collective-permute-done.4 = bf16[1,272,128]{2,1,0:T(8,128)(2,1)S(1)} collective-permute-done((bf16[1,272,128]{2,1,0:T(8,128)(2,1)S(1)}, bf16[1,272,128]{2,1,0:T(8,128)(2,1)S(1)}, u32[]{:S(2)}, u32[]{:S(2)}) %collective-permute-start.4) | collective-permute-done | bytes 69664 | tf_op jit(solution)/shard_map/ppermute | solution.py:331
  19.6 0.1 collective-permute-start.6
  19.7 0.1 fusion.2.start_ref
  19.8 1.2 %collective-permute-done.2.last_ref = bf16[2,272,128]{2,1,0:T(8,128)(2,1)S(1)} collective-permute-done((bf16[2,272,128]{2,1,0:T(8,128)(2,1)S(1)}, bf16[2,272,128]{2,1,0:T(8,128)(2,1)S(1)}, u32[]{:S(2)}, u32[]{:S(2)}) %collective-permute-start.2) | collective-permute-done | bytes 139296 | tf_op jit(solution)/shard_map/ppermute | solution.py:331
  21.0 0.3 %collective-permute-done.6.crossed_ref = bf16[6,272,128]{2,1,0:T(8,128)(2,1)S(1)} collective-permute-done((bf16[6,272,128]{2,1,0:T(8,128)(2,1)S(1)}, bf16[6,272,128]{2,1,0:T(8,128)(2,1)S(1)}, u32[]{:S(2)}, u32[]{:S(2)}) %collective-permute-start.6) | collective-permute-done | bytes 417824 | tf_op jit(solution)/shard_map/ppermute | solution.py:368
  21.4 2.5 %merge_blocks.1 = (bf16[8192,256]{1,0:T(8,128)(2,1)}, f32[4,256]{1,0:T(4,128)S(1)}, bf16[64,256]{1,0:T(8,128)(2,1)S(1)}, bf16[3,512,256]{2,1,0:T(8,128)(2,1)S(1)}) custom-call(s32[1,16]{1,0:T(1,128)S(1)} %fusion.2.start_ref, bf16[64,64]{1,0:T(8,128)(2,1)S(1)} %select_convert_fusion.pick_ref, bf16[4,8192]{1,0:T(4,128)(2,1)S(1)} %maximum_select_fusion.features_ref, ...), custom_call_target="tpu_custom_call" | custom-call | flops 234881024 | bytes 7340032 | tf_op jit(solution)/shard_map/merge_blocks/pallas_call | solution.py:247
  23.9 1.4 %finish_rows.1 = (bf16[8192,256]{1,0:T(8,128)(2,1)}, bf16[4,256]{1,0:T(4,128)(2,1)}, bf16[4,2048]{1,0:T(4,128)(2,1)}) custom-call(s32[1,16]{1,0:T(1,128)S(1)} %fusion.2.start_ref, bf16[64,256]{1,0:T(8,128)(2,1)S(1)} %get-tuple-element.61.up_ref, bf16[4,8192]{1,0:T(4,128)(2,1)S(1)} %maximum_select_fusion.features_ref, ...), custom_call_target="tpu_custom_call", output_to_operand_aliasing={{0}: (6, {})} | custom-call | flops 33554432 | bytes 1048576 | tf_op jit(solution)/shard_map/finish_rows/pallas_call | solution.py:276
  (32 shorter events, 0.3 us)
Async XLA Ops:
  0.6 0.9 %copy-start = (bf16[64,1024]{1,0:T(8,128)(2,1)S(1)}, bf16[64,1024]{1,0:T(8,128)(2,1)}, u32[]{:S(2)}) copy-start(bf16[64,1024]{1,0:T(8,128)(2,1)} %param.17) | copy-start | bytes 393220
  0.6 7.8 %copy-start.1 = (bf16[4,4096]{1,0:T(4,128)(2,1)S(1)}, bf16[4,4096]{1,0:T(4,128)(2,1)}, u32[]{:S(2)}) copy-start(bf16[4,4096]{1,0:T(4,128)(2,1)} %param.10) | copy-start | bytes 98308
  0.7 9.8 %copy-start.2 = (s32[8]{0:T(128)S(1)}, s32[8]{0:T(128)}, u32[]{:S(2)}) copy-start(s32[8]{0:T(128)} %param.19) | copy-start | bytes 100
  1.6 8.9 %collective-permute-start = (bf16[1,272,128]{2,1,0:T(8,128)(2,1)S(1)}, bf16[1,272,128]{2,1,0:T(8,128)(2,1)S(1)}, u32[]{:S(2)}, u32[]{:S(2)}) collective-permute-start(bf16[1,272,128]{2,1,0:T(8,128)(2,1)S(1)} %bitcast.32), channel_id=1, source_target_pairs={{0,8},{1,9},{2,10},{3,11},{4,12},{5,13},{6,14},{7,15},{8,0},{9,1},... | collective-permute-start | bytes 208904 | tf_op jit(solution)/shard_map/ppermute | solution.py:331
  8.5 3.7 %collective-permute-start.5 = (bf16[4,4096]{1,0:T(4,128)(2,1)S(1)}, bf16[4,4096]{1,0:T(4,128)(2,1)S(1)}, u32[]{:S(2)}, u32[]{:S(2)}) collective-permute-start(bf16[4,4096]{1,0:T(4,128)(2,1)S(1)} %copy-done.1), channel_id=1, source_target_pairs={{0,1},{1,0},{2,3},{3,2},{4,5},{5,4},{6,7},{7,6},{8,9},{9,8},{10,11... | collective-permute-start | bytes 98312 | tf_op jit(solution)/shard_map/ppermute | solution.py:351
  8.6 8.8 %collective-permute-start.3 = (bf16[1,272,128]{2,1,0:T(8,128)(2,1)S(1)}, bf16[1,272,128]{2,1,0:T(8,128)(2,1)S(1)}, u32[]{:S(2)}, u32[]{:S(2)}) collective-permute-start(bf16[1,272,128]{2,1,0:T(8,128)(2,1)S(1)} %bitcast.34), channel_id=1, source_target_pairs={{0,2},{1,5},{2,0},{3,7},{4,6},{5,1},{6,4},{7,3},{8,10},{9,13},{10,... | collective-permute-start | bytes 208904 | tf_op jit(solution)/shard_map/ppermute | solution.py:331
  10.5 5.2 %collective-permute-start.1 = (bf16[2,272,128]{2,1,0:T(8,128)(2,1)S(1)}, bf16[2,272,128]{2,1,0:T(8,128)(2,1)S(1)}, u32[]{:S(2)}, u32[]{:S(2)}) collective-permute-start(bf16[2,272,128]{2,1,0:T(8,128)(2,1)S(1)} %pad_maximum_fusion.rest_1_), channel_id=1, source_target_pairs={{0,4},{1,3},{2,6},{3,1},{4,0},{5,7},{6,2},{7,5},{8,12},{9,11},{10,... | collective-permute-start | bytes 417800 | tf_op jit(solution)/shard_map/ppermute | solution.py:331
  15.2 4.4 %collective-permute-start.4 = (bf16[1,272,128]{2,1,0:T(8,128)(2,1)S(1)}, bf16[1,272,128]{2,1,0:T(8,128)(2,1)S(1)}, u32[]{:S(2)}, u32[]{:S(2)}) collective-permute-start(bf16[1,272,128]{2,1,0:T(8,128)(2,1)S(1)} %collective-permute-done), channel_id=1, source_target_pairs={{0,2},{1,5},{2,0},{3,7},{4,6},{5,1},{6,4},{7,3},{8,10},{9,13},{10,... | collective-permute-start | bytes 208904 | tf_op jit(solution)/shard_map/ppermute | solution.py:331
  15.8 5.3 %collective-permute-start.2 = (bf16[2,272,128]{2,1,0:T(8,128)(2,1)S(1)}, bf16[2,272,128]{2,1,0:T(8,128)(2,1)S(1)}, u32[]{:S(2)}, u32[]{:S(2)}) collective-permute-start(bf16[2,272,128]{2,1,0:T(8,128)(2,1)S(1)} %collective-permute-done.1), channel_id=1, source_target_pairs={{0,2},{1,5},{2,0},{3,7},{4,6},{5,1},{6,4},{7,3},{8,10},{9,13},{10,... | collective-permute-start | bytes 417800 | tf_op jit(solution)/shard_map/ppermute | solution.py:331
  19.6 1.8 %collective-permute-start.6 = (bf16[6,272,128]{2,1,0:T(8,128)(2,1)S(1)}, bf16[6,272,128]{2,1,0:T(8,128)(2,1)S(1)}, u32[]{:S(2)}, u32[]{:S(2)}) collective-permute-start(bf16[6,272,128]{2,1,0:T(8,128)(2,1)S(1)} %constant_dynamic-update-slice_fusion.5.slabs_ref), channel_id=1, source_target_pairs={{0,1},{1,0},{2,3},{3,2},{4,5},{5,4},{6,7},{7,6},{8,9},{9,8},{10,11... | collective-permute-start | bytes 1253384 | tf_op jit(solution)/shard_map/ppermute | solution.py:368
  21.0 2.9 %collective-permute-start.7 = (bf16[2,272,128]{2,1,0:T(8,128)(2,1)S(1)}, bf16[2,272,128]{2,1,0:T(8,128)(2,1)S(1)}, u32[]{:S(2)}, u32[]{:S(2)}) collective-permute-start(bf16[2,272,128]{2,1,0:T(8,128)(2,1)S(1)} %collective-permute-done.2.last_ref), channel_id=1, source_target_pairs={{0,1},{1,0},{2,3},{3,2},{4,5},{5,4},{6,7},{7,6},{8,9},{9,8},{10,11... | collective-permute-start | bytes 417800 | tf_op jit(solution)/shard_map/ppermute | solution.py:402

commit v13 on v11

--- a/solution.py
+++ b/solution.py
@@ -136,6 +136,21 @@
     )(*given, *([served] if fetch else []), *after)
 
 
+def gate_kernel(x_ref, after, out_ref):
+    del after
+    out_ref[...] = x_ref[...]
+
+
+def gate(x, after):
+    return pl.pallas_call(
+        gate_kernel,
+        out_shape=jax.ShapeDtypeStruct(x.shape, x.dtype),
+        in_specs=[VMEM, pl.BlockSpec(memory_space=pl.ANY)],
+        out_specs=VMEM,
+        name="gate_rows",
+    )(x, after)
+
+
 class Merge:
     def __init__(self, start_ref, merged, out_sem, width):
         self.start, self.merged, self.out_sem, self.width = start_ref[...], merged, out_sem, width
@@ -179,7 +194,8 @@
     up = jnp.dot(pick_ref[...], ups, preferred_element_type=jnp.float32).astype(jnp.bfloat16)
     up_ref[...] = up
     total = jnp.zeros(total_ref.shape, jnp.float32)
-    slabs = [ref.at[k] for ref in (slabs_ref, crossed_ref, last_ref) for k in range(ref.shape[0])]
+    refs = (slabs_ref, last_ref, crossed_ref)
+    slabs = [ref.at[k] for ref in refs for k in range(ref.shape[0])]
     keep = len(slabs) - left
     stores = []
     for i, slab in enumerate(slabs):
@@ -337,31 +353,27 @@
     slabs = jnp.concatenate([*panels(block), below], axis=0)[None]
 
     given = in_hbm(lengths, queries, fresh_token_key, stored_keys, stored_values)
-    *early, final = range(len(bits))
-    parts = []
-    split = rows // 2
+    *early, first, second, third = range(len(bits))
     for step in early:
-        came = exchange(slabs, step)
-        if step == 0:
-            parts.append(attend(range(split), given, after=[slabs]))
-            parts[0], hid_other, owner_rank = lax.optimization_barrier(
-                (parts[0], hidden_in, owner_rank)
-            )
-            hid_other = lax.ppermute(hid_other, "tensor", swap)
-            came, parts[0] = lax.optimization_barrier((came, parts[0]))
-        elif step == 1:
-            *part, served = attend(
-                range(split, rows), given, *in_hbm(served_value_weight), [slabs]
-            )
-            came, part = lax.optimization_barrier((came, part))
-            parts.append(part)
-        slabs = jnp.concatenate([slabs, came], axis=0)
-    last = exchange(slabs, final)
-
+        slabs = jnp.concatenate([slabs, exchange(slabs, step)], axis=0)
+
+    split = rows - rows // 4
+    came = exchange(slabs, first)
+    ahead = exchange(slabs, second)
+    parts = [attend(range(split), given, after=[slabs])]
+    parts[0], hid_other = lax.optimization_barrier((parts[0], hidden_in))
+    hid_other = lax.ppermute(hid_other, "tensor", swap)
+    came, ahead, parts[0] = lax.optimization_barrier((came, ahead, parts[0]))
+    slabs = jnp.concatenate([slabs, came, ahead], axis=0)
+    came = exchange(came, second)
+    images = exchange(slabs, third)
+    *part, served = attend(range(split, rows), given, *in_hbm(served_value_weight), [slabs])
+    came, part, owner_rank = lax.optimization_barrier((came, part, owner_rank))
+    parts.append(part)
+    last = exchange(came, third)
+    slabs = jnp.concatenate([slabs, came], axis=0)
     features = jnp.concatenate([hidden_in, hid_other], axis=1)
     features = jnp.where(core == 0, features, jnp.concatenate([hid_other, hidden_in], axis=1))
-    crossed, features = lax.optimization_barrier((slabs, features))
-    crossed = lax.ppermute(crossed, "tensor", swap)
 
     slab = jnp.arange(n, dtype=jnp.int32)
     sources = []
@@ -372,9 +384,8 @@
         sources.append(source)
     mine = jnp.where(core == 0, sources[0], sources[1])
     theirs = jnp.where(core == 0, sources[1], sources[0])
-    count = slabs.shape[0]
-    source = jnp.concatenate([mine[:count], theirs[:count], mine[count:], theirs[count:]])
-    half = jnp.where((jnp.arange(2 * n) // count) % 2 == 0, core, 1 - core)
+    source = jnp.concatenate([mine, theirs])
+    half = jnp.concatenate([jnp.full((n,), core), jnp.full((n,), 1 - core)])
     place = jnp.sum(jnp.where(owner_rank[None, :] == source[:, None], slab[None, :], 0), axis=1)
     start = (place * full + half * width).astype(jnp.int32)[None]
 
@@ -390,9 +401,13 @@
     context, own_weight = (
         jnp.concatenate(pair, axis=0).reshape(queries.shape) for pair in zip(*parts)
     )
-    last, start, pick, context, own_weight = lax.optimization_barrier(
-        (last, start, pick, context, own_weight)
-    )
+    crossed, start, features = lax.optimization_barrier((slabs, start, features))
+    crossed = lax.ppermute(crossed, "tensor", swap)
+    start = gate(start, images)
+    last, start, pick, context, own_weight, features, crossed = lax.optimization_barrier(
+        (last, start, pick, context, own_weight, features, crossed)
+    )
+    last = jnp.concatenate([images, last], axis=0)
     last_crossed = lax.ppermute(last, "tensor", swap)
     merged, total, up, left = merge(per, start, pick, features, served, slabs, crossed, last)
     return tuple(

time: 25.9 us -> 32.1 us (1.24)
  local copies, waits for them, and re-layouts: 1.11 us -> 7.46 us
  waiting for transfers between devices: 6.27 us -> 2.03 us
  Pallas kernels: 10 us -> 11.8 us
  starting transfers between devices: 7.12 us -> 8.87 us
  other arithmetic: 0.31 us -> 0.83 us
    unnamed x12 -> x21, local copies, waits for them, and re-layouts: 0.19 us -> 6.7 us
    ppermute x3 -> x5, waiting for transfers between devices: 6.26 us -> 0.95 us  [exchange(): return lax.ppermute(x, ('replica', 'tensor'), pairs)]
    ppermute x3 -> x5, starting transfers between devices: 6.98 us -> 8.35 us  [exchange(): return lax.ppermute(x, ('replica', 'tensor'), pairs)]
    pallas_call x0 -> x1, Pallas kernels: none -> 1.17 us  [gate(): pl.pallas_call(gate_kernel, out_shape=jax.ShapeDtypeStruct(x.shape, x.dty...]
    ppermute x1, waiting for transfers between devices: 0.01 us -> 1.07 us  [body(): hid_other = lax.ppermute(hid_other, 'tensor', swap)]
    pallas_call x2, Pallas kernels: 5.7 us -> 6.37 us  [attend(): pl.pallas_call(functools.partial(attend_kernel, rows, fetch), out_shape=o...]
    broadcast_in_dim x0 -> x1, other arithmetic: none -> 0.52 us  [body(): start = (place * full + half * width).astype(jnp.int32)[None]]
    ppermute x1, starting transfers between devices: 0.01 us -> 0.44 us  [body(): last_crossed = lax.ppermute(last, 'tensor', swap)]
  transfers between devices with their start and end apart: 6 -> 8, of which waited for: 3 -> 2; matrix products, arithmetic and copies ran while one was open for 2% -> 6% of each run, Pallas kernels for 32% -> 31%
where the time goes in v13:
time: 32.1 us; the launch traced here: 31.9 us
  Pallas kernels  11.8 us (37%)
  starting transfers between devices  8.87 us (28%)
  local copies, waits for them, and re-layouts  7.46 us (23%)
  waiting for transfers between devices  2.03 us (6%)
  between operations  0.84 us (3%)
  other arithmetic  0.83 us (3%)
    ppermute x5, starting transfers between devices, exchange(): return lax.ppermute(x, ('replica', 'tensor'), pairs)  8.35 us
    unnamed x21, local copies, waits for them, and re-layouts  6.7 us
    pallas_call x2, Pallas kernels, attend(): pl.pallas_call(functools.partial(attend_kernel, rows, fetch), out_shape=o...  6.37 us
    pallas_call x1, Pallas kernels, merge(): pl.pallas_call(functools.partial(merge_kernel, per, left), out_shape=(jax...  2.37 us
    pallas_call x1, Pallas kernels, finish(): pl.pallas_call(final_kernel, out_shape=[jax.ShapeDtypeStruct(shape, jnp.b...  1.93 us
    pallas_call x1, Pallas kernels, gate(): pl.pallas_call(gate_kernel, out_shape=jax.ShapeDtypeStruct(x.shape, x.dty...  1.17 us
    ppermute x1, waiting for transfers between devices, body(): hid_other = lax.ppermute(hid_other, 'tensor', swap)  1.07 us
    ppermute x5, waiting for transfers between devices, exchange(): return lax.ppermute(x, ('replica', 'tensor'), pairs)  0.95 us
  transfers between devices with their start and end apart: 8, of which 2 were waited for; matrix products, arithmetic and copies ran while one was open for 6% of the time, Pallas kernels for 31%

profile of v13, /device:TPU:0, one launch (start us, length us, event | category | flops | bytes accessed | tf_op | source)
XLA Modules:
  0.0 31.9 jit_solution(8081952166678943370)
XLA Ops:
  0.7 0.7 %fusion.1 = (bf16[8,128]{1,0:T(8,128)(2,1)S(1)}, bf16[8,128]{1,0:T(8,128)(2,1)S(1)}) fusion(bf16[8,256]{1,0:T(8,128)(2,1)} %param.18), kind=kLoop, calls=%fused_computation.34 | loop fusion | bytes 8192 | tf_op jit(solution)/shard_map/slice | solution.py:317
  1.4 0.1 copy-done
  1.6 3.1 %collective-permute-start.1 = (bf16[1,272,128]{2,1,0:T(8,128)(2,1)S(1)}, bf16[1,272,128]{2,1,0:T(8,128)(2,1)S(1)}, u32[]{:S(2)}, u32[]{:S(2)}) collective-permute-start(bf16[1,272,128]{2,1,0:T(8,128)(2,1)S(1)} %bitcast.13), channel_id=1, source_target_pairs={{0,4},{1,3},{2,6},{3,1},{4,0},{5,7},{6,2},{7,5},{8,12},{9,11},{10,... | collective-permute-start | bytes 208904 | tf_op jit(solution)/shard_map/ppermute | solution.py:347
  4.7 2.6 %collective-permute-start = (bf16[1,272,128]{2,1,0:T(8,128)(2,1)S(1)}, bf16[1,272,128]{2,1,0:T(8,128)(2,1)S(1)}, u32[]{:S(2)}, u32[]{:S(2)}) collective-permute-start(bf16[1,272,128]{2,1,0:T(8,128)(2,1)S(1)} %bitcast.14), channel_id=1, source_target_pairs={{0,8},{1,9},{2,10},{3,11},{4,12},{5,13},{6,14},{7,15},{8,0},{9,1},... | collective-permute-start | bytes 208904 | tf_op jit(solution)/shard_map/ppermute | solution.py:347
  7.3 3.8 %attend_cache.2 = (f32[3,16,128]{2,1,0:T(8,128)S(1)}, f32[3,16,128]{2,1,0:T(8,128)S(1)}) custom-call(s32[4]{0:T(128)} %lengths_hbm.3, bf16[4,2048]{1,0:T(4,128)(2,1)} %q_hbm.3, bf16[4,256]{1,0:T(4,128)(2,1)} %own_k_hbm.3, bf16[4,1024,256]{2,1,0:T(8,128)(2,1)} %k_hbm.3, bf16[4,1024,256]{2,1,0:T(8,128)(2,1)} %v_hbm.3, bf16[1,272,128]{2,1,0:T(8,128)(2,1)S(1)} %bitcast.15), custom_call_target="tpu_custom_call" | custom-call | flops 50331648 | bytes 3145728 | tf_op jit(solution)/shard_map/attend_cache/pallas_call | solution.py:113
  11.1 0.1 collective-permute-start.4
  11.2 0.1 pad_add_fusion
  11.3 1.1 %collective-permute-done.4 = bf16[4,4096]{1,0:T(4,128)(2,1)S(1)} collective-permute-done((bf16[4,4096]{1,0:T(4,128)(2,1)S(1)}, bf16[4,4096]{1,0:T(4,128)(2,1)S(1)}, u32[]{:S(2)}, u32[]{:S(2)}) %collective-permute-start.4) | collective-permute-done | bytes 32800 | tf_op jit(solution)/shard_map/ppermute | solution.py:365
  12.4 0.5 %collective-permute-start.2 = (bf16[1,272,128]{2,1,0:T(8,128)(2,1)S(1)}, bf16[1,272,128]{2,1,0:T(8,128)(2,1)S(1)}, u32[]{:S(2)}, u32[]{:S(2)}) collective-permute-start(bf16[1,272,128]{2,1,0:T(8,128)(2,1)S(1)} %collective-permute-done), channel_id=1, source_target_pairs={{0,4},{1,3},{2,6},{3,1},{4,0},{5,7},{6,2},{7,5},{8,12},{9,11},{10,... | collective-permute-start | bytes 208904 | tf_op jit(solution)/shard_map/ppermute | solution.py:347
  13.0 1.6 %collective-permute-start.5 = (bf16[3,272,128]{2,1,0:T(8,128)(2,1)S(1)}, bf16[3,272,128]{2,1,0:T(8,128)(2,1)S(1)}, u32[]{:S(2)}, u32[]{:S(2)}) collective-permute-start(bf16[3,272,128]{2,1,0:T(8,128)(2,1)S(1)} %pad_maximum_fusion.1.rest_1_), channel_id=1, source_target_pairs={{0,2},{1,5},{2,0},{3,7},{4,6},{5,1},{6,4},{7,3},{8,10},{9,13},{10,... | collective-permute-start | bytes 626696 | tf_op jit(solution)/shard_map/ppermute | solution.py:347
  14.6 2.6 %attend_cache.3 = (f32[1,16,128]{2,1,0:T(8,128)S(1)}, f32[1,16,128]{2,1,0:T(8,128)S(1)}, bf16[8192,256]{1,0:T(8,128)(2,1)S(1)}) custom-call(s32[4]{0:T(128)} %lengths_hbm.3, bf16[4,2048]{1,0:T(4,128)(2,1)} %q_hbm.3, bf16[4,256]{1,0:T(4,128)(2,1)} %own_k_hbm.3, bf16[4,1024,256]{2,1,0:T(8,128)(2,1)} %k_hbm.3, bf16[4,1024,256]{2,1,0:T(8,128)(2,1)} %v_hbm.3, ...), custom_call_target="tpu_custom_call" | custom-call | flops 16777216 | bytes 1048576 | tf_op jit(solution)/shard_map/attend_cache/pallas_call | solution.py:113
  17.2 2.0 %copy-done.1 = bf16[8192,256]{1,0:T(8,128)(2,1)} copy-done((bf16[8192,256]{1,0:T(8,128)(2,1)}, bf16[8192,256]{1,0:T(8,128)(2,1)S(1)}, u32[]{:S(2)}) %copy-start.1) | copy-done | bytes 4194328
  19.2 0.1 select_reduce_fusion
  19.3 0.5 %add_bitcast_fusion.x_ref = s32[1,16]{1,0:T(1,128)} fusion(s32[8]{0:T(128)S(1)} %broadcast_in_dim.38, s32[]{:T(128)S(6)} %sub.17, s32[16]{0:T(128)S(1)} %select_reduce_fusion), kind=kLoop, calls=%fused_computation.27 | loop fusion | flops 48 | bytes 164 | tf_op jit(solution)/shard_map/broadcast_in_dim | solution.py:390
  19.9 0.6 %collective-permute-start.3 = (bf16[1,272,128]{2,1,0:T(8,128)(2,1)S(1)}, bf16[1,272,128]{2,1,0:T(8,128)(2,1)S(1)}, u32[]{:S(2)}, u32[]{:S(2)}) collective-permute-start(bf16[1,272,128]{2,1,0:T(8,128)(2,1)S(1)} %collective-permute-done.2), channel_id=1, source_target_pairs={{0,2},{1,5},{2,0},{3,7},{4,6},{5,1},{6,4},{7,3},{8,10},{9,13},{10,... | collective-permute-start | bytes 208904 | tf_op jit(solution)/shard_map/ppermute | solution.py:347
  20.5 0.7 %copy-done.4 = bf16[3,272,128]{2,1,0:T(8,128)(2,1)} copy-done((bf16[3,272,128]{2,1,0:T(8,128)(2,1)}, bf16[3,272,128]{2,1,0:T(8,128)(2,1)S(1)}, u32[]{:S(2)}) %copy-start.4) | copy-done | bytes 208920
  21.2 1.2 %gate_rows.1.start_ref = s32[1,16]{1,0:T(1,128)} custom-call(s32[1,16]{1,0:T(1,128)} %add_bitcast_fusion.x_ref, bf16[3,272,128]{2,1,0:T(8,128)(2,1)} %copy-done.4), custom_call_target="tpu_custom_call" | custom-call | tf_op jit(solution)/shard_map/gate_rows/pallas_call | solution.py:145
  22.3 0.9 %constant_dynamic-update-slice_fusion.6 = bf16[4,272,128]{2,1,0:T(8,128)(2,1)S(1)} fusion(bf16[3,272,128]{2,1,0:T(8,128)(2,1)} %copy-done.4), kind=kLoop, calls=%fused_computation.15 | loop fusion | bytes 417792
  23.3 0.9 %collective-permute-done.3 = bf16[1,272,128]{2,1,0:T(8,128)(2,1)S(1)} collective-permute-done((bf16[1,272,128]{2,1,0:T(8,128)(2,1)S(1)}, bf16[1,272,128]{2,1,0:T(8,128)(2,1)S(1)}, u32[]{:S(2)}, u32[]{:S(2)}) %collective-permute-start.3) | collective-permute-done | bytes 69664 | tf_op jit(solution)/shard_map/ppermute | solution.py:347
  24.2 0.4 %collective-permute-start.7 = (bf16[4,272,128]{2,1,0:T(8,128)(2,1)S(1)}, bf16[4,272,128]{2,1,0:T(8,128)(2,1)S(1)}, u32[]{:S(2)}, u32[]{:S(2)}) collective-permute-start(bf16[4,272,128]{2,1,0:T(8,128)(2,1)S(1)} %constant_dynamic-update-slice_fusion.5.last_ref), channel_id=1, source_target_pairs={{0,1},{1,0},{2,3},{3,2},{4,5},{5,4},{6,7},{7,6},{8,9},{9,8},{10,11... | collective-permute-start | bytes 835592 | tf_op jit(solution)/shard_map/ppermute | solution.py:411
  24.7 2.2 %copy-done.2 = bf16[8192,256]{1,0:T(8,128)(2,1)S(1)} copy-done((bf16[8192,256]{1,0:T(8,128)(2,1)S(1)}, bf16[8192,256]{1,0:T(8,128)(2,1)}, u32[]{:S(2)}) %copy-start.2) | copy-done | bytes 4194328
  26.9 0.7 %copy-done.3 = s32[1,16]{1,0:T(1,128)S(1)} copy-done((s32[1,16]{1,0:T(1,128)S(1)}, s32[1,16]{1,0:T(1,128)}, u32[]{:S(2)}) %copy-start.3) | copy-done | bytes 88
  27.5 2.4 %merge_blocks.1 = (bf16[8192,256]{1,0:T(8,128)(2,1)}, f32[4,256]{1,0:T(4,128)S(1)}, bf16[64,256]{1,0:T(8,128)(2,1)S(1)}, bf16[3,512,256]{2,1,0:T(8,128)(2,1)S(1)}) custom-call(s32[1,16]{1,0:T(1,128)S(1)} %copy-done.3, bf16[64,64]{1,0:T(8,128)(2,1)S(1)} %select_convert_fusion.pick_ref, bf16[4,8192]{1,0:T(4,128)(2,1)S(1)} %maximum_select_fusion.features_ref, ...), custom_call_target="tpu_custom_call" | custom-call | flops 201326592 | bytes 6291456 | tf_op jit(solution)/shard_map/merge_blocks/pallas_call | solution.py:263
  29.9 1.9 %finish_rows.1 = (bf16[8192,256]{1,0:T(8,128)(2,1)}, bf16[4,256]{1,0:T(4,128)(2,1)}, bf16[4,2048]{1,0:T(4,128)(2,1)}) custom-call(s32[1,16]{1,0:T(1,128)S(1)} %copy-done.3, bf16[64,256]{1,0:T(8,128)(2,1)S(1)} %get-tuple-element.61.up_ref, bf16[4,8192]{1,0:T(4,128)(2,1)S(1)} %maximum_select_fusion.features_ref, ...), custom_call_target="tpu_custom_call", output_to_operand_aliasing={{0}: (6, {})} | custom-call | flops 67108864 | bytes 2097152 | tf_op jit(solution)/shard_map/finish_rows/pallas_call | solution.py:292
  (34 shorter events, 0.3 us)
Async XLA Ops:
  0.6 0.9 %copy-start = (bf16[64,1024]{1,0:T(8,128)(2,1)S(1)}, bf16[64,1024]{1,0:T(8,128)(2,1)}, u32[]{:S(2)}) copy-start(bf16[64,1024]{1,0:T(8,128)(2,1)} %param.17) | copy-start | bytes 393220
  0.6 10.4 %copy-start.5 = (bf16[4,4096]{1,0:T(4,128)(2,1)S(1)}, bf16[4,4096]{1,0:T(4,128)(2,1)}, u32[]{:S(2)}) copy-start(bf16[4,4096]{1,0:T(4,128)(2,1)} %param.10) | copy-start | bytes 98308
  1.6 10.8 %collective-permute-start.1 = (bf16[1,272,128]{2,1,0:T(8,128)(2,1)S(1)}, bf16[1,272,128]{2,1,0:T(8,128)(2,1)S(1)}, u32[]{:S(2)}, u32[]{:S(2)}) collective-permute-start(bf16[1,272,128]{2,1,0:T(8,128)(2,1)S(1)} %bitcast.13), channel_id=1, source_target_pairs={{0,4},{1,3},{2,6},{3,1},{4,0},{5,7},{6,2},{7,5},{8,12},{9,11},{10,... | collective-permute-start | bytes 208904 | tf_op jit(solution)/shard_map/ppermute | solution.py:347
  4.7 7.7 %collective-permute-start = (bf16[1,272,128]{2,1,0:T(8,128)(2,1)S(1)}, bf16[1,272,128]{2,1,0:T(8,128)(2,1)S(1)}, u32[]{:S(2)}, u32[]{:S(2)}) collective-permute-start(bf16[1,272,128]{2,1,0:T(8,128)(2,1)S(1)} %bitcast.14), channel_id=1, source_target_pairs={{0,8},{1,9},{2,10},{3,11},{4,12},{5,13},{6,14},{7,15},{8,0},{9,1},... | collective-permute-start | bytes 208904 | tf_op jit(solution)/shard_map/ppermute | solution.py:347
  11.1 1.3 %collective-permute-start.4 = (bf16[4,4096]{1,0:T(4,128)(2,1)S(1)}, bf16[4,4096]{1,0:T(4,128)(2,1)S(1)}, u32[]{:S(2)}, u32[]{:S(2)}) collective-permute-start(bf16[4,4096]{1,0:T(4,128)(2,1)S(1)} %copy-done.5), channel_id=1, source_target_pairs={{0,1},{1,0},{2,3},{3,2},{4,5},{5,4},{6,7},{7,6},{8,9},{9,8},{10,11... | collective-permute-start | bytes 98312 | tf_op jit(solution)/shard_map/ppermute | solution.py:365
  12.4 6.8 %collective-permute-start.2 = (bf16[1,272,128]{2,1,0:T(8,128)(2,1)S(1)}, bf16[1,272,128]{2,1,0:T(8,128)(2,1)S(1)}, u32[]{:S(2)}, u32[]{:S(2)}) collective-permute-start(bf16[1,272,128]{2,1,0:T(8,128)(2,1)S(1)} %collective-permute-done), channel_id=1, source_target_pairs={{0,4},{1,3},{2,6},{3,1},{4,0},{5,7},{6,2},{7,5},{8,12},{9,11},{10,... | collective-permute-start | bytes 208904 | tf_op jit(solution)/shard_map/ppermute | solution.py:347
  13.0 6.3 %copy-start.6 = (s32[8]{0:T(128)S(1)}, s32[8]{0:T(128)}, u32[]{:S(2)}) copy-start(s32[8]{0:T(128)} %param.19) | copy-start | bytes 100
  13.0 7.5 %collective-permute-start.5 = (bf16[3,272,128]{2,1,0:T(8,128)(2,1)S(1)}, bf16[3,272,128]{2,1,0:T(8,128)(2,1)S(1)}, u32[]{:S(2)}, u32[]{:S(2)}) collective-permute-start(bf16[3,272,128]{2,1,0:T(8,128)(2,1)S(1)} %pad_maximum_fusion.1.rest_1_), channel_id=1, source_target_pairs={{0,2},{1,5},{2,0},{3,7},{4,6},{5,1},{6,4},{7,3},{8,10},{9,13},{10,... | collective-permute-start | bytes 626696 | tf_op jit(solution)/shard_map/ppermute | solution.py:347
  17.2 2.0 %copy-start.1 = (bf16[8192,256]{1,0:T(8,128)(2,1)}, bf16[8192,256]{1,0:T(8,128)(2,1)S(1)}, u32[]{:S(2)}) copy-start(bf16[8192,256]{1,0:T(8,128)(2,1)S(1)} %get-tuple-element.58.served_ref) | copy-start | bytes 12582916
  19.8 4.4 %collective-permute-start.6 = (bf16[4,272,128]{2,1,0:T(8,128)(2,1)S(1)}, bf16[4,272,128]{2,1,0:T(8,128)(2,1)S(1)}, u32[]{:S(2)}, u32[]{:S(2)}) collective-permute-start(bf16[4,272,128]{2,1,0:T(8,128)(2,1)S(1)} %pad_maximum_fusion.slabs_ref), channel_id=1, source_target_pairs={{0,1},{1,0},{2,3},{3,2},{4,5},{5,4},{6,7},{7,6},{8,9},{9,8},{10,11... | collective-permute-start | bytes 835592 | tf_op jit(solution)/shard_map/ppermute | solution.py:405
  19.9 4.4 %collective-permute-start.3 = (bf16[1,272,128]{2,1,0:T(8,128)(2,1)S(1)}, bf16[1,272,128]{2,1,0:T(8,128)(2,1)S(1)}, u32[]{:S(2)}, u32[]{:S(2)}) collective-permute-start(bf16[1,272,128]{2,1,0:T(8,128)(2,1)S(1)} %collective-permute-done.2), channel_id=1, source_target_pairs={{0,2},{1,5},{2,0},{3,7},{4,6},{5,1},{6,4},{7,3},{8,10},{9,13},{10,... | collective-permute-start | bytes 208904 | tf_op jit(solution)/shard_map/ppermute | solution.py:347
  20.5 0.7 %copy-start.4 = (bf16[3,272,128]{2,1,0:T(8,128)(2,1)}, bf16[3,272,128]{2,1,0:T(8,128)(2,1)S(1)}, u32[]{:S(2)}) copy-start(bf16[3,272,128]{2,1,0:T(8,128)(2,1)S(1)} %collective-permute-done.5.after) | copy-start | bytes 626692
  24.2 5.7 %collective-permute-start.7 = (bf16[4,272,128]{2,1,0:T(8,128)(2,1)S(1)}, bf16[4,272,128]{2,1,0:T(8,128)(2,1)S(1)}, u32[]{:S(2)}, u32[]{:S(2)}) collective-permute-start(bf16[4,272,128]{2,1,0:T(8,128)(2,1)S(1)} %constant_dynamic-update-slice_fusion.5.last_ref), channel_id=1, source_target_pairs={{0,1},{1,0},{2,3},{3,2},{4,5},{5,4},{6,7},{7,6},{8,9},{9,8},{10,11... | collective-permute-start | bytes 835592 | tf_op jit(solution)/shard_map/ppermute | solution.py:411
  24.7 2.2 %copy-start.2 = (bf16[8192,256]{1,0:T(8,128)(2,1)S(1)}, bf16[8192,256]{1,0:T(8,128)(2,1)}, u32[]{:S(2)}) copy-start(bf16[8192,256]{1,0:T(8,128)(2,1)} %copy-done.1) | copy-start | bytes 12582916
  26.9 0.7 %copy-start.3 = (s32[1,16]{1,0:T(1,128)S(1)}, s32[1,16]{1,0:T(1,128)}, u32[]{:S(2)}) copy-start(s32[1,16]{1,0:T(1,128)} %gate_rows.1.start_ref) | copy-start | bytes 196

commit v14 on v13

--- a/solution.py
+++ b/solution.py
@@ -147,6 +147,7 @@
         out_shape=jax.ShapeDtypeStruct(x.shape, x.dtype),
         in_specs=[VMEM, pl.BlockSpec(memory_space=pl.ANY)],
         out_specs=VMEM,
+        compiler_params=pltpu.CompilerParams(vmem_limit_bytes=2**20),
         name="gate_rows",
     )(x, after)
 

time: 32.1 us -> 26.5 us (0.83)
  local copies, waits for them, and re-layouts: 7.46 us -> 1 us
  waiting for transfers between devices: 2.03 us -> 3.5 us
  Pallas kernels: 11.8 us -> 10.7 us
  starting transfers between devices: 8.87 us -> 9.85 us
  other arithmetic: 0.83 us -> 0.32 us
    unnamed x21 -> x13, local copies, waits for them, and re-layouts: 6.7 us -> 0.24 us
    ppermute x5, waiting for transfers between devices: 0.95 us -> 2.43 us  [exchange(): return lax.ppermute(x, ('replica', 'tensor'), pairs)]
    ppermute x5, starting transfers between devices: 8.35 us -> 9.64 us  [exchange(): return lax.ppermute(x, ('replica', 'tensor'), pairs)]
    pallas_call x1, Pallas kernels: 1.17 us -> 0.01 us  [gate(): pl.pallas_call(gate_kernel, out_shape=jax.ShapeDtypeStruct(x.shape, x.dty...]
    broadcast_in_dim x1, other arithmetic: 0.52 us -> 0.01 us  [body(): start = (place * full + half * width).astype(jnp.int32)[None]]
    ppermute x1, starting transfers between devices: 0.44 us -> 0.07 us  [body(): last_crossed = lax.ppermute(last, 'tensor', swap)]
  transfers between devices with their start and end apart: 8 -> 8, of which waited for: 2 -> 2; matrix products, arithmetic and copies ran while one was open for 6% -> 1% of each run, Pallas kernels for 31% -> 33%
where the time goes in v14:
time: 26.5 us; the launch traced here: 26.2 us
  Pallas kernels  10.7 us (40%)
  starting transfers between devices  9.85 us (37%)
  waiting for transfers between devices  3.5 us (13%)
  local copies, waits for them, and re-layouts  1 us (4%)
  between operations  0.86 us (3%)
  other arithmetic  0.32 us (1%)
    ppermute x5, starting transfers between devices, exchange(): return lax.ppermute(x, ('replica', 'tensor'), pairs)  9.64 us
    pallas_call x2, Pallas kernels, attend(): pl.pallas_call(functools.partial(attend_kernel, rows, fetch), out_shape=o...  6.37 us
    ppermute x5, waiting for transfers between devices, exchange(): return lax.ppermute(x, ('replica', 'tensor'), pairs)  2.43 us
    pallas_call x1, Pallas kernels, merge(): pl.pallas_call(functools.partial(merge_kernel, per, left), out_shape=(jax...  2.39 us
    pallas_call x1, Pallas kernels, finish(): pl.pallas_call(final_kernel, out_shape=[jax.ShapeDtypeStruct(shape, jnp.b...  1.93 us
    ppermute x1, waiting for transfers between devices, body(): hid_other = lax.ppermute(hid_other, 'tensor', swap)  1.07 us
    slice x1, local copies, waits for them, and re-layouts, panels(): return [x[:, i:i + PANEL] for i in range(0, x.shape[1], PANEL)]  0.74 us
  transfers between devices with their start and end apart: 8, of which 2 were waited for; matrix products, arithmetic and copies ran while one was open for 1% of the time, Pallas kernels for 33%

profile of v14, /device:TPU:0, one launch (start us, length us, event | category | flops | bytes accessed | tf_op | source)
XLA Modules:
  0.0 26.2 jit_solution(11779330690216102796)
XLA Ops:
  0.6 0.0 copy-start
  0.7 0.7 %fusion.1 = (bf16[8,128]{1,0:T(8,128)(2,1)S(1)}, bf16[8,128]{1,0:T(8,128)(2,1)S(1)}) fusion(bf16[8,256]{1,0:T(8,128)(2,1)} %param.18), kind=kLoop, calls=%fused_computation.34 | loop fusion | bytes 8192 | tf_op jit(solution)/shard_map/slice | solution.py:318
  1.4 0.1 copy-done
  1.6 3.1 %collective-permute-start.1 = (bf16[1,272,128]{2,1,0:T(8,128)(2,1)S(1)}, bf16[1,272,128]{2,1,0:T(8,128)(2,1)S(1)}, u32[]{:S(2)}, u32[]{:S(2)}) collective-permute-start(bf16[1,272,128]{2,1,0:T(8,128)(2,1)S(1)} %bitcast.13), channel_id=1, source_target_pairs={{0,4},{1,3},{2,6},{3,1},{4,0},{5,7},{6,2},{7,5},{8,12},{9,11},{10,... | collective-permute-start | bytes 208904 | tf_op jit(solution)/shard_map/ppermute | solution.py:348
  4.7 2.6 %collective-permute-start = (bf16[1,272,128]{2,1,0:T(8,128)(2,1)S(1)}, bf16[1,272,128]{2,1,0:T(8,128)(2,1)S(1)}, u32[]{:S(2)}, u32[]{:S(2)}) collective-permute-start(bf16[1,272,128]{2,1,0:T(8,128)(2,1)S(1)} %bitcast.14), channel_id=1, source_target_pairs={{0,8},{1,9},{2,10},{3,11},{4,12},{5,13},{6,14},{7,15},{8,0},{9,1},... | collective-permute-start | bytes 208904 | tf_op jit(solution)/shard_map/ppermute | solution.py:348
  7.3 3.8 %attend_cache.2 = (f32[3,16,128]{2,1,0:T(8,128)S(1)}, f32[3,16,128]{2,1,0:T(8,128)S(1)}) custom-call(s32[4]{0:T(128)} %lengths_hbm.3, bf16[4,2048]{1,0:T(4,128)(2,1)} %q_hbm.3, bf16[4,256]{1,0:T(4,128)(2,1)} %own_k_hbm.3, bf16[4,1024,256]{2,1,0:T(8,128)(2,1)} %k_hbm.3, bf16[4,1024,256]{2,1,0:T(8,128)(2,1)} %v_hbm.3, bf16[1,272,128]{2,1,0:T(8,128)(2,1)S(1)} %bitcast.15), custom_call_target="tpu_custom_call" | custom-call | flops 50331648 | bytes 3145728 | tf_op jit(solution)/shard_map/attend_cache/pallas_call | solution.py:113
  11.1 0.1 collective-permute-start.4
  11.2 0.1 pad_add_fusion
  11.3 1.1 %collective-permute-done.4 = bf16[4,4096]{1,0:T(4,128)(2,1)S(1)} collective-permute-done((bf16[4,4096]{1,0:T(4,128)(2,1)S(1)}, bf16[4,4096]{1,0:T(4,128)(2,1)S(1)}, u32[]{:S(2)}, u32[]{:S(2)}) %collective-permute-start.4) | collective-permute-done | bytes 32800 | tf_op jit(solution)/shard_map/ppermute | solution.py:366
  12.4 0.0 collective-permute-done.1
  12.4 0.0 collective-permute-done
  12.4 0.5 %collective-permute-start.2 = (bf16[1,272,128]{2,1,0:T(8,128)(2,1)S(1)}, bf16[1,272,128]{2,1,0:T(8,128)(2,1)S(1)}, u32[]{:S(2)}, u32[]{:S(2)}) collective-permute-start(bf16[1,272,128]{2,1,0:T(8,128)(2,1)S(1)} %collective-permute-done), channel_id=1, source_target_pairs={{0,4},{1,3},{2,6},{3,1},{4,0},{5,7},{6,2},{7,5},{8,12},{9,11},{10,... | collective-permute-start | bytes 208904 | tf_op jit(solution)/shard_map/ppermute | solution.py:348
  13.0 0.0 copy-start.2
  13.0 1.6 %collective-permute-start.5 = (bf16[3,272,128]{2,1,0:T(8,128)(2,1)S(1)}, bf16[3,272,128]{2,1,0:T(8,128)(2,1)S(1)}, u32[]{:S(2)}, u32[]{:S(2)}) collective-permute-start(bf16[3,272,128]{2,1,0:T(8,128)(2,1)S(1)} %pad_maximum_fusion.1.rest_1_), channel_id=1, source_target_pairs={{0,2},{1,5},{2,0},{3,7},{4,6},{5,1},{6,4},{7,3},{8,10},{9,13},{10,... | collective-permute-start | bytes 626696 | tf_op jit(solution)/shard_map/ppermute | solution.py:348
  14.6 2.6 %attend_cache.3 = (f32[1,16,128]{2,1,0:T(8,128)S(1)}, f32[1,16,128]{2,1,0:T(8,128)S(1)}, bf16[8192,256]{1,0:T(8,128)(2,1)S(1)}) custom-call(s32[4]{0:T(128)} %lengths_hbm.3, bf16[4,2048]{1,0:T(4,128)(2,1)} %q_hbm.3, bf16[4,256]{1,0:T(4,128)(2,1)} %own_k_hbm.3, bf16[4,1024,256]{2,1,0:T(8,128)(2,1)} %k_hbm.3, bf16[4,1024,256]{2,1,0:T(8,128)(2,1)} %v_hbm.3, ...), custom_call_target="tpu_custom_call" | custom-call | flops 16777216 | bytes 1048576 | tf_op jit(solution)/shard_map/attend_cache/pallas_call | solution.py:113
  17.2 0.0 collective-permute-done.2
  17.2 0.1 select_reduce_fusion
  17.3 0.1 collective-permute-start.6
  17.4 1.9 %collective-permute-start.3 = (bf16[1,272,128]{2,1,0:T(8,128)(2,1)S(1)}, bf16[1,272,128]{2,1,0:T(8,128)(2,1)S(1)}, u32[]{:S(2)}, u32[]{:S(2)}) collective-permute-start(bf16[1,272,128]{2,1,0:T(8,128)(2,1)S(1)} %collective-permute-done.2), channel_id=1, source_target_pairs={{0,2},{1,5},{2,0},{3,7},{4,6},{5,1},{6,4},{7,3},{8,10},{9,13},{10,... | collective-permute-start | bytes 208904 | tf_op jit(solution)/shard_map/ppermute | solution.py:348
  19.3 0.0 collective-permute-done.5.after
  19.4 2.4 %collective-permute-done.3 = bf16[1,272,128]{2,1,0:T(8,128)(2,1)S(1)} collective-permute-done((bf16[1,272,128]{2,1,0:T(8,128)(2,1)S(1)}, bf16[1,272,128]{2,1,0:T(8,128)(2,1)S(1)}, u32[]{:S(2)}, u32[]{:S(2)}) %collective-permute-start.3) | collective-permute-done | bytes 69664 | tf_op jit(solution)/shard_map/ppermute | solution.py:348
  21.8 0.1 collective-permute-start.7
  21.9 2.4 %merge_blocks.1 = (bf16[8192,256]{1,0:T(8,128)(2,1)}, f32[4,256]{1,0:T(4,128)S(1)}, bf16[64,256]{1,0:T(8,128)(2,1)S(1)}, bf16[3,512,256]{2,1,0:T(8,128)(2,1)S(1)}) custom-call(s32[1,16]{1,0:T(1,128)S(1)} %gate_rows.1.start_ref, bf16[64,64]{1,0:T(8,128)(2,1)S(1)} %select_convert_fusion.pick_ref, bf16[4,8192]{1,0:T(4,128)(2,1)S(1)} %maximum_select_fusion.features_ref, ...), custom_call_target="tpu_custom_call" | custom-call | flops 201326592 | bytes 6291456 | tf_op jit(solution)/shard_map/merge_blocks/pallas_call | solution.py:264
  24.3 1.9 %finish_rows.1 = (bf16[8192,256]{1,0:T(8,128)(2,1)}, bf16[4,256]{1,0:T(4,128)(2,1)}, bf16[4,2048]{1,0:T(4,128)(2,1)}) custom-call(s32[1,16]{1,0:T(1,128)S(1)} %gate_rows.1.start_ref, bf16[64,256]{1,0:T(8,128)(2,1)S(1)} %get-tuple-element.61.up_ref, bf16[4,8192]{1,0:T(4,128)(2,1)S(1)} %maximum_select_fusion.features_ref, ...), custom_call_target="tpu_custom_call", output_to_operand_aliasing={{0}: (6, {})} | custom-call | flops 67108864 | bytes 2097152 | tf_op jit(solution)/shard_map/finish_rows/pallas_call | solution.py:293
  (26 shorter events, 0.3 us)
Async XLA Ops:
  0.6 0.9 %copy-start = (bf16[64,1024]{1,0:T(8,128)(2,1)S(1)}, bf16[64,1024]{1,0:T(8,128)(2,1)}, u32[]{:S(2)}) copy-start(bf16[64,1024]{1,0:T(8,128)(2,1)} %param.17) | copy-start | bytes 393220
  0.6 10.4 %copy-start.1 = (bf16[4,4096]{1,0:T(4,128)(2,1)S(1)}, bf16[4,4096]{1,0:T(4,128)(2,1)}, u32[]{:S(2)}) copy-start(bf16[4,4096]{1,0:T(4,128)(2,1)} %param.10) | copy-start | bytes 98308
  1.6 10.8 %collective-permute-start.1 = (bf16[1,272,128]{2,1,0:T(8,128)(2,1)S(1)}, bf16[1,272,128]{2,1,0:T(8,128)(2,1)S(1)}, u32[]{:S(2)}, u32[]{:S(2)}) collective-permute-start(bf16[1,272,128]{2,1,0:T(8,128)(2,1)S(1)} %bitcast.13), channel_id=1, source_target_pairs={{0,4},{1,3},{2,6},{3,1},{4,0},{5,7},{6,2},{7,5},{8,12},{9,11},{10,... | collective-permute-start | bytes 208904 | tf_op jit(solution)/shard_map/ppermute | solution.py:348
  4.7 7.7 %collective-permute-start = (bf16[1,272,128]{2,1,0:T(8,128)(2,1)S(1)}, bf16[1,272,128]{2,1,0:T(8,128)(2,1)S(1)}, u32[]{:S(2)}, u32[]{:S(2)}) collective-permute-start(bf16[1,272,128]{2,1,0:T(8,128)(2,1)S(1)} %bitcast.14), channel_id=1, source_target_pairs={{0,8},{1,9},{2,10},{3,11},{4,12},{5,13},{6,14},{7,15},{8,0},{9,1},... | collective-permute-start | bytes 208904 | tf_op jit(solution)/shard_map/ppermute | solution.py:348
  11.1 1.3 %collective-permute-start.4 = (bf16[4,4096]{1,0:T(4,128)(2,1)S(1)}, bf16[4,4096]{1,0:T(4,128)(2,1)S(1)}, u32[]{:S(2)}, u32[]{:S(2)}) collective-permute-start(bf16[4,4096]{1,0:T(4,128)(2,1)S(1)} %copy-done.1), channel_id=1, source_target_pairs={{0,1},{1,0},{2,3},{3,2},{4,5},{5,4},{6,7},{7,6},{8,9},{9,8},{10,11... | collective-permute-start | bytes 98312 | tf_op jit(solution)/shard_map/ppermute | solution.py:366
  12.4 4.7 %collective-permute-start.2 = (bf16[1,272,128]{2,1,0:T(8,128)(2,1)S(1)}, bf16[1,272,128]{2,1,0:T(8,128)(2,1)S(1)}, u32[]{:S(2)}, u32[]{:S(2)}) collective-permute-start(bf16[1,272,128]{2,1,0:T(8,128)(2,1)S(1)} %collective-permute-done), channel_id=1, source_target_pairs={{0,4},{1,3},{2,6},{3,1},{4,0},{5,7},{6,2},{7,5},{8,12},{9,11},{10,... | collective-permute-start | bytes 208904 | tf_op jit(solution)/shard_map/ppermute | solution.py:348
  13.0 4.3 %copy-start.2 = (s32[8]{0:T(128)S(1)}, s32[8]{0:T(128)}, u32[]{:S(2)}) copy-start(s32[8]{0:T(128)} %param.19) | copy-start | bytes 100
  13.0 6.4 %collective-permute-start.5 = (bf16[3,272,128]{2,1,0:T(8,128)(2,1)S(1)}, bf16[3,272,128]{2,1,0:T(8,128)(2,1)S(1)}, u32[]{:S(2)}, u32[]{:S(2)}) collective-permute-start(bf16[3,272,128]{2,1,0:T(8,128)(2,1)S(1)} %pad_maximum_fusion.1.rest_1_), channel_id=1, source_target_pairs={{0,2},{1,5},{2,0},{3,7},{4,6},{5,1},{6,4},{7,3},{8,10},{9,13},{10,... | collective-permute-start | bytes 626696 | tf_op jit(solution)/shard_map/ppermute | solution.py:348
  17.3 4.5 %collective-permute-start.6 = (bf16[4,272,128]{2,1,0:T(8,128)(2,1)S(1)}, bf16[4,272,128]{2,1,0:T(8,128)(2,1)S(1)}, u32[]{:S(2)}, u32[]{:S(2)}) collective-permute-start(bf16[4,272,128]{2,1,0:T(8,128)(2,1)S(1)} %pad_maximum_fusion.slabs_ref), channel_id=1, source_target_pairs={{0,1},{1,0},{2,3},{3,2},{4,5},{5,4},{6,7},{7,6},{8,9},{9,8},{10,11... | collective-permute-start | bytes 835592 | tf_op jit(solution)/shard_map/ppermute | solution.py:406
  17.4 4.4 %collective-permute-start.3 = (bf16[1,272,128]{2,1,0:T(8,128)(2,1)S(1)}, bf16[1,272,128]{2,1,0:T(8,128)(2,1)S(1)}, u32[]{:S(2)}, u32[]{:S(2)}) collective-permute-start(bf16[1,272,128]{2,1,0:T(8,128)(2,1)S(1)} %collective-permute-done.2), channel_id=1, source_target_pairs={{0,2},{1,5},{2,0},{3,7},{4,6},{5,1},{6,4},{7,3},{8,10},{9,13},{10,... | collective-permute-start | bytes 208904 | tf_op jit(solution)/shard_map/ppermute | solution.py:348
  21.8 2.5 %collective-permute-start.7 = (bf16[4,272,128]{2,1,0:T(8,128)(2,1)S(1)}, bf16[4,272,128]{2,1,0:T(8,128)(2,1)S(1)}, u32[]{:S(2)}, u32[]{:S(2)}) collective-permute-start(bf16[4,272,128]{2,1,0:T(8,128)(2,1)S(1)} %constant_dynamic-update-slice_fusion.5.last_ref), channel_id=1, source_target_pairs={{0,1},{1,0},{2,3},{3,2},{4,5},{5,4},{6,7},{7,6},{8,9},{9,8},{10,11... | collective-permute-start | bytes 835592 | tf_op jit(solution)/shard_map/ppermute | solution.py:412

commit v15 on v13

--- a/solution.py
+++ b/solution.py
@@ -134,21 +134,6 @@
         ),
         name="attend_cache",
     )(*given, *([served] if fetch else []), *after)
-
-
-def gate_kernel(x_ref, after, out_ref):
-    del after
-    out_ref[...] = x_ref[...]
-
-
-def gate(x, after):
-    return pl.pallas_call(
-        gate_kernel,
-        out_shape=jax.ShapeDtypeStruct(x.shape, x.dtype),
-        in_specs=[VMEM, pl.BlockSpec(memory_space=pl.ANY)],
-        out_specs=VMEM,
-        name="gate_rows",
-    )(x, after)
 
 
 class Merge:
@@ -357,21 +342,25 @@
     for step in early:
         slabs = jnp.concatenate([slabs, exchange(slabs, step)], axis=0)
 
-    split = rows - rows // 4
+    cuts = [0, rows // 2, rows - rows // 4, rows]
+    first_rows, second_rows, third_rows = (range(*cut) for cut in zip(cuts, cuts[1:]))
     came = exchange(slabs, first)
     ahead = exchange(slabs, second)
-    parts = [attend(range(split), given, after=[slabs])]
-    parts[0], hid_other = lax.optimization_barrier((parts[0], hidden_in))
+    *part, served = attend(first_rows, given, *in_hbm(served_value_weight), [slabs])
+    parts = [part]
+    part, hid_other = lax.optimization_barrier((part, hidden_in))
     hid_other = lax.ppermute(hid_other, "tensor", swap)
-    came, ahead, parts[0] = lax.optimization_barrier((came, ahead, parts[0]))
+    came, part = lax.optimization_barrier((came, part))
     slabs = jnp.concatenate([slabs, came, ahead], axis=0)
     came = exchange(came, second)
     images = exchange(slabs, third)
-    *part, served = attend(range(split, rows), given, *in_hbm(served_value_weight), [slabs])
-    came, part, owner_rank = lax.optimization_barrier((came, part, owner_rank))
-    parts.append(part)
+    parts.append(attend(second_rows, given, after=[slabs]))
+    came, parts[1], hid_other, owner_rank = lax.optimization_barrier(
+        (came, parts[1], hid_other, owner_rank)
+    )
     last = exchange(came, third)
     slabs = jnp.concatenate([slabs, came], axis=0)
+    parts.append(attend(third_rows, given, after=[images]))
     features = jnp.concatenate([hidden_in, hid_other], axis=1)
     features = jnp.where(core == 0, features, jnp.concatenate([hid_other, hidden_in], axis=1))
 
@@ -401,9 +390,8 @@
     context, own_weight = (
         jnp.concatenate(pair, axis=0).reshape(queries.shape) for pair in zip(*parts)
     )
-    crossed, start, features = lax.optimization_barrier((slabs, start, features))
+    crossed, start = lax.optimization_barrier((slabs, start))
     crossed = lax.ppermute(crossed, "tensor", swap)
-    start = gate(start, images)
     last, start, pick, context, own_weight, features, crossed = lax.optimization_barrier(
         (last, start, pick, context, own_weight, features, crossed)
     )

time: 32.1 us -> 26.4 us (0.82)
  local copies, waits for them, and re-layouts: 7.46 us -> 3.06 us
  starting transfers between devices: 8.87 us -> 10.6 us
  waiting for transfers between devices: 2.03 us -> 0.39 us
  Pallas kernels: 11.8 us -> 11 us
  other arithmetic: 0.83 us -> 0.32 us
    unnamed x21 -> x17, local copies, waits for them, and re-layouts: 6.7 us -> 2.3 us
    ppermute x5, starting transfers between devices: 8.35 us -> 9.99 us  [exchange(): return lax.ppermute(x, ('replica', 'tensor'), pairs)]
    pallas_call x1 -> x0, Pallas kernels: 1.17 us -> none  [gate(): pl.pallas_call(gate_kernel, out_shape=jax.ShapeDtypeStruct(x.shape, x.dty...]
    ppermute x1, waiting for transfers between devices: 1.07 us -> 0.01 us  [body(): hid_other = lax.ppermute(hid_other, 'tensor', swap)]
    ppermute x5, waiting for transfers between devices: 0.95 us -> 0.38 us  [exchange(): return lax.ppermute(x, ('replica', 'tensor'), pairs)]
    broadcast_in_dim x1, other arithmetic: 0.52 us -> 0.01 us  [body(): start = (place * full + half * width).astype(jnp.int32)[None]]
    pallas_call x2 -> x3, Pallas kernels: 6.37 us -> 6.7 us  [attend(): pl.pallas_call(functools.partial(attend_kernel, rows, fetch), out_shape=o...]
  transfers between devices with their start and end apart: 8 -> 8, of which waited for: 2 -> 1; matrix products, arithmetic and copies ran while one was open for 6% -> 1% of each run, Pallas kernels for 31% -> 35%
where the time goes in v15:
time: 26.4 us; the launch traced here: 26.2 us
  Pallas kernels  11 us (42%)
  starting transfers between devices  10.6 us (40%)
  local copies, waits for them, and re-layouts  3.06 us (12%)
  between operations  0.82 us (3%)
  waiting for transfers between devices  0.39 us (1%)
  other arithmetic  0.32 us (1%)
    ppermute x5, starting transfers between devices, exchange(): return lax.ppermute(x, ('replica', 'tensor'), pairs)  9.99 us
    pallas_call x3, Pallas kernels, attend(): pl.pallas_call(functools.partial(attend_kernel, rows, fetch), out_shape=o...  6.7 us
    pallas_call x1, Pallas kernels, merge(): pl.pallas_call(functools.partial(merge_kernel, per, left), out_shape=(jax...  2.39 us
    unnamed x17, local copies, waits for them, and re-layouts  2.3 us
    pallas_call x1, Pallas kernels, finish(): pl.pallas_call(final_kernel, out_shape=[jax.ShapeDtypeStruct(shape, jnp.b...  1.93 us
    slice x1, local copies, waits for them, and re-layouts, panels(): return [x[:, i:i + PANEL] for i in range(0, x.shape[1], PANEL)]  0.74 us
    ppermute x1, starting transfers between devices, body(): last_crossed = lax.ppermute(last, 'tensor', swap)  0.55 us
  transfers between devices with their start and end apart: 8, of which 1 were waited for; matrix products, arithmetic and copies ran while one was open for 1% of the time, Pallas kernels for 35%

profile of v15, /device:TPU:0, one launch (start us, length us, event | category | flops | bytes accessed | tf_op | source)
XLA Modules:
  0.0 26.2 jit_solution(16197204056247356259)
XLA Ops:
  0.6 0.0 copy-start
  0.7 0.7 %fusion.1 = (bf16[8,128]{1,0:T(8,128)(2,1)S(1)}, bf16[8,128]{1,0:T(8,128)(2,1)S(1)}) fusion(bf16[8,256]{1,0:T(8,128)(2,1)} %param.18), kind=kLoop, calls=%fused_computation.34 | loop fusion | bytes 8192 | tf_op jit(solution)/shard_map/slice | solution.py:302
  1.4 0.2 copy-done
  1.6 0.0 copy-start.3
  1.7 3.1 %collective-permute-start.2 = (bf16[1,272,128]{2,1,0:T(8,128)(2,1)S(1)}, bf16[1,272,128]{2,1,0:T(8,128)(2,1)S(1)}, u32[]{:S(2)}, u32[]{:S(2)}) collective-permute-start(bf16[1,272,128]{2,1,0:T(8,128)(2,1)S(1)} %bitcast.13), channel_id=1, source_target_pairs={{0,4},{1,3},{2,6},{3,1},{4,0},{5,7},{6,2},{7,5},{8,12},{9,11},{10,... | collective-permute-start | bytes 208904 | tf_op jit(solution)/shard_map/ppermute | solution.py:332
  4.7 2.6 %collective-permute-start = (bf16[1,272,128]{2,1,0:T(8,128)(2,1)S(1)}, bf16[1,272,128]{2,1,0:T(8,128)(2,1)S(1)}, u32[]{:S(2)}, u32[]{:S(2)}) collective-permute-start(bf16[1,272,128]{2,1,0:T(8,128)(2,1)S(1)} %bitcast.14), channel_id=1, source_target_pairs={{0,8},{1,9},{2,10},{3,11},{4,12},{5,13},{6,14},{7,15},{8,0},{9,1},... | collective-permute-start | bytes 208904 | tf_op jit(solution)/shard_map/ppermute | solution.py:332
  7.3 2.9 %attend_cache.4 = (f32[2,16,128]{2,1,0:T(8,128)S(1)}, f32[2,16,128]{2,1,0:T(8,128)S(1)}, bf16[8192,256]{1,0:T(8,128)(2,1)S(1)}) custom-call(s32[4]{0:T(128)} %lengths_hbm.5, bf16[4,2048]{1,0:T(4,128)(2,1)} %q_hbm.5, bf16[4,256]{1,0:T(4,128)(2,1)} %own_k_hbm.5, bf16[4,1024,256]{2,1,0:T(8,128)(2,1)} %k_hbm.5, bf16[4,1024,256]{2,1,0:T(8,128)(2,1)} %v_hbm.5, ...), custom_call_target="tpu_custom_call" | custom-call | flops 33554432 | bytes 2097152 | tf_op jit(solution)/shard_map/attend_cache/pallas_call | solution.py:113
  10.3 0.0 copy-start.1
  10.3 2.0 %copy-done.1 = bf16[8192,256]{1,0:T(8,128)(2,1)} copy-done((bf16[8192,256]{1,0:T(8,128)(2,1)}, bf16[8192,256]{1,0:T(8,128)(2,1)S(1)}, u32[]{:S(2)}) %copy-start.1) | copy-done | bytes 4194328
  12.3 0.0 collective-permute-start.3
  12.4 0.1 pad_add_fusion
  12.4 0.8 %collective-permute-start.1 = (bf16[1,272,128]{2,1,0:T(8,128)(2,1)S(1)}, bf16[1,272,128]{2,1,0:T(8,128)(2,1)S(1)}, u32[]{:S(2)}, u32[]{:S(2)}) collective-permute-start(bf16[1,272,128]{2,1,0:T(8,128)(2,1)S(1)} %collective-permute-done), channel_id=1, source_target_pairs={{0,4},{1,3},{2,6},{3,1},{4,0},{5,7},{6,2},{7,5},{8,12},{9,11},{10,... | collective-permute-start | bytes 208904 | tf_op jit(solution)/shard_map/ppermute | solution.py:332
  13.3 0.0 copy-start.2
  13.3 1.3 %collective-permute-start.5 = (bf16[3,272,128]{2,1,0:T(8,128)(2,1)S(1)}, bf16[3,272,128]{2,1,0:T(8,128)(2,1)S(1)}, u32[]{:S(2)}, u32[]{:S(2)}) collective-permute-start(bf16[3,272,128]{2,1,0:T(8,128)(2,1)S(1)} %pad_maximum_fusion.1.rest_0_), channel_id=1, source_target_pairs={{0,2},{1,5},{2,0},{3,7},{4,6},{5,1},{6,4},{7,3},{8,10},{9,13},{10,... | collective-permute-start | bytes 626696 | tf_op jit(solution)/shard_map/ppermute | solution.py:332
  14.5 1.9 %attend_cache.3 = (f32[1,16,128]{2,1,0:T(8,128)S(1)}, f32[1,16,128]{2,1,0:T(8,128)S(1)}) custom-call(s32[4]{0:T(128)} %lengths_hbm.5, bf16[4,2048]{1,0:T(4,128)(2,1)} %q_hbm.5, bf16[4,256]{1,0:T(4,128)(2,1)} %own_k_hbm.5, bf16[4,1024,256]{2,1,0:T(8,128)(2,1)} %k_hbm.5, bf16[4,1024,256]{2,1,0:T(8,128)(2,1)} %v_hbm.5, ...), custom_call_target="tpu_custom_call" | custom-call | flops 16777216 | bytes 1048576 | tf_op jit(solution)/shard_map/attend_cache/pallas_call | solution.py:113
  16.4 0.3 %collective-permute-done.1 = bf16[1,272,128]{2,1,0:T(8,128)(2,1)S(1)} collective-permute-done((bf16[1,272,128]{2,1,0:T(8,128)(2,1)S(1)}, bf16[1,272,128]{2,1,0:T(8,128)(2,1)S(1)}, u32[]{:S(2)}, u32[]{:S(2)}) %collective-permute-start.1) | collective-permute-done | bytes 69664 | tf_op jit(solution)/shard_map/ppermute | solution.py:332
  16.8 2.3 %collective-permute-start.4 = (bf16[1,272,128]{2,1,0:T(8,128)(2,1)S(1)}, bf16[1,272,128]{2,1,0:T(8,128)(2,1)S(1)}, u32[]{:S(2)}, u32[]{:S(2)}) collective-permute-start(bf16[1,272,128]{2,1,0:T(8,128)(2,1)S(1)} %collective-permute-done.1), channel_id=1, source_target_pairs={{0,2},{1,5},{2,0},{3,7},{4,6},{5,1},{6,4},{7,3},{8,10},{9,13},{10,... | collective-permute-start | bytes 208904 | tf_op jit(solution)/shard_map/ppermute | solution.py:332
  19.0 0.1 select_reduce_fusion
  19.2 0.1 collective-permute-start.6
  19.3 1.9 %attend_cache.5 = (f32[1,16,128]{2,1,0:T(8,128)S(1)}, f32[1,16,128]{2,1,0:T(8,128)S(1)}) custom-call(s32[4]{0:T(128)} %lengths_hbm.5, bf16[4,2048]{1,0:T(4,128)(2,1)} %q_hbm.5, bf16[4,256]{1,0:T(4,128)(2,1)} %own_k_hbm.5, bf16[4,1024,256]{2,1,0:T(8,128)(2,1)} %k_hbm.5, bf16[4,1024,256]{2,1,0:T(8,128)(2,1)} %v_hbm.5, ...), custom_call_target="tpu_custom_call" | custom-call | flops 16777216 | bytes 1048576 | tf_op jit(solution)/shard_map/attend_cache/pallas_call | solution.py:113
  21.3 0.0 collective-permute-done.4
  21.3 0.5 %collective-permute-start.7 = (bf16[4,272,128]{2,1,0:T(8,128)(2,1)S(1)}, bf16[4,272,128]{2,1,0:T(8,128)(2,1)S(1)}, u32[]{:S(2)}, u32[]{:S(2)}) collective-permute-start(bf16[4,272,128]{2,1,0:T(8,128)(2,1)S(1)} %constant_dynamic-update-slice_fusion.5.last_ref), channel_id=1, source_target_pairs={{0,1},{1,0},{2,3},{3,2},{4,5},{5,4},{6,7},{7,6},{8,9},{9,8},{10,11... | collective-permute-start | bytes 835592 | tf_op jit(solution)/shard_map/ppermute | solution.py:399
  21.9 2.4 %merge_blocks.1 = (bf16[8192,256]{1,0:T(8,128)(2,1)}, f32[4,256]{1,0:T(4,128)S(1)}, bf16[64,256]{1,0:T(8,128)(2,1)S(1)}, bf16[3,512,256]{2,1,0:T(8,128)(2,1)S(1)}) custom-call(s32[1,16]{1,0:T(1,128)S(1)} %add_bitcast_fusion.start_ref, bf16[64,64]{1,0:T(8,128)(2,1)S(1)} %select_convert_fusion.pick_ref, bf16[4,8192]{1,0:T(4,128)(2,1)S(1)} %maximum_select_fusion.features_ref, ...), custom_call_target="tpu_custom_call" | custom-call | flops 201326592 | bytes 6291456 | tf_op jit(solution)/shard_map/merge_blocks/pallas_call | solution.py:248
  24.3 1.9 %finish_rows.1 = (bf16[8192,256]{1,0:T(8,128)(2,1)}, bf16[4,256]{1,0:T(4,128)(2,1)}, bf16[4,2048]{1,0:T(4,128)(2,1)}) custom-call(s32[1,16]{1,0:T(1,128)S(1)} %add_bitcast_fusion.start_ref, bf16[64,256]{1,0:T(8,128)(2,1)S(1)} %get-tuple-element.53.up_ref, bf16[4,8192]{1,0:T(4,128)(2,1)S(1)} %maximum_select_fusion.features_ref, ...), custom_call_target="tpu_custom_call", output_to_operand_aliasing={{0}: (6, {})} | custom-call | flops 67108864 | bytes 2097152 | tf_op jit(solution)/shard_map/finish_rows/pallas_call | solution.py:277
  (30 shorter events, 0.3 us)
Async XLA Ops:
  0.6 0.9 %copy-start = (bf16[64,1024]{1,0:T(8,128)(2,1)S(1)}, bf16[64,1024]{1,0:T(8,128)(2,1)}, u32[]{:S(2)}) copy-start(bf16[64,1024]{1,0:T(8,128)(2,1)} %param.17) | copy-start | bytes 393220
  1.6 10.7 %copy-start.3 = (bf16[4,4096]{1,0:T(4,128)(2,1)S(1)}, bf16[4,4096]{1,0:T(4,128)(2,1)}, u32[]{:S(2)}) copy-start(bf16[4,4096]{1,0:T(4,128)(2,1)} %param.10) | copy-start | bytes 98308
  1.7 11.6 %collective-permute-start.2 = (bf16[1,272,128]{2,1,0:T(8,128)(2,1)S(1)}, bf16[1,272,128]{2,1,0:T(8,128)(2,1)S(1)}, u32[]{:S(2)}, u32[]{:S(2)}) collective-permute-start(bf16[1,272,128]{2,1,0:T(8,128)(2,1)S(1)} %bitcast.13), channel_id=1, source_target_pairs={{0,4},{1,3},{2,6},{3,1},{4,0},{5,7},{6,2},{7,5},{8,12},{9,11},{10,... | collective-permute-start | bytes 208904 | tf_op jit(solution)/shard_map/ppermute | solution.py:332
  4.7 7.7 %collective-permute-start = (bf16[1,272,128]{2,1,0:T(8,128)(2,1)S(1)}, bf16[1,272,128]{2,1,0:T(8,128)(2,1)S(1)}, u32[]{:S(2)}, u32[]{:S(2)}) collective-permute-start(bf16[1,272,128]{2,1,0:T(8,128)(2,1)S(1)} %bitcast.14), channel_id=1, source_target_pairs={{0,8},{1,9},{2,10},{3,11},{4,12},{5,13},{6,14},{7,15},{8,0},{9,1},... | collective-permute-start | bytes 208904 | tf_op jit(solution)/shard_map/ppermute | solution.py:332
  10.3 2.0 %copy-start.1 = (bf16[8192,256]{1,0:T(8,128)(2,1)}, bf16[8192,256]{1,0:T(8,128)(2,1)S(1)}, u32[]{:S(2)}) copy-start(bf16[8192,256]{1,0:T(8,128)(2,1)S(1)} %get-tuple-element.50.served_ref) | copy-start | bytes 12582916
  12.3 6.7 %copy-start.4 = (s32[8]{0:T(128)S(1)}, s32[8]{0:T(128)}, u32[]{:S(2)}) copy-start(s32[8]{0:T(128)} %param.19) | copy-start | bytes 100
  12.3 4.1 %collective-permute-start.3 = (bf16[4,4096]{1,0:T(4,128)(2,1)S(1)}, bf16[4,4096]{1,0:T(4,128)(2,1)S(1)}, u32[]{:S(2)}, u32[]{:S(2)}) collective-permute-start(bf16[4,4096]{1,0:T(4,128)(2,1)S(1)} %copy-done.3), channel_id=1, source_target_pairs={{0,1},{1,0},{2,3},{3,2},{4,5},{5,4},{6,7},{7,6},{8,9},{9,8},{10,11... | collective-permute-start | bytes 98312 | tf_op jit(solution)/shard_map/ppermute | solution.py:352
  12.4 4.3 %collective-permute-start.1 = (bf16[1,272,128]{2,1,0:T(8,128)(2,1)S(1)}, bf16[1,272,128]{2,1,0:T(8,128)(2,1)S(1)}, u32[]{:S(2)}, u32[]{:S(2)}) collective-permute-start(bf16[1,272,128]{2,1,0:T(8,128)(2,1)S(1)} %collective-permute-done), channel_id=1, source_target_pairs={{0,4},{1,3},{2,6},{3,1},{4,0},{5,7},{6,2},{7,5},{8,12},{9,11},{10,... | collective-permute-start | bytes 208904 | tf_op jit(solution)/shard_map/ppermute | solution.py:332
  13.3 8.6 %copy-start.2 = (bf16[8192,256]{1,0:T(8,128)(2,1)S(1)}, bf16[8192,256]{1,0:T(8,128)(2,1)}, u32[]{:S(2)}) copy-start(bf16[8192,256]{1,0:T(8,128)(2,1)} %copy-done.1) | copy-start | bytes 12582916
  13.3 6.0 %collective-permute-start.5 = (bf16[3,272,128]{2,1,0:T(8,128)(2,1)S(1)}, bf16[3,272,128]{2,1,0:T(8,128)(2,1)S(1)}, u32[]{:S(2)}, u32[]{:S(2)}) collective-permute-start(bf16[3,272,128]{2,1,0:T(8,128)(2,1)S(1)} %pad_maximum_fusion.1.rest_0_), channel_id=1, source_target_pairs={{0,2},{1,5},{2,0},{3,7},{4,6},{5,1},{6,4},{7,3},{8,10},{9,13},{10,... | collective-permute-start | bytes 626696 | tf_op jit(solution)/shard_map/ppermute | solution.py:332
  16.8 4.5 %collective-permute-start.4 = (bf16[1,272,128]{2,1,0:T(8,128)(2,1)S(1)}, bf16[1,272,128]{2,1,0:T(8,128)(2,1)S(1)}, u32[]{:S(2)}, u32[]{:S(2)}) collective-permute-start(bf16[1,272,128]{2,1,0:T(8,128)(2,1)S(1)} %collective-permute-done.1), channel_id=1, source_target_pairs={{0,2},{1,5},{2,0},{3,7},{4,6},{5,1},{6,4},{7,3},{8,10},{9,13},{10,... | collective-permute-start | bytes 208904 | tf_op jit(solution)/shard_map/ppermute | solution.py:332
  19.2 2.1 %collective-permute-start.6 = (bf16[4,272,128]{2,1,0:T(8,128)(2,1)S(1)}, bf16[4,272,128]{2,1,0:T(8,128)(2,1)S(1)}, u32[]{:S(2)}, u32[]{:S(2)}) collective-permute-start(bf16[4,272,128]{2,1,0:T(8,128)(2,1)S(1)} %pad_maximum_fusion.slabs_ref), channel_id=1, source_target_pairs={{0,1},{1,0},{2,3},{3,2},{4,5},{5,4},{6,7},{7,6},{8,9},{9,8},{10,11... | collective-permute-start | bytes 835592 | tf_op jit(solution)/shard_map/ppermute | solution.py:394
  21.3 2.9 %collective-permute-start.7 = (bf16[4,272,128]{2,1,0:T(8,128)(2,1)S(1)}, bf16[4,272,128]{2,1,0:T(8,128)(2,1)S(1)}, u32[]{:S(2)}, u32[]{:S(2)}) collective-permute-start(bf16[4,272,128]{2,1,0:T(8,128)(2,1)S(1)} %constant_dynamic-update-slice_fusion.5.last_ref), channel_id=1, source_target_pairs={{0,1},{1,0},{2,3},{3,2},{4,5},{5,4},{6,7},{7,6},{8,9},{9,8},{10,11... | collective-permute-start | bytes 835592 | tf_op jit(solution)/shard_map/ppermute | solution.py:399

commit v16 on v15

--- a/solution.py
+++ b/solution.py
@@ -344,20 +344,21 @@
 
     cuts = [0, rows // 2, rows - rows // 4, rows]
     first_rows, second_rows, third_rows = (range(*cut) for cut in zip(cuts, cuts[1:]))
+    hid_other = lax.ppermute(hidden_in, "tensor", swap)
     came = exchange(slabs, first)
-    ahead = exchange(slabs, second)
-    *part, served = attend(first_rows, given, *in_hbm(served_value_weight), [slabs])
+    part = attend(first_rows, given, after=[slabs])
+    part, ahead = lax.optimization_barrier((part, slabs))
+    ahead = exchange(ahead, second)
+    came, part = lax.optimization_barrier((came, part))
     parts = [part]
-    part, hid_other = lax.optimization_barrier((part, hidden_in))
-    hid_other = lax.ppermute(hid_other, "tensor", swap)
-    came, part = lax.optimization_barrier((came, part))
     slabs = jnp.concatenate([slabs, came, ahead], axis=0)
     came = exchange(came, second)
     images = exchange(slabs, third)
-    parts.append(attend(second_rows, given, after=[slabs]))
-    came, parts[1], hid_other, owner_rank = lax.optimization_barrier(
-        (came, parts[1], hid_other, owner_rank)
-    )
+    *part, served = attend(second_rows, given, *in_hbm(served_value_weight), [slabs])
+    came, part, hid_other, owner_rank = lax.optimization_barrier(
+        (came, part, hid_other, owner_rank)
+    )
+    parts.append(part)
     last = exchange(came, third)
     slabs = jnp.concatenate([slabs, came], axis=0)
     parts.append(attend(third_rows, given, after=[images]))

time: 26.4 us -> 26.2 us (level)
  waiting for transfers between devices: 0.39 us -> 3.7 us
  local copies, waits for them, and re-layouts: 3.06 us -> 0.83 us
  starting transfers between devices: 10.6 us -> 8.71 us
  Pallas kernels: 11 us -> 11.5 us
    ppermute x5, waiting for transfers between devices: 0.38 us -> 3.69 us  [exchange(): return lax.ppermute(x, ('replica', 'tensor'), pairs)]
    unnamed x17 -> x13, local copies, waits for them, and re-layouts: 2.3 us -> 0.1 us
    ppermute x5, starting transfers between devices: 9.99 us -> 8.05 us  [exchange(): return lax.ppermute(x, ('replica', 'tensor'), pairs)]
    pallas_call x3, Pallas kernels: 6.7 us -> 7.23 us  [attend(): pl.pallas_call(functools.partial(attend_kernel, rows, fetch), out_shape=o...]
    ppermute x1, starting transfers between devices: 0.01 us -> 0.52 us  [body(): hid_other = lax.ppermute(hidden_in, 'tensor', swap)]
    ppermute x1, starting transfers between devices: 0.55 us -> 0.07 us  [body(): last_crossed = lax.ppermute(last, 'tensor', swap)]
  transfers between devices with their start and end apart: 8 -> 8, of which waited for: 1 -> 3; matrix products, arithmetic and copies ran while one was open for 1% -> 4% of each run, Pallas kernels for 35% -> 37%
where the time goes in v16:
time: 26.2 us; the launch traced here: 25.9 us
  Pallas kernels  11.5 us (44%)
  starting transfers between devices  8.71 us (33%)
  waiting for transfers between devices  3.7 us (14%)
  local copies, waits for them, and re-layouts  0.83 us (3%)
  between operations  0.82 us (3%)
  other arithmetic  0.32 us (1%)
    ppermute x5, starting transfers between devices, exchange(): return lax.ppermute(x, ('replica', 'tensor'), pairs)  8.05 us
    pallas_call x3, Pallas kernels, attend(): pl.pallas_call(functools.partial(attend_kernel, rows, fetch), out_shape=o...  7.23 us
    ppermute x5, waiting for transfers between devices, exchange(): return lax.ppermute(x, ('replica', 'tensor'), pairs)  3.69 us
    pallas_call x1, Pallas kernels, merge(): pl.pallas_call(functools.partial(merge_kernel, per, left), out_shape=(jax...  2.39 us
    pallas_call x1, Pallas kernels, finish(): pl.pallas_call(final_kernel, out_shape=[jax.ShapeDtypeStruct(shape, jnp.b...  1.93 us
    slice x1, local copies, waits for them, and re-layouts, panels(): return [x[:, i:i + PANEL] for i in range(0, x.shape[1], PANEL)]  0.7 us
  transfers between devices with their start and end apart: 8, of which 3 were waited for; matrix products, arithmetic and copies ran while one was open for 4% of the time, Pallas kernels for 37%

profile of v16, /device:TPU:0, one launch (start us, length us, event | category | flops | bytes accessed | tf_op | source)
XLA Modules:
  0.0 25.9 jit_solution(16850942260307604161)
XLA Ops:
  0.6 0.0 copy-start
  0.6 0.5 %collective-permute-start.3 = (bf16[4,4096]{1,0:T(4,128)(2,1)}, bf16[4,4096]{1,0:T(4,128)(2,1)S(1)}, u32[]{:S(2)}, u32[]{:S(2)}) collective-permute-start(bf16[4,4096]{1,0:T(4,128)(2,1)} %param.10), channel_id=1, source_target_pairs={{0,1},{1,0},{2,3},{3,2},{4,5},{5,4},{6,7},{7,6},{8,9},{9,8},{10,11... | collective-permute-start | bytes 98312 | tf_op jit(solution)/shard_map/ppermute | solution.py:347
  1.2 0.7 %fusion.1 = (bf16[8,128]{1,0:T(8,128)(2,1)S(1)}, bf16[8,128]{1,0:T(8,128)(2,1)S(1)}) fusion(bf16[8,256]{1,0:T(8,128)(2,1)} %param.18), kind=kLoop, calls=%fused_computation.34 | loop fusion | bytes 8192 | tf_op jit(solution)/shard_map/slice | solution.py:302
  1.9 3.8 %collective-permute-start = (bf16[1,272,128]{2,1,0:T(8,128)(2,1)S(1)}, bf16[1,272,128]{2,1,0:T(8,128)(2,1)S(1)}, u32[]{:S(2)}, u32[]{:S(2)}) collective-permute-start(bf16[1,272,128]{2,1,0:T(8,128)(2,1)S(1)} %bitcast.13), channel_id=1, source_target_pairs={{0,8},{1,9},{2,10},{3,11},{4,12},{5,13},{6,14},{7,15},{8,0},{9,1},... | collective-permute-start | bytes 208904 | tf_op jit(solution)/shard_map/ppermute | solution.py:332
  5.7 2.8 %attend_cache.3 = (f32[2,16,128]{2,1,0:T(8,128)S(1)}, f32[2,16,128]{2,1,0:T(8,128)S(1)}) custom-call(s32[4]{0:T(128)} %lengths_hbm.5, bf16[4,2048]{1,0:T(4,128)(2,1)} %q_hbm.5, bf16[4,256]{1,0:T(4,128)(2,1)} %own_k_hbm.5, bf16[4,1024,256]{2,1,0:T(8,128)(2,1)} %k_hbm.5, bf16[4,1024,256]{2,1,0:T(8,128)(2,1)} %v_hbm.5, bf16[1,272,128]{2,1,0:T(8,128)(2,1)S(1)} %bitcast.14), custom_call_target="tpu_custom_call" | custom-call | flops 33554432 | bytes 2097152 | tf_op jit(solution)/shard_map/attend_cache/pallas_call | solution.py:113
  8.5 1.6 %collective-permute-start.2 = (bf16[1,272,128]{2,1,0:T(8,128)(2,1)S(1)}, bf16[1,272,128]{2,1,0:T(8,128)(2,1)S(1)}, u32[]{:S(2)}, u32[]{:S(2)}) collective-permute-start(bf16[1,272,128]{2,1,0:T(8,128)(2,1)S(1)} %bitcast.15), channel_id=1, source_target_pairs={{0,4},{1,3},{2,6},{3,1},{4,0},{5,7},{6,2},{7,5},{8,12},{9,11},{10,... | collective-permute-start | bytes 208904 | tf_op jit(solution)/shard_map/ppermute | solution.py:332
  10.2 0.1 pad_add_fusion
  10.2 0.5 %collective-permute-start.1 = (bf16[1,272,128]{2,1,0:T(8,128)(2,1)S(1)}, bf16[1,272,128]{2,1,0:T(8,128)(2,1)S(1)}, u32[]{:S(2)}, u32[]{:S(2)}) collective-permute-start(bf16[1,272,128]{2,1,0:T(8,128)(2,1)S(1)} %collective-permute-done), channel_id=1, source_target_pairs={{0,4},{1,3},{2,6},{3,1},{4,0},{5,7},{6,2},{7,5},{8,12},{9,11},{10,... | collective-permute-start | bytes 208904 | tf_op jit(solution)/shard_map/ppermute | solution.py:332
  10.7 2.1 %collective-permute-done.2 = bf16[1,272,128]{2,1,0:T(8,128)(2,1)S(1)} collective-permute-done((bf16[1,272,128]{2,1,0:T(8,128)(2,1)S(1)}, bf16[1,272,128]{2,1,0:T(8,128)(2,1)S(1)}, u32[]{:S(2)}, u32[]{:S(2)}) %collective-permute-start.2) | collective-permute-done | bytes 69664 | tf_op jit(solution)/shard_map/ppermute | solution.py:332
  12.9 0.0 copy-start.2
  12.9 0.0 copy-start.1
  12.9 1.6 %collective-permute-start.5 = (bf16[3,272,128]{2,1,0:T(8,128)(2,1)S(1)}, bf16[3,272,128]{2,1,0:T(8,128)(2,1)S(1)}, u32[]{:S(2)}, u32[]{:S(2)}) collective-permute-start(bf16[3,272,128]{2,1,0:T(8,128)(2,1)S(1)} %pad_maximum_fusion.1.rest_1_), channel_id=1, source_target_pairs={{0,2},{1,5},{2,0},{3,7},{4,6},{5,1},{6,4},{7,3},{8,10},{9,13},{10,... | collective-permute-start | bytes 626696 | tf_op jit(solution)/shard_map/ppermute | solution.py:332
  14.5 2.6 %attend_cache.4 = (f32[1,16,128]{2,1,0:T(8,128)S(1)}, f32[1,16,128]{2,1,0:T(8,128)S(1)}, bf16[8192,256]{1,0:T(8,128)(2,1)S(1)}) custom-call(s32[4]{0:T(128)} %lengths_hbm.5, bf16[4,2048]{1,0:T(4,128)(2,1)} %q_hbm.5, bf16[4,256]{1,0:T(4,128)(2,1)} %own_k_hbm.5, bf16[4,1024,256]{2,1,0:T(8,128)(2,1)} %k_hbm.5, bf16[4,1024,256]{2,1,0:T(8,128)(2,1)} %v_hbm.5, ...), custom_call_target="tpu_custom_call" | custom-call | flops 16777216 | bytes 1048576 | tf_op jit(solution)/shard_map/attend_cache/pallas_call | solution.py:113
  17.1 0.0 collective-permute-done.3
  17.1 0.6 %collective-permute-start.4 = (bf16[1,272,128]{2,1,0:T(8,128)(2,1)S(1)}, bf16[1,272,128]{2,1,0:T(8,128)(2,1)S(1)}, u32[]{:S(2)}, u32[]{:S(2)}) collective-permute-start(bf16[1,272,128]{2,1,0:T(8,128)(2,1)S(1)} %collective-permute-done.1), channel_id=1, source_target_pairs={{0,2},{1,5},{2,0},{3,7},{4,6},{5,1},{6,4},{7,3},{8,10},{9,13},{10,... | collective-permute-start | bytes 208904 | tf_op jit(solution)/shard_map/ppermute | solution.py:332
  17.7 0.1 select_reduce_fusion
  17.8 0.1 collective-permute-start.6
  18.0 0.8 %collective-permute-done.5.rest_0_ = bf16[3,272,128]{2,1,0:T(8,128)(2,1)S(1)} collective-permute-done((bf16[3,272,128]{2,1,0:T(8,128)(2,1)S(1)}, bf16[3,272,128]{2,1,0:T(8,128)(2,1)S(1)}, u32[]{:S(2)}, u32[]{:S(2)}) %collective-permute-start.5) | collective-permute-done | bytes 208928 | tf_op jit(solution)/shard_map/ppermute | solution.py:332
  18.8 1.9 %attend_cache.5 = (f32[1,16,128]{2,1,0:T(8,128)S(1)}, f32[1,16,128]{2,1,0:T(8,128)S(1)}) custom-call(s32[4]{0:T(128)} %lengths_hbm.5, bf16[4,2048]{1,0:T(4,128)(2,1)} %q_hbm.5, bf16[4,256]{1,0:T(4,128)(2,1)} %own_k_hbm.5, bf16[4,1024,256]{2,1,0:T(8,128)(2,1)} %k_hbm.5, bf16[4,1024,256]{2,1,0:T(8,128)(2,1)} %v_hbm.5, ...), custom_call_target="tpu_custom_call" | custom-call | flops 16777216 | bytes 1048576 | tf_op jit(solution)/shard_map/attend_cache/pallas_call | solution.py:113
  20.7 0.7 %collective-permute-done.4 = bf16[1,272,128]{2,1,0:T(8,128)(2,1)S(1)} collective-permute-done((bf16[1,272,128]{2,1,0:T(8,128)(2,1)S(1)}, bf16[1,272,128]{2,1,0:T(8,128)(2,1)S(1)}, u32[]{:S(2)}, u32[]{:S(2)}) %collective-permute-start.4) | collective-permute-done | bytes 69664 | tf_op jit(solution)/shard_map/ppermute | solution.py:332
  21.5 0.0 collective-permute-done.6.crossed_ref
  21.5 0.1 collective-permute-start.7
  21.6 2.4 %merge_blocks.1 = (bf16[8192,256]{1,0:T(8,128)(2,1)}, f32[4,256]{1,0:T(4,128)S(1)}, bf16[64,256]{1,0:T(8,128)(2,1)S(1)}, bf16[3,512,256]{2,1,0:T(8,128)(2,1)S(1)}) custom-call(s32[1,16]{1,0:T(1,128)S(1)} %add_bitcast_fusion.start_ref, bf16[64,64]{1,0:T(8,128)(2,1)S(1)} %select_convert_fusion.pick_ref, bf16[4,8192]{1,0:T(4,128)(2,1)S(1)} %maximum_select_fusion.features_ref, ...), custom_call_target="tpu_custom_call" | custom-call | flops 201326592 | bytes 6291456 | tf_op jit(solution)/shard_map/merge_blocks/pallas_call | solution.py:248
  24.0 1.9 %finish_rows.1 = (bf16[8192,256]{1,0:T(8,128)(2,1)}, bf16[4,256]{1,0:T(4,128)(2,1)}, bf16[4,2048]{1,0:T(4,128)(2,1)}) custom-call(s32[1,16]{1,0:T(1,128)S(1)} %add_bitcast_fusion.start_ref, bf16[64,256]{1,0:T(8,128)(2,1)S(1)} %get-tuple-element.63.up_ref, bf16[4,8192]{1,0:T(4,128)(2,1)S(1)} %maximum_select_fusion.features_ref, ...), custom_call_target="tpu_custom_call", output_to_operand_aliasing={{0}: (6, {})} | custom-call | flops 67108864 | bytes 2097152 | tf_op jit(solution)/shard_map/finish_rows/pallas_call | solution.py:277
  (26 shorter events, 0.3 us)
Async XLA Ops:
  0.6 1.2 %copy-start = (bf16[64,1024]{1,0:T(8,128)(2,1)S(1)}, bf16[64,1024]{1,0:T(8,128)(2,1)}, u32[]{:S(2)}) copy-start(bf16[64,1024]{1,0:T(8,128)(2,1)} %param.17) | copy-start | bytes 393220
  0.6 16.5 %collective-permute-start.3 = (bf16[4,4096]{1,0:T(4,128)(2,1)}, bf16[4,4096]{1,0:T(4,128)(2,1)S(1)}, u32[]{:S(2)}, u32[]{:S(2)}) collective-permute-start(bf16[4,4096]{1,0:T(4,128)(2,1)} %param.10), channel_id=1, source_target_pairs={{0,1},{1,0},{2,3},{3,2},{4,5},{5,4},{6,7},{7,6},{8,9},{9,8},{10,11... | collective-permute-start | bytes 98312 | tf_op jit(solution)/shard_map/ppermute | solution.py:347
  1.9 8.3 %collective-permute-start = (bf16[1,272,128]{2,1,0:T(8,128)(2,1)S(1)}, bf16[1,272,128]{2,1,0:T(8,128)(2,1)S(1)}, u32[]{:S(2)}, u32[]{:S(2)}) collective-permute-start(bf16[1,272,128]{2,1,0:T(8,128)(2,1)S(1)} %bitcast.13), channel_id=1, source_target_pairs={{0,8},{1,9},{2,10},{3,11},{4,12},{5,13},{6,14},{7,15},{8,0},{9,1},... | collective-permute-start | bytes 208904 | tf_op jit(solution)/shard_map/ppermute | solution.py:332
  8.5 4.4 %collective-permute-start.2 = (bf16[1,272,128]{2,1,0:T(8,128)(2,1)S(1)}, bf16[1,272,128]{2,1,0:T(8,128)(2,1)S(1)}, u32[]{:S(2)}, u32[]{:S(2)}) collective-permute-start(bf16[1,272,128]{2,1,0:T(8,128)(2,1)S(1)} %bitcast.15), channel_id=1, source_target_pairs={{0,4},{1,3},{2,6},{3,1},{4,0},{5,7},{6,2},{7,5},{8,12},{9,11},{10,... | collective-permute-start | bytes 208904 | tf_op jit(solution)/shard_map/ppermute | solution.py:332
  10.2 6.9 %collective-permute-start.1 = (bf16[1,272,128]{2,1,0:T(8,128)(2,1)S(1)}, bf16[1,272,128]{2,1,0:T(8,128)(2,1)S(1)}, u32[]{:S(2)}, u32[]{:S(2)}) collective-permute-start(bf16[1,272,128]{2,1,0:T(8,128)(2,1)S(1)} %collective-permute-done), channel_id=1, source_target_pairs={{0,4},{1,3},{2,6},{3,1},{4,0},{5,7},{6,2},{7,5},{8,12},{9,11},{10,... | collective-permute-start | bytes 208904 | tf_op jit(solution)/shard_map/ppermute | solution.py:332
  12.9 4.8 %copy-start.2 = (s32[8]{0:T(128)S(1)}, s32[8]{0:T(128)}, u32[]{:S(2)}) copy-start(s32[8]{0:T(128)} %param.19) | copy-start | bytes 100
  12.9 5.0 %copy-start.1 = (bf16[4,4096]{1,0:T(4,128)(2,1)S(1)}, bf16[4,4096]{1,0:T(4,128)(2,1)}, u32[]{:S(2)}) copy-start(bf16[4,4096]{1,0:T(4,128)(2,1)} %param.10) | copy-start | bytes 98308
  12.9 5.9 %collective-permute-start.5 = (bf16[3,272,128]{2,1,0:T(8,128)(2,1)S(1)}, bf16[3,272,128]{2,1,0:T(8,128)(2,1)S(1)}, u32[]{:S(2)}, u32[]{:S(2)}) collective-permute-start(bf16[3,272,128]{2,1,0:T(8,128)(2,1)S(1)} %pad_maximum_fusion.1.rest_1_), channel_id=1, source_target_pairs={{0,2},{1,5},{2,0},{3,7},{4,6},{5,1},{6,4},{7,3},{8,10},{9,13},{10,... | collective-permute-start | bytes 626696 | tf_op jit(solution)/shard_map/ppermute | solution.py:332
  17.1 4.4 %collective-permute-start.4 = (bf16[1,272,128]{2,1,0:T(8,128)(2,1)S(1)}, bf16[1,272,128]{2,1,0:T(8,128)(2,1)S(1)}, u32[]{:S(2)}, u32[]{:S(2)}) collective-permute-start(bf16[1,272,128]{2,1,0:T(8,128)(2,1)S(1)} %collective-permute-done.1), channel_id=1, source_target_pairs={{0,2},{1,5},{2,0},{3,7},{4,6},{5,1},{6,4},{7,3},{8,10},{9,13},{10,... | collective-permute-start | bytes 208904 | tf_op jit(solution)/shard_map/ppermute | solution.py:332
  17.8 3.7 %collective-permute-start.6 = (bf16[4,272,128]{2,1,0:T(8,128)(2,1)S(1)}, bf16[4,272,128]{2,1,0:T(8,128)(2,1)S(1)}, u32[]{:S(2)}, u32[]{:S(2)}) collective-permute-start(bf16[4,272,128]{2,1,0:T(8,128)(2,1)S(1)} %pad_maximum_fusion.slabs_ref), channel_id=1, source_target_pairs={{0,1},{1,0},{2,3},{3,2},{4,5},{5,4},{6,7},{7,6},{8,9},{9,8},{10,11... | collective-permute-start | bytes 835592 | tf_op jit(solution)/shard_map/ppermute | solution.py:395
  21.5 2.5 %collective-permute-start.7 = (bf16[4,272,128]{2,1,0:T(8,128)(2,1)S(1)}, bf16[4,272,128]{2,1,0:T(8,128)(2,1)S(1)}, u32[]{:S(2)}, u32[]{:S(2)}) collective-permute-start(bf16[4,272,128]{2,1,0:T(8,128)(2,1)S(1)} %constant_dynamic-update-slice_fusion.5.last_ref), channel_id=1, source_target_pairs={{0,1},{1,0},{2,3},{3,2},{4,5},{5,4},{6,7},{7,6},{8,9},{9,8},{10,11... | collective-permute-start | bytes 835592 | tf_op jit(solution)/shard_map/ppermute | solution.py:400

commit v17 on v16

--- a/solution.py
+++ b/solution.py
@@ -347,12 +347,10 @@
     hid_other = lax.ppermute(hidden_in, "tensor", swap)
     came = exchange(slabs, first)
     part = attend(first_rows, given, after=[slabs])
-    part, ahead = lax.optimization_barrier((part, slabs))
-    ahead = exchange(ahead, second)
     came, part = lax.optimization_barrier((came, part))
     parts = [part]
-    slabs = jnp.concatenate([slabs, came, ahead], axis=0)
-    came = exchange(came, second)
+    slabs = jnp.concatenate([slabs, came], axis=0)
+    came = exchange(slabs, second)
     images = exchange(slabs, third)
     *part, served = attend(second_rows, given, *in_hbm(served_value_weight), [slabs])
     came, part, hid_other, owner_rank = lax.optimization_barrier(
@@ -360,7 +358,7 @@
     )
     parts.append(part)
     last = exchange(came, third)
-    slabs = jnp.concatenate([slabs, came], axis=0)
+    slabs = jnp.concatenate([slabs, came, images], axis=0)
     parts.append(attend(third_rows, given, after=[images]))
     features = jnp.concatenate([hidden_in, hid_other], axis=1)
     features = jnp.where(core == 0, features, jnp.concatenate([hid_other, hidden_in], axis=1))
@@ -396,7 +394,6 @@
     last, start, pick, context, own_weight, features, crossed = lax.optimization_barrier(
         (last, start, pick, context, own_weight, features, crossed)
     )
-    last = jnp.concatenate([images, last], axis=0)
     last_crossed = lax.ppermute(last, "tensor", swap)
     merged, total, up, left = merge(per, start, pick, features, served, slabs, crossed, last)
     return tuple(

time: 26.2 us -> 25.3 us (0.966)
  starting transfers between devices: 8.71 us -> 7.4 us
  waiting for transfers between devices: 3.7 us -> 4.58 us
  Pallas kernels: 11.5 us -> 11.1 us
    ppermute x5 -> x4, starting transfers between devices: 8.05 us -> 6.81 us  [exchange(): return lax.ppermute(x, ('replica', 'tensor'), pairs)]
    ppermute x5 -> x4, waiting for transfers between devices: 3.69 us -> 4.57 us  [exchange(): return lax.ppermute(x, ('replica', 'tensor'), pairs)]
    pallas_call x1, Pallas kernels: 1.93 us -> 1.38 us  [finish(): pl.pallas_call(final_kernel, out_shape=[jax.ShapeDtypeStruct(shape, jnp.b...]
  transfers between devices with their start and end apart: 8 -> 7, of which waited for: 3 -> 3; matrix products, arithmetic and copies ran while one was open for 4% -> 4% of each run, Pallas kernels for 37% -> 39%
where the time goes in v17:
time: 25.3 us; the launch traced here: 25 us
  Pallas kernels  11.1 us (44%)
  starting transfers between devices  7.4 us (29%)
  waiting for transfers between devices  4.58 us (18%)
  local copies, waits for them, and re-layouts  0.8 us (3%)
  between operations  0.78 us (3%)
  other arithmetic  0.32 us (1%)
    pallas_call x3, Pallas kernels, attend(): pl.pallas_call(functools.partial(attend_kernel, rows, fetch), out_shape=o...  7.24 us
    ppermute x4, starting transfers between devices, exchange(): return lax.ppermute(x, ('replica', 'tensor'), pairs)  6.81 us
    ppermute x4, waiting for transfers between devices, exchange(): return lax.ppermute(x, ('replica', 'tensor'), pairs)  4.57 us
    pallas_call x1, Pallas kernels, merge(): pl.pallas_call(functools.partial(merge_kernel, per, left), out_shape=(jax...  2.51 us
    pallas_call x1, Pallas kernels, finish(): pl.pallas_call(final_kernel, out_shape=[jax.ShapeDtypeStruct(shape, jnp.b...  1.38 us
    slice x1, local copies, waits for them, and re-layouts, panels(): return [x[:, i:i + PANEL] for i in range(0, x.shape[1], PANEL)]  0.7 us
    ppermute x1, starting transfers between devices, body(): hid_other = lax.ppermute(hidden_in, 'tensor', swap)  0.52 us
  transfers between devices with their start and end apart: 7, of which 3 were waited for; matrix products, arithmetic and copies ran while one was open for 4% of the time, Pallas kernels for 39%

profile of v17, /device:TPU:0, one launch (start us, length us, event | category | flops | bytes accessed | tf_op | source)
XLA Modules:
  0.0 25.0 jit_solution(4310912442047692155)
XLA Ops:
  0.6 0.0 copy-start
  0.6 0.5 %collective-permute-start.2 = (bf16[4,4096]{1,0:T(4,128)(2,1)}, bf16[4,4096]{1,0:T(4,128)(2,1)S(1)}, u32[]{:S(2)}, u32[]{:S(2)}) collective-permute-start(bf16[4,4096]{1,0:T(4,128)(2,1)} %param.10), channel_id=1, source_target_pairs={{0,1},{1,0},{2,3},{3,2},{4,5},{5,4},{6,7},{7,6},{8,9},{9,8},{10,11... | collective-permute-start | bytes 98312 | tf_op jit(solution)/shard_map/ppermute | solution.py:347
  1.2 0.7 %fusion.1 = (bf16[8,128]{1,0:T(8,128)(2,1)S(1)}, bf16[8,128]{1,0:T(8,128)(2,1)S(1)}) fusion(bf16[8,256]{1,0:T(8,128)(2,1)} %param.18), kind=kLoop, calls=%fused_computation.32 | loop fusion | bytes 8192 | tf_op jit(solution)/shard_map/slice | solution.py:302
  1.9 3.8 %collective-permute-start = (bf16[1,272,128]{2,1,0:T(8,128)(2,1)S(1)}, bf16[1,272,128]{2,1,0:T(8,128)(2,1)S(1)}, u32[]{:S(2)}, u32[]{:S(2)}) collective-permute-start(bf16[1,272,128]{2,1,0:T(8,128)(2,1)S(1)} %bitcast.13), channel_id=1, source_target_pairs={{0,8},{1,9},{2,10},{3,11},{4,12},{5,13},{6,14},{7,15},{8,0},{9,1},... | collective-permute-start | bytes 208904 | tf_op jit(solution)/shard_map/ppermute | solution.py:332
  5.7 2.8 %attend_cache.3 = (f32[2,16,128]{2,1,0:T(8,128)S(1)}, f32[2,16,128]{2,1,0:T(8,128)S(1)}) custom-call(s32[4]{0:T(128)} %lengths_hbm.5, bf16[4,2048]{1,0:T(4,128)(2,1)} %q_hbm.5, bf16[4,256]{1,0:T(4,128)(2,1)} %own_k_hbm.5, bf16[4,1024,256]{2,1,0:T(8,128)(2,1)} %k_hbm.5, bf16[4,1024,256]{2,1,0:T(8,128)(2,1)} %v_hbm.5, bf16[1,272,128]{2,1,0:T(8,128)(2,1)S(1)} %bitcast.14), custom_call_target="tpu_custom_call" | custom-call | flops 33554432 | bytes 2097152 | tf_op jit(solution)/shard_map/attend_cache/pallas_call | solution.py:113
  8.5 1.4 %collective-permute-done = bf16[1,272,128]{2,1,0:T(8,128)(2,1)S(1)} collective-permute-done((bf16[1,272,128]{2,1,0:T(8,128)(2,1)S(1)}, bf16[1,272,128]{2,1,0:T(8,128)(2,1)S(1)}, u32[]{:S(2)}, u32[]{:S(2)}) %collective-permute-start) | collective-permute-done | bytes 69664 | tf_op jit(solution)/shard_map/ppermute | solution.py:332
  10.0 0.8 %collective-permute-start.1 = (bf16[2,272,128]{2,1,0:T(8,128)(2,1)S(1)}, bf16[2,272,128]{2,1,0:T(8,128)(2,1)S(1)}, u32[]{:S(2)}, u32[]{:S(2)}) collective-permute-start(bf16[2,272,128]{2,1,0:T(8,128)(2,1)S(1)} %pad_maximum_fusion.1.rest_1_), channel_id=1, source_target_pairs={{0,4},{1,3},{2,6},{3,1},{4,0},{5,7},{6,2},{7,5},{8,12},{9,11},{10,... | collective-permute-start | bytes 417800 | tf_op jit(solution)/shard_map/ppermute | solution.py:332
  10.8 0.1 pad_add_fusion
  10.9 1.6 %collective-permute-start.4 = (bf16[2,272,128]{2,1,0:T(8,128)(2,1)S(1)}, bf16[2,272,128]{2,1,0:T(8,128)(2,1)S(1)}, u32[]{:S(2)}, u32[]{:S(2)}) collective-permute-start(bf16[2,272,128]{2,1,0:T(8,128)(2,1)S(1)} %pad_maximum_fusion.1.rest_1_), channel_id=1, source_target_pairs={{0,2},{1,5},{2,0},{3,7},{4,6},{5,1},{6,4},{7,3},{8,10},{9,13},{10,... | collective-permute-start | bytes 417800 | tf_op jit(solution)/shard_map/ppermute | solution.py:332
  12.5 2.6 %attend_cache.4 = (f32[1,16,128]{2,1,0:T(8,128)S(1)}, f32[1,16,128]{2,1,0:T(8,128)S(1)}, bf16[8192,256]{1,0:T(8,128)(2,1)S(1)}) custom-call(s32[4]{0:T(128)} %lengths_hbm.5, bf16[4,2048]{1,0:T(4,128)(2,1)} %q_hbm.5, bf16[4,256]{1,0:T(4,128)(2,1)} %own_k_hbm.5, bf16[4,1024,256]{2,1,0:T(8,128)(2,1)} %k_hbm.5, bf16[4,1024,256]{2,1,0:T(8,128)(2,1)} %v_hbm.5, ...), custom_call_target="tpu_custom_call" | custom-call | flops 16777216 | bytes 1048576 | tf_op jit(solution)/shard_map/attend_cache/pallas_call | solution.py:113
  15.1 0.0 collective-permute-done.2
  15.1 1.0 %collective-permute-done.1 = bf16[2,272,128]{2,1,0:T(8,128)(2,1)S(1)} collective-permute-done((bf16[2,272,128]{2,1,0:T(8,128)(2,1)S(1)}, bf16[2,272,128]{2,1,0:T(8,128)(2,1)S(1)}, u32[]{:S(2)}, u32[]{:S(2)}) %collective-permute-start.1) | collective-permute-done | bytes 139296 | tf_op jit(solution)/shard_map/ppermute | solution.py:332
  16.0 0.7 %collective-permute-start.3 = (bf16[2,272,128]{2,1,0:T(8,128)(2,1)S(1)}, bf16[2,272,128]{2,1,0:T(8,128)(2,1)S(1)}, u32[]{:S(2)}, u32[]{:S(2)}) collective-permute-start(bf16[2,272,128]{2,1,0:T(8,128)(2,1)S(1)} %collective-permute-done.1), channel_id=1, source_target_pairs={{0,2},{1,5},{2,0},{3,7},{4,6},{5,1},{6,4},{7,3},{8,10},{9,13},{10,... | collective-permute-start | bytes 417800 | tf_op jit(solution)/shard_map/ppermute | solution.py:332
  16.7 0.1 select_reduce_fusion
  16.8 0.0 collective-permute-done.4.rest_0_
  16.8 0.1 pad_maximum_fusion.slabs_ref
  16.9 0.1 collective-permute-start.5
  17.0 1.9 %attend_cache.5 = (f32[1,16,128]{2,1,0:T(8,128)S(1)}, f32[1,16,128]{2,1,0:T(8,128)S(1)}) custom-call(s32[4]{0:T(128)} %lengths_hbm.5, bf16[4,2048]{1,0:T(4,128)(2,1)} %q_hbm.5, bf16[4,256]{1,0:T(4,128)(2,1)} %own_k_hbm.5, bf16[4,1024,256]{2,1,0:T(8,128)(2,1)} %k_hbm.5, bf16[4,1024,256]{2,1,0:T(8,128)(2,1)} %v_hbm.5, ...), custom_call_target="tpu_custom_call" | custom-call | flops 16777216 | bytes 1048576 | tf_op jit(solution)/shard_map/attend_cache/pallas_call | solution.py:113
  18.9 2.2 %collective-permute-done.3.last_ref = bf16[2,272,128]{2,1,0:T(8,128)(2,1)S(1)} collective-permute-done((bf16[2,272,128]{2,1,0:T(8,128)(2,1)S(1)}, bf16[2,272,128]{2,1,0:T(8,128)(2,1)S(1)}, u32[]{:S(2)}, u32[]{:S(2)}) %collective-permute-start.3) | collective-permute-done | bytes 139296 | tf_op jit(solution)/shard_map/ppermute | solution.py:332
  21.1 0.0 collective-permute-done.5.crossed_ref
  21.1 0.0 collective-permute-start.6
  21.1 2.5 %merge_blocks.1 = (bf16[8192,256]{1,0:T(8,128)(2,1)}, f32[4,256]{1,0:T(4,128)S(1)}, bf16[64,256]{1,0:T(8,128)(2,1)S(1)}, bf16[3,512,256]{2,1,0:T(8,128)(2,1)S(1)}) custom-call(s32[1,16]{1,0:T(1,128)S(1)} %add_bitcast_fusion.start_ref, bf16[64,64]{1,0:T(8,128)(2,1)S(1)} %select_convert_fusion.pick_ref, bf16[4,8192]{1,0:T(4,128)(2,1)S(1)} %maximum_select_fusion.features_ref, ...), custom_call_target="tpu_custom_call" | custom-call | flops 234881024 | bytes 7340032 | tf_op jit(solution)/shard_map/merge_blocks/pallas_call | solution.py:248
  23.6 0.0 collective-permute-done.6.last_ref
  23.6 1.4 %finish_rows.1 = (bf16[8192,256]{1,0:T(8,128)(2,1)}, bf16[4,256]{1,0:T(4,128)(2,1)}, bf16[4,2048]{1,0:T(4,128)(2,1)}) custom-call(s32[1,16]{1,0:T(1,128)S(1)} %add_bitcast_fusion.start_ref, bf16[64,256]{1,0:T(8,128)(2,1)S(1)} %get-tuple-element.57.up_ref, bf16[4,8192]{1,0:T(4,128)(2,1)S(1)} %maximum_select_fusion.features_ref, ...), custom_call_target="tpu_custom_call", output_to_operand_aliasing={{0}: (6, {})} | custom-call | flops 33554432 | bytes 1048576 | tf_op jit(solution)/shard_map/finish_rows/pallas_call | solution.py:277
  (22 shorter events, 0.2 us)
Async XLA Ops:
  0.6 1.2 %copy-start = (bf16[64,1024]{1,0:T(8,128)(2,1)S(1)}, bf16[64,1024]{1,0:T(8,128)(2,1)}, u32[]{:S(2)}) copy-start(bf16[64,1024]{1,0:T(8,128)(2,1)} %param.17) | copy-start | bytes 393220
  0.6 14.4 %collective-permute-start.2 = (bf16[4,4096]{1,0:T(4,128)(2,1)}, bf16[4,4096]{1,0:T(4,128)(2,1)S(1)}, u32[]{:S(2)}, u32[]{:S(2)}) collective-permute-start(bf16[4,4096]{1,0:T(4,128)(2,1)} %param.10), channel_id=1, source_target_pairs={{0,1},{1,0},{2,3},{3,2},{4,5},{5,4},{6,7},{7,6},{8,9},{9,8},{10,11... | collective-permute-start | bytes 98312 | tf_op jit(solution)/shard_map/ppermute | solution.py:347
  1.9 8.0 %collective-permute-start = (bf16[1,272,128]{2,1,0:T(8,128)(2,1)S(1)}, bf16[1,272,128]{2,1,0:T(8,128)(2,1)S(1)}, u32[]{:S(2)}, u32[]{:S(2)}) collective-permute-start(bf16[1,272,128]{2,1,0:T(8,128)(2,1)S(1)} %bitcast.13), channel_id=1, source_target_pairs={{0,8},{1,9},{2,10},{3,11},{4,12},{5,13},{6,14},{7,15},{8,0},{9,1},... | collective-permute-start | bytes 208904 | tf_op jit(solution)/shard_map/ppermute | solution.py:332
  10.0 6.1 %collective-permute-start.1 = (bf16[2,272,128]{2,1,0:T(8,128)(2,1)S(1)}, bf16[2,272,128]{2,1,0:T(8,128)(2,1)S(1)}, u32[]{:S(2)}, u32[]{:S(2)}) collective-permute-start(bf16[2,272,128]{2,1,0:T(8,128)(2,1)S(1)} %pad_maximum_fusion.1.rest_1_), channel_id=1, source_target_pairs={{0,4},{1,3},{2,6},{3,1},{4,0},{5,7},{6,2},{7,5},{8,12},{9,11},{10,... | collective-permute-start | bytes 417800 | tf_op jit(solution)/shard_map/ppermute | solution.py:332
  10.9 5.8 %copy-start.2 = (s32[8]{0:T(128)S(1)}, s32[8]{0:T(128)}, u32[]{:S(2)}) copy-start(s32[8]{0:T(128)} %param.19) | copy-start | bytes 100
  10.9 6.0 %copy-start.1 = (bf16[4,4096]{1,0:T(4,128)(2,1)S(1)}, bf16[4,4096]{1,0:T(4,128)(2,1)}, u32[]{:S(2)}) copy-start(bf16[4,4096]{1,0:T(4,128)(2,1)} %param.10) | copy-start | bytes 98308
  10.9 5.9 %collective-permute-start.4 = (bf16[2,272,128]{2,1,0:T(8,128)(2,1)S(1)}, bf16[2,272,128]{2,1,0:T(8,128)(2,1)S(1)}, u32[]{:S(2)}, u32[]{:S(2)}) collective-permute-start(bf16[2,272,128]{2,1,0:T(8,128)(2,1)S(1)} %pad_maximum_fusion.1.rest_1_), channel_id=1, source_target_pairs={{0,2},{1,5},{2,0},{3,7},{4,6},{5,1},{6,4},{7,3},{8,10},{9,13},{10,... | collective-permute-start | bytes 417800 | tf_op jit(solution)/shard_map/ppermute | solution.py:332
  16.0 5.1 %collective-permute-start.3 = (bf16[2,272,128]{2,1,0:T(8,128)(2,1)S(1)}, bf16[2,272,128]{2,1,0:T(8,128)(2,1)S(1)}, u32[]{:S(2)}, u32[]{:S(2)}) collective-permute-start(bf16[2,272,128]{2,1,0:T(8,128)(2,1)S(1)} %collective-permute-done.1), channel_id=1, source_target_pairs={{0,2},{1,5},{2,0},{3,7},{4,6},{5,1},{6,4},{7,3},{8,10},{9,13},{10,... | collective-permute-start | bytes 417800 | tf_op jit(solution)/shard_map/ppermute | solution.py:332
  16.9 4.2 %collective-permute-start.5 = (bf16[6,272,128]{2,1,0:T(8,128)(2,1)S(1)}, bf16[6,272,128]{2,1,0:T(8,128)(2,1)S(1)}, u32[]{:S(2)}, u32[]{:S(2)}) collective-permute-start(bf16[6,272,128]{2,1,0:T(8,128)(2,1)S(1)} %pad_maximum_fusion.slabs_ref), channel_id=1, source_target_pairs={{0,1},{1,0},{2,3},{3,2},{4,5},{5,4},{6,7},{7,6},{8,9},{9,8},{10,11... | collective-permute-start | bytes 1253384 | tf_op jit(solution)/shard_map/ppermute | solution.py:393
  21.1 2.5 %collective-permute-start.6 = (bf16[2,272,128]{2,1,0:T(8,128)(2,1)S(1)}, bf16[2,272,128]{2,1,0:T(8,128)(2,1)S(1)}, u32[]{:S(2)}, u32[]{:S(2)}) collective-permute-start(bf16[2,272,128]{2,1,0:T(8,128)(2,1)S(1)} %collective-permute-done.3.last_ref), channel_id=1, source_target_pairs={{0,1},{1,0},{2,3},{3,2},{4,5},{5,4},{6,7},{7,6},{8,9},{9,8},{10,11... | collective-permute-start | bytes 417800 | tf_op jit(solution)/shard_map/ppermute | solution.py:397

commit v18 on v17

--- a/solution.py
+++ b/solution.py
@@ -327,8 +327,12 @@
     bits = [n >> i for i in range(1, n.bit_length())]
     ways = [bits, bits[:-2] + bits[:-3:-1]]
 
-    def exchange(x, step):
-        pairs = [(2 * i + c, 2 * (i ^ ways[c][step]) + c) for i in range(n) for c in range(2)]
+    def exchange(x, *steps):
+        pairs = [
+            (2 * i + c, 2 * (i ^ sum(ways[c][step] for step in steps)) + c)
+            for i in range(n)
+            for c in range(2)
+        ]
         return lax.ppermute(x, ("replica", "tensor"), pairs)
 
     below = jnp.concatenate(panels(adapter_out), axis=0)
@@ -342,24 +346,21 @@
     for step in early:
         slabs = jnp.concatenate([slabs, exchange(slabs, step)], axis=0)
 
-    cuts = [0, rows // 2, rows - rows // 4, rows]
-    first_rows, second_rows, third_rows = (range(*cut) for cut in zip(cuts, cuts[1:]))
+    split = rows - rows // 4
     hid_other = lax.ppermute(hidden_in, "tensor", swap)
     came = exchange(slabs, first)
-    part = attend(first_rows, given, after=[slabs])
+    part = attend(range(split), given, after=[slabs])
     came, part = lax.optimization_barrier((came, part))
     parts = [part]
     slabs = jnp.concatenate([slabs, came], axis=0)
+    last = [exchange(slabs, third), exchange(slabs, second, third)]
     came = exchange(slabs, second)
-    images = exchange(slabs, third)
-    *part, served = attend(second_rows, given, *in_hbm(served_value_weight), [slabs])
+    *part, served = attend(range(split, rows), given, *in_hbm(served_value_weight), [slabs])
     came, part, hid_other, owner_rank = lax.optimization_barrier(
         (came, part, hid_other, owner_rank)
     )
     parts.append(part)
-    last = exchange(came, third)
-    slabs = jnp.concatenate([slabs, came, images], axis=0)
-    parts.append(attend(third_rows, given, after=[images]))
+    slabs = jnp.concatenate([slabs, came], axis=0)
     features = jnp.concatenate([hidden_in, hid_other], axis=1)
     features = jnp.where(core == 0, features, jnp.concatenate([hid_other, hidden_in], axis=1))
 
@@ -394,6 +395,7 @@
     last, start, pick, context, own_weight, features, crossed = lax.optimization_barrier(
         (last, start, pick, context, own_weight, features, crossed)
     )
+    last = jnp.concatenate(last, axis=0)
     last_crossed = lax.ppermute(last, "tensor", swap)
     merged, total, up, left = merge(per, start, pick, features, served, slabs, crossed, last)
     return tuple(

time: 25.3 us -> 25.3 us (level)
  starting transfers between devices: 7.4 us -> 7.99 us
  Pallas kernels: 11.1 us -> 10.7 us
    pallas_call x3 -> x2, Pallas kernels: 7.24 us -> 6.37 us  [attend(): pl.pallas_call(functools.partial(attend_kernel, rows, fetch), out_shape=o...]
    pallas_call x1, Pallas kernels: 1.38 us -> 1.93 us  [finish(): pl.pallas_call(final_kernel, out_shape=[jax.ShapeDtypeStruct(shape, jnp.b...]
    ppermute x4, starting transfers between devices: 6.81 us -> 7.33 us  [exchange(): return lax.ppermute(x, ('replica', 'tensor'), pairs)]
  transfers between devices with their start and end apart: 7 -> 7, of which waited for: 3 -> 3; matrix products, arithmetic and copies ran while one was open for 4% -> 4% of each run, Pallas kernels for 39% -> 35%
where the time goes in v18:
time: 25.3 us; the launch traced here: 25 us
  Pallas kernels  10.7 us (42%)
  starting transfers between devices  7.99 us (32%)
  waiting for transfers between devices  4.44 us (18%)
  local copies, waits for them, and re-layouts  0.83 us (3%)
  between operations  0.8 us (3%)
  other arithmetic  0.3 us (1%)
    ppermute x4, starting transfers between devices, exchange(): return lax.ppermute(x, ('replica', 'tensor'), pairs)  7.33 us
    pallas_call x2, Pallas kernels, attend(): pl.pallas_call(functools.partial(attend_kernel, rows, fetch), out_shape=o...  6.37 us
    ppermute x4, waiting for transfers between devices, exchange(): return lax.ppermute(x, ('replica', 'tensor'), pairs)  4.43 us
    pallas_call x1, Pallas kernels, merge(): pl.pallas_call(functools.partial(merge_kernel, per, left), out_shape=(jax...  2.39 us
    pallas_call x1, Pallas kernels, finish(): pl.pallas_call(final_kernel, out_shape=[jax.ShapeDtypeStruct(shape, jnp.b...  1.93 us
    slice x1, local copies, waits for them, and re-layouts, panels(): return [x[:, i:i + PANEL] for i in range(0, x.shape[1], PANEL)]  0.7 us
    ppermute x1, starting transfers between devices, body(): hid_other = lax.ppermute(hidden_in, 'tensor', swap)  0.52 us
  transfers between devices with their start and end apart: 7, of which 3 were waited for; matrix products, arithmetic and copies ran while one was open for 4% of the time, Pallas kernels for 35%

profile of v18, /device:TPU:0, one launch (start us, length us, event | category | flops | bytes accessed | tf_op | source)
XLA Modules:
  0.0 25.0 jit_solution(9201764501121289411)
XLA Ops:
  0.6 0.0 copy-start
  0.6 0.5 %collective-permute-start.4 = (bf16[4,4096]{1,0:T(4,128)(2,1)}, bf16[4,4096]{1,0:T(4,128)(2,1)S(1)}, u32[]{:S(2)}, u32[]{:S(2)}) collective-permute-start(bf16[4,4096]{1,0:T(4,128)(2,1)} %param.10), channel_id=1, source_target_pairs={{0,1},{1,0},{2,3},{3,2},{4,5},{5,4},{6,7},{7,6},{8,9},{9,8},{10,11... | collective-permute-start | bytes 98312 | tf_op jit(solution)/shard_map/ppermute | solution.py:350
  1.2 0.7 %fusion.1 = (bf16[8,128]{1,0:T(8,128)(2,1)S(1)}, bf16[8,128]{1,0:T(8,128)(2,1)S(1)}) fusion(bf16[8,256]{1,0:T(8,128)(2,1)} %param.18), kind=kLoop, calls=%fused_computation.34 | loop fusion | bytes 8192 | tf_op jit(solution)/shard_map/slice | solution.py:302
  1.9 0.0 copy-done
  1.9 3.8 %collective-permute-start = (bf16[1,272,128]{2,1,0:T(8,128)(2,1)S(1)}, bf16[1,272,128]{2,1,0:T(8,128)(2,1)S(1)}, u32[]{:S(2)}, u32[]{:S(2)}) collective-permute-start(bf16[1,272,128]{2,1,0:T(8,128)(2,1)S(1)} %bitcast.13), channel_id=1, source_target_pairs={{0,8},{1,9},{2,10},{3,11},{4,12},{5,13},{6,14},{7,15},{8,0},{9,1},... | collective-permute-start | bytes 208904 | tf_op jit(solution)/shard_map/ppermute | solution.py:336
  5.7 3.8 %attend_cache.2 = (f32[3,16,128]{2,1,0:T(8,128)S(1)}, f32[3,16,128]{2,1,0:T(8,128)S(1)}) custom-call(s32[4]{0:T(128)} %lengths_hbm.3, bf16[4,2048]{1,0:T(4,128)(2,1)} %q_hbm.3, bf16[4,256]{1,0:T(4,128)(2,1)} %own_k_hbm.3, bf16[4,1024,256]{2,1,0:T(8,128)(2,1)} %k_hbm.3, bf16[4,1024,256]{2,1,0:T(8,128)(2,1)} %v_hbm.3, bf16[1,272,128]{2,1,0:T(8,128)(2,1)S(1)} %bitcast.14), custom_call_target="tpu_custom_call" | custom-call | flops 50331648 | bytes 3145728 | tf_op jit(solution)/shard_map/attend_cache/pallas_call | solution.py:113
  9.5 0.4 %collective-permute-done = bf16[1,272,128]{2,1,0:T(8,128)(2,1)S(1)} collective-permute-done((bf16[1,272,128]{2,1,0:T(8,128)(2,1)S(1)}, bf16[1,272,128]{2,1,0:T(8,128)(2,1)S(1)}, u32[]{:S(2)}, u32[]{:S(2)}) %collective-permute-start) | collective-permute-done | bytes 69664 | tf_op jit(solution)/shard_map/ppermute | solution.py:336
  10.0 1.2 %collective-permute-start.3 = (bf16[2,272,128]{2,1,0:T(8,128)(2,1)S(1)}, bf16[2,272,128]{2,1,0:T(8,128)(2,1)S(1)}, u32[]{:S(2)}, u32[]{:S(2)}) collective-permute-start(bf16[2,272,128]{2,1,0:T(8,128)(2,1)S(1)} %pad_maximum_fusion.1.rest_1_), channel_id=1, source_target_pairs={{0,4},{1,3},{2,6},{3,1},{4,0},{5,7},{6,2},{7,5},{8,12},{9,11},{10,... | collective-permute-start | bytes 417800 | tf_op jit(solution)/shard_map/ppermute | solution.py:336
  11.2 0.1 pad_add_fusion
  11.3 1.9 %collective-permute-start.2 = (bf16[2,272,128]{2,1,0:T(8,128)(2,1)S(1)}, bf16[2,272,128]{2,1,0:T(8,128)(2,1)S(1)}, u32[]{:S(2)}, u32[]{:S(2)}) collective-permute-start(bf16[2,272,128]{2,1,0:T(8,128)(2,1)S(1)} %pad_maximum_fusion.1.rest_1_), channel_id=1, source_target_pairs={{0,6},{1,7},{2,4},{3,5},{4,2},{5,3},{6,0},{7,1},{8,14},{9,15},{10,... | collective-permute-start | bytes 417800 | tf_op jit(solution)/shard_map/ppermute | solution.py:336
  13.2 0.4 %collective-permute-start.1 = (bf16[2,272,128]{2,1,0:T(8,128)(2,1)S(1)}, bf16[2,272,128]{2,1,0:T(8,128)(2,1)S(1)}, u32[]{:S(2)}, u32[]{:S(2)}) collective-permute-start(bf16[2,272,128]{2,1,0:T(8,128)(2,1)S(1)} %pad_maximum_fusion.1.rest_1_), channel_id=1, source_target_pairs={{0,2},{1,5},{2,0},{3,7},{4,6},{5,1},{6,4},{7,3},{8,10},{9,13},{10,... | collective-permute-start | bytes 417800 | tf_op jit(solution)/shard_map/ppermute | solution.py:336
  13.6 2.6 %attend_cache.3 = (f32[1,16,128]{2,1,0:T(8,128)S(1)}, f32[1,16,128]{2,1,0:T(8,128)S(1)}, bf16[8192,256]{1,0:T(8,128)(2,1)S(1)}) custom-call(s32[4]{0:T(128)} %lengths_hbm.3, bf16[4,2048]{1,0:T(4,128)(2,1)} %q_hbm.3, bf16[4,256]{1,0:T(4,128)(2,1)} %own_k_hbm.3, bf16[4,1024,256]{2,1,0:T(8,128)(2,1)} %k_hbm.3, bf16[4,1024,256]{2,1,0:T(8,128)(2,1)} %v_hbm.3, ...), custom_call_target="tpu_custom_call" | custom-call | flops 16777216 | bytes 1048576 | tf_op jit(solution)/shard_map/attend_cache/pallas_call | solution.py:113
  16.2 0.0 collective-permute-done.4
  16.2 0.3 %collective-permute-done.3 = bf16[2,272,128]{2,1,0:T(8,128)(2,1)S(1)} collective-permute-done((bf16[2,272,128]{2,1,0:T(8,128)(2,1)S(1)}, bf16[2,272,128]{2,1,0:T(8,128)(2,1)S(1)}, u32[]{:S(2)}, u32[]{:S(2)}) %collective-permute-start.3) | collective-permute-done | bytes 139296 | tf_op jit(solution)/shard_map/ppermute | solution.py:336
  16.6 0.0 copy-done.2
  16.6 0.1 select_reduce_fusion
  16.7 0.1 collective-permute-start.5
  16.9 3.7 %collective-permute-done.2 = bf16[2,272,128]{2,1,0:T(8,128)(2,1)S(1)} collective-permute-done((bf16[2,272,128]{2,1,0:T(8,128)(2,1)S(1)}, bf16[2,272,128]{2,1,0:T(8,128)(2,1)S(1)}, u32[]{:S(2)}, u32[]{:S(2)}) %collective-permute-start.2) | collective-permute-done | bytes 139296 | tf_op jit(solution)/shard_map/ppermute | solution.py:336
  20.6 0.0 collective-permute-done.1
  20.6 0.0 collective-permute-done.5.crossed_ref
  20.6 0.1 collective-permute-start.6
  20.7 2.4 %merge_blocks.1 = (bf16[8192,256]{1,0:T(8,128)(2,1)}, f32[4,256]{1,0:T(4,128)S(1)}, bf16[64,256]{1,0:T(8,128)(2,1)S(1)}, bf16[3,512,256]{2,1,0:T(8,128)(2,1)S(1)}) custom-call(s32[1,16]{1,0:T(1,128)S(1)} %add_bitcast_fusion.start_ref, bf16[64,64]{1,0:T(8,128)(2,1)S(1)} %select_convert_fusion.pick_ref, bf16[4,8192]{1,0:T(4,128)(2,1)S(1)} %maximum_select_fusion.features_ref, ...), custom_call_target="tpu_custom_call" | custom-call | flops 201326592 | bytes 6291456 | tf_op jit(solution)/shard_map/merge_blocks/pallas_call | solution.py:248
  23.1 0.0 collective-permute-done.6.last_ref
  23.1 1.9 %finish_rows.1 = (bf16[8192,256]{1,0:T(8,128)(2,1)}, bf16[4,256]{1,0:T(4,128)(2,1)}, bf16[4,2048]{1,0:T(4,128)(2,1)}) custom-call(s32[1,16]{1,0:T(1,128)S(1)} %add_bitcast_fusion.start_ref, bf16[64,256]{1,0:T(8,128)(2,1)S(1)} %get-tuple-element.55.up_ref, bf16[4,8192]{1,0:T(4,128)(2,1)S(1)} %maximum_select_fusion.features_ref, ...), custom_call_target="tpu_custom_call", output_to_operand_aliasing={{0}: (6, {})} | custom-call | flops 67108864 | bytes 2097152 | tf_op jit(solution)/shard_map/finish_rows/pallas_call | solution.py:277
  (23 shorter events, 0.3 us)
Async XLA Ops:
  0.6 1.2 %copy-start = (bf16[64,1024]{1,0:T(8,128)(2,1)S(1)}, bf16[64,1024]{1,0:T(8,128)(2,1)}, u32[]{:S(2)}) copy-start(bf16[64,1024]{1,0:T(8,128)(2,1)} %param.17) | copy-start | bytes 393220
  0.6 15.6 %collective-permute-start.4 = (bf16[4,4096]{1,0:T(4,128)(2,1)}, bf16[4,4096]{1,0:T(4,128)(2,1)S(1)}, u32[]{:S(2)}, u32[]{:S(2)}) collective-permute-start(bf16[4,4096]{1,0:T(4,128)(2,1)} %param.10), channel_id=1, source_target_pairs={{0,1},{1,0},{2,3},{3,2},{4,5},{5,4},{6,7},{7,6},{8,9},{9,8},{10,11... | collective-permute-start | bytes 98312 | tf_op jit(solution)/shard_map/ppermute | solution.py:350
  1.9 8.0 %collective-permute-start = (bf16[1,272,128]{2,1,0:T(8,128)(2,1)S(1)}, bf16[1,272,128]{2,1,0:T(8,128)(2,1)S(1)}, u32[]{:S(2)}, u32[]{:S(2)}) collective-permute-start(bf16[1,272,128]{2,1,0:T(8,128)(2,1)S(1)} %bitcast.13), channel_id=1, source_target_pairs={{0,8},{1,9},{2,10},{3,11},{4,12},{5,13},{6,14},{7,15},{8,0},{9,1},... | collective-permute-start | bytes 208904 | tf_op jit(solution)/shard_map/ppermute | solution.py:336
  10.0 6.6 %collective-permute-start.3 = (bf16[2,272,128]{2,1,0:T(8,128)(2,1)S(1)}, bf16[2,272,128]{2,1,0:T(8,128)(2,1)S(1)}, u32[]{:S(2)}, u32[]{:S(2)}) collective-permute-start(bf16[2,272,128]{2,1,0:T(8,128)(2,1)S(1)} %pad_maximum_fusion.1.rest_1_), channel_id=1, source_target_pairs={{0,4},{1,3},{2,6},{3,1},{4,0},{5,7},{6,2},{7,5},{8,12},{9,11},{10,... | collective-permute-start | bytes 417800 | tf_op jit(solution)/shard_map/ppermute | solution.py:336
  11.3 5.3 %copy-start.2 = (s32[8]{0:T(128)S(1)}, s32[8]{0:T(128)}, u32[]{:S(2)}) copy-start(s32[8]{0:T(128)} %param.19) | copy-start | bytes 100
  11.3 5.4 %copy-start.1 = (bf16[4,4096]{1,0:T(4,128)(2,1)S(1)}, bf16[4,4096]{1,0:T(4,128)(2,1)}, u32[]{:S(2)}) copy-start(bf16[4,4096]{1,0:T(4,128)(2,1)} %param.10) | copy-start | bytes 98308
  11.3 9.3 %collective-permute-start.2 = (bf16[2,272,128]{2,1,0:T(8,128)(2,1)S(1)}, bf16[2,272,128]{2,1,0:T(8,128)(2,1)S(1)}, u32[]{:S(2)}, u32[]{:S(2)}) collective-permute-start(bf16[2,272,128]{2,1,0:T(8,128)(2,1)S(1)} %pad_maximum_fusion.1.rest_1_), channel_id=1, source_target_pairs={{0,6},{1,7},{2,4},{3,5},{4,2},{5,3},{6,0},{7,1},{8,14},{9,15},{10,... | collective-permute-start | bytes 417800 | tf_op jit(solution)/shard_map/ppermute | solution.py:336
  13.2 7.4 %collective-permute-start.1 = (bf16[2,272,128]{2,1,0:T(8,128)(2,1)S(1)}, bf16[2,272,128]{2,1,0:T(8,128)(2,1)S(1)}, u32[]{:S(2)}, u32[]{:S(2)}) collective-permute-start(bf16[2,272,128]{2,1,0:T(8,128)(2,1)S(1)} %pad_maximum_fusion.1.rest_1_), channel_id=1, source_target_pairs={{0,2},{1,5},{2,0},{3,7},{4,6},{5,1},{6,4},{7,3},{8,10},{9,13},{10,... | collective-permute-start | bytes 417800 | tf_op jit(solution)/shard_map/ppermute | solution.py:336
  16.7 3.9 %collective-permute-start.5 = (bf16[4,272,128]{2,1,0:T(8,128)(2,1)S(1)}, bf16[4,272,128]{2,1,0:T(8,128)(2,1)S(1)}, u32[]{:S(2)}, u32[]{:S(2)}) collective-permute-start(bf16[4,272,128]{2,1,0:T(8,128)(2,1)S(1)} %pad_maximum_fusion.slabs_ref), channel_id=1, source_target_pairs={{0,1},{1,0},{2,3},{3,2},{4,5},{5,4},{6,7},{7,6},{8,9},{9,8},{10,11... | collective-permute-start | bytes 835592 | tf_op jit(solution)/shard_map/ppermute | solution.py:394
  20.6 2.5 %collective-permute-start.6 = (bf16[4,272,128]{2,1,0:T(8,128)(2,1)S(1)}, bf16[4,272,128]{2,1,0:T(8,128)(2,1)S(1)}, u32[]{:S(2)}, u32[]{:S(2)}) collective-permute-start(bf16[4,272,128]{2,1,0:T(8,128)(2,1)S(1)} %constant_dynamic-update-slice_fusion.5.last_ref), channel_id=1, source_target_pairs={{0,1},{1,0},{2,3},{3,2},{4,5},{5,4},{6,7},{7,6},{8,9},{9,8},{10,11... | collective-permute-start | bytes 835592 | tf_op jit(solution)/shard_map/ppermute | solution.py:399

commit v19 on v18

--- a/solution.py
+++ b/solution.py
@@ -20,10 +20,7 @@
     return [pltpu.with_memory_space_constraint(x, pltpu.HBM) for x in arrays]
 
 
-def attend_kernel(rows, fetch, lengths_hbm, q_hbm, own_k_hbm, k_hbm, v_hbm, *rest):
-    rest = list(rest)
-    if fetch:
-        served_hbm, served_ref, served_sem = rest.pop(0), rest.pop(-10), rest.pop(-1)
+def attend_kernel(rows, lengths_hbm, q_hbm, own_k_hbm, k_hbm, v_hbm, *rest):
     context_ref, own_weight_ref, lengths, q_ref, own_k_ref, k_buf, v_buf, small_sem, k_sem, v_sem = (
         rest[-10:]
     )
@@ -45,9 +42,6 @@
     for i, row in enumerate(rows):
         for copy in copies(i, row):
             copy.start()
-    if fetch:
-        get_served = pltpu.make_async_copy(served_hbm, served_ref, served_sem)
-        get_served.start()
     for copy in smalls:
         copy.wait()
     queries = q_ref[...].astype(jnp.float32)
@@ -97,23 +91,18 @@
             )
         context_ref[i] = context
         own_weight_ref[i] = jnp.broadcast_to(weight_own, (heads, HEAD_SIZE))
-    if fetch:
-        get_served.wait()
-
-
-def attend(rows, given, served=None, after=()):
+
+
+def attend(rows, given, after):
     lengths, queries, own_key, stored_keys, stored_values = given
-    fetch = served is not None
     cache_len, width = stored_keys.shape[1:]
     heads = queries.shape[1] // HEAD_SIZE
     count = len(rows)
     out_shape = [jax.ShapeDtypeStruct((count, heads, HEAD_SIZE), jnp.float32)] * 2
-    if fetch:
-        out_shape += [jax.ShapeDtypeStruct(served.shape, served.dtype)]
     return pl.pallas_call(
-        functools.partial(attend_kernel, rows, fetch),
+        functools.partial(attend_kernel, rows),
         out_shape=out_shape,
-        in_specs=[HBM] * (5 + fetch) + [pl.BlockSpec(memory_space=pl.ANY)] * len(after),
+        in_specs=[HBM] * 5 + [pl.BlockSpec(memory_space=pl.ANY)] * len(after),
         out_specs=[VMEM] * len(out_shape),
         scratch_shapes=[
             pltpu.SMEM(lengths.shape, jnp.int32),
@@ -124,8 +113,7 @@
             pltpu.SemaphoreType.DMA((3,)),
             pltpu.SemaphoreType.DMA((count,)),
             pltpu.SemaphoreType.DMA((count,)),
-        ]
-        + [pltpu.SemaphoreType.DMA] * fetch,
+        ],
         compiler_params=pltpu.CompilerParams(vmem_limit_bytes=12 * 2**20),
         cost_estimate=pl.CostEstimate(
             flops=4 * count * heads * cache_len * width,
@@ -133,7 +121,38 @@
             transcendentals=count * heads * cache_len,
         ),
         name="attend_cache",
-    )(*given, *([served] if fetch else []), *after)
+    )(*given, *after)
+
+
+def fetch_kernel(pieces, source, after, into, sem):
+    del after
+    size = source.shape[0] // pieces
+    copies = [
+        pltpu.make_async_copy(
+            source.at[pl.ds(i * size, size)], into.at[pl.ds(i * size, size)], sem.at[i]
+        )
+        for i in range(pieces)
+    ]
+    for copy in copies:
+        copy.start()
+    for copy in copies:
+        copy.wait()
+
+
+def fetch(served, after):
+    pieces = 8
+    return pl.pallas_call(
+        functools.partial(fetch_kernel, pieces),
+        out_shape=jax.ShapeDtypeStruct(served.shape, served.dtype),
+        in_specs=[HBM, pl.BlockSpec(memory_space=pl.ANY)],
+        out_specs=VMEM,
+        scratch_shapes=[pltpu.SemaphoreType.DMA((pieces,))],
+        compiler_params=pltpu.CompilerParams(vmem_limit_bytes=12 * 2**20),
+        cost_estimate=pl.CostEstimate(
+            flops=0, bytes_accessed=4 * served.size, transcendentals=0
+        ),
+        name="fetch_served",
+    )(served, after)
 
 
 class Merge:
@@ -327,11 +346,11 @@
     bits = [n >> i for i in range(1, n.bit_length())]
     ways = [bits, bits[:-2] + bits[:-3:-1]]
 
-    def exchange(x, *steps):
+    def exchange(x, *steps, cores=(0, 1)):
         pairs = [
             (2 * i + c, 2 * (i ^ sum(ways[c][step] for step in steps)) + c)
             for i in range(n)
-            for c in range(2)
+            for c in cores
         ]
         return lax.ppermute(x, ("replica", "tensor"), pairs)
 
@@ -349,18 +368,23 @@
     split = rows - rows // 4
     hid_other = lax.ppermute(hidden_in, "tensor", swap)
     came = exchange(slabs, first)
-    part = attend(range(split), given, after=[slabs])
+    part = attend(range(split), given, [slabs])
     came, part = lax.optimization_barrier((came, part))
     parts = [part]
     slabs = jnp.concatenate([slabs, came], axis=0)
-    last = [exchange(slabs, third), exchange(slabs, second, third)]
+    images = exchange(slabs, third)
+    straight = exchange(slabs, second, third, cores=(0,))
     came = exchange(slabs, second)
-    *part, served = attend(range(split, rows), given, *in_hbm(served_value_weight), [slabs])
+    part = attend(range(split, rows), given, [slabs])
     came, part, hid_other, owner_rank = lax.optimization_barrier(
         (came, part, hid_other, owner_rank)
     )
     parts.append(part)
-    slabs = jnp.concatenate([slabs, came], axis=0)
+    relayed = exchange(came, third, cores=(1,))
+    served = fetch(*in_hbm(served_value_weight), came)
+    straight, relayed, served = lax.optimization_barrier((straight, relayed, served))
+    last = jnp.where(core == 0, straight, relayed)
+    slabs = jnp.concatenate([slabs, came, images], axis=0)
     features = jnp.concatenate([hidden_in, hid_other], axis=1)
     features = jnp.where(core == 0, features, jnp.concatenate([hid_other, hidden_in], axis=1))
 
@@ -395,7 +419,6 @@
     last, start, pick, context, own_weight, features, crossed = lax.optimization_barrier(
         (last, start, pick, context, own_weight, features, crossed)
     )
-    last = jnp.concatenate(last, axis=0)
     last_crossed = lax.ppermute(last, "tensor", swap)
     merged, total, up, left = merge(per, start, pick, features, served, slabs, crossed, last)
     return tuple(

time: 25.3 us -> 26.2 us (1.036)
  waiting for transfers between devices: 4.44 us -> 1.62 us
  starting transfers between devices: 7.99 us -> 10.5 us
  Pallas kernels: 10.7 us -> 11.8 us
    ppermute x4 -> x5, waiting for transfers between devices: 4.43 us -> 1.61 us  [exchange(): return lax.ppermute(x, ('replica', 'tensor'), pairs)]
    ppermute x4 -> x5, starting transfers between devices: 7.33 us -> 9.88 us  [exchange(): return lax.ppermute(x, ('replica', 'tensor'), pairs)]
    pallas_call x2 -> x3, Pallas kernels: 6.37 us -> 7.88 us  [the longest x2 5.66 us: attend(): pl.pallas_call(functools.partial(attend_kernel, rows), out_shape=out_shap...]
    pallas_call x1, Pallas kernels: 1.93 us -> 1.38 us  [finish(): pl.pallas_call(final_kernel, out_shape=[jax.ShapeDtypeStruct(shape, jnp.b...]
  transfers between devices with their start and end apart: 7 -> 8, of which waited for: 3 -> 2; matrix products, arithmetic and copies ran while one was open for 4% -> 4% of each run, Pallas kernels for 35% -> 40%
where the time goes in v19:
time: 26.2 us; the launch traced here: 25.9 us
  Pallas kernels  11.8 us (45%)
  starting transfers between devices  10.5 us (40%)
  waiting for transfers between devices  1.62 us (6%)
  between operations  0.85 us (3%)
  local copies, waits for them, and re-layouts  0.8 us (3%)
  other arithmetic  0.34 us (1%)
    ppermute x5, starting transfers between devices, exchange(): return lax.ppermute(x, ('replica', 'tensor'), pairs)  9.88 us
    pallas_call x2, Pallas kernels, attend(): pl.pallas_call(functools.partial(attend_kernel, rows), out_shape=out_shap...  5.66 us
    pallas_call x1, Pallas kernels, merge(): pl.pallas_call(functools.partial(merge_kernel, per, left), out_shape=(jax...  2.51 us
    pallas_call x1, Pallas kernels, fetch(): pl.pallas_call(functools.partial(fetch_kernel, pieces), out_shape=jax.Sha...  2.22 us
    ppermute x5, waiting for transfers between devices, exchange(): return lax.ppermute(x, ('replica', 'tensor'), pairs)  1.61 us
    pallas_call x1, Pallas kernels, finish(): pl.pallas_call(final_kernel, out_shape=[jax.ShapeDtypeStruct(shape, jnp.b...  1.38 us
    slice x1, local copies, waits for them, and re-layouts, panels(): return [x[:, i:i + PANEL] for i in range(0, x.shape[1], PANEL)]  0.7 us
  transfers between devices with their start and end apart: 8, of which 2 were waited for; matrix products, arithmetic and copies ran while one was open for 4% of the time, Pallas kernels for 40%

profile of v19, /device:TPU:0, one launch (start us, length us, event | category | flops | bytes accessed | tf_op | source)
XLA Modules:
  0.0 25.9 jit_solution(12019832908390901348)
XLA Ops:
  0.6 0.0 copy-start
  0.6 0.5 %collective-permute-start.3 = (bf16[4,4096]{1,0:T(4,128)(2,1)}, bf16[4,4096]{1,0:T(4,128)(2,1)S(1)}, u32[]{:S(2)}, u32[]{:S(2)}) collective-permute-start(bf16[4,4096]{1,0:T(4,128)(2,1)} %param.10), channel_id=1, source_target_pairs={{0,1},{1,0},{2,3},{3,2},{4,5},{5,4},{6,7},{7,6},{8,9},{9,8},{10,11... | collective-permute-start | bytes 98312 | tf_op jit(solution)/shard_map/ppermute | solution.py:369
  1.2 0.7 %fusion.1 = (bf16[8,128]{1,0:T(8,128)(2,1)S(1)}, bf16[8,128]{1,0:T(8,128)(2,1)S(1)}) fusion(bf16[8,256]{1,0:T(8,128)(2,1)} %param.18), kind=kLoop, calls=%fused_computation.33 | loop fusion | bytes 8192 | tf_op jit(solution)/shard_map/slice | solution.py:321
  1.9 3.8 %collective-permute-start = (bf16[1,272,128]{2,1,0:T(8,128)(2,1)S(1)}, bf16[1,272,128]{2,1,0:T(8,128)(2,1)S(1)}, u32[]{:S(2)}, u32[]{:S(2)}) collective-permute-start(bf16[1,272,128]{2,1,0:T(8,128)(2,1)S(1)} %bitcast.13), channel_id=1, source_target_pairs={{0,8},{1,9},{2,10},{3,11},{4,12},{5,13},{6,14},{7,15},{8,0},{9,1},... | collective-permute-start | bytes 208904 | tf_op jit(solution)/shard_map/ppermute | solution.py:355
  5.7 0.0 copy-start.1
  5.8 3.8 %attend_cache.2 = (f32[3,16,128]{2,1,0:T(8,128)S(1)}, f32[3,16,128]{2,1,0:T(8,128)S(1)}) custom-call(s32[4]{0:T(128)} %lengths_hbm.3, bf16[4,2048]{1,0:T(4,128)(2,1)} %q_hbm.3, bf16[4,256]{1,0:T(4,128)(2,1)} %own_k_hbm.3, bf16[4,1024,256]{2,1,0:T(8,128)(2,1)} %k_hbm.3, bf16[4,1024,256]{2,1,0:T(8,128)(2,1)} %v_hbm.3, bf16[1,272,128]{2,1,0:T(8,128)(2,1)S(1)} %bitcast.14), custom_call_target="tpu_custom_call" | custom-call | flops 50331648 | bytes 3145728 | tf_op jit(solution)/shard_map/attend_cache/pallas_call | solution.py:102
  9.5 0.4 %collective-permute-done = bf16[1,272,128]{2,1,0:T(8,128)(2,1)S(1)} collective-permute-done((bf16[1,272,128]{2,1,0:T(8,128)(2,1)S(1)}, bf16[1,272,128]{2,1,0:T(8,128)(2,1)S(1)}, u32[]{:S(2)}, u32[]{:S(2)}) %collective-permute-start) | collective-permute-done | bytes 69664 | tf_op jit(solution)/shard_map/ppermute | solution.py:355
  10.0 1.3 %collective-permute-start.2 = (bf16[2,272,128]{2,1,0:T(8,128)(2,1)S(1)}, bf16[2,272,128]{2,1,0:T(8,128)(2,1)S(1)}, u32[]{:S(2)}, u32[]{:S(2)}) collective-permute-start(bf16[2,272,128]{2,1,0:T(8,128)(2,1)S(1)} %pad_maximum_fusion.1.rest_0_), channel_id=1, source_target_pairs={{0,4},{1,3},{2,6},{3,1},{4,0},{5,7},{6,2},{7,5},{8,12},{9,11},{10,... | collective-permute-start | bytes 417800 | tf_op jit(solution)/shard_map/ppermute | solution.py:355
  11.2 0.1 pad_add_fusion
  11.3 1.5 %collective-permute-start.5 = (bf16[2,272,128]{2,1,0:T(8,128)(2,1)S(1)}, bf16[2,272,128]{2,1,0:T(8,128)(2,1)S(1)}, u32[]{:S(2)}, u32[]{:S(2)}) collective-permute-start(bf16[2,272,128]{2,1,0:T(8,128)(2,1)S(1)} %pad_maximum_fusion.1.rest_0_), channel_id=1, source_target_pairs={{0,2},{1,5},{2,0},{3,7},{4,6},{5,1},{6,4},{7,3},{8,10},{9,13},{10,... | collective-permute-start | bytes 417800 | tf_op jit(solution)/shard_map/ppermute | solution.py:355
  12.8 2.7 %collective-permute-start.1 = (bf16[2,272,128]{2,1,0:T(8,128)(2,1)S(1)}, bf16[2,272,128]{2,1,0:T(8,128)(2,1)S(1)}, u32[]{:S(2)}, u32[]{:S(2)}) collective-permute-start(bf16[2,272,128]{2,1,0:T(8,128)(2,1)S(1)} %pad_maximum_fusion.1.rest_0_), channel_id=1, source_target_pairs={{0,6},{2,4},{4,2},{6,0},{8,14},{10,12},{12,10},{14,8},{16,22},{18,... | collective-permute-start | bytes 417800 | tf_op jit(solution)/shard_map/ppermute | solution.py:355
  15.5 1.9 %attend_cache.3 = (f32[1,16,128]{2,1,0:T(8,128)S(1)}, f32[1,16,128]{2,1,0:T(8,128)S(1)}) custom-call(s32[4]{0:T(128)} %lengths_hbm.3, bf16[4,2048]{1,0:T(4,128)(2,1)} %q_hbm.3, bf16[4,256]{1,0:T(4,128)(2,1)} %own_k_hbm.3, bf16[4,1024,256]{2,1,0:T(8,128)(2,1)} %k_hbm.3, bf16[4,1024,256]{2,1,0:T(8,128)(2,1)} %v_hbm.3, ...), custom_call_target="tpu_custom_call" | custom-call | flops 16777216 | bytes 1048576 | tf_op jit(solution)/shard_map/attend_cache/pallas_call | solution.py:102
  17.4 0.0 collective-permute-done.3
  17.4 0.7 %collective-permute-start.4 = (bf16[2,272,128]{2,1,0:T(8,128)(2,1)S(1)}, bf16[2,272,128]{2,1,0:T(8,128)(2,1)S(1)}, u32[]{:S(2)}, u32[]{:S(2)}) collective-permute-start(bf16[2,272,128]{2,1,0:T(8,128)(2,1)S(1)} %collective-permute-done.2.after), channel_id=1, source_target_pairs={{1,5},{3,7},{5,1},{7,3},{9,13},{11,15},{13,9},{15,11},{17,21},{19,... | collective-permute-start | bytes 417800 | tf_op jit(solution)/shard_map/ppermute | solution.py:355
  18.1 0.1 select_reduce_fusion
  18.2 0.0 collective-permute-done.5
  18.2 0.1 pad_maximum_fusion.slabs_ref
  18.3 0.1 collective-permute-start.6
  18.5 2.2 %fetch_served.1.served_ref = bf16[8192,256]{1,0:T(8,128)(2,1)S(1)} custom-call(bf16[8192,256]{1,0:T(8,128)(2,1)} %source.1, bf16[2,272,128]{2,1,0:T(8,128)(2,1)S(1)} %collective-permute-done.2.after), custom_call_target="tpu_custom_call" | custom-call | bytes 8388608 | tf_op jit(solution)/shard_map/fetch_served/pallas_call | solution.py:144
  20.7 1.2 %collective-permute-done.1 = bf16[2,272,128]{2,1,0:T(8,128)(2,1)S(1)} collective-permute-done((bf16[2,272,128]{2,1,0:T(8,128)(2,1)S(1)}, bf16[2,272,128]{2,1,0:T(8,128)(2,1)S(1)}, u32[]{:S(2)}, u32[]{:S(2)}) %collective-permute-start.1) | collective-permute-done | bytes 139296 | tf_op jit(solution)/shard_map/ppermute | solution.py:355
  21.9 0.0 collective-permute-done.4
  21.9 0.1 collective-permute-start.7
  22.0 2.5 %merge_blocks.1 = (bf16[8192,256]{1,0:T(8,128)(2,1)}, f32[4,256]{1,0:T(4,128)S(1)}, bf16[64,256]{1,0:T(8,128)(2,1)S(1)}, bf16[3,512,256]{2,1,0:T(8,128)(2,1)S(1)}) custom-call(s32[1,16]{1,0:T(1,128)S(1)} %add_bitcast_fusion.start_ref, bf16[64,64]{1,0:T(8,128)(2,1)S(1)} %select_convert_fusion.pick_ref, bf16[4,8192]{1,0:T(4,128)(2,1)S(1)} %maximum_select_fusion.features_ref, ...), custom_call_target="tpu_custom_call" | custom-call | flops 234881024 | bytes 7340032 | tf_op jit(solution)/shard_map/merge_blocks/pallas_call | solution.py:267
  24.5 1.4 %finish_rows.1 = (bf16[8192,256]{1,0:T(8,128)(2,1)}, bf16[4,256]{1,0:T(4,128)(2,1)}, bf16[4,2048]{1,0:T(4,128)(2,1)}) custom-call(s32[1,16]{1,0:T(1,128)S(1)} %add_bitcast_fusion.start_ref, bf16[64,256]{1,0:T(8,128)(2,1)S(1)} %get-tuple-element.57.up_ref, bf16[4,8192]{1,0:T(4,128)(2,1)S(1)} %maximum_select_fusion.features_ref, ...), custom_call_target="tpu_custom_call", output_to_operand_aliasing={{0}: (6, {})} | custom-call | flops 33554432 | bytes 1048576 | tf_op jit(solution)/shard_map/finish_rows/pallas_call | solution.py:296
  (25 shorter events, 0.2 us)
Async XLA Ops:
  0.6 1.2 %copy-start = (bf16[64,1024]{1,0:T(8,128)(2,1)S(1)}, bf16[64,1024]{1,0:T(8,128)(2,1)}, u32[]{:S(2)}) copy-start(bf16[64,1024]{1,0:T(8,128)(2,1)} %param.17) | copy-start | bytes 393220
  0.6 16.8 %collective-permute-start.3 = (bf16[4,4096]{1,0:T(4,128)(2,1)}, bf16[4,4096]{1,0:T(4,128)(2,1)S(1)}, u32[]{:S(2)}, u32[]{:S(2)}) collective-permute-start(bf16[4,4096]{1,0:T(4,128)(2,1)} %param.10), channel_id=1, source_target_pairs={{0,1},{1,0},{2,3},{3,2},{4,5},{5,4},{6,7},{7,6},{8,9},{9,8},{10,11... | collective-permute-start | bytes 98312 | tf_op jit(solution)/shard_map/ppermute | solution.py:369
  1.9 8.0 %collective-permute-start = (bf16[1,272,128]{2,1,0:T(8,128)(2,1)S(1)}, bf16[1,272,128]{2,1,0:T(8,128)(2,1)S(1)}, u32[]{:S(2)}, u32[]{:S(2)}) collective-permute-start(bf16[1,272,128]{2,1,0:T(8,128)(2,1)S(1)} %bitcast.13), channel_id=1, source_target_pairs={{0,8},{1,9},{2,10},{3,11},{4,12},{5,13},{6,14},{7,15},{8,0},{9,1},... | collective-permute-start | bytes 208904 | tf_op jit(solution)/shard_map/ppermute | solution.py:355
  5.7 12.4 %copy-start.2 = (s32[8]{0:T(128)S(1)}, s32[8]{0:T(128)}, u32[]{:S(2)}) copy-start(s32[8]{0:T(128)} %param.19) | copy-start | bytes 100
  5.7 12.6 %copy-start.1 = (bf16[4,4096]{1,0:T(4,128)(2,1)S(1)}, bf16[4,4096]{1,0:T(4,128)(2,1)}, u32[]{:S(2)}) copy-start(bf16[4,4096]{1,0:T(4,128)(2,1)} %param.10) | copy-start | bytes 98308
  10.0 7.4 %collective-permute-start.2 = (bf16[2,272,128]{2,1,0:T(8,128)(2,1)S(1)}, bf16[2,272,128]{2,1,0:T(8,128)(2,1)S(1)}, u32[]{:S(2)}, u32[]{:S(2)}) collective-permute-start(bf16[2,272,128]{2,1,0:T(8,128)(2,1)S(1)} %pad_maximum_fusion.1.rest_0_), channel_id=1, source_target_pairs={{0,4},{1,3},{2,6},{3,1},{4,0},{5,7},{6,2},{7,5},{8,12},{9,11},{10,... | collective-permute-start | bytes 417800 | tf_op jit(solution)/shard_map/ppermute | solution.py:355
  11.3 6.9 %collective-permute-start.5 = (bf16[2,272,128]{2,1,0:T(8,128)(2,1)S(1)}, bf16[2,272,128]{2,1,0:T(8,128)(2,1)S(1)}, u32[]{:S(2)}, u32[]{:S(2)}) collective-permute-start(bf16[2,272,128]{2,1,0:T(8,128)(2,1)S(1)} %pad_maximum_fusion.1.rest_0_), channel_id=1, source_target_pairs={{0,2},{1,5},{2,0},{3,7},{4,6},{5,1},{6,4},{7,3},{8,10},{9,13},{10,... | collective-permute-start | bytes 417800 | tf_op jit(solution)/shard_map/ppermute | solution.py:355
  12.8 9.1 %collective-permute-start.1 = (bf16[2,272,128]{2,1,0:T(8,128)(2,1)S(1)}, bf16[2,272,128]{2,1,0:T(8,128)(2,1)S(1)}, u32[]{:S(2)}, u32[]{:S(2)}) collective-permute-start(bf16[2,272,128]{2,1,0:T(8,128)(2,1)S(1)} %pad_maximum_fusion.1.rest_0_), channel_id=1, source_target_pairs={{0,6},{2,4},{4,2},{6,0},{8,14},{10,12},{12,10},{14,8},{16,22},{18,... | collective-permute-start | bytes 417800 | tf_op jit(solution)/shard_map/ppermute | solution.py:355
  17.4 4.5 %collective-permute-start.4 = (bf16[2,272,128]{2,1,0:T(8,128)(2,1)S(1)}, bf16[2,272,128]{2,1,0:T(8,128)(2,1)S(1)}, u32[]{:S(2)}, u32[]{:S(2)}) collective-permute-start(bf16[2,272,128]{2,1,0:T(8,128)(2,1)S(1)} %collective-permute-done.2.after), channel_id=1, source_target_pairs={{1,5},{3,7},{5,1},{7,3},{9,13},{11,15},{13,9},{15,11},{17,21},{19,... | collective-permute-start | bytes 417800 | tf_op jit(solution)/shard_map/ppermute | solution.py:355
  18.3 3.7 %collective-permute-start.6 = (bf16[6,272,128]{2,1,0:T(8,128)(2,1)S(1)}, bf16[6,272,128]{2,1,0:T(8,128)(2,1)S(1)}, u32[]{:S(2)}, u32[]{:S(2)}) collective-permute-start(bf16[6,272,128]{2,1,0:T(8,128)(2,1)S(1)} %pad_maximum_fusion.slabs_ref), channel_id=1, source_target_pairs={{0,1},{1,0},{2,3},{3,2},{4,5},{5,4},{6,7},{7,6},{8,9},{9,8},{10,11... | collective-permute-start | bytes 1253384 | tf_op jit(solution)/shard_map/ppermute | solution.py:418
  21.9 2.6 %collective-permute-start.7 = (bf16[2,272,128]{2,1,0:T(8,128)(2,1)S(1)}, bf16[2,272,128]{2,1,0:T(8,128)(2,1)S(1)}, u32[]{:S(2)}, u32[]{:S(2)}) collective-permute-start(bf16[2,272,128]{2,1,0:T(8,128)(2,1)S(1)} %broadcast_select_fusion.last_ref), channel_id=1, source_target_pairs={{0,1},{1,0},{2,3},{3,2},{4,5},{5,4},{6,7},{7,6},{8,9},{9,8},{10,11... | collective-permute-start | bytes 417800 | tf_op jit(solution)/shard_map/ppermute | solution.py:422

commit v20 on v17

--- a/solution.py
+++ b/solution.py
@@ -325,7 +325,7 @@
     rank = n * per
 
     bits = [n >> i for i in range(1, n.bit_length())]
-    ways = [bits, bits[:-2] + bits[:-3:-1]]
+    ways = [bits[:-2] + bits[:-3:-1], bits]
 
     def exchange(x, step):
         pairs = [(2 * i + c, 2 * (i ^ ways[c][step]) + c) for i in range(n) for c in range(2)]

time: 25.3 us -> 25.5 us (level)
  waiting for transfers between devices: 4.58 us -> 5.17 us
  starting transfers between devices: 7.4 us -> 7.03 us
    ppermute x4, waiting for transfers between devices: 4.57 us -> 5.17 us  [exchange(): return lax.ppermute(x, ('replica', 'tensor'), pairs)]
    ppermute x4, starting transfers between devices: 6.81 us -> 6.44 us  [exchange(): return lax.ppermute(x, ('replica', 'tensor'), pairs)]
  transfers between devices with their start and end apart: 7 -> 7, of which waited for: 3 -> 4; matrix products, arithmetic and copies ran while one was open for 4% -> 4% of each run, Pallas kernels for 39% -> 39%
where the time goes in v20:
time: 25.5 us; the launch traced here: 25.2 us
  Pallas kernels  11.1 us (44%)
  starting transfers between devices  7.03 us (28%)
  waiting for transfers between devices  5.17 us (20%)
  local copies, waits for them, and re-layouts  0.8 us (3%)
  between operations  0.78 us (3%)
  other arithmetic  0.32 us (1%)
    pallas_call x3, Pallas kernels, attend(): pl.pallas_call(functools.partial(attend_kernel, rows, fetch), out_shape=o...  7.24 us
    ppermute x4, starting transfers between devices, exchange(): return lax.ppermute(x, ('replica', 'tensor'), pairs)  6.44 us
    ppermute x4, waiting for transfers between devices, exchange(): return lax.ppermute(x, ('replica', 'tensor'), pairs)  5.17 us
    pallas_call x1, Pallas kernels, merge(): pl.pallas_call(functools.partial(merge_kernel, per, left), out_shape=(jax...  2.51 us
    pallas_call x1, Pallas kernels, finish(): pl.pallas_call(final_kernel, out_shape=[jax.ShapeDtypeStruct(shape, jnp.b...  1.38 us
    slice x1, local copies, waits for them, and re-layouts, panels(): return [x[:, i:i + PANEL] for i in range(0, x.shape[1], PANEL)]  0.7 us
    ppermute x1, starting transfers between devices, body(): hid_other = lax.ppermute(hidden_in, 'tensor', swap)  0.52 us
  transfers between devices with their start and end apart: 7, of which 4 were waited for; matrix products, arithmetic and copies ran while one was open for 4% of the time, Pallas kernels for 39%

profile of v20, /device:TPU:0, one launch (start us, length us, event | category | flops | bytes accessed | tf_op | source)
XLA Modules:
  0.0 25.2 jit_solution(18436275610726083355)
XLA Ops:
  0.6 0.0 copy-start
  0.6 0.5 %collective-permute-start.2 = (bf16[4,4096]{1,0:T(4,128)(2,1)}, bf16[4,4096]{1,0:T(4,128)(2,1)S(1)}, u32[]{:S(2)}, u32[]{:S(2)}) collective-permute-start(bf16[4,4096]{1,0:T(4,128)(2,1)} %param.10), channel_id=1, source_target_pairs={{0,1},{1,0},{2,3},{3,2},{4,5},{5,4},{6,7},{7,6},{8,9},{9,8},{10,11... | collective-permute-start | bytes 98312 | tf_op jit(solution)/shard_map/ppermute | solution.py:347
  1.2 0.7 %fusion.1 = (bf16[8,128]{1,0:T(8,128)(2,1)S(1)}, bf16[8,128]{1,0:T(8,128)(2,1)S(1)}) fusion(bf16[8,256]{1,0:T(8,128)(2,1)} %param.18), kind=kLoop, calls=%fused_computation.32 | loop fusion | bytes 8192 | tf_op jit(solution)/shard_map/slice | solution.py:302
  1.9 0.0 copy-done
  1.9 3.8 %collective-permute-start = (bf16[1,272,128]{2,1,0:T(8,128)(2,1)S(1)}, bf16[1,272,128]{2,1,0:T(8,128)(2,1)S(1)}, u32[]{:S(2)}, u32[]{:S(2)}) collective-permute-start(bf16[1,272,128]{2,1,0:T(8,128)(2,1)S(1)} %bitcast.13), channel_id=1, source_target_pairs={{0,8},{1,9},{2,10},{3,11},{4,12},{5,13},{6,14},{7,15},{8,0},{9,1},... | collective-permute-start | bytes 208904 | tf_op jit(solution)/shard_map/ppermute | solution.py:332
  5.7 2.8 %attend_cache.3 = (f32[2,16,128]{2,1,0:T(8,128)S(1)}, f32[2,16,128]{2,1,0:T(8,128)S(1)}) custom-call(s32[4]{0:T(128)} %lengths_hbm.5, bf16[4,2048]{1,0:T(4,128)(2,1)} %q_hbm.5, bf16[4,256]{1,0:T(4,128)(2,1)} %own_k_hbm.5, bf16[4,1024,256]{2,1,0:T(8,128)(2,1)} %k_hbm.5, bf16[4,1024,256]{2,1,0:T(8,128)(2,1)} %v_hbm.5, bf16[1,272,128]{2,1,0:T(8,128)(2,1)S(1)} %bitcast.14), custom_call_target="tpu_custom_call" | custom-call | flops 33554432 | bytes 2097152 | tf_op jit(solution)/shard_map/attend_cache/pallas_call | solution.py:113
  8.5 1.4 %collective-permute-done = bf16[1,272,128]{2,1,0:T(8,128)(2,1)S(1)} collective-permute-done((bf16[1,272,128]{2,1,0:T(8,128)(2,1)S(1)}, bf16[1,272,128]{2,1,0:T(8,128)(2,1)S(1)}, u32[]{:S(2)}, u32[]{:S(2)}) %collective-permute-start) | collective-permute-done | bytes 69664 | tf_op jit(solution)/shard_map/ppermute | solution.py:332
  10.0 1.7 %collective-permute-start.1 = (bf16[2,272,128]{2,1,0:T(8,128)(2,1)S(1)}, bf16[2,272,128]{2,1,0:T(8,128)(2,1)S(1)}, u32[]{:S(2)}, u32[]{:S(2)}) collective-permute-start(bf16[2,272,128]{2,1,0:T(8,128)(2,1)S(1)} %pad_maximum_fusion.1.rest_1_), channel_id=1, source_target_pairs={{0,2},{1,5},{2,0},{3,7},{4,6},{5,1},{6,4},{7,3},{8,10},{9,13},{10,... | collective-permute-start | bytes 417800 | tf_op jit(solution)/shard_map/ppermute | solution.py:332
  11.6 0.1 pad_add_fusion
  11.7 0.7 %collective-permute-start.4 = (bf16[2,272,128]{2,1,0:T(8,128)(2,1)S(1)}, bf16[2,272,128]{2,1,0:T(8,128)(2,1)S(1)}, u32[]{:S(2)}, u32[]{:S(2)}) collective-permute-start(bf16[2,272,128]{2,1,0:T(8,128)(2,1)S(1)} %pad_maximum_fusion.1.rest_1_), channel_id=1, source_target_pairs={{0,4},{1,3},{2,6},{3,1},{4,0},{5,7},{6,2},{7,5},{8,12},{9,11},{10,... | collective-permute-start | bytes 417800 | tf_op jit(solution)/shard_map/ppermute | solution.py:332
  12.4 2.6 %attend_cache.4 = (f32[1,16,128]{2,1,0:T(8,128)S(1)}, f32[1,16,128]{2,1,0:T(8,128)S(1)}, bf16[8192,256]{1,0:T(8,128)(2,1)S(1)}) custom-call(s32[4]{0:T(128)} %lengths_hbm.5, bf16[4,2048]{1,0:T(4,128)(2,1)} %q_hbm.5, bf16[4,256]{1,0:T(4,128)(2,1)} %own_k_hbm.5, bf16[4,1024,256]{2,1,0:T(8,128)(2,1)} %k_hbm.5, bf16[4,1024,256]{2,1,0:T(8,128)(2,1)} %v_hbm.5, ...), custom_call_target="tpu_custom_call" | custom-call | flops 16777216 | bytes 1048576 | tf_op jit(solution)/shard_map/attend_cache/pallas_call | solution.py:113
  15.0 0.0 collective-permute-done.2
  15.0 1.2 %collective-permute-done.1 = bf16[2,272,128]{2,1,0:T(8,128)(2,1)S(1)} collective-permute-done((bf16[2,272,128]{2,1,0:T(8,128)(2,1)S(1)}, bf16[2,272,128]{2,1,0:T(8,128)(2,1)S(1)}, u32[]{:S(2)}, u32[]{:S(2)}) %collective-permute-start.1) | collective-permute-done | bytes 139296 | tf_op jit(solution)/shard_map/ppermute | solution.py:332
  16.3 0.3 %collective-permute-start.3 = (bf16[2,272,128]{2,1,0:T(8,128)(2,1)S(1)}, bf16[2,272,128]{2,1,0:T(8,128)(2,1)S(1)}, u32[]{:S(2)}, u32[]{:S(2)}) collective-permute-start(bf16[2,272,128]{2,1,0:T(8,128)(2,1)S(1)} %collective-permute-done.1), channel_id=1, source_target_pairs={{0,4},{1,3},{2,6},{3,1},{4,0},{5,7},{6,2},{7,5},{8,12},{9,11},{10,... | collective-permute-start | bytes 417800 | tf_op jit(solution)/shard_map/ppermute | solution.py:332
  16.6 0.1 select_reduce_fusion
  16.7 0.1 collective-permute-done.4.rest_0_
  16.8 0.1 collective-permute-start.5
  17.0 1.9 %attend_cache.5 = (f32[1,16,128]{2,1,0:T(8,128)S(1)}, f32[1,16,128]{2,1,0:T(8,128)S(1)}) custom-call(s32[4]{0:T(128)} %lengths_hbm.5, bf16[4,2048]{1,0:T(4,128)(2,1)} %q_hbm.5, bf16[4,256]{1,0:T(4,128)(2,1)} %own_k_hbm.5, bf16[4,1024,256]{2,1,0:T(8,128)(2,1)} %k_hbm.5, bf16[4,1024,256]{2,1,0:T(8,128)(2,1)} %v_hbm.5, ...), custom_call_target="tpu_custom_call" | custom-call | flops 16777216 | bytes 1048576 | tf_op jit(solution)/shard_map/attend_cache/pallas_call | solution.py:113
  18.9 2.4 %collective-permute-done.3.last_ref = bf16[2,272,128]{2,1,0:T(8,128)(2,1)S(1)} collective-permute-done((bf16[2,272,128]{2,1,0:T(8,128)(2,1)S(1)}, bf16[2,272,128]{2,1,0:T(8,128)(2,1)S(1)}, u32[]{:S(2)}, u32[]{:S(2)}) %collective-permute-start.3) | collective-permute-done | bytes 139296 | tf_op jit(solution)/shard_map/ppermute | solution.py:332
  21.3 0.0 collective-permute-done.5.crossed_ref
  21.3 0.0 collective-permute-start.6
  21.3 2.5 %merge_blocks.1 = (bf16[8192,256]{1,0:T(8,128)(2,1)}, f32[4,256]{1,0:T(4,128)S(1)}, bf16[64,256]{1,0:T(8,128)(2,1)S(1)}, bf16[3,512,256]{2,1,0:T(8,128)(2,1)S(1)}) custom-call(s32[1,16]{1,0:T(1,128)S(1)} %add_bitcast_fusion.start_ref, bf16[64,64]{1,0:T(8,128)(2,1)S(1)} %select_convert_fusion.pick_ref, bf16[4,8192]{1,0:T(4,128)(2,1)S(1)} %maximum_select_fusion.features_ref, ...), custom_call_target="tpu_custom_call" | custom-call | flops 234881024 | bytes 7340032 | tf_op jit(solution)/shard_map/merge_blocks/pallas_call | solution.py:248
  23.8 0.0 collective-permute-done.6.last_ref
  23.9 1.4 %finish_rows.1 = (bf16[8192,256]{1,0:T(8,128)(2,1)}, bf16[4,256]{1,0:T(4,128)(2,1)}, bf16[4,2048]{1,0:T(4,128)(2,1)}) custom-call(s32[1,16]{1,0:T(1,128)S(1)} %add_bitcast_fusion.start_ref, bf16[64,256]{1,0:T(8,128)(2,1)S(1)} %get-tuple-element.57.up_ref, bf16[4,8192]{1,0:T(4,128)(2,1)S(1)} %maximum_select_fusion.features_ref, ...), custom_call_target="tpu_custom_call", output_to_operand_aliasing={{0}: (6, {})} | custom-call | flops 33554432 | bytes 1048576 | tf_op jit(solution)/shard_map/finish_rows/pallas_call | solution.py:277
  (22 shorter events, 0.2 us)
Async XLA Ops:
  0.6 1.2 %copy-start = (bf16[64,1024]{1,0:T(8,128)(2,1)S(1)}, bf16[64,1024]{1,0:T(8,128)(2,1)}, u32[]{:S(2)}) copy-start(bf16[64,1024]{1,0:T(8,128)(2,1)} %param.17) | copy-start | bytes 393220
  0.6 14.4 %collective-permute-start.2 = (bf16[4,4096]{1,0:T(4,128)(2,1)}, bf16[4,4096]{1,0:T(4,128)(2,1)S(1)}, u32[]{:S(2)}, u32[]{:S(2)}) collective-permute-start(bf16[4,4096]{1,0:T(4,128)(2,1)} %param.10), channel_id=1, source_target_pairs={{0,1},{1,0},{2,3},{3,2},{4,5},{5,4},{6,7},{7,6},{8,9},{9,8},{10,11... | collective-permute-start | bytes 98312 | tf_op jit(solution)/shard_map/ppermute | solution.py:347
  1.9 8.0 %collective-permute-start = (bf16[1,272,128]{2,1,0:T(8,128)(2,1)S(1)}, bf16[1,272,128]{2,1,0:T(8,128)(2,1)S(1)}, u32[]{:S(2)}, u32[]{:S(2)}) collective-permute-start(bf16[1,272,128]{2,1,0:T(8,128)(2,1)S(1)} %bitcast.13), channel_id=1, source_target_pairs={{0,8},{1,9},{2,10},{3,11},{4,12},{5,13},{6,14},{7,15},{8,0},{9,1},... | collective-permute-start | bytes 208904 | tf_op jit(solution)/shard_map/ppermute | solution.py:332
  10.0 6.3 %collective-permute-start.1 = (bf16[2,272,128]{2,1,0:T(8,128)(2,1)S(1)}, bf16[2,272,128]{2,1,0:T(8,128)(2,1)S(1)}, u32[]{:S(2)}, u32[]{:S(2)}) collective-permute-start(bf16[2,272,128]{2,1,0:T(8,128)(2,1)S(1)} %pad_maximum_fusion.1.rest_1_), channel_id=1, source_target_pairs={{0,2},{1,5},{2,0},{3,7},{4,6},{5,1},{6,4},{7,3},{8,10},{9,13},{10,... | collective-permute-start | bytes 417800 | tf_op jit(solution)/shard_map/ppermute | solution.py:332
  11.7 4.8 %copy-start.2 = (s32[8]{0:T(128)S(1)}, s32[8]{0:T(128)}, u32[]{:S(2)}) copy-start(s32[8]{0:T(128)} %param.19) | copy-start | bytes 100
  11.7 5.2 %copy-start.1 = (bf16[4,4096]{1,0:T(4,128)(2,1)S(1)}, bf16[4,4096]{1,0:T(4,128)(2,1)}, u32[]{:S(2)}) copy-start(bf16[4,4096]{1,0:T(4,128)(2,1)} %param.10) | copy-start | bytes 98308
  11.7 5.1 %collective-permute-start.4 = (bf16[2,272,128]{2,1,0:T(8,128)(2,1)S(1)}, bf16[2,272,128]{2,1,0:T(8,128)(2,1)S(1)}, u32[]{:S(2)}, u32[]{:S(2)}) collective-permute-start(bf16[2,272,128]{2,1,0:T(8,128)(2,1)S(1)} %pad_maximum_fusion.1.rest_1_), channel_id=1, source_target_pairs={{0,4},{1,3},{2,6},{3,1},{4,0},{5,7},{6,2},{7,5},{8,12},{9,11},{10,... | collective-permute-start | bytes 417800 | tf_op jit(solution)/shard_map/ppermute | solution.py:332
  16.3 5.1 %collective-permute-start.3 = (bf16[2,272,128]{2,1,0:T(8,128)(2,1)S(1)}, bf16[2,272,128]{2,1,0:T(8,128)(2,1)S(1)}, u32[]{:S(2)}, u32[]{:S(2)}) collective-permute-start(bf16[2,272,128]{2,1,0:T(8,128)(2,1)S(1)} %collective-permute-done.1), channel_id=1, source_target_pairs={{0,4},{1,3},{2,6},{3,1},{4,0},{5,7},{6,2},{7,5},{8,12},{9,11},{10,... | collective-permute-start | bytes 417800 | tf_op jit(solution)/shard_map/ppermute | solution.py:332
  16.8 4.5 %collective-permute-start.5 = (bf16[6,272,128]{2,1,0:T(8,128)(2,1)S(1)}, bf16[6,272,128]{2,1,0:T(8,128)(2,1)S(1)}, u32[]{:S(2)}, u32[]{:S(2)}) collective-permute-start(bf16[6,272,128]{2,1,0:T(8,128)(2,1)S(1)} %pad_maximum_fusion.slabs_ref), channel_id=1, source_target_pairs={{0,1},{1,0},{2,3},{3,2},{4,5},{5,4},{6,7},{7,6},{8,9},{9,8},{10,11... | collective-permute-start | bytes 1253384 | tf_op jit(solution)/shard_map/ppermute | solution.py:393
  21.3 2.5 %collective-permute-start.6 = (bf16[2,272,128]{2,1,0:T(8,128)(2,1)S(1)}, bf16[2,272,128]{2,1,0:T(8,128)(2,1)S(1)}, u32[]{:S(2)}, u32[]{:S(2)}) collective-permute-start(bf16[2,272,128]{2,1,0:T(8,128)(2,1)S(1)} %collective-permute-done.3.last_ref), channel_id=1, source_target_pairs={{0,1},{1,0},{2,3},{3,2},{4,5},{5,4},{6,7},{7,6},{8,9},{9,8},{10,11... | collective-permute-start | bytes 417800 | tf_op jit(solution)/shard_map/ppermute | solution.py:397

commit v21 on v18

--- a/solution.py
+++ b/solution.py
@@ -346,14 +346,15 @@
     for step in early:
         slabs = jnp.concatenate([slabs, exchange(slabs, step)], axis=0)
 
-    split = rows - rows // 4
+    split = rows // 2
     hid_other = lax.ppermute(hidden_in, "tensor", swap)
     came = exchange(slabs, first)
     part = attend(range(split), given, after=[slabs])
     came, part = lax.optimization_barrier((came, part))
     parts = [part]
     slabs = jnp.concatenate([slabs, came], axis=0)
-    last = [exchange(slabs, third), exchange(slabs, second, third)]
+    images = exchange(slabs, third)
+    last = exchange(slabs, second, third)
     came = exchange(slabs, second)
     *part, served = attend(range(split, rows), given, *in_hbm(served_value_weight), [slabs])
     came, part, hid_other, owner_rank = lax.optimization_barrier(
@@ -391,12 +392,13 @@
         jnp.concatenate(pair, axis=0).reshape(queries.shape) for pair in zip(*parts)
     )
     crossed, start = lax.optimization_barrier((slabs, start))
-    crossed = lax.ppermute(crossed, "tensor", swap)
+    crossed = [lax.ppermute(x, "tensor", swap) for x in (crossed, images)]
+    crossed = jnp.concatenate(crossed, axis=0)
     last, start, pick, context, own_weight, features, crossed = lax.optimization_barrier(
         (last, start, pick, context, own_weight, features, crossed)
     )
-    last = jnp.concatenate(last, axis=0)
     last_crossed = lax.ppermute(last, "tensor", swap)
+    last = jnp.concatenate([images, last], axis=0)
     merged, total, up, left = merge(per, start, pick, features, served, slabs, crossed, last)
     return tuple(
         finish(

time: 25.3 us -> 24.6 us (0.972)
  the two profiles are of different devices: /device:TPU:0 before, /device:TPU:21 now
where the time goes in v21:
time: 24.6 us; the launch traced here: 24.4 us
  starting transfers between devices  10.2 us (41%)
  Pallas kernels  9.6 us (39%)
  waiting for transfers between devices  2.68 us (11%)
  local copies, waits for them, and re-layouts  0.8 us (3%)
  between operations  0.78 us (3%)
  other arithmetic  0.36 us (1%)
    pallas_call x2, Pallas kernels, attend(): pl.pallas_call(functools.partial(attend_kernel, rows, fetch), out_shape=o...  5.7 us
    ppermute x4, starting transfers between devices, exchange(): return lax.ppermute(x, ('replica', 'tensor'), pairs)  4.6 us
    ppermute x2, starting transfers between devices, body(): crossed = [lax.ppermute(x, 'tensor', swap) for x in (crossed, images)]  4.39 us
    pallas_call x1, Pallas kernels, merge(): pl.pallas_call(functools.partial(merge_kernel, per, left), out_shape=(jax...  2.52 us
    ppermute x4, waiting for transfers between devices, exchange(): return lax.ppermute(x, ('replica', 'tensor'), pairs)  1.78 us
    pallas_call x1, Pallas kernels, finish(): pl.pallas_call(final_kernel, out_shape=[jax.ShapeDtypeStruct(shape, jnp.b...  1.38 us
    ppermute x2, waiting for transfers between devices, body(): crossed = [lax.ppermute(x, 'tensor', swap) for x in (crossed, images)]  0.89 us
    ppermute x1, starting transfers between devices, body(): hid_other = lax.ppermute(hidden_in, 'tensor', swap)  0.74 us
  transfers between devices with their start and end apart: 8, of which 2 were waited for; matrix products, arithmetic and copies ran while one was open for 5% of the time, Pallas kernels for 34%

profile of v21, /device:TPU:21, one launch (start us, length us, event | category | flops | bytes accessed | tf_op | source)
XLA Modules:
  0.0 24.4 jit_solution(8048517757819275946)
XLA Ops:
  0.6 0.0 copy-start
  0.6 0.7 %collective-permute-start.3 = (bf16[4,4096]{1,0:T(4,128)(2,1)}, bf16[4,4096]{1,0:T(4,128)(2,1)S(1)}, u32[]{:S(2)}, u32[]{:S(2)}) collective-permute-start(bf16[4,4096]{1,0:T(4,128)(2,1)} %param.10), channel_id=1, source_target_pairs={{0,1},{1,0},{2,3},{3,2},{4,5},{5,4},{6,7},{7,6},{8,9},{9,8},{10,11... | collective-permute-start | bytes 98312 | tf_op jit(solution)/shard_map/ppermute | solution.py:350
  1.4 0.7 %fusion.1 = (bf16[8,128]{1,0:T(8,128)(2,1)S(1)}, bf16[8,128]{1,0:T(8,128)(2,1)S(1)}) fusion(bf16[8,256]{1,0:T(8,128)(2,1)} %param.18), kind=kLoop, calls=%fused_computation.34 | loop fusion | bytes 8192 | tf_op jit(solution)/shard_map/slice | solution.py:302
  2.2 0.2 collective-permute-start
  2.4 2.8 %attend_cache.2 = (f32[2,16,128]{2,1,0:T(8,128)S(1)}, f32[2,16,128]{2,1,0:T(8,128)S(1)}) custom-call(s32[4]{0:T(128)} %lengths_hbm.3, bf16[4,2048]{1,0:T(4,128)(2,1)} %q_hbm.3, bf16[4,256]{1,0:T(4,128)(2,1)} %own_k_hbm.3, bf16[4,1024,256]{2,1,0:T(8,128)(2,1)} %k_hbm.3, bf16[4,1024,256]{2,1,0:T(8,128)(2,1)} %v_hbm.3, bf16[1,272,128]{2,1,0:T(8,128)(2,1)S(1)} %bitcast.14), custom_call_target="tpu_custom_call" | custom-call | flops 33554432 | bytes 2097152 | tf_op jit(solution)/shard_map/attend_cache/pallas_call | solution.py:113
  5.1 1.8 %collective-permute-done = bf16[1,272,128]{2,1,0:T(8,128)(2,1)S(1)} collective-permute-done((bf16[1,272,128]{2,1,0:T(8,128)(2,1)S(1)}, bf16[1,272,128]{2,1,0:T(8,128)(2,1)S(1)}, u32[]{:S(2)}, u32[]{:S(2)}) %collective-permute-start) | collective-permute-done | bytes 69664 | tf_op jit(solution)/shard_map/ppermute | solution.py:336
  6.9 0.3 %collective-permute-start.2 = (bf16[2,272,128]{2,1,0:T(8,128)(2,1)S(1)}, bf16[2,272,128]{2,1,0:T(8,128)(2,1)S(1)}, u32[]{:S(2)}, u32[]{:S(2)}) collective-permute-start(bf16[2,272,128]{2,1,0:T(8,128)(2,1)S(1)} %pad_maximum_fusion.3.rest_1_), channel_id=1, source_target_pairs={{0,4},{1,3},{2,6},{3,1},{4,0},{5,7},{6,2},{7,5},{8,12},{9,11},{10,... | collective-permute-start | bytes 417800 | tf_op jit(solution)/shard_map/ppermute | solution.py:336
  7.2 0.1 pad_add_fusion
  7.3 3.1 %collective-permute-start.5 = (bf16[2,272,128]{2,1,0:T(8,128)(2,1)S(1)}, bf16[2,272,128]{2,1,0:T(8,128)(2,1)S(1)}, u32[]{:S(2)}, u32[]{:S(2)}) collective-permute-start(bf16[2,272,128]{2,1,0:T(8,128)(2,1)S(1)} %pad_maximum_fusion.3.rest_1_), channel_id=1, source_target_pairs={{0,2},{1,5},{2,0},{3,7},{4,6},{5,1},{6,4},{7,3},{8,10},{9,13},{10,... | collective-permute-start | bytes 417800 | tf_op jit(solution)/shard_map/ppermute | solution.py:336
  10.4 1.0 %collective-permute-start.1 = (bf16[2,272,128]{2,1,0:T(8,128)(2,1)S(1)}, bf16[2,272,128]{2,1,0:T(8,128)(2,1)S(1)}, u32[]{:S(2)}, u32[]{:S(2)}) collective-permute-start(bf16[2,272,128]{2,1,0:T(8,128)(2,1)S(1)} %pad_maximum_fusion.3.rest_1_), channel_id=1, source_target_pairs={{0,6},{1,7},{2,4},{3,5},{4,2},{5,3},{6,0},{7,1},{8,14},{9,15},{10,... | collective-permute-start | bytes 417800 | tf_op jit(solution)/shard_map/ppermute | solution.py:336
  11.4 2.9 %attend_cache.3 = (f32[2,16,128]{2,1,0:T(8,128)S(1)}, f32[2,16,128]{2,1,0:T(8,128)S(1)}, bf16[8192,256]{1,0:T(8,128)(2,1)S(1)}) custom-call(s32[4]{0:T(128)} %lengths_hbm.3, bf16[4,2048]{1,0:T(4,128)(2,1)} %q_hbm.3, bf16[4,256]{1,0:T(4,128)(2,1)} %own_k_hbm.3, bf16[4,1024,256]{2,1,0:T(8,128)(2,1)} %k_hbm.3, bf16[4,1024,256]{2,1,0:T(8,128)(2,1)} %v_hbm.3, ...), custom_call_target="tpu_custom_call" | custom-call | flops 33554432 | bytes 2097152 | tf_op jit(solution)/shard_map/attend_cache/pallas_call | solution.py:113
  14.4 0.0 collective-permute-done.3
  14.4 0.0 collective-permute-done.2
  14.4 0.1 select_reduce_fusion
  14.6 1.0 %collective-permute-start.4 = (bf16[4,272,128]{2,1,0:T(8,128)(2,1)S(1)}, bf16[4,272,128]{2,1,0:T(8,128)(2,1)S(1)}, u32[]{:S(2)}, u32[]{:S(2)}) collective-permute-start(bf16[4,272,128]{2,1,0:T(8,128)(2,1)S(1)} %pad_maximum_fusion.1.slabs_ref), channel_id=1, source_target_pairs={{0,1},{1,0},{2,3},{3,2},{4,5},{5,4},{6,7},{7,6},{8,9},{9,8},{10,11... | collective-permute-start | bytes 835592 | tf_op jit(solution)/shard_map/ppermute | solution.py:395
  15.6 0.0 collective-permute-done.5
  15.6 3.4 %collective-permute-start.6 = (bf16[2,272,128]{2,1,0:T(8,128)(2,1)S(1)}, bf16[2,272,128]{2,1,0:T(8,128)(2,1)S(1)}, u32[]{:S(2)}, u32[]{:S(2)}) collective-permute-start(bf16[2,272,128]{2,1,0:T(8,128)(2,1)S(1)} %collective-permute-done.5), channel_id=1, source_target_pairs={{0,1},{1,0},{2,3},{3,2},{4,5},{5,4},{6,7},{7,6},{8,9},{9,8},{10,11... | collective-permute-start | bytes 417800 | tf_op jit(solution)/shard_map/ppermute | solution.py:395
  19.1 0.9 %collective-permute-done.6 = bf16[2,272,128]{2,1,0:T(8,128)(2,1)S(1)} collective-permute-done((bf16[2,272,128]{2,1,0:T(8,128)(2,1)S(1)}, bf16[2,272,128]{2,1,0:T(8,128)(2,1)S(1)}, u32[]{:S(2)}, u32[]{:S(2)}) %collective-permute-start.6) | collective-permute-done | bytes 139296 | tf_op jit(solution)/shard_map/ppermute | solution.py:395
  19.9 0.0 collective-permute-done.4
  20.0 0.0 collective-permute-done.1
  20.0 0.4 %collective-permute-start.7 = (bf16[2,272,128]{2,1,0:T(8,128)(2,1)S(1)}, bf16[2,272,128]{2,1,0:T(8,128)(2,1)S(1)}, u32[]{:S(2)}, u32[]{:S(2)}) collective-permute-start(bf16[2,272,128]{2,1,0:T(8,128)(2,1)S(1)} %collective-permute-done.1), channel_id=1, source_target_pairs={{0,1},{1,0},{2,3},{3,2},{4,5},{5,4},{6,7},{7,6},{8,9},{9,8},{10,11... | collective-permute-start | bytes 417800 | tf_op jit(solution)/shard_map/ppermute | solution.py:400
  20.5 2.5 %merge_blocks.1 = (bf16[8192,256]{1,0:T(8,128)(2,1)}, f32[4,256]{1,0:T(4,128)S(1)}, bf16[64,256]{1,0:T(8,128)(2,1)S(1)}, bf16[3,512,256]{2,1,0:T(8,128)(2,1)S(1)}) custom-call(s32[1,16]{1,0:T(1,128)S(1)} %add_bitcast_fusion.start_ref, bf16[64,64]{1,0:T(8,128)(2,1)S(1)} %select_convert_fusion.pick_ref, bf16[4,8192]{1,0:T(4,128)(2,1)S(1)} %maximum_select_fusion.features_ref, ...), custom_call_target="tpu_custom_call" | custom-call | flops 234881024 | bytes 7340032 | tf_op jit(solution)/shard_map/merge_blocks/pallas_call | solution.py:248
  23.0 0.0 collective-permute-done.7.last_ref
  23.0 1.4 %finish_rows.1 = (bf16[8192,256]{1,0:T(8,128)(2,1)}, bf16[4,256]{1,0:T(4,128)(2,1)}, bf16[4,2048]{1,0:T(4,128)(2,1)}) custom-call(s32[1,16]{1,0:T(1,128)S(1)} %add_bitcast_fusion.start_ref, bf16[64,256]{1,0:T(8,128)(2,1)S(1)} %get-tuple-element.53.up_ref, bf16[4,8192]{1,0:T(4,128)(2,1)S(1)} %maximum_select_fusion.features_ref, ...), custom_call_target="tpu_custom_call", output_to_operand_aliasing={{0}: (6, {})} | custom-call | flops 33554432 | bytes 1048576 | tf_op jit(solution)/shard_map/finish_rows/pallas_call | solution.py:277
  (25 shorter events, 0.3 us)
Async XLA Ops:
  0.6 1.5 %copy-start = (bf16[64,1024]{1,0:T(8,128)(2,1)S(1)}, bf16[64,1024]{1,0:T(8,128)(2,1)}, u32[]{:S(2)}) copy-start(bf16[64,1024]{1,0:T(8,128)(2,1)} %param.17) | copy-start | bytes 393220
  0.6 13.8 %collective-permute-start.3 = (bf16[4,4096]{1,0:T(4,128)(2,1)}, bf16[4,4096]{1,0:T(4,128)(2,1)S(1)}, u32[]{:S(2)}, u32[]{:S(2)}) collective-permute-start(bf16[4,4096]{1,0:T(4,128)(2,1)} %param.10), channel_id=1, source_target_pairs={{0,1},{1,0},{2,3},{3,2},{4,5},{5,4},{6,7},{7,6},{8,9},{9,8},{10,11... | collective-permute-start | bytes 98312 | tf_op jit(solution)/shard_map/ppermute | solution.py:350
  2.2 4.7 %collective-permute-start = (bf16[1,272,128]{2,1,0:T(8,128)(2,1)S(1)}, bf16[1,272,128]{2,1,0:T(8,128)(2,1)S(1)}, u32[]{:S(2)}, u32[]{:S(2)}) collective-permute-start(bf16[1,272,128]{2,1,0:T(8,128)(2,1)S(1)} %bitcast.13), channel_id=1, source_target_pairs={{0,8},{1,9},{2,10},{3,11},{4,12},{5,13},{6,14},{7,15},{8,0},{9,1},... | collective-permute-start | bytes 208904 | tf_op jit(solution)/shard_map/ppermute | solution.py:336
  6.9 7.5 %collective-permute-start.2 = (bf16[2,272,128]{2,1,0:T(8,128)(2,1)S(1)}, bf16[2,272,128]{2,1,0:T(8,128)(2,1)S(1)}, u32[]{:S(2)}, u32[]{:S(2)}) collective-permute-start(bf16[2,272,128]{2,1,0:T(8,128)(2,1)S(1)} %pad_maximum_fusion.3.rest_1_), channel_id=1, source_target_pairs={{0,4},{1,3},{2,6},{3,1},{4,0},{5,7},{6,2},{7,5},{8,12},{9,11},{10,... | collective-permute-start | bytes 417800 | tf_op jit(solution)/shard_map/ppermute | solution.py:336
  7.3 7.1 %copy-start.2 = (s32[8]{0:T(128)S(1)}, s32[8]{0:T(128)}, u32[]{:S(2)}) copy-start(s32[8]{0:T(128)} %param.19) | copy-start | bytes 100
  7.3 11.7 %copy-start.1 = (bf16[4,4096]{1,0:T(4,128)(2,1)S(1)}, bf16[4,4096]{1,0:T(4,128)(2,1)}, u32[]{:S(2)}) copy-start(bf16[4,4096]{1,0:T(4,128)(2,1)} %param.10) | copy-start | bytes 98308
  7.3 8.3 %collective-permute-start.5 = (bf16[2,272,128]{2,1,0:T(8,128)(2,1)S(1)}, bf16[2,272,128]{2,1,0:T(8,128)(2,1)S(1)}, u32[]{:S(2)}, u32[]{:S(2)}) collective-permute-start(bf16[2,272,128]{2,1,0:T(8,128)(2,1)S(1)} %pad_maximum_fusion.3.rest_1_), channel_id=1, source_target_pairs={{0,2},{1,5},{2,0},{3,7},{4,6},{5,1},{6,4},{7,3},{8,10},{9,13},{10,... | collective-permute-start | bytes 417800 | tf_op jit(solution)/shard_map/ppermute | solution.py:336
  10.4 9.6 %collective-permute-start.1 = (bf16[2,272,128]{2,1,0:T(8,128)(2,1)S(1)}, bf16[2,272,128]{2,1,0:T(8,128)(2,1)S(1)}, u32[]{:S(2)}, u32[]{:S(2)}) collective-permute-start(bf16[2,272,128]{2,1,0:T(8,128)(2,1)S(1)} %pad_maximum_fusion.3.rest_1_), channel_id=1, source_target_pairs={{0,6},{1,7},{2,4},{3,5},{4,2},{5,3},{6,0},{7,1},{8,14},{9,15},{10,... | collective-permute-start | bytes 417800 | tf_op jit(solution)/shard_map/ppermute | solution.py:336
  14.6 5.4 %collective-permute-start.4 = (bf16[4,272,128]{2,1,0:T(8,128)(2,1)S(1)}, bf16[4,272,128]{2,1,0:T(8,128)(2,1)S(1)}, u32[]{:S(2)}, u32[]{:S(2)}) collective-permute-start(bf16[4,272,128]{2,1,0:T(8,128)(2,1)S(1)} %pad_maximum_fusion.1.slabs_ref), channel_id=1, source_target_pairs={{0,1},{1,0},{2,3},{3,2},{4,5},{5,4},{6,7},{7,6},{8,9},{9,8},{10,11... | collective-permute-start | bytes 835592 | tf_op jit(solution)/shard_map/ppermute | solution.py:395
  15.6 4.4 %collective-permute-start.6 = (bf16[2,272,128]{2,1,0:T(8,128)(2,1)S(1)}, bf16[2,272,128]{2,1,0:T(8,128)(2,1)S(1)}, u32[]{:S(2)}, u32[]{:S(2)}) collective-permute-start(bf16[2,272,128]{2,1,0:T(8,128)(2,1)S(1)} %collective-permute-done.5), channel_id=1, source_target_pairs={{0,1},{1,0},{2,3},{3,2},{4,5},{5,4},{6,7},{7,6},{8,9},{9,8},{10,11... | collective-permute-start | bytes 417800 | tf_op jit(solution)/shard_map/ppermute | solution.py:395
  20.0 3.0 %collective-permute-start.7 = (bf16[2,272,128]{2,1,0:T(8,128)(2,1)S(1)}, bf16[2,272,128]{2,1,0:T(8,128)(2,1)S(1)}, u32[]{:S(2)}, u32[]{:S(2)}) collective-permute-start(bf16[2,272,128]{2,1,0:T(8,128)(2,1)S(1)} %collective-permute-done.1), channel_id=1, source_target_pairs={{0,1},{1,0},{2,3},{3,2},{4,5},{5,4},{6,7},{7,6},{8,9},{9,8},{10,11... | collective-permute-start | bytes 417800 | tf_op jit(solution)/shard_map/ppermute | solution.py:400

commit v22 on v21

--- a/solution.py
+++ b/solution.py
@@ -325,7 +325,7 @@
     rank = n * per
 
     bits = [n >> i for i in range(1, n.bit_length())]
-    ways = [bits, bits[:-2] + bits[:-3:-1]]
+    ways = [bits[:-2] + bits[:-3:-1], bits]
 
     def exchange(x, *steps):
         pairs = [

time: 24.6 us -> 24.7 us (level)
  the two profiles are of different devices: /device:TPU:21 before, /device:TPU:0 now
where the time goes in v22:
time: 24.7 us; the launch traced here: 24.5 us
  Pallas kernels  9.6 us (39%)
  starting transfers between devices  8.61 us (35%)
  waiting for transfers between devices  4.32 us (17%)
  local copies, waits for them, and re-layouts  0.8 us (3%)
  between operations  0.78 us (3%)
  other arithmetic  0.36 us (1%)
    ppermute x4, starting transfers between devices, exchange(): return lax.ppermute(x, ('replica', 'tensor'), pairs)  7.33 us
    pallas_call x2, Pallas kernels, attend(): pl.pallas_call(functools.partial(attend_kernel, rows, fetch), out_shape=o...  5.7 us
    ppermute x4, waiting for transfers between devices, exchange(): return lax.ppermute(x, ('replica', 'tensor'), pairs)  3.17 us
    pallas_call x1, Pallas kernels, merge(): pl.pallas_call(functools.partial(merge_kernel, per, left), out_shape=(jax...  2.52 us
    pallas_call x1, Pallas kernels, finish(): pl.pallas_call(final_kernel, out_shape=[jax.ShapeDtypeStruct(shape, jnp.b...  1.38 us
    ppermute x2, waiting for transfers between devices, body(): crossed = [lax.ppermute(x, 'tensor', swap) for x in (crossed, images)]  1.14 us
    slice x1, local copies, waits for them, and re-layouts, panels(): return [x[:, i:i + PANEL] for i in range(0, x.shape[1], PANEL)]  0.7 us
    ppermute x2, starting transfers between devices, body(): crossed = [lax.ppermute(x, 'tensor', swap) for x in (crossed, images)]  0.56 us
  transfers between devices with their start and end apart: 8, of which 3 were waited for; matrix products, arithmetic and copies ran while one was open for 5% of the time, Pallas kernels for 34%

profile of v22, /device:TPU:0, one launch (start us, length us, event | category | flops | bytes accessed | tf_op | source)
XLA Modules:
  0.0 24.5 jit_solution(10315333407449166712)
XLA Ops:
  0.6 0.0 copy-start
  0.6 0.5 %collective-permute-start.3 = (bf16[4,4096]{1,0:T(4,128)(2,1)}, bf16[4,4096]{1,0:T(4,128)(2,1)S(1)}, u32[]{:S(2)}, u32[]{:S(2)}) collective-permute-start(bf16[4,4096]{1,0:T(4,128)(2,1)} %param.10), channel_id=1, source_target_pairs={{0,1},{1,0},{2,3},{3,2},{4,5},{5,4},{6,7},{7,6},{8,9},{9,8},{10,11... | collective-permute-start | bytes 98312 | tf_op jit(solution)/shard_map/ppermute | solution.py:350
  1.2 0.7 %fusion.1 = (bf16[8,128]{1,0:T(8,128)(2,1)S(1)}, bf16[8,128]{1,0:T(8,128)(2,1)S(1)}) fusion(bf16[8,256]{1,0:T(8,128)(2,1)} %param.18), kind=kLoop, calls=%fused_computation.34 | loop fusion | bytes 8192 | tf_op jit(solution)/shard_map/slice | solution.py:302
  1.9 3.8 %collective-permute-start = (bf16[1,272,128]{2,1,0:T(8,128)(2,1)S(1)}, bf16[1,272,128]{2,1,0:T(8,128)(2,1)S(1)}, u32[]{:S(2)}, u32[]{:S(2)}) collective-permute-start(bf16[1,272,128]{2,1,0:T(8,128)(2,1)S(1)} %bitcast.13), channel_id=1, source_target_pairs={{0,8},{1,9},{2,10},{3,11},{4,12},{5,13},{6,14},{7,15},{8,0},{9,1},... | collective-permute-start | bytes 208904 | tf_op jit(solution)/shard_map/ppermute | solution.py:336
  5.7 2.8 %attend_cache.2 = (f32[2,16,128]{2,1,0:T(8,128)S(1)}, f32[2,16,128]{2,1,0:T(8,128)S(1)}) custom-call(s32[4]{0:T(128)} %lengths_hbm.3, bf16[4,2048]{1,0:T(4,128)(2,1)} %q_hbm.3, bf16[4,256]{1,0:T(4,128)(2,1)} %own_k_hbm.3, bf16[4,1024,256]{2,1,0:T(8,128)(2,1)} %k_hbm.3, bf16[4,1024,256]{2,1,0:T(8,128)(2,1)} %v_hbm.3, bf16[1,272,128]{2,1,0:T(8,128)(2,1)S(1)} %bitcast.14), custom_call_target="tpu_custom_call" | custom-call | flops 33554432 | bytes 2097152 | tf_op jit(solution)/shard_map/attend_cache/pallas_call | solution.py:113
  8.5 1.4 %collective-permute-done = bf16[1,272,128]{2,1,0:T(8,128)(2,1)S(1)} collective-permute-done((bf16[1,272,128]{2,1,0:T(8,128)(2,1)S(1)}, bf16[1,272,128]{2,1,0:T(8,128)(2,1)S(1)}, u32[]{:S(2)}, u32[]{:S(2)}) %collective-permute-start) | collective-permute-done | bytes 69664 | tf_op jit(solution)/shard_map/ppermute | solution.py:336
  10.0 1.7 %collective-permute-start.2 = (bf16[2,272,128]{2,1,0:T(8,128)(2,1)S(1)}, bf16[2,272,128]{2,1,0:T(8,128)(2,1)S(1)}, u32[]{:S(2)}, u32[]{:S(2)}) collective-permute-start(bf16[2,272,128]{2,1,0:T(8,128)(2,1)S(1)} %pad_maximum_fusion.3.rest_1_), channel_id=1, source_target_pairs={{0,2},{1,5},{2,0},{3,7},{4,6},{5,1},{6,4},{7,3},{8,10},{9,13},{10,... | collective-permute-start | bytes 417800 | tf_op jit(solution)/shard_map/ppermute | solution.py:336
  11.6 0.1 pad_add_fusion
  11.7 0.7 %collective-permute-start.5 = (bf16[2,272,128]{2,1,0:T(8,128)(2,1)S(1)}, bf16[2,272,128]{2,1,0:T(8,128)(2,1)S(1)}, u32[]{:S(2)}, u32[]{:S(2)}) collective-permute-start(bf16[2,272,128]{2,1,0:T(8,128)(2,1)S(1)} %pad_maximum_fusion.3.rest_1_), channel_id=1, source_target_pairs={{0,4},{1,3},{2,6},{3,1},{4,0},{5,7},{6,2},{7,5},{8,12},{9,11},{10,... | collective-permute-start | bytes 417800 | tf_op jit(solution)/shard_map/ppermute | solution.py:336
  12.4 1.2 %collective-permute-start.1 = (bf16[2,272,128]{2,1,0:T(8,128)(2,1)S(1)}, bf16[2,272,128]{2,1,0:T(8,128)(2,1)S(1)}, u32[]{:S(2)}, u32[]{:S(2)}) collective-permute-start(bf16[2,272,128]{2,1,0:T(8,128)(2,1)S(1)} %pad_maximum_fusion.3.rest_1_), channel_id=1, source_target_pairs={{0,6},{1,7},{2,4},{3,5},{4,2},{5,3},{6,0},{7,1},{8,14},{9,15},{10,... | collective-permute-start | bytes 417800 | tf_op jit(solution)/shard_map/ppermute | solution.py:336
  13.6 2.9 %attend_cache.3 = (f32[2,16,128]{2,1,0:T(8,128)S(1)}, f32[2,16,128]{2,1,0:T(8,128)S(1)}, bf16[8192,256]{1,0:T(8,128)(2,1)S(1)}) custom-call(s32[4]{0:T(128)} %lengths_hbm.3, bf16[4,2048]{1,0:T(4,128)(2,1)} %q_hbm.3, bf16[4,256]{1,0:T(4,128)(2,1)} %own_k_hbm.3, bf16[4,1024,256]{2,1,0:T(8,128)(2,1)} %k_hbm.3, bf16[4,1024,256]{2,1,0:T(8,128)(2,1)} %v_hbm.3, ...), custom_call_target="tpu_custom_call" | custom-call | flops 33554432 | bytes 2097152 | tf_op jit(solution)/shard_map/attend_cache/pallas_call | solution.py:113
  16.6 0.0 collective-permute-done.3
  16.6 1.7 %collective-permute-done.2 = bf16[2,272,128]{2,1,0:T(8,128)(2,1)S(1)} collective-permute-done((bf16[2,272,128]{2,1,0:T(8,128)(2,1)S(1)}, bf16[2,272,128]{2,1,0:T(8,128)(2,1)S(1)}, u32[]{:S(2)}, u32[]{:S(2)}) %collective-permute-start.2) | collective-permute-done | bytes 139296 | tf_op jit(solution)/shard_map/ppermute | solution.py:336
  18.3 0.1 select_reduce_fusion
  18.4 0.1 collective-permute-start.4
  18.5 0.0 collective-permute-done.5
  18.5 0.5 %collective-permute-start.6 = (bf16[2,272,128]{2,1,0:T(8,128)(2,1)S(1)}, bf16[2,272,128]{2,1,0:T(8,128)(2,1)S(1)}, u32[]{:S(2)}, u32[]{:S(2)}) collective-permute-start(bf16[2,272,128]{2,1,0:T(8,128)(2,1)S(1)} %collective-permute-done.5), channel_id=1, source_target_pairs={{0,1},{1,0},{2,3},{3,2},{4,5},{5,4},{6,7},{7,6},{8,9},{9,8},{10,11... | collective-permute-start | bytes 417800 | tf_op jit(solution)/shard_map/ppermute | solution.py:395
  19.1 1.1 %collective-permute-done.6 = bf16[2,272,128]{2,1,0:T(8,128)(2,1)S(1)} collective-permute-done((bf16[2,272,128]{2,1,0:T(8,128)(2,1)S(1)}, bf16[2,272,128]{2,1,0:T(8,128)(2,1)S(1)}, u32[]{:S(2)}, u32[]{:S(2)}) %collective-permute-start.6) | collective-permute-done | bytes 139296 | tf_op jit(solution)/shard_map/ppermute | solution.py:395
  20.3 0.0 collective-permute-done.4
  20.3 0.0 collective-permute-done.1
  20.3 0.2 collective-permute-start.7
  20.6 2.5 %merge_blocks.1 = (bf16[8192,256]{1,0:T(8,128)(2,1)}, f32[4,256]{1,0:T(4,128)S(1)}, bf16[64,256]{1,0:T(8,128)(2,1)S(1)}, bf16[3,512,256]{2,1,0:T(8,128)(2,1)S(1)}) custom-call(s32[1,16]{1,0:T(1,128)S(1)} %add_bitcast_fusion.start_ref, bf16[64,64]{1,0:T(8,128)(2,1)S(1)} %select_convert_fusion.pick_ref, bf16[4,8192]{1,0:T(4,128)(2,1)S(1)} %maximum_select_fusion.features_ref, ...), custom_call_target="tpu_custom_call" | custom-call | flops 234881024 | bytes 7340032 | tf_op jit(solution)/shard_map/merge_blocks/pallas_call | solution.py:248
  23.1 0.0 collective-permute-done.7.last_ref
  23.1 1.4 %finish_rows.1 = (bf16[8192,256]{1,0:T(8,128)(2,1)}, bf16[4,256]{1,0:T(4,128)(2,1)}, bf16[4,2048]{1,0:T(4,128)(2,1)}) custom-call(s32[1,16]{1,0:T(1,128)S(1)} %add_bitcast_fusion.start_ref, bf16[64,256]{1,0:T(8,128)(2,1)S(1)} %get-tuple-element.53.up_ref, bf16[4,8192]{1,0:T(4,128)(2,1)S(1)} %maximum_select_fusion.features_ref, ...), custom_call_target="tpu_custom_call", output_to_operand_aliasing={{0}: (6, {})} | custom-call | flops 33554432 | bytes 1048576 | tf_op jit(solution)/shard_map/finish_rows/pallas_call | solution.py:277
  (25 shorter events, 0.3 us)
Async XLA Ops:
  0.6 1.2 %copy-start = (bf16[64,1024]{1,0:T(8,128)(2,1)S(1)}, bf16[64,1024]{1,0:T(8,128)(2,1)}, u32[]{:S(2)}) copy-start(bf16[64,1024]{1,0:T(8,128)(2,1)} %param.17) | copy-start | bytes 393220
  0.6 15.9 %collective-permute-start.3 = (bf16[4,4096]{1,0:T(4,128)(2,1)}, bf16[4,4096]{1,0:T(4,128)(2,1)S(1)}, u32[]{:S(2)}, u32[]{:S(2)}) collective-permute-start(bf16[4,4096]{1,0:T(4,128)(2,1)} %param.10), channel_id=1, source_target_pairs={{0,1},{1,0},{2,3},{3,2},{4,5},{5,4},{6,7},{7,6},{8,9},{9,8},{10,11... | collective-permute-start | bytes 98312 | tf_op jit(solution)/shard_map/ppermute | solution.py:350
  1.9 8.0 %collective-permute-start = (bf16[1,272,128]{2,1,0:T(8,128)(2,1)S(1)}, bf16[1,272,128]{2,1,0:T(8,128)(2,1)S(1)}, u32[]{:S(2)}, u32[]{:S(2)}) collective-permute-start(bf16[1,272,128]{2,1,0:T(8,128)(2,1)S(1)} %bitcast.13), channel_id=1, source_target_pairs={{0,8},{1,9},{2,10},{3,11},{4,12},{5,13},{6,14},{7,15},{8,0},{9,1},... | collective-permute-start | bytes 208904 | tf_op jit(solution)/shard_map/ppermute | solution.py:336
  10.0 8.3 %collective-permute-start.2 = (bf16[2,272,128]{2,1,0:T(8,128)(2,1)S(1)}, bf16[2,272,128]{2,1,0:T(8,128)(2,1)S(1)}, u32[]{:S(2)}, u32[]{:S(2)}) collective-permute-start(bf16[2,272,128]{2,1,0:T(8,128)(2,1)S(1)} %pad_maximum_fusion.3.rest_1_), channel_id=1, source_target_pairs={{0,2},{1,5},{2,0},{3,7},{4,6},{5,1},{6,4},{7,3},{8,10},{9,13},{10,... | collective-permute-start | bytes 417800 | tf_op jit(solution)/shard_map/ppermute | solution.py:336
  11.7 6.6 %copy-start.2 = (s32[8]{0:T(128)S(1)}, s32[8]{0:T(128)}, u32[]{:S(2)}) copy-start(s32[8]{0:T(128)} %param.19) | copy-start | bytes 100
  11.7 7.3 %copy-start.1 = (bf16[4,4096]{1,0:T(4,128)(2,1)S(1)}, bf16[4,4096]{1,0:T(4,128)(2,1)}, u32[]{:S(2)}) copy-start(bf16[4,4096]{1,0:T(4,128)(2,1)} %param.10) | copy-start | bytes 98308
  11.7 6.8 %collective-permute-start.5 = (bf16[2,272,128]{2,1,0:T(8,128)(2,1)S(1)}, bf16[2,272,128]{2,1,0:T(8,128)(2,1)S(1)}, u32[]{:S(2)}, u32[]{:S(2)}) collective-permute-start(bf16[2,272,128]{2,1,0:T(8,128)(2,1)S(1)} %pad_maximum_fusion.3.rest_1_), channel_id=1, source_target_pairs={{0,4},{1,3},{2,6},{3,1},{4,0},{5,7},{6,2},{7,5},{8,12},{9,11},{10,... | collective-permute-start | bytes 417800 | tf_op jit(solution)/shard_map/ppermute | solution.py:336
  12.4 7.9 %collective-permute-start.1 = (bf16[2,272,128]{2,1,0:T(8,128)(2,1)S(1)}, bf16[2,272,128]{2,1,0:T(8,128)(2,1)S(1)}, u32[]{:S(2)}, u32[]{:S(2)}) collective-permute-start(bf16[2,272,128]{2,1,0:T(8,128)(2,1)S(1)} %pad_maximum_fusion.3.rest_1_), channel_id=1, source_target_pairs={{0,6},{1,7},{2,4},{3,5},{4,2},{5,3},{6,0},{7,1},{8,14},{9,15},{10,... | collective-permute-start | bytes 417800 | tf_op jit(solution)/shard_map/ppermute | solution.py:336
  18.4 1.8 %collective-permute-start.4 = (bf16[4,272,128]{2,1,0:T(8,128)(2,1)S(1)}, bf16[4,272,128]{2,1,0:T(8,128)(2,1)S(1)}, u32[]{:S(2)}, u32[]{:S(2)}) collective-permute-start(bf16[4,272,128]{2,1,0:T(8,128)(2,1)S(1)} %pad_maximum_fusion.1.slabs_ref), channel_id=1, source_target_pairs={{0,1},{1,0},{2,3},{3,2},{4,5},{5,4},{6,7},{7,6},{8,9},{9,8},{10,11... | collective-permute-start | bytes 835592 | tf_op jit(solution)/shard_map/ppermute | solution.py:395
  18.5 1.7 %collective-permute-start.6 = (bf16[2,272,128]{2,1,0:T(8,128)(2,1)S(1)}, bf16[2,272,128]{2,1,0:T(8,128)(2,1)S(1)}, u32[]{:S(2)}, u32[]{:S(2)}) collective-permute-start(bf16[2,272,128]{2,1,0:T(8,128)(2,1)S(1)} %collective-permute-done.5), channel_id=1, source_target_pairs={{0,1},{1,0},{2,3},{3,2},{4,5},{5,4},{6,7},{7,6},{8,9},{9,8},{10,11... | collective-permute-start | bytes 417800 | tf_op jit(solution)/shard_map/ppermute | solution.py:395
  20.3 2.8 %collective-permute-start.7 = (bf16[2,272,128]{2,1,0:T(8,128)(2,1)S(1)}, bf16[2,272,128]{2,1,0:T(8,128)(2,1)S(1)}, u32[]{:S(2)}, u32[]{:S(2)}) collective-permute-start(bf16[2,272,128]{2,1,0:T(8,128)(2,1)S(1)} %collective-permute-done.1), channel_id=1, source_target_pairs={{0,1},{1,0},{2,3},{3,2},{4,5},{5,4},{6,7},{7,6},{8,9},{9,8},{10,11... | collective-permute-start | bytes 417800 | tf_op jit(solution)/shard_map/ppermute | solution.py:400

commit v23 on v21

--- a/solution.py
+++ b/solution.py
@@ -353,8 +353,8 @@
     came, part = lax.optimization_barrier((came, part))
     parts = [part]
     slabs = jnp.concatenate([slabs, came], axis=0)
+    last = exchange(slabs, second, third)
     images = exchange(slabs, third)
-    last = exchange(slabs, second, third)
     came = exchange(slabs, second)
     *part, served = attend(range(split, rows), given, *in_hbm(served_value_weight), [slabs])
     came, part, hid_other, owner_rank = lax.optimization_barrier(
@@ -392,13 +392,12 @@
         jnp.concatenate(pair, axis=0).reshape(queries.shape) for pair in zip(*parts)
     )
     crossed, start = lax.optimization_barrier((slabs, start))
-    crossed = [lax.ppermute(x, "tensor", swap) for x in (crossed, images)]
-    crossed = jnp.concatenate(crossed, axis=0)
+    crossed = lax.ppermute(crossed, "tensor", swap)
     last, start, pick, context, own_weight, features, crossed = lax.optimization_barrier(
         (last, start, pick, context, own_weight, features, crossed)
     )
+    last = jnp.concatenate([images, last], axis=0)
     last_crossed = lax.ppermute(last, "tensor", swap)
-    last = jnp.concatenate([images, last], axis=0)
     merged, total, up, left = merge(per, start, pick, features, served, slabs, crossed, last)
     return tuple(
         finish(

time: 24.6 us -> 23.8 us (0.967)
  the two profiles are of different devices: /device:TPU:21 before, /device:TPU:0 now
where the time goes in v23:
time: 23.8 us; the launch traced here: 23.6 us
  Pallas kernels  10 us (42%)
  starting transfers between devices  7.99 us (34%)
  waiting for transfers between devices  3.6 us (15%)
  local copies, waits for them, and re-layouts  0.83 us (3%)
  between operations  0.81 us (3%)
  other arithmetic  0.3 us (1%)
    ppermute x4, starting transfers between devices, exchange(): return lax.ppermute(x, ('replica', 'tensor'), pairs)  7.33 us
    pallas_call x2, Pallas kernels, attend(): pl.pallas_call(functools.partial(attend_kernel, rows, fetch), out_shape=o...  5.7 us
    ppermute x4, waiting for transfers between devices, exchange(): return lax.ppermute(x, ('replica', 'tensor'), pairs)  3.59 us
    pallas_call x1, Pallas kernels, merge(): pl.pallas_call(functools.partial(merge_kernel, per, left), out_shape=(jax...  2.39 us
    pallas_call x1, Pallas kernels, finish(): pl.pallas_call(final_kernel, out_shape=[jax.ShapeDtypeStruct(shape, jnp.b...  1.93 us
    slice x1, local copies, waits for them, and re-layouts, panels(): return [x[:, i:i + PANEL] for i in range(0, x.shape[1], PANEL)]  0.7 us
    ppermute x1, starting transfers between devices, body(): hid_other = lax.ppermute(hidden_in, 'tensor', swap)  0.52 us
  transfers between devices with their start and end apart: 7, of which 2 were waited for; matrix products, arithmetic and copies ran while one was open for 5% of the time, Pallas kernels for 34%

profile of v23, /device:TPU:0, one launch (start us, length us, event | category | flops | bytes accessed | tf_op | source)
XLA Modules:
  0.0 23.6 jit_solution(640025224552184608)
XLA Ops:
  0.6 0.0 copy-start
  0.6 0.5 %collective-permute-start.3 = (bf16[4,4096]{1,0:T(4,128)(2,1)}, bf16[4,4096]{1,0:T(4,128)(2,1)S(1)}, u32[]{:S(2)}, u32[]{:S(2)}) collective-permute-start(bf16[4,4096]{1,0:T(4,128)(2,1)} %param.10), channel_id=1, source_target_pairs={{0,1},{1,0},{2,3},{3,2},{4,5},{5,4},{6,7},{7,6},{8,9},{9,8},{10,11... | collective-permute-start | bytes 98312 | tf_op jit(solution)/shard_map/ppermute | solution.py:350
  1.2 0.7 %fusion.1 = (bf16[8,128]{1,0:T(8,128)(2,1)S(1)}, bf16[8,128]{1,0:T(8,128)(2,1)S(1)}) fusion(bf16[8,256]{1,0:T(8,128)(2,1)} %param.18), kind=kLoop, calls=%fused_computation.34 | loop fusion | bytes 8192 | tf_op jit(solution)/shard_map/slice | solution.py:302
  1.9 0.0 copy-done
  1.9 3.8 %collective-permute-start = (bf16[1,272,128]{2,1,0:T(8,128)(2,1)S(1)}, bf16[1,272,128]{2,1,0:T(8,128)(2,1)S(1)}, u32[]{:S(2)}, u32[]{:S(2)}) collective-permute-start(bf16[1,272,128]{2,1,0:T(8,128)(2,1)S(1)} %bitcast.13), channel_id=1, source_target_pairs={{0,8},{1,9},{2,10},{3,11},{4,12},{5,13},{6,14},{7,15},{8,0},{9,1},... | collective-permute-start | bytes 208904 | tf_op jit(solution)/shard_map/ppermute | solution.py:336
  5.7 2.8 %attend_cache.2 = (f32[2,16,128]{2,1,0:T(8,128)S(1)}, f32[2,16,128]{2,1,0:T(8,128)S(1)}) custom-call(s32[4]{0:T(128)} %lengths_hbm.3, bf16[4,2048]{1,0:T(4,128)(2,1)} %q_hbm.3, bf16[4,256]{1,0:T(4,128)(2,1)} %own_k_hbm.3, bf16[4,1024,256]{2,1,0:T(8,128)(2,1)} %k_hbm.3, bf16[4,1024,256]{2,1,0:T(8,128)(2,1)} %v_hbm.3, bf16[1,272,128]{2,1,0:T(8,128)(2,1)S(1)} %bitcast.14), custom_call_target="tpu_custom_call" | custom-call | flops 33554432 | bytes 2097152 | tf_op jit(solution)/shard_map/attend_cache/pallas_call | solution.py:113
  8.5 1.4 %collective-permute-done = bf16[1,272,128]{2,1,0:T(8,128)(2,1)S(1)} collective-permute-done((bf16[1,272,128]{2,1,0:T(8,128)(2,1)S(1)}, bf16[1,272,128]{2,1,0:T(8,128)(2,1)S(1)}, u32[]{:S(2)}, u32[]{:S(2)}) %collective-permute-start) | collective-permute-done | bytes 69664 | tf_op jit(solution)/shard_map/ppermute | solution.py:336
  10.0 0.8 %collective-permute-start.2 = (bf16[2,272,128]{2,1,0:T(8,128)(2,1)S(1)}, bf16[2,272,128]{2,1,0:T(8,128)(2,1)S(1)}, u32[]{:S(2)}, u32[]{:S(2)}) collective-permute-start(bf16[2,272,128]{2,1,0:T(8,128)(2,1)S(1)} %pad_maximum_fusion.1.rest_1_), channel_id=1, source_target_pairs={{0,4},{1,3},{2,6},{3,1},{4,0},{5,7},{6,2},{7,5},{8,12},{9,11},{10,... | collective-permute-start | bytes 417800 | tf_op jit(solution)/shard_map/ppermute | solution.py:336
  10.8 0.1 pad_add_fusion
  10.9 1.6 %collective-permute-start.5 = (bf16[2,272,128]{2,1,0:T(8,128)(2,1)S(1)}, bf16[2,272,128]{2,1,0:T(8,128)(2,1)S(1)}, u32[]{:S(2)}, u32[]{:S(2)}) collective-permute-start(bf16[2,272,128]{2,1,0:T(8,128)(2,1)S(1)} %pad_maximum_fusion.1.rest_1_), channel_id=1, source_target_pairs={{0,2},{1,5},{2,0},{3,7},{4,6},{5,1},{6,4},{7,3},{8,10},{9,13},{10,... | collective-permute-start | bytes 417800 | tf_op jit(solution)/shard_map/ppermute | solution.py:336
  12.5 1.2 %collective-permute-start.1 = (bf16[2,272,128]{2,1,0:T(8,128)(2,1)S(1)}, bf16[2,272,128]{2,1,0:T(8,128)(2,1)S(1)}, u32[]{:S(2)}, u32[]{:S(2)}) collective-permute-start(bf16[2,272,128]{2,1,0:T(8,128)(2,1)S(1)} %pad_maximum_fusion.1.rest_1_), channel_id=1, source_target_pairs={{0,6},{1,7},{2,4},{3,5},{4,2},{5,3},{6,0},{7,1},{8,14},{9,15},{10,... | collective-permute-start | bytes 417800 | tf_op jit(solution)/shard_map/ppermute | solution.py:336
  13.6 2.9 %attend_cache.3 = (f32[2,16,128]{2,1,0:T(8,128)S(1)}, f32[2,16,128]{2,1,0:T(8,128)S(1)}, bf16[8192,256]{1,0:T(8,128)(2,1)S(1)}) custom-call(s32[4]{0:T(128)} %lengths_hbm.3, bf16[4,2048]{1,0:T(4,128)(2,1)} %q_hbm.3, bf16[4,256]{1,0:T(4,128)(2,1)} %own_k_hbm.3, bf16[4,1024,256]{2,1,0:T(8,128)(2,1)} %k_hbm.3, bf16[4,1024,256]{2,1,0:T(8,128)(2,1)} %v_hbm.3, ...), custom_call_target="tpu_custom_call" | custom-call | flops 33554432 | bytes 2097152 | tf_op jit(solution)/shard_map/attend_cache/pallas_call | solution.py:113
  16.6 0.0 collective-permute-done.3
  16.6 0.0 collective-permute-done.2
  16.6 0.0 copy-done.2
  16.6 0.1 select_reduce_fusion
  16.7 0.1 collective-permute-start.4
  16.9 0.0 collective-permute-done.5
  17.0 2.1 %collective-permute-done.1 = bf16[2,272,128]{2,1,0:T(8,128)(2,1)S(1)} collective-permute-done((bf16[2,272,128]{2,1,0:T(8,128)(2,1)S(1)}, bf16[2,272,128]{2,1,0:T(8,128)(2,1)S(1)}, u32[]{:S(2)}, u32[]{:S(2)}) %collective-permute-start.1) | collective-permute-done | bytes 139296 | tf_op jit(solution)/shard_map/ppermute | solution.py:336
  19.1 0.0 collective-permute-done.4.crossed_ref
  19.1 0.1 collective-permute-start.6
  19.2 2.4 %merge_blocks.1 = (bf16[8192,256]{1,0:T(8,128)(2,1)}, f32[4,256]{1,0:T(4,128)S(1)}, bf16[64,256]{1,0:T(8,128)(2,1)S(1)}, bf16[3,512,256]{2,1,0:T(8,128)(2,1)S(1)}) custom-call(s32[1,16]{1,0:T(1,128)S(1)} %add_bitcast_fusion.start_ref, bf16[64,64]{1,0:T(8,128)(2,1)S(1)} %select_convert_fusion.pick_ref, bf16[4,8192]{1,0:T(4,128)(2,1)S(1)} %maximum_select_fusion.features_ref, ...), custom_call_target="tpu_custom_call" | custom-call | flops 201326592 | bytes 6291456 | tf_op jit(solution)/shard_map/merge_blocks/pallas_call | solution.py:248
  21.6 0.0 collective-permute-done.6.last_ref
  21.6 1.9 %finish_rows.1 = (bf16[8192,256]{1,0:T(8,128)(2,1)}, bf16[4,256]{1,0:T(4,128)(2,1)}, bf16[4,2048]{1,0:T(4,128)(2,1)}) custom-call(s32[1,16]{1,0:T(1,128)S(1)} %add_bitcast_fusion.start_ref, bf16[64,256]{1,0:T(8,128)(2,1)S(1)} %get-tuple-element.53.up_ref, bf16[4,8192]{1,0:T(4,128)(2,1)S(1)} %maximum_select_fusion.features_ref, ...), custom_call_target="tpu_custom_call", output_to_operand_aliasing={{0}: (6, {})} | custom-call | flops 67108864 | bytes 2097152 | tf_op jit(solution)/shard_map/finish_rows/pallas_call | solution.py:277
  (23 shorter events, 0.3 us)
Async XLA Ops:
  0.6 1.2 %copy-start = (bf16[64,1024]{1,0:T(8,128)(2,1)S(1)}, bf16[64,1024]{1,0:T(8,128)(2,1)}, u32[]{:S(2)}) copy-start(bf16[64,1024]{1,0:T(8,128)(2,1)} %param.17) | copy-start | bytes 393220
  0.6 15.9 %collective-permute-start.3 = (bf16[4,4096]{1,0:T(4,128)(2,1)}, bf16[4,4096]{1,0:T(4,128)(2,1)S(1)}, u32[]{:S(2)}, u32[]{:S(2)}) collective-permute-start(bf16[4,4096]{1,0:T(4,128)(2,1)} %param.10), channel_id=1, source_target_pairs={{0,1},{1,0},{2,3},{3,2},{4,5},{5,4},{6,7},{7,6},{8,9},{9,8},{10,11... | collective-permute-start | bytes 98312 | tf_op jit(solution)/shard_map/ppermute | solution.py:350
  1.9 8.0 %collective-permute-start = (bf16[1,272,128]{2,1,0:T(8,128)(2,1)S(1)}, bf16[1,272,128]{2,1,0:T(8,128)(2,1)S(1)}, u32[]{:S(2)}, u32[]{:S(2)}) collective-permute-start(bf16[1,272,128]{2,1,0:T(8,128)(2,1)S(1)} %bitcast.13), channel_id=1, source_target_pairs={{0,8},{1,9},{2,10},{3,11},{4,12},{5,13},{6,14},{7,15},{8,0},{9,1},... | collective-permute-start | bytes 208904 | tf_op jit(solution)/shard_map/ppermute | solution.py:336
  10.0 6.6 %collective-permute-start.2 = (bf16[2,272,128]{2,1,0:T(8,128)(2,1)S(1)}, bf16[2,272,128]{2,1,0:T(8,128)(2,1)S(1)}, u32[]{:S(2)}, u32[]{:S(2)}) collective-permute-start(bf16[2,272,128]{2,1,0:T(8,128)(2,1)S(1)} %pad_maximum_fusion.1.rest_1_), channel_id=1, source_target_pairs={{0,4},{1,3},{2,6},{3,1},{4,0},{5,7},{6,2},{7,5},{8,12},{9,11},{10,... | collective-permute-start | bytes 417800 | tf_op jit(solution)/shard_map/ppermute | solution.py:336
  10.9 5.7 %copy-start.2 = (s32[8]{0:T(128)S(1)}, s32[8]{0:T(128)}, u32[]{:S(2)}) copy-start(s32[8]{0:T(128)} %param.19) | copy-start | bytes 100
  10.9 5.9 %copy-start.1 = (bf16[4,4096]{1,0:T(4,128)(2,1)S(1)}, bf16[4,4096]{1,0:T(4,128)(2,1)}, u32[]{:S(2)}) copy-start(bf16[4,4096]{1,0:T(4,128)(2,1)} %param.10) | copy-start | bytes 98308
  10.9 6.0 %collective-permute-start.5 = (bf16[2,272,128]{2,1,0:T(8,128)(2,1)S(1)}, bf16[2,272,128]{2,1,0:T(8,128)(2,1)S(1)}, u32[]{:S(2)}, u32[]{:S(2)}) collective-permute-start(bf16[2,272,128]{2,1,0:T(8,128)(2,1)S(1)} %pad_maximum_fusion.1.rest_1_), channel_id=1, source_target_pairs={{0,2},{1,5},{2,0},{3,7},{4,6},{5,1},{6,4},{7,3},{8,10},{9,13},{10,... | collective-permute-start | bytes 417800 | tf_op jit(solution)/shard_map/ppermute | solution.py:336
  12.5 6.7 %collective-permute-start.1 = (bf16[2,272,128]{2,1,0:T(8,128)(2,1)S(1)}, bf16[2,272,128]{2,1,0:T(8,128)(2,1)S(1)}, u32[]{:S(2)}, u32[]{:S(2)}) collective-permute-start(bf16[2,272,128]{2,1,0:T(8,128)(2,1)S(1)} %pad_maximum_fusion.1.rest_1_), channel_id=1, source_target_pairs={{0,6},{1,7},{2,4},{3,5},{4,2},{5,3},{6,0},{7,1},{8,14},{9,15},{10,... | collective-permute-start | bytes 417800 | tf_op jit(solution)/shard_map/ppermute | solution.py:336
  16.7 2.4 %collective-permute-start.4 = (bf16[4,272,128]{2,1,0:T(8,128)(2,1)S(1)}, bf16[4,272,128]{2,1,0:T(8,128)(2,1)S(1)}, u32[]{:S(2)}, u32[]{:S(2)}) collective-permute-start(bf16[4,272,128]{2,1,0:T(8,128)(2,1)S(1)} %pad_maximum_fusion.slabs_ref), channel_id=1, source_target_pairs={{0,1},{1,0},{2,3},{3,2},{4,5},{5,4},{6,7},{7,6},{8,9},{9,8},{10,11... | collective-permute-start | bytes 835592 | tf_op jit(solution)/shard_map/ppermute | solution.py:395
  19.1 2.5 %collective-permute-start.6 = (bf16[4,272,128]{2,1,0:T(8,128)(2,1)S(1)}, bf16[4,272,128]{2,1,0:T(8,128)(2,1)S(1)}, u32[]{:S(2)}, u32[]{:S(2)}) collective-permute-start(bf16[4,272,128]{2,1,0:T(8,128)(2,1)S(1)} %constant_dynamic-update-slice_fusion.5.last_ref), channel_id=1, source_target_pairs={{0,1},{1,0},{2,3},{3,2},{4,5},{5,4},{6,7},{7,6},{8,9},{9,8},{10,11... | collective-permute-start | bytes 835592 | tf_op jit(solution)/shard_map/ppermute | solution.py:400

commit v24 on v23

--- a/solution.py
+++ b/solution.py
@@ -136,6 +136,29 @@
     )(*given, *([served] if fetch else []), *after)
 
 
+def base_kernel(features_ref, served_ref, after, base_ref):
+    del after
+    base_ref[...] = jnp.dot(
+        features_ref[...], served_ref[...], preferred_element_type=jnp.float32
+    )
+
+
+def base_value(features, served, after):
+    rows, depth = features.shape
+    cols = served.shape[1]
+    return pl.pallas_call(
+        base_kernel,
+        out_shape=jax.ShapeDtypeStruct((rows, cols), jnp.float32),
+        in_specs=[VMEM, VMEM, pl.BlockSpec(memory_space=pl.ANY)],
+        out_specs=VMEM,
+        compiler_params=pltpu.CompilerParams(vmem_limit_bytes=12 * 2**20),
+        cost_estimate=pl.CostEstimate(
+            flops=2 * rows * depth * cols, bytes_accessed=0, transcendentals=0
+        ),
+        name="base_value",
+    )(features, served, after)
+
+
 class Merge:
     def __init__(self, start_ref, merged, out_sem, width):
         self.start, self.merged, self.out_sem, self.width = start_ref[...], merged, out_sem, width
@@ -157,7 +180,10 @@
             block, up, (((0,), (0,)), ((), ())), preferred_element_type=jnp.float32
         )
         fold = (served_ref[rows, :].astype(jnp.float32) + update).astype(jnp.bfloat16)
-        part = jnp.dot(features_ref[:, rows], fold, preferred_element_type=jnp.float32)
+        part = lax.dot_general(
+            features_ref[:, rows], block, (((1,), (1,)), ((), ())),
+            preferred_element_type=jnp.float32,
+        )
         return fold, total + part
 
 
@@ -198,7 +224,7 @@
 
 
 def final_kernel(start_ref, up_ref, features_ref, served_ref, left_ref, last_ref, merged_in,
-                 total_ref, context_ref, own_weight_ref, merged, fresh_hbm, attended_hbm, m_buf,
+                 total_ref, context_ref, own_weight_ref, base_ref, merged, fresh_hbm, attended_hbm, m_buf,
                  out_sem, fresh_ref, attended_ref, small_sem):
     del merged_in
     count, width = last_ref.shape[0], m_buf.shape[1]
@@ -218,7 +244,12 @@
         m_buf[i] = fold
         stores.append(merge.store(m_buf.at[i], rows, i))
         stores[-1].start()
-    fresh = total.astype(jnp.bfloat16)
+    high = total.astype(jnp.bfloat16)
+    low = (total - high.astype(jnp.float32)).astype(jnp.bfloat16)
+    fresh = base_ref[...]
+    for part in (low, high):
+        fresh = fresh + jnp.dot(part, up_ref[...], preferred_element_type=jnp.float32)
+    fresh = fresh.astype(jnp.bfloat16)
     fresh_ref[...] = fresh
     put_fresh = pltpu.make_async_copy(fresh_ref, fresh_hbm, small_sem.at[0])
     put_fresh.start()
@@ -249,7 +280,7 @@
         functools.partial(merge_kernel, per, left),
         out_shape=(
             jax.ShapeDtypeStruct((depth, cols), jnp.bfloat16),
-            jax.ShapeDtypeStruct((features.shape[0], cols), jnp.float32),
+            jax.ShapeDtypeStruct((features.shape[0], rank), jnp.float32),
             jax.ShapeDtypeStruct((rank, cols), jnp.bfloat16),
             jax.ShapeDtypeStruct((left, width, cols), jnp.bfloat16),
         ),
@@ -269,17 +300,17 @@
     )(start, pick, features, served, slabs, crossed, last)
 
 
-def finish(start, up, features, served, left, last, merged, total, context, own_weight):
+def finish(start, up, features, served, left, last, merged, total, context, own_weight, base):
     count = last.shape[0]
     depth, cols = served.shape
     width = depth // start.shape[1]
-    smalls = [total.shape, context.shape]
+    smalls = [base.shape, context.shape]
     return pl.pallas_call(
         final_kernel,
         out_shape=[
             jax.ShapeDtypeStruct(shape, jnp.bfloat16) for shape in [(depth, cols), *smalls]
         ],
-        in_specs=[VMEM] * 6 + [HBM] + [VMEM] * 3,
+        in_specs=[VMEM] * 6 + [HBM] + [VMEM] * 4,
         out_specs=[HBM] * 3,
         input_output_aliases={6: 0},
         scratch_shapes=[
@@ -295,7 +326,7 @@
             transcendentals=0,
         ),
         name="finish_rows",
-    )(start, up, features, served, left, last, merged, total, context, own_weight)
+    )(start, up, features, served, left, last, merged, total, context, own_weight, base)
 
 
 def panels(x):
@@ -393,15 +424,17 @@
     )
     crossed, start = lax.optimization_barrier((slabs, start))
     crossed = lax.ppermute(crossed, "tensor", swap)
-    last, start, pick, context, own_weight, features, crossed = lax.optimization_barrier(
-        (last, start, pick, context, own_weight, features, crossed)
+    base = base_value(features, served, slabs)
+    last, start, pick, context, own_weight, features, crossed, base = lax.optimization_barrier(
+        (last, start, pick, context, own_weight, features, crossed, base)
     )
     last = jnp.concatenate([images, last], axis=0)
     last_crossed = lax.ppermute(last, "tensor", swap)
     merged, total, up, left = merge(per, start, pick, features, served, slabs, crossed, last)
     return tuple(
         finish(
-            start, up, features, served, left, last_crossed, merged, total, context, own_weight
+            start, up, features, served, left, last_crossed, merged, total, context, own_weight,
+            base,
         )
     )
 

time: 23.8 us -> 23 us (0.966)
  waiting for transfers between devices: 3.6 us -> 2.95 us
    pallas_call x0 -> x1, Pallas kernels: none -> 0.65 us  [base_value(): pl.pallas_call(base_kernel, out_shape=jax.ShapeDtypeStruct((rows, cols),...]
    ppermute x4, waiting for transfers between devices: 3.59 us -> 2.94 us  [exchange(): return lax.ppermute(x, ('replica', 'tensor'), pairs)]
    pallas_call x1, Pallas kernels: 1.93 us -> 1.49 us  [finish(): pl.pallas_call(final_kernel, out_shape=[jax.ShapeDtypeStruct(shape, jnp.b...]
    pallas_call x1, Pallas kernels: 2.39 us -> 1.99 us  [merge(): pl.pallas_call(functools.partial(merge_kernel, per, left), out_shape=(jax...]
  transfers between devices with their start and end apart: 7 -> 7, of which waited for: 2 -> 2; matrix products, arithmetic and copies ran while one was open for 5% -> 5% of each run, Pallas kernels for 34% -> 37%
where the time goes in v24:
time: 23 us; the launch traced here: 22.7 us
  Pallas kernels  9.83 us (43%)
  starting transfers between devices  7.99 us (35%)
  waiting for transfers between devices  2.95 us (13%)
  local copies, waits for them, and re-layouts  0.83 us (4%)
  between operations  0.81 us (4%)
  other arithmetic  0.3 us (1%)
    ppermute x4, starting transfers between devices, exchange(): return lax.ppermute(x, ('replica', 'tensor'), pairs)  7.33 us
    pallas_call x2, Pallas kernels, attend(): pl.pallas_call(functools.partial(attend_kernel, rows, fetch), out_shape=o...  5.7 us
    ppermute x4, waiting for transfers between devices, exchange(): return lax.ppermute(x, ('replica', 'tensor'), pairs)  2.94 us
    pallas_call x1, Pallas kernels, merge(): pl.pallas_call(functools.partial(merge_kernel, per, left), out_shape=(jax...  1.99 us
    pallas_call x1, Pallas kernels, finish(): pl.pallas_call(final_kernel, out_shape=[jax.ShapeDtypeStruct(shape, jnp.b...  1.49 us
    slice x1, local copies, waits for them, and re-layouts, panels(): return [x[:, i:i + PANEL] for i in range(0, x.shape[1], PANEL)]  0.7 us
    pallas_call x1, Pallas kernels, base_value(): pl.pallas_call(base_kernel, out_shape=jax.ShapeDtypeStruct((rows, cols),...  0.65 us
    ppermute x1, starting transfers between devices, body(): hid_other = lax.ppermute(hidden_in, 'tensor', swap)  0.52 us
  transfers between devices with their start and end apart: 7, of which 2 were waited for; matrix products, arithmetic and copies ran while one was open for 5% of the time, Pallas kernels for 37%

profile of v24, /device:TPU:0, one launch (start us, length us, event | category | flops | bytes accessed | tf_op | source)
XLA Modules:
  0.0 22.7 jit_solution(9350344655042869934)
XLA Ops:
  0.6 0.0 copy-start
  0.6 0.5 %collective-permute-start.3 = (bf16[4,4096]{1,0:T(4,128)(2,1)}, bf16[4,4096]{1,0:T(4,128)(2,1)S(1)}, u32[]{:S(2)}, u32[]{:S(2)}) collective-permute-start(bf16[4,4096]{1,0:T(4,128)(2,1)} %param.10), channel_id=1, source_target_pairs={{0,1},{1,0},{2,3},{3,2},{4,5},{5,4},{6,7},{7,6},{8,9},{9,8},{10,11... | collective-permute-start | bytes 98312 | tf_op jit(solution)/shard_map/ppermute | solution.py:381
  1.2 0.7 %fusion.1 = (bf16[8,128]{1,0:T(8,128)(2,1)S(1)}, bf16[8,128]{1,0:T(8,128)(2,1)S(1)}) fusion(bf16[8,256]{1,0:T(8,128)(2,1)} %param.18), kind=kLoop, calls=%fused_computation.34 | loop fusion | bytes 8192 | tf_op jit(solution)/shard_map/slice | solution.py:333
  1.9 0.0 copy-done
  1.9 3.8 %collective-permute-start = (bf16[1,272,128]{2,1,0:T(8,128)(2,1)S(1)}, bf16[1,272,128]{2,1,0:T(8,128)(2,1)S(1)}, u32[]{:S(2)}, u32[]{:S(2)}) collective-permute-start(bf16[1,272,128]{2,1,0:T(8,128)(2,1)S(1)} %bitcast.13), channel_id=1, source_target_pairs={{0,8},{1,9},{2,10},{3,11},{4,12},{5,13},{6,14},{7,15},{8,0},{9,1},... | collective-permute-start | bytes 208904 | tf_op jit(solution)/shard_map/ppermute | solution.py:367
  5.7 2.8 %attend_cache.2 = (f32[2,16,128]{2,1,0:T(8,128)S(1)}, f32[2,16,128]{2,1,0:T(8,128)S(1)}) custom-call(s32[4]{0:T(128)} %lengths_hbm.3, bf16[4,2048]{1,0:T(4,128)(2,1)} %q_hbm.3, bf16[4,256]{1,0:T(4,128)(2,1)} %own_k_hbm.3, bf16[4,1024,256]{2,1,0:T(8,128)(2,1)} %k_hbm.3, bf16[4,1024,256]{2,1,0:T(8,128)(2,1)} %v_hbm.3, bf16[1,272,128]{2,1,0:T(8,128)(2,1)S(1)} %bitcast.14), custom_call_target="tpu_custom_call" | custom-call | flops 33554432 | bytes 2097152 | tf_op jit(solution)/shard_map/attend_cache/pallas_call | solution.py:113
  8.5 1.4 %collective-permute-done = bf16[1,272,128]{2,1,0:T(8,128)(2,1)S(1)} collective-permute-done((bf16[1,272,128]{2,1,0:T(8,128)(2,1)S(1)}, bf16[1,272,128]{2,1,0:T(8,128)(2,1)S(1)}, u32[]{:S(2)}, u32[]{:S(2)}) %collective-permute-start) | collective-permute-done | bytes 69664 | tf_op jit(solution)/shard_map/ppermute | solution.py:367
  10.0 0.8 %collective-permute-start.2 = (bf16[2,272,128]{2,1,0:T(8,128)(2,1)S(1)}, bf16[2,272,128]{2,1,0:T(8,128)(2,1)S(1)}, u32[]{:S(2)}, u32[]{:S(2)}) collective-permute-start(bf16[2,272,128]{2,1,0:T(8,128)(2,1)S(1)} %pad_maximum_fusion.1.rest_1_), channel_id=1, source_target_pairs={{0,4},{1,3},{2,6},{3,1},{4,0},{5,7},{6,2},{7,5},{8,12},{9,11},{10,... | collective-permute-start | bytes 417800 | tf_op jit(solution)/shard_map/ppermute | solution.py:367
  10.8 0.1 pad_add_fusion
  10.9 1.6 %collective-permute-start.5 = (bf16[2,272,128]{2,1,0:T(8,128)(2,1)S(1)}, bf16[2,272,128]{2,1,0:T(8,128)(2,1)S(1)}, u32[]{:S(2)}, u32[]{:S(2)}) collective-permute-start(bf16[2,272,128]{2,1,0:T(8,128)(2,1)S(1)} %pad_maximum_fusion.1.rest_1_), channel_id=1, source_target_pairs={{0,2},{1,5},{2,0},{3,7},{4,6},{5,1},{6,4},{7,3},{8,10},{9,13},{10,... | collective-permute-start | bytes 417800 | tf_op jit(solution)/shard_map/ppermute | solution.py:367
  12.5 1.2 %collective-permute-start.1 = (bf16[2,272,128]{2,1,0:T(8,128)(2,1)S(1)}, bf16[2,272,128]{2,1,0:T(8,128)(2,1)S(1)}, u32[]{:S(2)}, u32[]{:S(2)}) collective-permute-start(bf16[2,272,128]{2,1,0:T(8,128)(2,1)S(1)} %pad_maximum_fusion.1.rest_1_), channel_id=1, source_target_pairs={{0,6},{1,7},{2,4},{3,5},{4,2},{5,3},{6,0},{7,1},{8,14},{9,15},{10,... | collective-permute-start | bytes 417800 | tf_op jit(solution)/shard_map/ppermute | solution.py:367
  13.6 2.9 %attend_cache.3 = (f32[2,16,128]{2,1,0:T(8,128)S(1)}, f32[2,16,128]{2,1,0:T(8,128)S(1)}, bf16[8192,256]{1,0:T(8,128)(2,1)S(1)}) custom-call(s32[4]{0:T(128)} %lengths_hbm.3, bf16[4,2048]{1,0:T(4,128)(2,1)} %q_hbm.3, bf16[4,256]{1,0:T(4,128)(2,1)} %own_k_hbm.3, bf16[4,1024,256]{2,1,0:T(8,128)(2,1)} %k_hbm.3, bf16[4,1024,256]{2,1,0:T(8,128)(2,1)} %v_hbm.3, ...), custom_call_target="tpu_custom_call" | custom-call | flops 33554432 | bytes 2097152 | tf_op jit(solution)/shard_map/attend_cache/pallas_call | solution.py:113
  16.6 0.0 collective-permute-done.3
  16.6 0.0 collective-permute-done.2
  16.6 0.1 select_reduce_fusion
  16.7 0.1 collective-permute-start.4
  16.9 0.7 %base_value.1.base_ref = f32[4,256]{1,0:T(4,128)S(1)} custom-call(bf16[4,8192]{1,0:T(4,128)(2,1)S(1)} %maximum_select_fusion.features_ref, bf16[8192,256]{1,0:T(8,128)(2,1)S(1)} %get-tuple-element.48.served_ref, bf16[4,272,128]{2,1,0:T(8,128)(2,1)S(1)} %pad_maximum_fusion.after.slabs_ref), custom_call_target="tpu_custom_call" | custom-call | flops 16777216 | tf_op jit(solution)/shard_map/base_value/pallas_call | solution.py:149
  17.6 0.0 collective-permute-done.5
  17.6 1.5 %collective-permute-done.1 = bf16[2,272,128]{2,1,0:T(8,128)(2,1)S(1)} collective-permute-done((bf16[2,272,128]{2,1,0:T(8,128)(2,1)S(1)}, bf16[2,272,128]{2,1,0:T(8,128)(2,1)S(1)}, u32[]{:S(2)}, u32[]{:S(2)}) %collective-permute-start.1) | collective-permute-done | bytes 139296 | tf_op jit(solution)/shard_map/ppermute | solution.py:367
  19.1 0.0 collective-permute-done.4.crossed_ref
  19.1 0.1 collective-permute-start.6
  19.2 2.0 %merge_blocks.1 = (bf16[8192,256]{1,0:T(8,128)(2,1)}, f32[4,64]{1,0:T(4,128)S(1)}, bf16[64,256]{1,0:T(8,128)(2,1)S(1)}, bf16[3,512,256]{2,1,0:T(8,128)(2,1)S(1)}) custom-call(s32[1,16]{1,0:T(1,128)S(1)} %add_bitcast_fusion.start_ref, bf16[64,64]{1,0:T(8,128)(2,1)S(1)} %select_convert_fusion.pick_ref, bf16[4,8192]{1,0:T(4,128)(2,1)S(1)} %maximum_select_fusion.features_ref, ...), custom_call_target="tpu_custom_call" | custom-call | flops 201326592 | bytes 6291456 | tf_op jit(solution)/shard_map/merge_blocks/pallas_call | solution.py:279
  21.2 0.0 collective-permute-done.6.last_ref
  21.2 1.5 %finish_rows.1 = (bf16[8192,256]{1,0:T(8,128)(2,1)}, bf16[4,256]{1,0:T(4,128)(2,1)}, bf16[4,2048]{1,0:T(4,128)(2,1)}) custom-call(s32[1,16]{1,0:T(1,128)S(1)} %add_bitcast_fusion.start_ref, bf16[64,256]{1,0:T(8,128)(2,1)S(1)} %get-tuple-element.54.up_ref, bf16[4,8192]{1,0:T(4,128)(2,1)S(1)} %maximum_select_fusion.features_ref, ...), custom_call_target="tpu_custom_call", output_to_operand_aliasing={{0}: (6, {})} | custom-call | flops 67108864 | bytes 2097152 | tf_op jit(solution)/shard_map/finish_rows/pallas_call | solution.py:308
  (24 shorter events, 0.3 us)
Async XLA Ops:
  0.6 1.2 %copy-start = (bf16[64,1024]{1,0:T(8,128)(2,1)S(1)}, bf16[64,1024]{1,0:T(8,128)(2,1)}, u32[]{:S(2)}) copy-start(bf16[64,1024]{1,0:T(8,128)(2,1)} %param.17) | copy-start | bytes 393220
  0.6 15.9 %collective-permute-start.3 = (bf16[4,4096]{1,0:T(4,128)(2,1)}, bf16[4,4096]{1,0:T(4,128)(2,1)S(1)}, u32[]{:S(2)}, u32[]{:S(2)}) collective-permute-start(bf16[4,4096]{1,0:T(4,128)(2,1)} %param.10), channel_id=1, source_target_pairs={{0,1},{1,0},{2,3},{3,2},{4,5},{5,4},{6,7},{7,6},{8,9},{9,8},{10,11... | collective-permute-start | bytes 98312 | tf_op jit(solution)/shard_map/ppermute | solution.py:381
  1.9 8.0 %collective-permute-start = (bf16[1,272,128]{2,1,0:T(8,128)(2,1)S(1)}, bf16[1,272,128]{2,1,0:T(8,128)(2,1)S(1)}, u32[]{:S(2)}, u32[]{:S(2)}) collective-permute-start(bf16[1,272,128]{2,1,0:T(8,128)(2,1)S(1)} %bitcast.13), channel_id=1, source_target_pairs={{0,8},{1,9},{2,10},{3,11},{4,12},{5,13},{6,14},{7,15},{8,0},{9,1},... | collective-permute-start | bytes 208904 | tf_op jit(solution)/shard_map/ppermute | solution.py:367
  10.0 6.6 %collective-permute-start.2 = (bf16[2,272,128]{2,1,0:T(8,128)(2,1)S(1)}, bf16[2,272,128]{2,1,0:T(8,128)(2,1)S(1)}, u32[]{:S(2)}, u32[]{:S(2)}) collective-permute-start(bf16[2,272,128]{2,1,0:T(8,128)(2,1)S(1)} %pad_maximum_fusion.1.rest_1_), channel_id=1, source_target_pairs={{0,4},{1,3},{2,6},{3,1},{4,0},{5,7},{6,2},{7,5},{8,12},{9,11},{10,... | collective-permute-start | bytes 417800 | tf_op jit(solution)/shard_map/ppermute | solution.py:367
  10.9 5.7 %copy-start.2 = (s32[8]{0:T(128)S(1)}, s32[8]{0:T(128)}, u32[]{:S(2)}) copy-start(s32[8]{0:T(128)} %param.19) | copy-start | bytes 100
  10.9 5.9 %copy-start.1 = (bf16[4,4096]{1,0:T(4,128)(2,1)S(1)}, bf16[4,4096]{1,0:T(4,128)(2,1)}, u32[]{:S(2)}) copy-start(bf16[4,4096]{1,0:T(4,128)(2,1)} %param.10) | copy-start | bytes 98308
  10.9 6.7 %collective-permute-start.5 = (bf16[2,272,128]{2,1,0:T(8,128)(2,1)S(1)}, bf16[2,272,128]{2,1,0:T(8,128)(2,1)S(1)}, u32[]{:S(2)}, u32[]{:S(2)}) collective-permute-start(bf16[2,272,128]{2,1,0:T(8,128)(2,1)S(1)} %pad_maximum_fusion.1.rest_1_), channel_id=1, source_target_pairs={{0,2},{1,5},{2,0},{3,7},{4,6},{5,1},{6,4},{7,3},{8,10},{9,13},{10,... | collective-permute-start | bytes 417800 | tf_op jit(solution)/shard_map/ppermute | solution.py:367
  12.5 6.7 %collective-permute-start.1 = (bf16[2,272,128]{2,1,0:T(8,128)(2,1)S(1)}, bf16[2,272,128]{2,1,0:T(8,128)(2,1)S(1)}, u32[]{:S(2)}, u32[]{:S(2)}) collective-permute-start(bf16[2,272,128]{2,1,0:T(8,128)(2,1)S(1)} %pad_maximum_fusion.1.rest_1_), channel_id=1, source_target_pairs={{0,6},{1,7},{2,4},{3,5},{4,2},{5,3},{6,0},{7,1},{8,14},{9,15},{10,... | collective-permute-start | bytes 417800 | tf_op jit(solution)/shard_map/ppermute | solution.py:367
  16.7 2.4 %collective-permute-start.4 = (bf16[4,272,128]{2,1,0:T(8,128)(2,1)S(1)}, bf16[4,272,128]{2,1,0:T(8,128)(2,1)S(1)}, u32[]{:S(2)}, u32[]{:S(2)}) collective-permute-start(bf16[4,272,128]{2,1,0:T(8,128)(2,1)S(1)} %pad_maximum_fusion.after.slabs_ref), channel_id=1, source_target_pairs={{0,1},{1,0},{2,3},{3,2},{4,5},{5,4},{6,7},{7,6},{8,9},{9,8},{10,11... | collective-permute-start | bytes 835592 | tf_op jit(solution)/shard_map/ppermute | solution.py:426
  19.1 2.1 %collective-permute-start.6 = (bf16[4,272,128]{2,1,0:T(8,128)(2,1)S(1)}, bf16[4,272,128]{2,1,0:T(8,128)(2,1)S(1)}, u32[]{:S(2)}, u32[]{:S(2)}) collective-permute-start(bf16[4,272,128]{2,1,0:T(8,128)(2,1)S(1)} %constant_dynamic-update-slice_fusion.5.last_ref), channel_id=1, source_target_pairs={{0,1},{1,0},{2,3},{3,2},{4,5},{5,4},{6,7},{7,6},{8,9},{9,8},{10,11... | collective-permute-start | bytes 835592 | tf_op jit(solution)/shard_map/ppermute | solution.py:432

commit v25 on v24

--- a/solution.py
+++ b/solution.py
@@ -271,7 +271,7 @@
 
 
 def merge(per, start, pick, features, served, slabs, crossed, last):
-    left = 3
+    left = 1
     count = slabs.shape[0] + crossed.shape[0] + last.shape[0]
     rank = pick.shape[0]
     depth, cols = served.shape

time: 23 us -> 23.2 us (level)
    pallas_call x1, Pallas kernels: 1.99 us -> 2.23 us  [merge(): pl.pallas_call(functools.partial(merge_kernel, per, left), out_shape=(jax...]
where the time goes in v25:
time: 23.2 us; the launch traced here: 22.9 us
  Pallas kernels  10 us (43%)
  starting transfers between devices  7.99 us (34%)
  waiting for transfers between devices  2.95 us (13%)
  local copies, waits for them, and re-layouts  0.83 us (4%)
  between operations  0.81 us (3%)
  other arithmetic  0.3 us (1%)
    ppermute x4, starting transfers between devices, exchange(): return lax.ppermute(x, ('replica', 'tensor'), pairs)  7.33 us
    pallas_call x2, Pallas kernels, attend(): pl.pallas_call(functools.partial(attend_kernel, rows, fetch), out_shape=o...  5.7 us
    ppermute x4, waiting for transfers between devices, exchange(): return lax.ppermute(x, ('replica', 'tensor'), pairs)  2.94 us
    pallas_call x1, Pallas kernels, merge(): pl.pallas_call(functools.partial(merge_kernel, per, left), out_shape=(jax...  2.23 us
    pallas_call x1, Pallas kernels, finish(): pl.pallas_call(final_kernel, out_shape=[jax.ShapeDtypeStruct(shape, jnp.b...  1.47 us
    slice x1, local copies, waits for them, and re-layouts, panels(): return [x[:, i:i + PANEL] for i in range(0, x.shape[1], PANEL)]  0.7 us
    pallas_call x1, Pallas kernels, base_value(): pl.pallas_call(base_kernel, out_shape=jax.ShapeDtypeStruct((rows, cols),...  0.65 us
    ppermute x1, starting transfers between devices, body(): hid_other = lax.ppermute(hidden_in, 'tensor', swap)  0.52 us
  transfers between devices with their start and end apart: 7, of which 2 were waited for; matrix products, arithmetic and copies ran while one was open for 5% of the time, Pallas kernels for 37%

profile of v25, /device:TPU:0, one launch (start us, length us, event | category | flops | bytes accessed | tf_op | source)
XLA Modules:
  0.0 22.9 jit_solution(9274711591384087433)
XLA Ops:
  0.6 0.0 copy-start
  0.6 0.5 %collective-permute-start.3 = (bf16[4,4096]{1,0:T(4,128)(2,1)}, bf16[4,4096]{1,0:T(4,128)(2,1)S(1)}, u32[]{:S(2)}, u32[]{:S(2)}) collective-permute-start(bf16[4,4096]{1,0:T(4,128)(2,1)} %param.10), channel_id=1, source_target_pairs={{0,1},{1,0},{2,3},{3,2},{4,5},{5,4},{6,7},{7,6},{8,9},{9,8},{10,11... | collective-permute-start | bytes 98312 | tf_op jit(solution)/shard_map/ppermute | solution.py:381
  1.2 0.7 %fusion.1 = (bf16[8,128]{1,0:T(8,128)(2,1)S(1)}, bf16[8,128]{1,0:T(8,128)(2,1)S(1)}) fusion(bf16[8,256]{1,0:T(8,128)(2,1)} %param.18), kind=kLoop, calls=%fused_computation.34 | loop fusion | bytes 8192 | tf_op jit(solution)/shard_map/slice | solution.py:333
  1.9 0.0 copy-done
  1.9 3.8 %collective-permute-start = (bf16[1,272,128]{2,1,0:T(8,128)(2,1)S(1)}, bf16[1,272,128]{2,1,0:T(8,128)(2,1)S(1)}, u32[]{:S(2)}, u32[]{:S(2)}) collective-permute-start(bf16[1,272,128]{2,1,0:T(8,128)(2,1)S(1)} %bitcast.13), channel_id=1, source_target_pairs={{0,8},{1,9},{2,10},{3,11},{4,12},{5,13},{6,14},{7,15},{8,0},{9,1},... | collective-permute-start | bytes 208904 | tf_op jit(solution)/shard_map/ppermute | solution.py:367
  5.7 2.8 %attend_cache.2 = (f32[2,16,128]{2,1,0:T(8,128)S(1)}, f32[2,16,128]{2,1,0:T(8,128)S(1)}) custom-call(s32[4]{0:T(128)} %lengths_hbm.3, bf16[4,2048]{1,0:T(4,128)(2,1)} %q_hbm.3, bf16[4,256]{1,0:T(4,128)(2,1)} %own_k_hbm.3, bf16[4,1024,256]{2,1,0:T(8,128)(2,1)} %k_hbm.3, bf16[4,1024,256]{2,1,0:T(8,128)(2,1)} %v_hbm.3, bf16[1,272,128]{2,1,0:T(8,128)(2,1)S(1)} %bitcast.14), custom_call_target="tpu_custom_call" | custom-call | flops 33554432 | bytes 2097152 | tf_op jit(solution)/shard_map/attend_cache/pallas_call | solution.py:113
  8.5 1.4 %collective-permute-done = bf16[1,272,128]{2,1,0:T(8,128)(2,1)S(1)} collective-permute-done((bf16[1,272,128]{2,1,0:T(8,128)(2,1)S(1)}, bf16[1,272,128]{2,1,0:T(8,128)(2,1)S(1)}, u32[]{:S(2)}, u32[]{:S(2)}) %collective-permute-start) | collective-permute-done | bytes 69664 | tf_op jit(solution)/shard_map/ppermute | solution.py:367
  10.0 0.8 %collective-permute-start.2 = (bf16[2,272,128]{2,1,0:T(8,128)(2,1)S(1)}, bf16[2,272,128]{2,1,0:T(8,128)(2,1)S(1)}, u32[]{:S(2)}, u32[]{:S(2)}) collective-permute-start(bf16[2,272,128]{2,1,0:T(8,128)(2,1)S(1)} %pad_maximum_fusion.1.rest_1_), channel_id=1, source_target_pairs={{0,4},{1,3},{2,6},{3,1},{4,0},{5,7},{6,2},{7,5},{8,12},{9,11},{10,... | collective-permute-start | bytes 417800 | tf_op jit(solution)/shard_map/ppermute | solution.py:367
  10.8 0.1 pad_add_fusion
  10.9 1.6 %collective-permute-start.5 = (bf16[2,272,128]{2,1,0:T(8,128)(2,1)S(1)}, bf16[2,272,128]{2,1,0:T(8,128)(2,1)S(1)}, u32[]{:S(2)}, u32[]{:S(2)}) collective-permute-start(bf16[2,272,128]{2,1,0:T(8,128)(2,1)S(1)} %pad_maximum_fusion.1.rest_1_), channel_id=1, source_target_pairs={{0,2},{1,5},{2,0},{3,7},{4,6},{5,1},{6,4},{7,3},{8,10},{9,13},{10,... | collective-permute-start | bytes 417800 | tf_op jit(solution)/shard_map/ppermute | solution.py:367
  12.5 1.2 %collective-permute-start.1 = (bf16[2,272,128]{2,1,0:T(8,128)(2,1)S(1)}, bf16[2,272,128]{2,1,0:T(8,128)(2,1)S(1)}, u32[]{:S(2)}, u32[]{:S(2)}) collective-permute-start(bf16[2,272,128]{2,1,0:T(8,128)(2,1)S(1)} %pad_maximum_fusion.1.rest_1_), channel_id=1, source_target_pairs={{0,6},{1,7},{2,4},{3,5},{4,2},{5,3},{6,0},{7,1},{8,14},{9,15},{10,... | collective-permute-start | bytes 417800 | tf_op jit(solution)/shard_map/ppermute | solution.py:367
  13.6 2.9 %attend_cache.3 = (f32[2,16,128]{2,1,0:T(8,128)S(1)}, f32[2,16,128]{2,1,0:T(8,128)S(1)}, bf16[8192,256]{1,0:T(8,128)(2,1)S(1)}) custom-call(s32[4]{0:T(128)} %lengths_hbm.3, bf16[4,2048]{1,0:T(4,128)(2,1)} %q_hbm.3, bf16[4,256]{1,0:T(4,128)(2,1)} %own_k_hbm.3, bf16[4,1024,256]{2,1,0:T(8,128)(2,1)} %k_hbm.3, bf16[4,1024,256]{2,1,0:T(8,128)(2,1)} %v_hbm.3, ...), custom_call_target="tpu_custom_call" | custom-call | flops 33554432 | bytes 2097152 | tf_op jit(solution)/shard_map/attend_cache/pallas_call | solution.py:113
  16.6 0.0 collective-permute-done.3
  16.6 0.0 collective-permute-done.2
  16.6 0.1 select_reduce_fusion
  16.7 0.1 collective-permute-start.4
  16.9 0.7 %base_value.1.base_ref = f32[4,256]{1,0:T(4,128)S(1)} custom-call(bf16[4,8192]{1,0:T(4,128)(2,1)S(1)} %maximum_select_fusion.features_ref, bf16[8192,256]{1,0:T(8,128)(2,1)S(1)} %get-tuple-element.48.served_ref, bf16[4,272,128]{2,1,0:T(8,128)(2,1)S(1)} %pad_maximum_fusion.after.slabs_ref), custom_call_target="tpu_custom_call" | custom-call | flops 16777216 | tf_op jit(solution)/shard_map/base_value/pallas_call | solution.py:149
  17.6 0.0 collective-permute-done.5
  17.6 1.5 %collective-permute-done.1 = bf16[2,272,128]{2,1,0:T(8,128)(2,1)S(1)} collective-permute-done((bf16[2,272,128]{2,1,0:T(8,128)(2,1)S(1)}, bf16[2,272,128]{2,1,0:T(8,128)(2,1)S(1)}, u32[]{:S(2)}, u32[]{:S(2)}) %collective-permute-start.1) | collective-permute-done | bytes 139296 | tf_op jit(solution)/shard_map/ppermute | solution.py:367
  19.1 0.0 collective-permute-done.4.crossed_ref
  19.1 0.1 collective-permute-start.6
  19.2 2.2 %merge_blocks.1 = (bf16[8192,256]{1,0:T(8,128)(2,1)}, f32[4,64]{1,0:T(4,128)S(1)}, bf16[64,256]{1,0:T(8,128)(2,1)S(1)}, bf16[1,512,256]{2,1,0:T(8,128)(2,1)S(1)}) custom-call(s32[1,16]{1,0:T(1,128)S(1)} %add_bitcast_fusion.start_ref, bf16[64,64]{1,0:T(8,128)(2,1)S(1)} %select_convert_fusion.pick_ref, bf16[4,8192]{1,0:T(4,128)(2,1)S(1)} %maximum_select_fusion.features_ref, ...), custom_call_target="tpu_custom_call" | custom-call | flops 201326592 | bytes 6291456 | tf_op jit(solution)/shard_map/merge_blocks/pallas_call | solution.py:279
  21.4 0.0 collective-permute-done.6.last_ref
  21.5 1.5 %finish_rows.1 = (bf16[8192,256]{1,0:T(8,128)(2,1)}, bf16[4,256]{1,0:T(4,128)(2,1)}, bf16[4,2048]{1,0:T(4,128)(2,1)}) custom-call(s32[1,16]{1,0:T(1,128)S(1)} %add_bitcast_fusion.start_ref, bf16[64,256]{1,0:T(8,128)(2,1)S(1)} %get-tuple-element.54.up_ref, bf16[4,8192]{1,0:T(4,128)(2,1)S(1)} %maximum_select_fusion.features_ref, ...), custom_call_target="tpu_custom_call", output_to_operand_aliasing={{0}: (6, {})} | custom-call | flops 67108864 | bytes 2097152 | tf_op jit(solution)/shard_map/finish_rows/pallas_call | solution.py:308
  (24 shorter events, 0.3 us)
Async XLA Ops:
  0.6 1.2 %copy-start = (bf16[64,1024]{1,0:T(8,128)(2,1)S(1)}, bf16[64,1024]{1,0:T(8,128)(2,1)}, u32[]{:S(2)}) copy-start(bf16[64,1024]{1,0:T(8,128)(2,1)} %param.17) | copy-start | bytes 393220
  0.6 15.9 %collective-permute-start.3 = (bf16[4,4096]{1,0:T(4,128)(2,1)}, bf16[4,4096]{1,0:T(4,128)(2,1)S(1)}, u32[]{:S(2)}, u32[]{:S(2)}) collective-permute-start(bf16[4,4096]{1,0:T(4,128)(2,1)} %param.10), channel_id=1, source_target_pairs={{0,1},{1,0},{2,3},{3,2},{4,5},{5,4},{6,7},{7,6},{8,9},{9,8},{10,11... | collective-permute-start | bytes 98312 | tf_op jit(solution)/shard_map/ppermute | solution.py:381
  1.9 8.0 %collective-permute-start = (bf16[1,272,128]{2,1,0:T(8,128)(2,1)S(1)}, bf16[1,272,128]{2,1,0:T(8,128)(2,1)S(1)}, u32[]{:S(2)}, u32[]{:S(2)}) collective-permute-start(bf16[1,272,128]{2,1,0:T(8,128)(2,1)S(1)} %bitcast.13), channel_id=1, source_target_pairs={{0,8},{1,9},{2,10},{3,11},{4,12},{5,13},{6,14},{7,15},{8,0},{9,1},... | collective-permute-start | bytes 208904 | tf_op jit(solution)/shard_map/ppermute | solution.py:367
  10.0 6.6 %collective-permute-start.2 = (bf16[2,272,128]{2,1,0:T(8,128)(2,1)S(1)}, bf16[2,272,128]{2,1,0:T(8,128)(2,1)S(1)}, u32[]{:S(2)}, u32[]{:S(2)}) collective-permute-start(bf16[2,272,128]{2,1,0:T(8,128)(2,1)S(1)} %pad_maximum_fusion.1.rest_1_), channel_id=1, source_target_pairs={{0,4},{1,3},{2,6},{3,1},{4,0},{5,7},{6,2},{7,5},{8,12},{9,11},{10,... | collective-permute-start | bytes 417800 | tf_op jit(solution)/shard_map/ppermute | solution.py:367
  10.9 5.7 %copy-start.2 = (s32[8]{0:T(128)S(1)}, s32[8]{0:T(128)}, u32[]{:S(2)}) copy-start(s32[8]{0:T(128)} %param.19) | copy-start | bytes 100
  10.9 5.9 %copy-start.1 = (bf16[4,4096]{1,0:T(4,128)(2,1)S(1)}, bf16[4,4096]{1,0:T(4,128)(2,1)}, u32[]{:S(2)}) copy-start(bf16[4,4096]{1,0:T(4,128)(2,1)} %param.10) | copy-start | bytes 98308
  10.9 6.7 %collective-permute-start.5 = (bf16[2,272,128]{2,1,0:T(8,128)(2,1)S(1)}, bf16[2,272,128]{2,1,0:T(8,128)(2,1)S(1)}, u32[]{:S(2)}, u32[]{:S(2)}) collective-permute-start(bf16[2,272,128]{2,1,0:T(8,128)(2,1)S(1)} %pad_maximum_fusion.1.rest_1_), channel_id=1, source_target_pairs={{0,2},{1,5},{2,0},{3,7},{4,6},{5,1},{6,4},{7,3},{8,10},{9,13},{10,... | collective-permute-start | bytes 417800 | tf_op jit(solution)/shard_map/ppermute | solution.py:367
  12.5 6.7 %collective-permute-start.1 = (bf16[2,272,128]{2,1,0:T(8,128)(2,1)S(1)}, bf16[2,272,128]{2,1,0:T(8,128)(2,1)S(1)}, u32[]{:S(2)}, u32[]{:S(2)}) collective-permute-start(bf16[2,272,128]{2,1,0:T(8,128)(2,1)S(1)} %pad_maximum_fusion.1.rest_1_), channel_id=1, source_target_pairs={{0,6},{1,7},{2,4},{3,5},{4,2},{5,3},{6,0},{7,1},{8,14},{9,15},{10,... | collective-permute-start | bytes 417800 | tf_op jit(solution)/shard_map/ppermute | solution.py:367
  16.7 2.4 %collective-permute-start.4 = (bf16[4,272,128]{2,1,0:T(8,128)(2,1)S(1)}, bf16[4,272,128]{2,1,0:T(8,128)(2,1)S(1)}, u32[]{:S(2)}, u32[]{:S(2)}) collective-permute-start(bf16[4,272,128]{2,1,0:T(8,128)(2,1)S(1)} %pad_maximum_fusion.after.slabs_ref), channel_id=1, source_target_pairs={{0,1},{1,0},{2,3},{3,2},{4,5},{5,4},{6,7},{7,6},{8,9},{9,8},{10,11... | collective-permute-start | bytes 835592 | tf_op jit(solution)/shard_map/ppermute | solution.py:426
  19.1 2.3 %collective-permute-start.6 = (bf16[4,272,128]{2,1,0:T(8,128)(2,1)S(1)}, bf16[4,272,128]{2,1,0:T(8,128)(2,1)S(1)}, u32[]{:S(2)}, u32[]{:S(2)}) collective-permute-start(bf16[4,272,128]{2,1,0:T(8,128)(2,1)S(1)} %constant_dynamic-update-slice_fusion.5.last_ref), channel_id=1, source_target_pairs={{0,1},{1,0},{2,3},{3,2},{4,5},{5,4},{6,7},{7,6},{8,9},{9,8},{10,11... | collective-permute-start | bytes 835592 | tf_op jit(solution)/shard_map/ppermute | solution.py:432

commit v26 on v25

--- a/solution.py
+++ b/solution.py
@@ -271,7 +271,7 @@
 
 
 def merge(per, start, pick, features, served, slabs, crossed, last):
-    left = 1
+    left = 6
     count = slabs.shape[0] + crossed.shape[0] + last.shape[0]
     rank = pick.shape[0]
     depth, cols = served.shape

time: 23.2 us -> 22.9 us (0.987)
    pallas_call x1, Pallas kernels: 2.23 us -> 1.71 us  [merge(): pl.pallas_call(functools.partial(merge_kernel, per, left), out_shape=(jax...]
    pallas_call x1, Pallas kernels: 1.47 us -> 1.72 us  [finish(): pl.pallas_call(final_kernel, out_shape=[jax.ShapeDtypeStruct(shape, jnp.b...]
  transfers between devices with their start and end apart: 7 -> 7, of which waited for: 2 -> 2; matrix products, arithmetic and copies ran while one was open for 5% -> 5% of each run, Pallas kernels for 37% -> 36%
where the time goes in v26:
time: 22.9 us; the launch traced here: 22.7 us
  Pallas kernels  9.78 us (43%)
  starting transfers between devices  7.99 us (35%)
  waiting for transfers between devices  2.95 us (13%)
  local copies, waits for them, and re-layouts  0.83 us (4%)
  between operations  0.81 us (4%)
  other arithmetic  0.3 us (1%)
    ppermute x4, starting transfers between devices, exchange(): return lax.ppermute(x, ('replica', 'tensor'), pairs)  7.33 us
    pallas_call x2, Pallas kernels, attend(): pl.pallas_call(functools.partial(attend_kernel, rows, fetch), out_shape=o...  5.7 us
    ppermute x4, waiting for transfers between devices, exchange(): return lax.ppermute(x, ('replica', 'tensor'), pairs)  2.94 us
    pallas_call x1, Pallas kernels, finish(): pl.pallas_call(final_kernel, out_shape=[jax.ShapeDtypeStruct(shape, jnp.b...  1.72 us
    pallas_call x1, Pallas kernels, merge(): pl.pallas_call(functools.partial(merge_kernel, per, left), out_shape=(jax...  1.71 us
    slice x1, local copies, waits for them, and re-layouts, panels(): return [x[:, i:i + PANEL] for i in range(0, x.shape[1], PANEL)]  0.7 us
    pallas_call x1, Pallas kernels, base_value(): pl.pallas_call(base_kernel, out_shape=jax.ShapeDtypeStruct((rows, cols),...  0.65 us
    ppermute x1, starting transfers between devices, body(): hid_other = lax.ppermute(hidden_in, 'tensor', swap)  0.52 us
  transfers between devices with their start and end apart: 7, of which 2 were waited for; matrix products, arithmetic and copies ran while one was open for 5% of the time, Pallas kernels for 36%

profile of v26, /device:TPU:0, one launch (start us, length us, event | category | flops | bytes accessed | tf_op | source)
XLA Modules:
  0.0 22.7 jit_solution(2568829326396045921)
XLA Ops:
  0.6 0.0 copy-start
  0.6 0.5 %collective-permute-start.3 = (bf16[4,4096]{1,0:T(4,128)(2,1)}, bf16[4,4096]{1,0:T(4,128)(2,1)S(1)}, u32[]{:S(2)}, u32[]{:S(2)}) collective-permute-start(bf16[4,4096]{1,0:T(4,128)(2,1)} %param.10), channel_id=1, source_target_pairs={{0,1},{1,0},{2,3},{3,2},{4,5},{5,4},{6,7},{7,6},{8,9},{9,8},{10,11... | collective-permute-start | bytes 98312 | tf_op jit(solution)/shard_map/ppermute | solution.py:381
  1.2 0.7 %fusion.1 = (bf16[8,128]{1,0:T(8,128)(2,1)S(1)}, bf16[8,128]{1,0:T(8,128)(2,1)S(1)}) fusion(bf16[8,256]{1,0:T(8,128)(2,1)} %param.18), kind=kLoop, calls=%fused_computation.34 | loop fusion | bytes 8192 | tf_op jit(solution)/shard_map/slice | solution.py:333
  1.9 0.0 copy-done
  1.9 3.8 %collective-permute-start = (bf16[1,272,128]{2,1,0:T(8,128)(2,1)S(1)}, bf16[1,272,128]{2,1,0:T(8,128)(2,1)S(1)}, u32[]{:S(2)}, u32[]{:S(2)}) collective-permute-start(bf16[1,272,128]{2,1,0:T(8,128)(2,1)S(1)} %bitcast.13), channel_id=1, source_target_pairs={{0,8},{1,9},{2,10},{3,11},{4,12},{5,13},{6,14},{7,15},{8,0},{9,1},... | collective-permute-start | bytes 208904 | tf_op jit(solution)/shard_map/ppermute | solution.py:367
  5.7 2.8 %attend_cache.2 = (f32[2,16,128]{2,1,0:T(8,128)S(1)}, f32[2,16,128]{2,1,0:T(8,128)S(1)}) custom-call(s32[4]{0:T(128)} %lengths_hbm.3, bf16[4,2048]{1,0:T(4,128)(2,1)} %q_hbm.3, bf16[4,256]{1,0:T(4,128)(2,1)} %own_k_hbm.3, bf16[4,1024,256]{2,1,0:T(8,128)(2,1)} %k_hbm.3, bf16[4,1024,256]{2,1,0:T(8,128)(2,1)} %v_hbm.3, bf16[1,272,128]{2,1,0:T(8,128)(2,1)S(1)} %bitcast.14), custom_call_target="tpu_custom_call" | custom-call | flops 33554432 | bytes 2097152 | tf_op jit(solution)/shard_map/attend_cache/pallas_call | solution.py:113
  8.5 1.4 %collective-permute-done = bf16[1,272,128]{2,1,0:T(8,128)(2,1)S(1)} collective-permute-done((bf16[1,272,128]{2,1,0:T(8,128)(2,1)S(1)}, bf16[1,272,128]{2,1,0:T(8,128)(2,1)S(1)}, u32[]{:S(2)}, u32[]{:S(2)}) %collective-permute-start) | collective-permute-done | bytes 69664 | tf_op jit(solution)/shard_map/ppermute | solution.py:367
  10.0 0.8 %collective-permute-start.2 = (bf16[2,272,128]{2,1,0:T(8,128)(2,1)S(1)}, bf16[2,272,128]{2,1,0:T(8,128)(2,1)S(1)}, u32[]{:S(2)}, u32[]{:S(2)}) collective-permute-start(bf16[2,272,128]{2,1,0:T(8,128)(2,1)S(1)} %pad_maximum_fusion.1.rest_1_), channel_id=1, source_target_pairs={{0,4},{1,3},{2,6},{3,1},{4,0},{5,7},{6,2},{7,5},{8,12},{9,11},{10,... | collective-permute-start | bytes 417800 | tf_op jit(solution)/shard_map/ppermute | solution.py:367
  10.8 0.1 pad_add_fusion
  10.9 1.6 %collective-permute-start.5 = (bf16[2,272,128]{2,1,0:T(8,128)(2,1)S(1)}, bf16[2,272,128]{2,1,0:T(8,128)(2,1)S(1)}, u32[]{:S(2)}, u32[]{:S(2)}) collective-permute-start(bf16[2,272,128]{2,1,0:T(8,128)(2,1)S(1)} %pad_maximum_fusion.1.rest_1_), channel_id=1, source_target_pairs={{0,2},{1,5},{2,0},{3,7},{4,6},{5,1},{6,4},{7,3},{8,10},{9,13},{10,... | collective-permute-start | bytes 417800 | tf_op jit(solution)/shard_map/ppermute | solution.py:367
  12.5 1.2 %collective-permute-start.1 = (bf16[2,272,128]{2,1,0:T(8,128)(2,1)S(1)}, bf16[2,272,128]{2,1,0:T(8,128)(2,1)S(1)}, u32[]{:S(2)}, u32[]{:S(2)}) collective-permute-start(bf16[2,272,128]{2,1,0:T(8,128)(2,1)S(1)} %pad_maximum_fusion.1.rest_1_), channel_id=1, source_target_pairs={{0,6},{1,7},{2,4},{3,5},{4,2},{5,3},{6,0},{7,1},{8,14},{9,15},{10,... | collective-permute-start | bytes 417800 | tf_op jit(solution)/shard_map/ppermute | solution.py:367
  13.6 2.9 %attend_cache.3 = (f32[2,16,128]{2,1,0:T(8,128)S(1)}, f32[2,16,128]{2,1,0:T(8,128)S(1)}, bf16[8192,256]{1,0:T(8,128)(2,1)S(1)}) custom-call(s32[4]{0:T(128)} %lengths_hbm.3, bf16[4,2048]{1,0:T(4,128)(2,1)} %q_hbm.3, bf16[4,256]{1,0:T(4,128)(2,1)} %own_k_hbm.3, bf16[4,1024,256]{2,1,0:T(8,128)(2,1)} %k_hbm.3, bf16[4,1024,256]{2,1,0:T(8,128)(2,1)} %v_hbm.3, ...), custom_call_target="tpu_custom_call" | custom-call | flops 33554432 | bytes 2097152 | tf_op jit(solution)/shard_map/attend_cache/pallas_call | solution.py:113
  16.6 0.0 collective-permute-done.3
  16.6 0.0 collective-permute-done.2
  16.6 0.1 select_reduce_fusion
  16.7 0.1 collective-permute-start.4
  16.9 0.7 %base_value.1.base_ref = f32[4,256]{1,0:T(4,128)S(1)} custom-call(bf16[4,8192]{1,0:T(4,128)(2,1)S(1)} %maximum_select_fusion.features_ref, bf16[8192,256]{1,0:T(8,128)(2,1)S(1)} %get-tuple-element.48.served_ref, bf16[4,272,128]{2,1,0:T(8,128)(2,1)S(1)} %pad_maximum_fusion.after.slabs_ref), custom_call_target="tpu_custom_call" | custom-call | flops 16777216 | tf_op jit(solution)/shard_map/base_value/pallas_call | solution.py:149
  17.6 0.0 collective-permute-done.5
  17.6 1.5 %collective-permute-done.1 = bf16[2,272,128]{2,1,0:T(8,128)(2,1)S(1)} collective-permute-done((bf16[2,272,128]{2,1,0:T(8,128)(2,1)S(1)}, bf16[2,272,128]{2,1,0:T(8,128)(2,1)S(1)}, u32[]{:S(2)}, u32[]{:S(2)}) %collective-permute-start.1) | collective-permute-done | bytes 139296 | tf_op jit(solution)/shard_map/ppermute | solution.py:367
  19.1 0.0 collective-permute-done.4.crossed_ref
  19.1 0.1 collective-permute-start.6
  19.2 1.7 %merge_blocks.1 = (bf16[8192,256]{1,0:T(8,128)(2,1)}, f32[4,64]{1,0:T(4,128)S(1)}, bf16[64,256]{1,0:T(8,128)(2,1)S(1)}, bf16[6,512,256]{2,1,0:T(8,128)(2,1)S(1)}) custom-call(s32[1,16]{1,0:T(1,128)S(1)} %add_bitcast_fusion.start_ref, bf16[64,64]{1,0:T(8,128)(2,1)S(1)} %select_convert_fusion.pick_ref, bf16[4,8192]{1,0:T(4,128)(2,1)S(1)} %maximum_select_fusion.features_ref, ...), custom_call_target="tpu_custom_call" | custom-call | flops 201326592 | bytes 6291456 | tf_op jit(solution)/shard_map/merge_blocks/pallas_call | solution.py:279
  20.9 0.0 collective-permute-done.6.last_ref
  20.9 1.7 %finish_rows.1 = (bf16[8192,256]{1,0:T(8,128)(2,1)}, bf16[4,256]{1,0:T(4,128)(2,1)}, bf16[4,2048]{1,0:T(4,128)(2,1)}) custom-call(s32[1,16]{1,0:T(1,128)S(1)} %add_bitcast_fusion.start_ref, bf16[64,256]{1,0:T(8,128)(2,1)S(1)} %get-tuple-element.54.up_ref, bf16[4,8192]{1,0:T(4,128)(2,1)S(1)} %maximum_select_fusion.features_ref, ...), custom_call_target="tpu_custom_call", output_to_operand_aliasing={{0}: (6, {})} | custom-call | flops 67108864 | bytes 2097152 | tf_op jit(solution)/shard_map/finish_rows/pallas_call | solution.py:308
  (24 shorter events, 0.3 us)
Async XLA Ops:
  0.6 1.2 %copy-start = (bf16[64,1024]{1,0:T(8,128)(2,1)S(1)}, bf16[64,1024]{1,0:T(8,128)(2,1)}, u32[]{:S(2)}) copy-start(bf16[64,1024]{1,0:T(8,128)(2,1)} %param.17) | copy-start | bytes 393220
  0.6 15.9 %collective-permute-start.3 = (bf16[4,4096]{1,0:T(4,128)(2,1)}, bf16[4,4096]{1,0:T(4,128)(2,1)S(1)}, u32[]{:S(2)}, u32[]{:S(2)}) collective-permute-start(bf16[4,4096]{1,0:T(4,128)(2,1)} %param.10), channel_id=1, source_target_pairs={{0,1},{1,0},{2,3},{3,2},{4,5},{5,4},{6,7},{7,6},{8,9},{9,8},{10,11... | collective-permute-start | bytes 98312 | tf_op jit(solution)/shard_map/ppermute | solution.py:381
  1.9 8.0 %collective-permute-start = (bf16[1,272,128]{2,1,0:T(8,128)(2,1)S(1)}, bf16[1,272,128]{2,1,0:T(8,128)(2,1)S(1)}, u32[]{:S(2)}, u32[]{:S(2)}) collective-permute-start(bf16[1,272,128]{2,1,0:T(8,128)(2,1)S(1)} %bitcast.13), channel_id=1, source_target_pairs={{0,8},{1,9},{2,10},{3,11},{4,12},{5,13},{6,14},{7,15},{8,0},{9,1},... | collective-permute-start | bytes 208904 | tf_op jit(solution)/shard_map/ppermute | solution.py:367
  10.0 6.6 %collective-permute-start.2 = (bf16[2,272,128]{2,1,0:T(8,128)(2,1)S(1)}, bf16[2,272,128]{2,1,0:T(8,128)(2,1)S(1)}, u32[]{:S(2)}, u32[]{:S(2)}) collective-permute-start(bf16[2,272,128]{2,1,0:T(8,128)(2,1)S(1)} %pad_maximum_fusion.1.rest_1_), channel_id=1, source_target_pairs={{0,4},{1,3},{2,6},{3,1},{4,0},{5,7},{6,2},{7,5},{8,12},{9,11},{10,... | collective-permute-start | bytes 417800 | tf_op jit(solution)/shard_map/ppermute | solution.py:367
  10.9 5.7 %copy-start.2 = (s32[8]{0:T(128)S(1)}, s32[8]{0:T(128)}, u32[]{:S(2)}) copy-start(s32[8]{0:T(128)} %param.19) | copy-start | bytes 100
  10.9 5.9 %copy-start.1 = (bf16[4,4096]{1,0:T(4,128)(2,1)S(1)}, bf16[4,4096]{1,0:T(4,128)(2,1)}, u32[]{:S(2)}) copy-start(bf16[4,4096]{1,0:T(4,128)(2,1)} %param.10) | copy-start | bytes 98308
  10.9 6.7 %collective-permute-start.5 = (bf16[2,272,128]{2,1,0:T(8,128)(2,1)S(1)}, bf16[2,272,128]{2,1,0:T(8,128)(2,1)S(1)}, u32[]{:S(2)}, u32[]{:S(2)}) collective-permute-start(bf16[2,272,128]{2,1,0:T(8,128)(2,1)S(1)} %pad_maximum_fusion.1.rest_1_), channel_id=1, source_target_pairs={{0,2},{1,5},{2,0},{3,7},{4,6},{5,1},{6,4},{7,3},{8,10},{9,13},{10,... | collective-permute-start | bytes 417800 | tf_op jit(solution)/shard_map/ppermute | solution.py:367
  12.5 6.7 %collective-permute-start.1 = (bf16[2,272,128]{2,1,0:T(8,128)(2,1)S(1)}, bf16[2,272,128]{2,1,0:T(8,128)(2,1)S(1)}, u32[]{:S(2)}, u32[]{:S(2)}) collective-permute-start(bf16[2,272,128]{2,1,0:T(8,128)(2,1)S(1)} %pad_maximum_fusion.1.rest_1_), channel_id=1, source_target_pairs={{0,6},{1,7},{2,4},{3,5},{4,2},{5,3},{6,0},{7,1},{8,14},{9,15},{10,... | collective-permute-start | bytes 417800 | tf_op jit(solution)/shard_map/ppermute | solution.py:367
  16.7 2.4 %collective-permute-start.4 = (bf16[4,272,128]{2,1,0:T(8,128)(2,1)S(1)}, bf16[4,272,128]{2,1,0:T(8,128)(2,1)S(1)}, u32[]{:S(2)}, u32[]{:S(2)}) collective-permute-start(bf16[4,272,128]{2,1,0:T(8,128)(2,1)S(1)} %pad_maximum_fusion.after.slabs_ref), channel_id=1, source_target_pairs={{0,1},{1,0},{2,3},{3,2},{4,5},{5,4},{6,7},{7,6},{8,9},{9,8},{10,11... | collective-permute-start | bytes 835592 | tf_op jit(solution)/shard_map/ppermute | solution.py:426
  19.1 1.8 %collective-permute-start.6 = (bf16[4,272,128]{2,1,0:T(8,128)(2,1)S(1)}, bf16[4,272,128]{2,1,0:T(8,128)(2,1)S(1)}, u32[]{:S(2)}, u32[]{:S(2)}) collective-permute-start(bf16[4,272,128]{2,1,0:T(8,128)(2,1)S(1)} %constant_dynamic-update-slice_fusion.5.last_ref), channel_id=1, source_target_pairs={{0,1},{1,0},{2,3},{3,2},{4,5},{5,4},{6,7},{7,6},{8,9},{9,8},{10,11... | collective-permute-start | bytes 835592 | tf_op jit(solution)/shard_map/ppermute | solution.py:432
